TPU v7x, 512 devices: a whole 4x4x16 slice. The times are simulated.
512 devices in a mesh: dp: 128 (over z_hi, x, y, core), width: 4 (over z_lo).
Axes of the slice: x: 4, y: 4, z: 16 (z_hi: 4, z_lo: 4; z = z_hi * 4 + z_lo), core: 2. Of those that a mesh axis runs over, the one named last changes fastest.
Arguments:
- image: bfloat16 [16384, 1152], P('dp', 'width'), may hold values from -4 to 4
- text: bfloat16 [16384, 1152], P('dp', 'width'), may hold values from -8 to 8
- log_temp: float32 [], replicated, may hold values from 2.7 to 2.9
- bias: float32 [], replicated, may hold values from -8 to -7
Outputs:
- loss: float32 [], replicated
- grad_image: bfloat16 [16384, 1152], P('dp', 'width')
- grad_text: bfloat16 [16384, 1152], P('dp', 'width')
- grad_log_temp: float32 [], replicated
- grad_bias: float32 [], replicated
All inputs are finite; a program needn't handle non-finite values.
Results may differ from a plain program's by a relative error of at most 0.0052.
Values may be sent and summed in bfloat16 or wider, within the bound.
No kernel may reach another device: no remote copies, remote signals or barrier semaphores. Data moves between devices by JAX's collectives and lax.ppermute only.
A program may use at most 64 MiB of HBM per device.

v0:
```python
import jax
import jax.numpy as jnp
from jax import lax
from jax.sharding import PartitionSpec as P

epsilon = 1e-06


def unit_rows(rows_in):
    values = rows_in.astype(jnp.float32)
    inverse = lax.rsqrt(jnp.sum(values * values, axis=1, keepdims=True) + epsilon)
    return (values * inverse, inverse)


def block_terms(left, right, left_ids, right_ids, scale, bias):
    product = lax.dot_general(
        left, right, (((1,), (1,)), ((), ())), preferred_element_type=jnp.float32
    )
    logits = scale * product + bias
    signs = jnp.where(left_ids[:, None] == right_ids[None, :], 1.0, -1.0).astype(jnp.float32)
    slope = -signs * jax.nn.sigmoid(-signs * logits)
    weights = (scale * slope).astype(jnp.bfloat16)
    sums = (
        jnp.sum(jax.nn.softplus(-signs * logits)),
        jnp.sum(slope * product) * scale,
        jnp.sum(slope),
    )
    return (weights, sums)


def unit_back(grad, unit, inverse):
    return (grad - unit * jnp.sum(unit * grad, axis=1, keepdims=True)) * inverse


def shards(image, text, log_temp, bias):
    rows = image.shape[0]
    local_width = image.shape[1]
    quarter = rows // lax.axis_size("width")
    blocks = lax.axis_size("dp")
    full_image, full_text = (
        lax.all_gather(image, "width", axis=1, tiled=True),
        lax.all_gather(text, "width", axis=1, tiled=True),
    )
    image_unit, image_inverse = unit_rows(full_image)
    text_unit, text_inverse = unit_rows(full_text)
    image_half = image_unit.astype(jnp.bfloat16)
    text_half = text_unit.astype(jnp.bfloat16)
    column = lax.axis_index("width")
    block = lax.axis_index("dp")
    offset = column * quarter
    home = block * rows
    home_ids = home + lax.iota(jnp.int32, rows)
    text_piece = lax.dynamic_slice_in_dim(text_half, offset, quarter, 0)
    image_piece = lax.dynamic_slice_in_dim(image_half, offset, quarter, 0)
    scale = jnp.exp(log_temp)

    def piece_ids(count):
        spot = lax.iota(jnp.int32, count)
        return spot // quarter * rows + offset + spot % quarter

    piece = lax.all_gather(text_piece, "dp", axis=0, tiled=True)
    weights, sums = block_terms(image_half, piece, home_ids, piece_ids(piece.shape[0]), scale, bias)
    grad = jnp.dot(weights, piece, preferred_element_type=jnp.float32)
    totals = tuple((term for term in sums))
    piece = lax.all_gather(image_piece, "dp", axis=0, tiled=True)
    weights, unused = block_terms(
        text_half, piece, home_ids, piece_ids(piece.shape[0]), scale, bias
    )
    grad_text_unit = jnp.dot(weights, piece, preferred_element_type=jnp.float32)
    loss_total, temp_total, bias_total = lax.psum(
        (totals[0], totals[1], totals[2]), ("dp", "width")
    )
    count = rows * blocks
    start_column = column * local_width
    image_all, text_all = lax.psum((grad, grad_text_unit), "width")
    image_final = unit_back(image_all, image_unit, image_inverse)
    text_final = unit_back(text_all, text_unit, text_inverse)
    grad_image = lax.dynamic_slice_in_dim(image_final, start_column, local_width, 1).astype(
        jnp.bfloat16
    )
    grad_text = lax.dynamic_slice_in_dim(text_final, start_column, local_width, 1).astype(
        jnp.bfloat16
    )
    return (loss_total / count, grad_image, grad_text, temp_total / count, bias_total / count)


def solution(mesh):
    placed = (P("dp", "width"), P("dp", "width"), P(), P())
    return jax.shard_map(
        shards,
        mesh=mesh,
        in_specs=placed,
        out_specs=(P(), P("dp", "width"), P("dp", "width"), P(), P()),
        check_vma=False,
    )
```

profile of v0, /device:TPU:1, one launch (start us, length us, event | category | flops | bytes accessed | tf_op | source)
XLA Modules:
  0.0 454.1 jit_solution(8848302695284347237)
XLA Ops:
  7.2 0.0 copy-start
  7.2 0.0 all-gather.5.cloned.1.call-start
  7.2 14.0 %all_gather.12 = bf16[128,1152]{0,1:T(8,128)(2,1)S(1)} all-gather(bf16[128,288]{0,1:T(8,128)(2,1)} %param.4), channel_id=1, replica_groups=mesh['dp'=128,'width'=4] {'width'}, dimensions={1}, use_global_device_ids=true | all-gather | bytes 368640 | tf_op jit(solution)/shard_map/all_gather | solution.py:41
  21.2 0.2 copy.13
  21.4 0.1 fusion.19
  21.6 0.1 fusion.37
  21.7 0.6 constant_dynamic-slice_fusion
  22.3 0.0 all-gather.5.cloned.1.call-update
  22.4 0.0 all-gather.3.cloned.1.call-start
  22.4 0.0 copy-done
  22.4 11.7 %all_gather.13 = bf16[128,1152]{0,1:T(8,128)(2,1)S(1)} all-gather(bf16[128,288]{0,1:T(8,128)(2,1)S(1)} %copy-done), channel_id=1, replica_groups=mesh['dp'=128,'width'=4] {'width'}, dimensions={1}, use_global_device_ids=true | all-gather | bytes 368640 | tf_op jit(solution)/shard_map/all_gather | solution.py:42
  34.1 0.2 copy.14
  34.3 0.1 fusion.20
  34.5 0.1 fusion.38
  34.6 0.6 constant_dynamic-slice_fusion.1
  35.3 0.0 all-gather.3.cloned.1.call-update
  35.3 0.0 all-reduce.4.cloned.1.call-start
  36.7 138.0 %all-gather.5.cloned.1.call-done = bf16[4096,1152]{1,0:T(8,128)(2,1)} async-done(((bf16[32,1152]{1,0:T(8,128)(2,1)}), bf16[4096,1152]{1,0:T(8,128)(2,1)}) %all-gather.5.cloned.1.call-update) | async-done | bytes 9437200 | tf_op jit(solution)/shard_map/all_gather | solution.py:65
  174.7 12.0 %fusion.10 = f32[128,1152]{1,0:T(8,128)} fusion(bf16[4096,1152]{1,0:T(8,128)(2,1)} %all-gather.5.cloned.1.call-done, bf16[128,1152]{1,0:T(8,128)(2,1)S(1)} %fusion.38, f32[]{:T(128)S(6)} %copy.20, f32[]{:T(128)S(6)} %exp.13, s32[4096]{0:T(1024)S(1)} %fusion.33, s32[128]{0:T(128)S(1)} %iota_add_fusion), kind=kOutput, calls=%fused_computation.17 | convolution fusion | flops 2422210560 | bytes 10338824 | tf_op jit(solution)/shard_map/dot_general | solution.py:69
  186.6 135.0 %all-gather.3.cloned.1.call-done = bf16[4096,1152]{1,0:T(8,128)(2,1)} async-done(((bf16[32,1152]{1,0:T(8,128)(2,1)}), bf16[4096,1152]{1,0:T(8,128)(2,1)}) %all-gather.3.cloned.1.call-update) | async-done | bytes 9437200 | tf_op jit(solution)/shard_map/all_gather | solution.py:61
  321.7 0.0 copy-start.1
  321.7 8.6 %fusion.39 = (f32[]{:T(128)}, f32[]{:T(128)}, f32[]{:T(128)}, f32[128,4096]{1,0:T(8,128)S(1)}) fusion(f32[]{:T(128)S(6)} %copy.20, f32[]{:T(128)S(6)} %exp.13, s32[4096]{0:T(1024)S(1)} %fusion.33, s32[128]{0:T(128)S(1)} %iota_add_fusion, bf16[128,1152]{1,0:T(8,128)(2,1)S(1)} %fusion.37, bf16[4096,1152]{1,0:T(8,128)(2,1)} %all-gather.3.cloned.1.call-done), kind=kOutput, calls=%fused_computation.65 | convolution fusion | flops 1218445312 | bytes 11846164 | tf_op jit(solution)/shard_map/dot_general | solution.py:16
  330.3 0.0 copy-done.1
  330.3 2.8 fusion.11
  333.1 0.0 all-reduce.4.cloned.1.call-update
  333.8 103.0 %all-reduce = (f32[]{:T(128)}, f32[]{:T(128)}, f32[]{:T(128)}) all-reduce(f32[]{:T(128)} %get-tuple-element.17, f32[]{:T(128)S(6)} %mul.138, f32[]{:T(128)} %get-tuple-element.15), channel_id=1, replica_groups=mesh['dp'=128,'width'=4] {'dp','width'}, use_global_device_ids=true, to_apply=%region_3.4 | all-reduce | flops 3 | bytes 24 | tf_op jit(solution)/shard_map/psum | solution.py:70
  438.8 0.0 all-reduce.4.cloned.1.call-done
  438.8 1.6 multiply_reduce_fusion.1
  440.4 1.2 fusion.24
  441.5 0.7 copy.15
  442.3 1.2 fusion.22
  443.5 0.7 copy.16
  (4 shorter events, 0.0 us)
Async XLA Ops:
  7.2 15.3 %copy-start = (bf16[128,288]{0,1:T(8,128)(2,1)S(1)}, bf16[128,288]{0,1:T(8,128)(2,1)}, u32[]{:S(2)}) copy-start(bf16[128,288]{0,1:T(8,128)(2,1)} %param.5) | copy-start | bytes 221188
  7.2 167.5 %all-gather.5.cloned.1.call-start = ((), (), s32[]{:S(2)}) async-start(), calls=%async_computation.1 | async-start | bytes 9510912 | tf_op jit(solution)/shard_map/all_gather | solution.py:65
  22.4 299.3 %all-gather.3.cloned.1.call-start = ((), (), s32[]{:S(2)}) async-start(), calls=%async_computation | async-start | bytes 9510912 | tf_op jit(solution)/shard_map/all_gather | solution.py:61
  35.3 403.5 %all-reduce.4.cloned.1.call-start = ((), (), s32[]{:S(2)}) async-start(), calls=%async_computation.2 | async-start | bytes 2359296 | tf_op jit(solution)/shard_map/psum | solution.py:75
  321.7 8.6 %copy-start.1 = (bf16[4096,1152]{1,0:T(8,128)(2,1)S(1)}, bf16[4096,1152]{1,0:T(8,128)(2,1)}, u32[]{:S(2)}) copy-start(bf16[4096,1152]{1,0:T(8,128)(2,1)} %all-gather.3.cloned.1.call-done) | copy-start | bytes 28311556
Sparse Core Ops, SparseCore 0:
  22.5 152.1 all-gather.4
  179.7 141.9 all-gather.2
  333.3 75.9 all-reduce.3
where the time goes:
time: 455 us; the launch traced here: 454 us
  waiting for transfers between devices  273 us (60%)
  blocking collectives  129 us (28%)
  matrix products  23.4 us (5%)
  between operations  21.2 us (5%)
    all_gather x1, waiting for transfers between devices, shards(): piece = lax.all_gather(image_piece, 'dp', axis=0, tiled=True)  138 us
    all_gather x1, waiting for transfers between devices, shards(): piece = lax.all_gather(text_piece, 'dp', axis=0, tiled=True)  135 us
    psum x1, blocking collectives, shards(): lax.psum((totals[0], totals[1], totals[2]), ('dp', 'width'))  103 us
    all_gather x1, blocking collectives, shards(): lax.all_gather(image, 'width', axis=1, tiled=True)  14 us
    dot_general x1, matrix products, shards(): grad_text_unit = jnp.dot(weights, piece, preferred_element_type=jnp.float32)  12 us
    all_gather x1, blocking collectives, shards(): lax.all_gather(text, 'width', axis=1, tiled=True)  11.7 us
  transfers between devices with their start and end apart: 3, of which 2 were waited for; matrix products, arithmetic and copies ran while one was open for 3% of the time, Pallas kernels for 0%

commit v1 on v0

v1 whole, which is shorter than its diff:
```python
import functools
import math

import jax
import jax.numpy as jnp
from jax import lax
from jax.experimental import pallas as pl
from jax.experimental.pallas import tpu as pltpu
from jax.sharding import Mesh, PartitionSpec as P

epsilon = 1e-06
log2e = 1.0 / math.log(2.0)


def unit_rows(rows_in):
    values = rows_in.astype(jnp.float32)
    inverse = lax.rsqrt(jnp.sum(values * values, axis=1, keepdims=True) + epsilon)
    return (values * inverse, inverse)


def unit_back(grad, unit, inverse):
    return (grad - unit * jnp.sum(unit * grad, axis=1, keepdims=True)) * inverse


def fold(values):
    rows, columns = values.shape
    part = jnp.sum(values.reshape(rows // 8, 8, columns), axis=0)
    return sum(part[:, c : c + 128] for c in range(0, columns, 128))


def pair_kernel(params, left_ids, right_ids, left, right, back, weights_out, sums_out):
    scale = params[0]
    bias = params[1]
    rows = left.shape[0]
    tile = 256
    loss_sum = jnp.zeros((8, 128), jnp.float32)
    temp_sum = jnp.zeros((8, 128), jnp.float32)
    bias_sum = jnp.zeros((8, 128), jnp.float32)
    for start in range(0, rows, tile):
        here = pl.ds(start, tile)
        product = lax.dot_general(
            left[here, :], right[...], (((1,), (1,)), ((), ())), preferred_element_type=jnp.float32
        )
        logits = scale * product + bias
        same = left_ids[here, :] == right_ids[...]
        turned = jnp.where(same, -logits, logits)
        grown = jnp.exp(turned)
        share = grown / (1.0 + grown)
        slope = jnp.where(same, -share, share)
        weights = (scale * slope).astype(jnp.bfloat16)
        weights_out[here, :] = weights
        back[here, :] = jnp.dot(
            weights, right[...], preferred_element_type=jnp.float32
        ).astype(jnp.bfloat16)
        quarter = tile // 4
        a, b, c, d = (grown[k * quarter : (k + 1) * quarter, :] for k in range(4))
        ab = a + (b + a * b)
        cd = c + (d + c * d)
        loss_sum += fold(jnp.log1p(ab + (cd + ab * cd)))
        temp_sum += fold(slope * product)
        bias_sum += fold(slope)
    sums_out[0:8, :] = loss_sum
    sums_out[8:16, :] = temp_sum
    sums_out[16:24, :] = bias_sum


def pair_block(params, left_ids, right_ids, left, right):
    rows, width = left.shape
    columns = right.shape[0]
    vmem = pl.BlockSpec(memory_space=pltpu.VMEM)
    return pl.pallas_call(
        pair_kernel,
        out_shape=(
            jax.ShapeDtypeStruct((rows, width), jnp.bfloat16),
            jax.ShapeDtypeStruct((rows, columns), jnp.bfloat16),
            jax.ShapeDtypeStruct((24, 128), jnp.float32),
        ),
        in_specs=[pl.BlockSpec(memory_space=pltpu.SMEM)] + [vmem] * 4,
        out_specs=(vmem, vmem, vmem),
        compiler_params=pltpu.CompilerParams(vmem_limit_bytes=48 * 1024 * 1024),
        cost_estimate=pl.CostEstimate(
            flops=4 * rows * columns * width,
            bytes_accessed=6 * rows * width,
            transcendentals=2 * rows * columns,
        ),
        name="pair_block",
    )(params, left_ids, right_ids, left, right)


def text_kernel(first_weights, second_weights, first, second, back):
    contract = (((0,), (0,)), ((), ()))
    total = lax.dot_general(
        first_weights[...], first[...], contract, preferred_element_type=jnp.float32
    ) + lax.dot_general(
        second_weights[...], second[...], contract, preferred_element_type=jnp.float32
    )
    back[...] = total.astype(jnp.bfloat16)


def text_block(first_weights, second_weights, first, second):
    rows, width = first.shape
    columns = first_weights.shape[1]
    vmem = pl.BlockSpec(memory_space=pltpu.VMEM)
    return pl.pallas_call(
        text_kernel,
        out_shape=jax.ShapeDtypeStruct((columns, width), jnp.bfloat16),
        in_specs=[vmem] * 4,
        out_specs=vmem,
        compiler_params=pltpu.CompilerParams(vmem_limit_bytes=48 * 1024 * 1024),
        cost_estimate=pl.CostEstimate(
            flops=4 * rows * columns * width,
            bytes_accessed=8 * rows * width,
            transcendentals=0,
        ),
        name="text_block",
    )(first_weights, second_weights, first, second)


def spread(rows, axis):
    count = lax.axis_size(axis)
    return lax.all_to_all(jnp.broadcast_to(rows[None], (count,) + rows.shape), axis, 0, 0)


def swap_core(value):
    return lax.ppermute(value, "core", [(0, 1), (1, 0)])


def total_over(value, axis):
    count = lax.axis_size(axis)
    parts = lax.all_to_all(jnp.broadcast_to(value[None], (count,) + value.shape), axis, 0, 0)
    return jnp.sum(parts, axis=0)


def shards(image, text, log_temp, bias):
    rows, strip = image.shape
    zl_count = lax.axis_size("zl")
    zh_count = lax.axis_size("zh")
    x_count = lax.axis_size("x")
    y_count = lax.axis_size("y")
    width = strip * zl_count
    piece = rows // zl_count
    zh, x, y, core, zl = (lax.axis_index(name) for name in ("zh", "x", "y", "core", "zl"))
    scale = jnp.exp(log_temp)

    packed = jnp.concatenate(
        [
            image.reshape(zl_count, piece, strip),
            jnp.broadcast_to(text[None], (zl_count, rows, strip)),
        ],
        axis=1,
    )
    arrived = lax.all_to_all(packed, "zl", 0, 0)
    image_own = arrived[:, :piece].transpose(1, 0, 2).reshape(piece, width)
    text_own = arrived[:, piece:].transpose(1, 0, 2).reshape(rows, width)
    image_unit, image_inverse = unit_rows(image_own)
    text_unit, text_inverse = unit_rows(text_own)

    image_rows = spread(image_unit.astype(jnp.bfloat16), "zh").reshape(zh_count * piece, width)
    text_rows = spread(text_unit.astype(jnp.bfloat16), "y").reshape(y_count * rows, width)
    image_rows = spread(image_rows, "x").reshape(x_count * zh_count * piece, width)
    other_rows = swap_core(image_rows)

    count = image_rows.shape[0]
    left_spot = lax.iota(jnp.int32, count) - (x * zh_count + zh) * piece
    left_ids = jnp.where((left_spot >= 0) & (left_spot < piece), left_spot, -1)[:, None]
    right_ids = (lax.iota(jnp.int32, y_count * rows) - (y * rows + zl * piece))[None, :]
    right_ids = jnp.where(right_ids >= 0, right_ids, -2)
    none_ids = jnp.full_like(left_ids, -1)
    params = jnp.stack([scale, bias])

    own_back, own_weights, own_sums = pair_block(params, left_ids, right_ids, image_rows, text_rows)
    other_back, other_weights, other_sums = pair_block(
        params, none_ids, right_ids, other_rows, text_rows
    )
    given_back = swap_core(other_back)
    text_back = text_block(own_weights, other_weights, image_rows, other_rows)

    sums = jnp.sum((own_sums + other_sums).reshape(3, 8, 128), axis=1)
    sums = total_over(sums, ("x", "y"))
    sums = total_over(sums, ("zh", "zl"))
    sums = jnp.sum(sums, axis=1)
    sums = sums + swap_core(sums)

    image_back = (own_back.astype(jnp.float32) + given_back.astype(jnp.float32)).astype(jnp.bfloat16)
    image_back = lax.all_to_all(image_back.reshape(x_count, zh_count * piece, width), "x", 0, 0)
    image_back = jnp.sum(image_back.astype(jnp.float32), axis=0).astype(jnp.bfloat16)
    image_back = lax.all_to_all(image_back.reshape(zh_count, piece, width), "zh", 0, 0)
    image_back = jnp.sum(image_back.astype(jnp.float32), axis=0)
    text_back = lax.all_to_all(text_back.reshape(y_count, rows, width), "y", 0, 0)
    text_back = jnp.sum(text_back.astype(jnp.float32), axis=0)

    image_final = unit_back(image_back, image_unit, image_inverse).astype(jnp.bfloat16)
    text_final = unit_back(text_back, text_unit, text_inverse).astype(jnp.bfloat16)
    packed = jnp.concatenate([image_final, text_final], axis=0)
    packed = packed.reshape(piece + rows, zl_count, strip).transpose(1, 0, 2)
    arrived = lax.all_to_all(packed, "zl", 0, 0)
    grad_image = arrived[:, :piece].reshape(rows, strip)
    grad_text = jnp.sum(arrived[:, piece:].astype(jnp.float32), axis=0).astype(jnp.bfloat16)

    pairs_count = rows * zh_count * x_count * y_count * 2
    return (
        sums[0] / pairs_count,
        grad_image,
        grad_text,
        scale * sums[1] / pairs_count,
        sums[2] / pairs_count,
    )


def solution(mesh):
    fine = Mesh(mesh.devices.reshape(4, 4, 4, 2, 4), ("zh", "x", "y", "core", "zl"))
    whole = P(("zh", "x", "y", "core"), "zl")
    return jax.shard_map(
        shards,
        mesh=fine,
        in_specs=(whole, whole, P(), P()),
        out_specs=(P(), whole, whole, P(), P()),
        check_vma=False,
    )
```

time: 455 us -> 225 us (0.49)
  the two profiles are of different devices: /device:TPU:1 before, /device:TPU:2 now
where the time goes in v1:
time: 225 us; the launch traced here: 224 us
  waiting for transfers between devices  86.3 us (38%)
  blocking collectives  52 us (23%)
  starting transfers between devices  44.2 us (20%)
  local copies, waits for them, and re-layouts  14.8 us (7%)
  other arithmetic  9.84 us (4%)
  Pallas kernels  9.22 us (4%)
  between operations  7.61 us (3%)
    all_to_all x1, blocking collectives, spread(): lax.all_to_all(jnp.broadcast_to(rows[None], (count,) + rows.shape), axis,...  32.5 us
    all_to_all x2, waiting for transfers between devices, spread(): lax.all_to_all(jnp.broadcast_to(rows[None], (count,) + rows.shape), axis,...  25.5 us
    all_to_all x1, blocking collectives, shards(): arrived = lax.all_to_all(packed, 'zl', 0, 0)  19.5 us
    all_to_all x1, waiting for transfers between devices, shards(): lax.all_to_all(image_back.reshape(zh_count, piece, width), 'zh', 0, 0)  17.1 us
    all_to_all x1, waiting for transfers between devices, shards(): lax.all_to_all(text_back.reshape(y_count, rows, width), 'y', 0, 0)  13.1 us
    all_to_all x2, waiting for transfers between devices, total_over(): lax.all_to_all(jnp.broadcast_to(value[None], (count,) + value.shape), axi...  12.6 us
    all_to_all x1, waiting for transfers between devices, shards(): lax.all_to_all(image_back.reshape(x_count, zh_count * piece, width), 'x',...  12.3 us
    all_to_all x2, starting transfers between devices, total_over(): lax.all_to_all(jnp.broadcast_to(value[None], (count,) + value.shape), axi...  9.5 us
  transfers between devices with their start and end apart: 11, of which 9 were waited for; matrix products, arithmetic and copies ran while one was open for 6% of the time, Pallas kernels for 2%

profile of v1, /device:TPU:2, one launch (start us, length us, event | category | flops | bytes accessed | tf_op | source)
XLA Modules:
  0.0 224.0 jit_solution(13751749522553210531)
XLA Ops:
  0.6 1.0 copy.66
  1.6 1.0 copy.67
  2.7 19.5 %all_to_all.50 = bf16[4,160,288]{2,1,0:T(8,128)(2,1)S(1)} all-to-all(bf16[4,160,288]{2,1,0:T(8,128)(2,1)S(1)} %pad_maximum_fusion), channel_id=1, replica_groups=mesh['zh'=4,'x'=4,'y'=4,'core'=2,'zl'=4] {'zl'}, dimensions={0} | all-to-all | bytes 737280 | tf_op jit(solution)/shard_map/all_to_all | solution.py:152
  22.8 32.5 %all_to_all.51 = bf16[4,32,1152]{2,1,0:T(8,128)(2,1)S(1)} all-to-all(bf16[4,32,1152]{2,1,0:T(8,128)(2,1)S(1)} %broadcast_in_dim.25), channel_id=1, replica_groups=mesh['zh'=4,'x'=4,'y'=4,'core'=2,'zl'=4] {'zh'}, dimensions={0} | all-to-all | bytes 589824 | tf_op jit(solution)/shard_map/all_to_all | solution.py:121
  55.3 1.1 broadcast_in_dim.27
  56.4 4.8 %all-to-all-start.2 = ((bf16[4,128,1152]{2,1,0:T(8,128)(2,1)}), bf16[4,128,1152]{2,1,0:T(8,128)(2,1)S(1)}, u32[]{:S(2)}, u32[]{:S(2)}) async-start(bf16[4,128,1152]{2,1,0:T(8,128)(2,1)} %broadcast_in_dim.27), calls=%async_computation.2 | async-start | bytes 2359296 | tf_op jit(solution)/shard_map/all_to_all | solution.py:121
  61.7 10.3 %all-to-all-done.2 = bf16[4,128,1152]{2,1,0:T(8,128)(2,1)S(1)} async-done(((bf16[4,128,1152]{2,1,0:T(8,128)(2,1)}), bf16[4,128,1152]{2,1,0:T(8,128)(2,1)S(1)}, u32[]{:S(2)}, u32[]{:S(2)}) %all-to-all-start.2) | async-done | bytes 1179680 | tf_op jit(solution)/shard_map/all_to_all | solution.py:121
  72.0 1.9 collective-permute-start
  74.2 1.1 broadcast_in_dim.28
  75.3 4.5 %all-to-all-start.3 = ((bf16[4,128,1152]{2,1,0:T(8,128)(2,1)}), bf16[4,128,1152]{2,1,0:T(8,128)(2,1)S(1)}, u32[]{:S(2)}, u32[]{:S(2)}) async-start(bf16[4,128,1152]{2,1,0:T(8,128)(2,1)} %broadcast_in_dim.28), calls=%async_computation.3 | async-start | bytes 2359296 | tf_op jit(solution)/shard_map/all_to_all | solution.py:121
  81.1 0.6 pad_maximum_fusion.1.params
  81.7 15.2 %all-to-all-done.3 = bf16[4,128,1152]{2,1,0:T(8,128)(2,1)S(1)} async-done(((bf16[4,128,1152]{2,1,0:T(8,128)(2,1)}), bf16[4,128,1152]{2,1,0:T(8,128)(2,1)S(1)}, u32[]{:S(2)}, u32[]{:S(2)}) %all-to-all-start.3) | async-done | bytes 1179680 | tf_op jit(solution)/shard_map/all_to_all | solution.py:121
  96.9 0.7 copy-done.6
  97.6 3.8 %pair_block.3 = (bf16[512,1152]{1,0:T(8,128)(2,1)}, bf16[512,512]{1,0:T(8,128)(2,1)S(1)}, f32[24,128]{1,0:T(8,128)S(1)}) custom-call(f32[2]{0:T(128)S(1)} %copy-done.6, s32[512,1]{1,0:T(8,128)S(1)} %broadcast_in_dim.21.left_ids, s32[1,512]{1,0:T(1,128)S(1)} %compare_select_fusion.right_ids, bf16[512,1152]{1,0:T(8,128)(2,1)S(1)} %collective-permute-done.left.second, ...), custom_call_target="tpu_custom_call" | custom-call | flops 1207959552 | bytes 3538944 | tf_op jit(solution)/shard_map/pair_block/pallas_call | solution.py:71
  101.4 0.8 copy-done.2
  102.2 1.9 collective-permute-start.2
  104.2 1.3 copy-done.1
  105.5 0.7 copy-done.7
  106.1 2.8 %pair_block.2 = (bf16[512,1152]{1,0:T(8,128)(2,1)S(1)}, bf16[512,512]{1,0:T(8,128)(2,1)S(1)}, f32[24,128]{1,0:T(8,128)S(1)}) custom-call(f32[2]{0:T(128)S(1)} %copy-done.7, s32[512,1]{1,0:T(8,128)S(1)} %fusion.5.left_ids, s32[1,512]{1,0:T(1,128)S(1)} %compare_select_fusion.right_ids, bf16[512,1152]{1,0:T(8,128)(2,1)S(1)} %bitcast.53, ...), custom_call_target="tpu_custom_call" | custom-call | flops 1207959552 | bytes 3538944 | tf_op jit(solution)/shard_map/pair_block/pallas_call | solution.py:71
  109.0 0.8 copy-done.4
  109.8 0.6 broadcast_in_dim.29
  110.4 5.3 %all-to-all-start.4 = ((f32[16,3,128]{2,1,0:T(4,128)}), f32[16,3,128]{2,1,0:T(4,128)}, u32[]{:S(2)}, u32[]{:S(2)}) async-start(f32[16,3,128]{2,1,0:T(4,128)} %broadcast_in_dim.29), calls=%async_computation.4 | async-start | bytes 65536 | tf_op jit(solution)/shard_map/all_to_all | solution.py:130
  115.8 2.6 %add_convert_fusion = bf16[512,1152]{1,0:T(8,128)(2,1)} fusion(bf16[512,1152]{1,0:T(8,128)(2,1)} %collective-permute-done.2, bf16[512,1152]{1,0:T(8,128)(2,1)S(1)} %get-tuple-element.13), kind=kLoop, calls=%fused_computation.1 | loop fusion | flops 2359296 | bytes 3538944 | tf_op jit(solution)/shard_map/convert_element_type | solution.py:184
  118.3 3.8 %all-to-all-done.4 = f32[16,3,128]{2,1,0:T(4,128)} async-done(((f32[16,3,128]{2,1,0:T(4,128)}), f32[16,3,128]{2,1,0:T(4,128)}, u32[]{:S(2)}, u32[]{:S(2)}) %all-to-all-start.4) | async-done | bytes 24608 | tf_op jit(solution)/shard_map/all_to_all | solution.py:130
  122.2 5.8 %all-to-all-start.6 = ((bf16[4,128,1152]{2,1,0:T(8,128)(2,1)}), bf16[4,128,1152]{2,1,0:T(8,128)(2,1)}, u32[]{:S(2)}, u32[]{:S(2)}) async-start(bf16[4,128,1152]{2,1,0:T(8,128)(2,1)} %bitcast.59), calls=%async_computation.6 | async-start | bytes 2359296 | tf_op jit(solution)/shard_map/all_to_all | solution.py:185
  128.0 2.6 %text_block.1 = bf16[512,1152]{1,0:T(8,128)(2,1)} custom-call(bf16[512,512]{1,0:T(8,128)(2,1)S(1)} %copy-done.5, bf16[512,512]{1,0:T(8,128)(2,1)S(1)} %copy-done.3, bf16[512,1152]{1,0:T(8,128)(2,1)S(1)} %bitcast.54, bf16[512,1152]{1,0:T(8,128)(2,1)S(1)} %collective-permute-done.left.second), custom_call_target="tpu_custom_call" | custom-call | flops 1207959552 | bytes 4718592 | tf_op jit(solution)/shard_map/text_block/pallas_call | solution.py:104
  130.6 12.3 %all-to-all-done.6 = bf16[4,128,1152]{2,1,0:T(8,128)(2,1)} async-done(((bf16[4,128,1152]{2,1,0:T(8,128)(2,1)}), bf16[4,128,1152]{2,1,0:T(8,128)(2,1)}, u32[]{:S(2)}, u32[]{:S(2)}) %all-to-all-start.6) | async-done | bytes 1179680 | tf_op jit(solution)/shard_map/all_to_all | solution.py:185
  142.9 3.5 %all-to-all-start.8 = ((bf16[4,128,1152]{2,1,0:T(8,128)(2,1)}), bf16[4,128,1152]{2,1,0:T(8,128)(2,1)S(1)}, u32[]{:S(2)}, u32[]{:S(2)}) async-start(bf16[4,128,1152]{2,1,0:T(8,128)(2,1)} %bitcast.14), calls=%async_computation.8 | async-start | bytes 2359296 | tf_op jit(solution)/shard_map/all_to_all | solution.py:189
  146.4 2.2 %reduce_sum.118 = bf16[128,1152]{1,0:T(8,128)(2,1)} reduce(bf16[4,128,1152]{2,1,0:T(8,128)(2,1)} %all-to-all-done.6, bf16[]{:T(256)} %constant.44.clone.1), dimensions={0}, to_apply=%region_5.6 | reduce | flops 442368 | bytes 1474562 | tf_op jit(solution)/shard_map/reduce_sum | solution.py:186
  148.7 13.1 %all-to-all-done.8 = bf16[4,128,1152]{2,1,0:T(8,128)(2,1)S(1)} async-done(((bf16[4,128,1152]{2,1,0:T(8,128)(2,1)}), bf16[4,128,1152]{2,1,0:T(8,128)(2,1)S(1)}, u32[]{:S(2)}, u32[]{:S(2)}) %all-to-all-start.8) | async-done | bytes 1179680 | tf_op jit(solution)/shard_map/all_to_all | solution.py:189
  161.8 6.9 %all-to-all-start.7 = ((bf16[4,32,1152]{2,1,0:T(8,128)(2,1)}), bf16[4,32,1152]{2,1,0:T(8,128)(2,1)S(1)}, u32[]{:S(2)}, u32[]{:S(2)}) async-start(bf16[4,32,1152]{2,1,0:T(8,128)(2,1)} %bitcast.12), calls=%async_computation.7 | async-start | bytes 589824 | tf_op jit(solution)/shard_map/all_to_all | solution.py:187
  168.6 0.8 reduce_sum.116
  169.8 0.6 copy-done.9
  170.7 17.1 %all-to-all-done.7 = bf16[4,32,1152]{2,1,0:T(8,128)(2,1)S(1)} async-done(((bf16[4,32,1152]{2,1,0:T(8,128)(2,1)}), bf16[4,32,1152]{2,1,0:T(8,128)(2,1)S(1)}, u32[]{:S(2)}, u32[]{:S(2)}) %all-to-all-start.7) | async-done | bytes 294944 | tf_op jit(solution)/shard_map/all_to_all | solution.py:187
  187.8 0.6 broadcast_in_dim.30
  188.4 4.2 %all-to-all-start.5 = ((f32[16,3,128]{2,1,0:T(4,128)}), f32[16,3,128]{2,1,0:T(4,128)S(1)}, u32[]{:S(2)}, u32[]{:S(2)}) async-start(f32[16,3,128]{2,1,0:T(4,128)} %broadcast_in_dim.30), calls=%async_computation.5 | async-start | bytes 65536 | tf_op jit(solution)/shard_map/all_to_all | solution.py:130
  192.8 1.1 fusion.13
  193.9 1.0 fusion.16
  195.1 0.3 maximum_bitcast_fusion
  195.4 1.1 copy.77
  196.5 8.7 %all-to-all-done.5 = f32[16,3,128]{2,1,0:T(4,128)S(1)} async-done(((f32[16,3,128]{2,1,0:T(4,128)}), f32[16,3,128]{2,1,0:T(4,128)S(1)}, u32[]{:S(2)}, u32[]{:S(2)}) %all-to-all-start.5) | async-done | bytes 24608 | tf_op jit(solution)/shard_map/all_to_all | solution.py:130
  205.2 3.5 %all-to-all-start.9 = ((bf16[4,160,288]{2,1,0:T(8,128)(2,1)}), bf16[4,160,288]{2,1,0:T(8,128)(2,1)S(1)}, u32[]{:S(2)}, u32[]{:S(2)}) async-start(bf16[4,160,288]{2,1,0:T(8,128)(2,1)} %copy.77), calls=%async_computation.9 | async-start | bytes 983040 | tf_op jit(solution)/shard_map/all_to_all | solution.py:196
  208.8 1.9 collective-permute-start.1
  210.7 1.1 collective-permute-done.1
  211.8 0.6 fusion.17
  214.4 4.6 %all-to-all-done.9 = bf16[4,160,288]{2,1,0:T(8,128)(2,1)S(1)} async-done(((bf16[4,160,288]{2,1,0:T(8,128)(2,1)}), bf16[4,160,288]{2,1,0:T(8,128)(2,1)S(1)}, u32[]{:S(2)}, u32[]{:S(2)}) %all-to-all-start.9) | async-done | bytes 368672 | tf_op jit(solution)/shard_map/all_to_all | solution.py:196
  219.1 0.7 copy.79
  219.8 0.7 copy.78
  (56 shorter events, 2.8 us)
Async XLA Ops:
  22.2 39.0 %copy-start.10 = (bf16[4,160,288]{2,1,0:T(8,128)(2,1)}, bf16[4,160,288]{2,1,0:T(8,128)(2,1)S(1)}, u32[]{:S(2)}) copy-start(bf16[4,160,288]{2,1,0:T(8,128)(2,1)S(1)} %all_to_all.50) | copy-start | bytes 1105924
  22.4 34.0 %copy-start.11 = (f32[32]{0:T(128)}, f32[32]{0:T(128)S(1)}, u32[]{:S(2)}) copy-start(f32[32]{0:T(128)S(1)} %add_rsqrt_fusion.1) | copy-start | bytes 388
  56.4 15.6 %all-to-all-start.2 = ((bf16[4,128,1152]{2,1,0:T(8,128)(2,1)}), bf16[4,128,1152]{2,1,0:T(8,128)(2,1)S(1)}, u32[]{:S(2)}, u32[]{:S(2)}) async-start(bf16[4,128,1152]{2,1,0:T(8,128)(2,1)} %broadcast_in_dim.27), calls=%async_computation.2 | async-start | bytes 2359296 | tf_op jit(solution)/shard_map/all_to_all | solution.py:121
  61.5 13.8 %copy-start.8 = (bf16[4,128,288]{1,2,0:T(8,128)(2,1)}, bf16[4,128,288]{1,2,0:T(8,128)(2,1)S(1)}, u32[]{:S(2)}) copy-start(bf16[4,128,288]{1,2,0:T(8,128)(2,1)S(1)} %copy.82) | copy-start | bytes 884740
  61.7 12.2 %copy-start.13 = (f32[128]{0:T(128)}, f32[128]{0:T(128)S(1)}, u32[]{:S(2)}) copy-start(f32[128]{0:T(128)S(1)} %add_rsqrt_fusion) | copy-start | bytes 1540
  72.0 24.9 %collective-permute-start = (bf16[512,1152]{1,0:T(8,128)(2,1)S(1)}, bf16[512,1152]{1,0:T(8,128)(2,1)S(1)}, u32[]{:S(2)}, u32[]{:S(2)}) collective-permute-start(bf16[512,1152]{1,0:T(8,128)(2,1)S(1)} %bitcast.52), channel_id=1, source_target_pairs={{0,4},{4,0},{1,5},{5,1},{2,6},{6,2},{3,7},{7,3},{8,12},{12,8},{9,1... | collective-permute-start | bytes 3538952 | tf_op jit(solution)/shard_map/ppermute | solution.py:125
  75.3 21.6 %all-to-all-start.3 = ((bf16[4,128,1152]{2,1,0:T(8,128)(2,1)}), bf16[4,128,1152]{2,1,0:T(8,128)(2,1)S(1)}, u32[]{:S(2)}, u32[]{:S(2)}) async-start(bf16[4,128,1152]{2,1,0:T(8,128)(2,1)} %broadcast_in_dim.28), calls=%async_computation.3 | async-start | bytes 2359296 | tf_op jit(solution)/shard_map/all_to_all | solution.py:121
  96.9 4.5 %copy-start = (bf16[4,128,1152]{2,1,0:T(8,128)(2,1)}, bf16[4,128,1152]{2,1,0:T(8,128)(2,1)S(1)}, u32[]{:S(2)}) copy-start(bf16[4,128,1152]{2,1,0:T(8,128)(2,1)S(1)} %all-to-all-done.3) | copy-start | bytes 3538948
  96.9 0.7 copy-start.6
  101.4 0.8 copy-start.2
  102.2 13.5 %collective-permute-start.2 = (bf16[512,1152]{1,0:T(8,128)(2,1)}, bf16[512,1152]{1,0:T(8,128)(2,1)}, u32[]{:S(2)}, u32[]{:S(2)}) collective-permute-start(bf16[512,1152]{1,0:T(8,128)(2,1)} %get-tuple-element.14), channel_id=1, source_target_pairs={{0,4},{4,0},{1,5},{5,1},{2,6},{6,2},{3,7},{7,3},{8,12},{12,8},{9,1... | collective-permute-start | bytes 3538952 | tf_op jit(solution)/shard_map/ppermute | solution.py:125
  104.2 1.3 copy-start.1
  105.5 0.7 copy-start.7
  109.0 0.8 copy-start.4
  110.4 11.7 %all-to-all-start.4 = ((f32[16,3,128]{2,1,0:T(4,128)}), f32[16,3,128]{2,1,0:T(4,128)}, u32[]{:S(2)}, u32[]{:S(2)}) async-start(f32[16,3,128]{2,1,0:T(4,128)} %broadcast_in_dim.29), calls=%async_computation.4 | async-start | bytes 65536 | tf_op jit(solution)/shard_map/all_to_all | solution.py:130
  122.2 5.8 %copy-start.3 = (bf16[512,512]{1,0:T(8,128)(2,1)S(1)}, bf16[512,512]{1,0:T(8,128)(2,1)}, u32[]{:S(2)}) copy-start(bf16[512,512]{1,0:T(8,128)(2,1)} %copy-done.2) | copy-start | bytes 1572868
  122.2 5.8 %copy-start.5 = (bf16[512,512]{1,0:T(8,128)(2,1)S(1)}, bf16[512,512]{1,0:T(8,128)(2,1)}, u32[]{:S(2)}) copy-start(bf16[512,512]{1,0:T(8,128)(2,1)} %copy-done.4) | copy-start | bytes 1572868
  122.2 20.8 %all-to-all-start.6 = ((bf16[4,128,1152]{2,1,0:T(8,128)(2,1)}), bf16[4,128,1152]{2,1,0:T(8,128)(2,1)}, u32[]{:S(2)}, u32[]{:S(2)}) async-start(bf16[4,128,1152]{2,1,0:T(8,128)(2,1)} %bitcast.59), calls=%async_computation.6 | async-start | bytes 2359296 | tf_op jit(solution)/shard_map/all_to_all | solution.py:185
  142.9 18.9 %all-to-all-start.8 = ((bf16[4,128,1152]{2,1,0:T(8,128)(2,1)}), bf16[4,128,1152]{2,1,0:T(8,128)(2,1)S(1)}, u32[]{:S(2)}, u32[]{:S(2)}) async-start(bf16[4,128,1152]{2,1,0:T(8,128)(2,1)} %bitcast.14), calls=%async_computation.8 | async-start | bytes 2359296 | tf_op jit(solution)/shard_map/all_to_all | solution.py:189
  161.8 26.0 %all-to-all-start.7 = ((bf16[4,32,1152]{2,1,0:T(8,128)(2,1)}), bf16[4,32,1152]{2,1,0:T(8,128)(2,1)S(1)}, u32[]{:S(2)}, u32[]{:S(2)}) async-start(bf16[4,32,1152]{2,1,0:T(8,128)(2,1)} %bitcast.12), calls=%async_computation.7 | async-start | bytes 589824 | tf_op jit(solution)/shard_map/all_to_all | solution.py:187
  169.4 1.0 copy-start.9
  169.4 1.0 copy-start.14
  170.5 22.2 %copy-start.12 = (f32[32]{0:T(128)S(1)}, f32[32]{0:T(128)}, u32[]{:S(2)}) copy-start(f32[32]{0:T(128)} %copy-done.11) | copy-start | bytes 388
  188.4 16.8 %all-to-all-start.5 = ((f32[16,3,128]{2,1,0:T(4,128)}), f32[16,3,128]{2,1,0:T(4,128)S(1)}, u32[]{:S(2)}, u32[]{:S(2)}) async-start(f32[16,3,128]{2,1,0:T(4,128)} %broadcast_in_dim.30), calls=%async_computation.5 | async-start | bytes 65536 | tf_op jit(solution)/shard_map/all_to_all | solution.py:130
  205.2 13.8 %all-to-all-start.9 = ((bf16[4,160,288]{2,1,0:T(8,128)(2,1)}), bf16[4,160,288]{2,1,0:T(8,128)(2,1)S(1)}, u32[]{:S(2)}, u32[]{:S(2)}) async-start(bf16[4,160,288]{2,1,0:T(8,128)(2,1)} %copy.77), calls=%async_computation.9 | async-start | bytes 983040 | tf_op jit(solution)/shard_map/all_to_all | solution.py:196
  208.8 3.0 %collective-permute-start.1 = (f32[3]{0:T(128)S(1)}, f32[3]{0:T(128)S(1)}, u32[]{:S(2)}, u32[]{:S(2)}) collective-permute-start(f32[3]{0:T(128)S(1)} %reduce_sum.117), channel_id=1, source_target_pairs={{0,4},{4,0},{1,5},{5,1},{2,6},{6,2},{3,7},{7,3},{8,12},{12,8},{9,1... | collective-permute-start | bytes 44 | tf_op jit(solution)/shard_map/ppermute | solution.py:125

commit v2 on v1

v2 whole, which is shorter than its diff:
```python
import functools

import jax
import jax.numpy as jnp
from jax import lax
from jax.experimental import pallas as pl
from jax.experimental.pallas import tpu as pltpu
from jax.sharding import Mesh, PartitionSpec as P

epsilon = 1e-06
lanes = 128
piece = 32
strips = 4
rest = 32
packed_rows = 72
carry_rows = 80
tiles = 9
vmem = pl.BlockSpec(memory_space=pltpu.VMEM)
smem = pl.BlockSpec(memory_space=pltpu.SMEM)


def call(kernel, out_shape, name, flops=0, special=0, specs=None):
    def run(*operands):
        moved = sum(a.size * a.dtype.itemsize for a in operands)
        moved += sum(a.size * a.dtype.itemsize for a in jax.tree.leaves(out_shape))
        return pl.pallas_call(
            kernel,
            out_shape=out_shape,
            in_specs=specs or [vmem] * len(operands),
            out_specs=jax.tree.map(lambda _: vmem, out_shape),
            compiler_params=pltpu.CompilerParams(vmem_limit_bytes=40 * 1024 * 1024),
            cost_estimate=pl.CostEstimate(
                flops=flops, bytes_accessed=moved, transcendentals=special
            ),
            name=name,
        )(*operands)

    return run


def shape(dims, dtype=jnp.bfloat16):
    return jax.ShapeDtypeStruct(dims, dtype)


def lane_group():
    return lax.broadcasted_iota(jnp.int32, (8, lanes), 1) // rest


def pack_kernel(image, out):
    count = out.shape[0] // strips
    for k in range(strips):
        rows = image[k * piece : (k + 1) * piece, :].astype(jnp.float32)
        last = rows[:, 2 * lanes :]
        last = jnp.concatenate([last[8 * g : 8 * g + 8] for g in range(4)], axis=1)
        chunk = jnp.concatenate([rows[:, :lanes], rows[:, lanes : 2 * lanes], last], axis=0)
        chunk = chunk.astype(jnp.bfloat16)
        for d in range(count):
            out[d * strips + k] = chunk


def unpack_rows(chunks, group):
    found = []
    lasts = []
    for chunk in chunks:
        found += [chunk[:piece], chunk[piece : 2 * piece]]
        lasts.append(chunk[2 * piece : 2 * piece + 8])
    last = []
    for g in range(4):
        value = jnp.zeros((8, lanes), jnp.float32)
        for s in range(strips):
            turn = rest * (s - g) % lanes
            moved = pltpu.roll(lasts[s], turn, 1) if turn else lasts[s]
            value = jnp.where(group == s, moved, value)
        last.append(value)
    found.append(jnp.concatenate(last, axis=0))
    return found


def unit_tiles(chunks, group):
    found = unpack_rows(chunks, group)
    squares = functools.reduce(lambda a, b: a + b, [t * t for t in found])
    inverse = lax.rsqrt(jnp.sum(squares, axis=1, keepdims=True) + epsilon)
    return [t * inverse for t in found], inverse


def read_chunks(arrived, h):
    return [arrived[h * strips + s].astype(jnp.float32) for s in range(strips)]


def unit_kernel(arrived, out):
    group = lane_group()
    for h in range(arrived.shape[0] // strips):
        units, _ = unit_tiles(read_chunks(arrived, h), group)
        for t in range(tiles):
            value = units[t].astype(jnp.bfloat16)
            for k in range(out.shape[0]):
                out[k, h * piece : (h + 1) * piece, t * lanes : (t + 1) * lanes] = value


def fold(values):
    rows, columns = values.shape
    part = jnp.sum(values.reshape(rows // 8, 8, columns), axis=0)
    return sum(part[:, c : c + lanes] for c in range(0, columns, lanes))


def pair_kernel(own, scales, spots, left, t0, t1, t2, t3, *rest_refs):
    if own:
        back, weights_out, sums_out, right = rest_refs
    else:
        first_sums, back, weights_out, sums_out, right = rest_refs
    scale = scales[0]
    bias = scales[1]
    rows = left.shape[0]
    part = t0.shape[0]
    for k, ref in enumerate((t0, t1, t2, t3)):
        right[k * part : (k + 1) * part, :] = ref[...]
    columns = 4 * part
    tile = 256
    loss_sum = jnp.zeros((8, lanes), jnp.float32)
    temp_sum = jnp.zeros((8, lanes), jnp.float32)
    bias_sum = jnp.zeros((8, lanes), jnp.float32)
    for start in range(0, rows, tile):
        here = pl.ds(start, tile)
        product = lax.dot_general(
            left[here, :], right[...], (((1,), (1,)), ((), ())), preferred_element_type=jnp.float32
        )
        logits = scale * product + bias
        if own:
            row = lax.broadcasted_iota(jnp.int32, (tile, 1), 0) + (start - spots[0])
            row = jnp.where((row >= 0) & (row < piece), row, -1)
            column = lax.broadcasted_iota(jnp.int32, (1, columns), 1) - spots[1]
            column = jnp.where(column >= 0, column, -2)
            same = row == column
            grown = jnp.exp(jnp.where(same, -logits, logits))
            share = grown / (1.0 + grown)
            slope = jnp.where(same, -share, share)
        else:
            grown = jnp.exp(logits)
            slope = grown / (1.0 + grown)
        weights = (scale * slope).astype(jnp.bfloat16)
        weights_out[here, :] = weights
        back[here, :] = jnp.dot(
            weights, right[...], preferred_element_type=jnp.float32
        ).astype(jnp.bfloat16)
        quarter = tile // 4
        a, b, c, d = (grown[k * quarter : (k + 1) * quarter, :] for k in range(4))
        ab = a + (b + a * b)
        cd = c + (d + c * d)
        loss_sum += fold(jnp.log1p(ab + (cd + ab * cd)))
        temp_sum += fold(slope * product)
        bias_sum += fold(slope)
    if own:
        sums_out[0:8, :] = loss_sum
        sums_out[8:16, :] = temp_sum
        sums_out[16:24, :] = bias_sum
    else:
        sums = []
        for k, found in enumerate((loss_sum, temp_sum, bias_sum)):
            sums.append(jnp.sum(found + first_sums[8 * k : 8 * k + 8, :], axis=0, keepdims=True))
        row = lax.broadcasted_iota(jnp.int32, (8, lanes), 0)
        total = jnp.where(
            row == 0, sums[0], jnp.where(row == 1, sums[1], jnp.where(row == 2, sums[2], 0.0))
        )
        for k in range(sums_out.shape[0]):
            sums_out[k] = total


def pair_block(own, scales, spots, left, texts, first_sums=None, copies=0):
    rows, width = left.shape
    columns = 4 * texts[0].shape[0]
    sums = shape((24, lanes), jnp.float32) if own else shape((copies, 8, lanes), jnp.float32)
    operands = [scales, spots, left] + list(texts) + ([] if own else [first_sums])
    moved = sum(a.size * a.dtype.itemsize for a in operands) * 2
    return pl.pallas_call(
        functools.partial(pair_kernel, own),
        out_shape=(shape((rows, width)), shape((rows, columns)), sums),
        in_specs=[smem, smem] + [vmem] * (len(operands) - 2),
        out_specs=(vmem, vmem, vmem),
        scratch_shapes=[pltpu.VMEM((columns, width), jnp.bfloat16)],
        compiler_params=pltpu.CompilerParams(vmem_limit_bytes=40 * 1024 * 1024),
        cost_estimate=pl.CostEstimate(
            flops=4 * rows * columns * width,
            bytes_accessed=moved,
            transcendentals=2 * rows * columns,
        ),
        name="pair_own" if own else "pair_other",
    )(*operands)


def text_kernel(first_weights, second_weights, first, second, *backs):
    contract = (((0,), (0,)), ((), ()))
    part = backs[0].shape[0]
    total = lax.dot_general(
        first_weights[...], first[...], contract, preferred_element_type=jnp.float32
    ) + lax.dot_general(
        second_weights[...], second[...], contract, preferred_element_type=jnp.float32
    )
    for k, back in enumerate(backs):
        back[...] = total[k * part : (k + 1) * part].astype(jnp.bfloat16)


def three_parts(value):
    high = value.astype(jnp.bfloat16).astype(jnp.float32)
    middle = (value - high).astype(jnp.bfloat16).astype(jnp.float32)
    return high, middle, value - high - middle


def combine_kernel(own, given, sums, out):
    count, total_rows, _ = out.shape
    block = own.shape[0] // count
    value = functools.reduce(lambda a, b: a + b, [sums[k] for k in range(sums.shape[0])])
    carried = jnp.concatenate(
        list(three_parts(value)) + [jnp.zeros((8, lanes), jnp.float32)], axis=0
    ).astype(jnp.bfloat16)
    for k in range(count):
        for t in range(tiles):
            rows = pl.ds(k * block, block)
            columns = pl.ds(t * lanes, lanes)
            value = own[rows, columns].astype(jnp.float32) + given[rows, columns].astype(jnp.float32)
            out[k, t * block : (t + 1) * block, :] = value.astype(jnp.bfloat16)
        out[k, tiles * block : total_rows, :] = carried


def finish_kernel(arrived, backs, out):
    group = lane_group()
    count = backs.shape[0]
    heads = arrived.shape[0] // strips
    block = heads * piece
    tail = tiles * block
    add = lambda a, b: a + b
    carried = functools.reduce(
        add, [backs[k, tail : tail + piece, :].astype(jnp.float32) for k in range(count)]
    )
    value = jnp.sum(carried[0:8] + carried[8:16] + carried[16:24], axis=1, keepdims=True)
    parts = three_parts(value)
    lane = lax.broadcasted_iota(jnp.int32, (8, lanes), 1)
    carry = jnp.zeros((8, lanes), jnp.float32)
    for k in range(3):
        carry = jnp.where(lane == k, parts[k], carry)
    for h in range(heads):
        units, inverse = unit_tiles(read_chunks(arrived, h), group)
        grads = []
        for t in range(tiles):
            start = t * block + h * piece
            grads.append(
                functools.reduce(
                    add,
                    [backs[k, start : start + piece, :].astype(jnp.float32) for k in range(count)],
                )
            )
        along = jnp.sum(
            functools.reduce(add, [u * g for u, g in zip(units, grads)]), axis=1, keepdims=True
        )
        final = [(g - u * along) * inverse for u, g in zip(units, grads)]
        for s in range(strips):
            last = jnp.zeros((8, lanes), jnp.float32)
            for g in range(4):
                turn = rest * (g - s) % lanes
                rows = final[tiles - 1][8 * g : 8 * g + 8]
                moved = pltpu.roll(rows, turn, 1) if turn else rows
                last = jnp.where(group == g, moved, last)
            chunk = jnp.concatenate([final[2 * s], final[2 * s + 1], last, carry], axis=0)
            out[h * strips + s] = chunk.astype(jnp.bfloat16)


def last_kernel(arrived, out, sums_out):
    heads = arrived.shape[0] // strips
    sums = jnp.zeros((8, lanes), jnp.float32)
    for s in range(strips):
        chunk = functools.reduce(
            lambda a, b: a + b,
            [arrived[h * strips + s].astype(jnp.float32) for h in range(heads)],
        )
        rows = pl.ds(s * piece, piece)
        out[rows, 0:lanes] = chunk[:piece].astype(jnp.bfloat16)
        out[rows, lanes : 2 * lanes] = chunk[piece : 2 * piece].astype(jnp.bfloat16)
        last = chunk[2 * piece : 2 * piece + 8]
        groups = [last] + [pltpu.roll(last, lanes - rest * g, 1) for g in range(1, 4)]
        value = jnp.concatenate(groups, axis=0)[:, :rest]
        out[rows, 2 * lanes : 2 * lanes + rest] = value.astype(jnp.bfloat16)
        sums = sums + chunk[2 * piece + 8 :]
    sums_out[...] = jnp.broadcast_to(jnp.sum(sums, axis=1, keepdims=True), sums.shape)


def swap_core(value):
    return lax.ppermute(value, "core", [(0, 1), (1, 0)])


def shift(value, axis, k):
    count = lax.axis_size(axis)
    return lax.ppermute(value, axis, [(i, (i + k) % count) for i in range(count)])


def shards(image, text, log_temp, bias):
    rows, strip = image.shape
    zh_count, x_count, y_count = (lax.axis_size(name) for name in ("zh", "x", "y"))
    width = strip * strips
    z_count = zh_count * strips
    block = zh_count * piece
    zh, x, zl = (lax.axis_index(name) for name in ("zh", "x", "zl"))
    scale = jnp.exp(log_temp)
    scales = jnp.stack([scale, bias])
    spots = jnp.stack([(x * zh_count + zh) * piece, zl * piece]).astype(jnp.int32)

    packed = call(pack_kernel, shape((z_count, packed_rows, lanes)), "pack")(image)
    image_chunks = lax.all_to_all(packed, ("zh", "zl"), 0, 0)

    found = lax.all_gather(text, "zl", axis=0)
    text_own = jnp.concatenate(
        [found[s, :, : 2 * lanes] for s in range(strips)]
        + [found[s, :, 2 * lanes :] for s in range(strips)],
        axis=1,
    ).astype(jnp.float32)
    text_inverse = lax.rsqrt(jnp.sum(text_own * text_own, axis=1, keepdims=True) + epsilon)
    text_unit = text_own * text_inverse
    text_half = text_unit.astype(jnp.bfloat16)
    texts = [text_half] + [shift(text_half, "y", k) for k in range(1, y_count)]

    units = call(unit_kernel, shape((x_count, block, width)), "unit")(image_chunks)
    image_rows = lax.all_to_all(units, "x", 0, 0).reshape(x_count * block, width)
    other_rows = swap_core(image_rows)

    own_back, own_weights, own_sums = pair_block(True, scales, spots, image_rows, texts)
    other_back, other_weights, sums = pair_block(
        False, scales, spots, other_rows, texts, own_sums, y_count * 2
    )
    given_back = swap_core(other_back)
    sums = lax.all_to_all(sums, ("y", "core"), 0, 0)
    text_backs = call(
        text_kernel,
        tuple(shape((rows, width)) for _ in range(y_count)),
        "text_back",
        flops=4 * image_rows.size * own_weights.shape[1],
    )(own_weights, other_weights, image_rows, other_rows)

    combined = call(combine_kernel, shape((x_count, tiles * block + piece, lanes)), "combine")(
        own_back, given_back, sums
    )
    combined = lax.all_to_all(combined, "x", 0, 0)
    finished = call(finish_kernel, shape((z_count, carry_rows, lanes)), "finish")(
        image_chunks, combined
    )
    finished = lax.all_to_all(finished, ("zh", "zl"), 0, 0)
    grad_image, sums = call(
        last_kernel, (shape((rows, strip)), shape((8, lanes), jnp.float32)), "last"
    )(finished)

    text_back = text_backs[0].astype(jnp.float32)
    for k in range(1, y_count):
        text_back = text_back + shift(text_backs[k], "y", -k).astype(jnp.float32)
    along = jnp.sum(text_unit * text_back, axis=1, keepdims=True)
    text_final = (text_back - text_unit * along) * text_inverse
    text_final = text_final.astype(jnp.bfloat16)
    text_strips = jnp.stack(
        [
            jnp.concatenate(
                [
                    text_final[:, 2 * lanes * s : 2 * lanes * (s + 1)],
                    text_final[:, 8 * lanes + rest * s : 8 * lanes + rest * (s + 1)],
                ],
                axis=1,
            )
            for s in range(strips)
        ]
    )
    grad_text = lax.dynamic_index_in_dim(text_strips, zl, 0, False).astype(jnp.float32)
    for k in range(1, strips):
        given = lax.dynamic_index_in_dim(text_strips, (zl + k) % strips, 0, False)
        grad_text = grad_text + shift(given, "zl", k).astype(jnp.float32)
    grad_text = grad_text.astype(jnp.bfloat16)

    pairs_count = rows * zh_count * x_count * y_count * 2
    return (
        sums[0, 0] / pairs_count,
        grad_image,
        grad_text,
        scale * sums[1, 0] / pairs_count,
        sums[2, 0] / pairs_count,
    )


def solution(mesh):
    fine = Mesh(mesh.devices.reshape(4, 4, 4, 2, 4), ("zh", "x", "y", "core", "zl"))
    whole = P(("zh", "x", "y", "core"), "zl")
    return jax.shard_map(
        shards,
        mesh=fine,
        in_specs=(whole, whole, P(), P()),
        out_specs=(P(), whole, whole, P(), P()),
        check_vma=False,
    )
```

time: 225 us -> 179 us (0.80)
  waiting for transfers between devices: 86.3 us -> 37.4 us
  local copies, waits for them, and re-layouts: 14.8 us -> 3.56 us
  blocking collectives: 52 us -> 62.2 us
  starting transfers between devices: 44.2 us -> 53.1 us
  other arithmetic: 9.84 us -> 1.2 us
  Pallas kernels: 9.22 us -> 12.9 us
    all_to_all x8 -> x3, waiting for transfers between devices: 85.2 us -> 14.9 us  [the longest x1 14.9 us: shards(): combined = lax.all_to_all(combined, 'x', 0, 0)]
    ppermute x0 -> x9, starting transfers between devices: none -> 32.4 us  [shift(): lax.ppermute(value, axis, [(i, (i + k) % count) for i in range(count)])]
    ppermute x0 -> x9, waiting for transfers between devices: none -> 22.5 us  [shift(): lax.ppermute(value, axis, [(i, (i + k) % count) for i in range(count)])]
    all_to_all x8 -> x3, starting transfers between devices: 38.4 us -> 16.9 us  [the longest x1 7.18 us: shards(): finished = lax.all_to_all(finished, ('zh', 'zl'), 0, 0)]
    all_gather x0 -> x1, blocking collectives: none -> 14.2 us  [shards(): found = lax.all_gather(text, 'zl', axis=0)]
    unnamed x35 -> x9, local copies, waits for them, and re-layouts: 8.49 us -> 2.5 us
    reduce_sum x11 -> x2, other arithmetic: 5 us -> 0.44 us  [the longest x1 0.3 us: shards(): along = jnp.sum(text_unit * text_back, axis=1, keepdims=True)]
    all_to_all x2, blocking collectives: 52 us -> 48 us  [the longest x1 34.3 us: shards(): image_chunks = lax.all_to_all(packed, ('zh', 'zl'), 0, 0)]
  transfers between devices with their start and end apart: 11 -> 14, of which waited for: 9 -> 6; matrix products, arithmetic and copies ran while one was open for 6% -> 1% of each run, Pallas kernels for 2% -> 4%
where the time goes in v2:
time: 179 us; the launch traced here: 178 us
  blocking collectives  62.2 us (35%)
  starting transfers between devices  53.1 us (30%)
  waiting for transfers between devices  37.4 us (21%)
  Pallas kernels  12.9 us (7%)
  between operations  7.49 us (4%)
  local copies, waits for them, and re-layouts  3.56 us (2%)
    all_to_all x1, blocking collectives, shards(): image_chunks = lax.all_to_all(packed, ('zh', 'zl'), 0, 0)  34.3 us
    ppermute x9, starting transfers between devices, shift(): lax.ppermute(value, axis, [(i, (i + k) % count) for i in range(count)])  32.4 us
    ppermute x9, waiting for transfers between devices, shift(): lax.ppermute(value, axis, [(i, (i + k) % count) for i in range(count)])  22.5 us
    all_to_all x1, waiting for transfers between devices, shards(): combined = lax.all_to_all(combined, 'x', 0, 0)  14.9 us
    all_gather x1, blocking collectives, shards(): found = lax.all_gather(text, 'zl', axis=0)  14.2 us
    all_to_all x1, blocking collectives, shards(): sums = lax.all_to_all(sums, ('y', 'core'), 0, 0)  13.7 us
    all_to_all x1, starting transfers between devices, shards(): finished = lax.all_to_all(finished, ('zh', 'zl'), 0, 0)  7.18 us
    pallas_call x2, Pallas kernels, pair_block(): pl.pallas_call(functools.partial(pair_kernel, own), out_shape=(shape((row...  6.5 us
  transfers between devices with their start and end apart: 14, of which 6 were waited for; matrix products, arithmetic and copies ran while one was open for 1% of the time, Pallas kernels for 4%

profile of v2, /device:TPU:2, one launch (start us, length us, event | category | flops | bytes accessed | tf_op | source)
XLA Modules:
  0.0 177.9 jit_solution(10083996443819243422)
XLA Ops:
  0.6 1.0 copy.9.image
  1.6 0.1 pack.1
  1.7 34.3 %all_to_all.25.arrived = bf16[16,72,128]{2,1,0:T(8,128)(2,1)S(1)} all-to-all(bf16[16,72,128]{2,1,0:T(8,128)(2,1)S(1)} %pack.1), channel_id=1, replica_groups=mesh['zh'=4,'x'=4,'y'=4,'core'=2,'zl'=4] {'zh','zl'}, dimensions={0} | all-to-all | bytes 589824 | tf_op jit(solution)/shard_map/all_to_all | solution.py:306
  36.0 1.4 unit.1
  37.4 5.0 %all-to-all-start.1 = ((bf16[4,128,1152]{2,1,0:T(8,128)(2,1)}), bf16[4,128,1152]{2,1,0:T(8,128)(2,1)S(1)}, u32[]{:S(2)}, u32[]{:S(2)}) async-start(bf16[4,128,1152]{2,1,0:T(8,128)(2,1)} %unit.1), calls=%async_computation.1 | async-start | bytes 2359296 | tf_op jit(solution)/shard_map/all_to_all | solution.py:320
  42.3 14.2 %all-gather = bf16[512,288]{0,1:T(8,128)(2,1)S(1)} all-gather(bf16[128,288]{0,1:T(8,128)(2,1)S(1)} %copy-done.2), channel_id=2, replica_groups=mesh['zh'=4,'x'=4,'y'=4,'core'=2,'zl'=4] {'zl'}, dimensions={0}, use_global_device_ids=true | all-gather | bytes 368640 | tf_op jit(solution)/shard_map/all_gather | solution.py:308
  56.5 0.2 copy.10
  56.8 0.1 concatenate.15
  57.0 1.9 %collective-permute-start.3 = (bf16[512,1152]{1,0:T(8,128)(2,1)S(1)}, bf16[512,1152]{1,0:T(8,128)(2,1)S(1)}, u32[]{:S(2)}, u32[]{:S(2)}) collective-permute-start(bf16[512,1152]{1,0:T(8,128)(2,1)S(1)} %bitcast.43), channel_id=1, source_target_pairs={{0,4},{4,0},{1,5},{5,1},{2,6},{6,2},{3,7},{7,3},{8,12},{12,8},{9,1... | collective-permute-start | bytes 3538952 | tf_op jit(solution)/shard_map/ppermute | solution.py:286
  58.9 0.1 fusion.7
  59.1 0.1 fusion.2.t0
  59.2 3.5 %collective-permute-start = (bf16[128,1152]{1,0:T(8,128)(2,1)S(1)}, bf16[128,1152]{1,0:T(8,128)(2,1)S(1)}, u32[]{:S(2)}, u32[]{:S(2)}) collective-permute-start(bf16[128,1152]{1,0:T(8,128)(2,1)S(1)} %fusion.2.t0), channel_id=1, source_target_pairs={{0,8},{8,16},{16,24},{24,0},{1,9},{9,17},{17,25},{25,1},{2,10},{10... | collective-permute-start | bytes 884744 | tf_op jit(solution)/shard_map/ppermute | solution.py:291
  62.7 4.8 %collective-permute-start.1 = (bf16[128,1152]{1,0:T(8,128)(2,1)S(1)}, bf16[128,1152]{1,0:T(8,128)(2,1)}, u32[]{:S(2)}, u32[]{:S(2)}) collective-permute-start(bf16[128,1152]{1,0:T(8,128)(2,1)S(1)} %fusion.2.t0), channel_id=1, source_target_pairs={{0,16},{8,24},{16,0},{24,8},{1,17},{9,25},{17,1},{25,9},{2,18},{10... | collective-permute-start | bytes 884744 | tf_op jit(solution)/shard_map/ppermute | solution.py:291
  67.5 3.3 %collective-permute-start.2 = (bf16[128,1152]{1,0:T(8,128)(2,1)S(1)}, bf16[128,1152]{1,0:T(8,128)(2,1)}, u32[]{:S(2)}, u32[]{:S(2)}) collective-permute-start(bf16[128,1152]{1,0:T(8,128)(2,1)S(1)} %fusion.2.t0), channel_id=1, source_target_pairs={{0,24},{8,0},{16,8},{24,16},{1,25},{9,1},{17,9},{25,17},{2,26},{10... | collective-permute-start | bytes 884744 | tf_op jit(solution)/shard_map/ppermute | solution.py:291
  72.1 0.1 pad_add_fusion.spots
  72.2 0.1 pad_maximum_fusion.1.scales
  72.3 0.0 collective-permute-done.t1
  72.3 7.1 %collective-permute-done.1.t2 = bf16[128,1152]{1,0:T(8,128)(2,1)} collective-permute-done((bf16[128,1152]{1,0:T(8,128)(2,1)S(1)}, bf16[128,1152]{1,0:T(8,128)(2,1)}, u32[]{:S(2)}, u32[]{:S(2)}) %collective-permute-start.1) | collective-permute-done | bytes 294944 | tf_op jit(solution)/shard_map/ppermute | solution.py:291
  79.4 1.4 collective-permute-done.2.t3
  80.7 3.4 %pair_own.1 = (bf16[512,1152]{1,0:T(8,128)(2,1)S(1)}, bf16[512,512]{1,0:T(8,128)(2,1)S(1)}, f32[24,128]{1,0:T(8,128)S(1)}) custom-call(f32[2]{0:T(128)S(1)} %pad_maximum_fusion.1.scales, s32[2]{0:T(128)S(1)} %pad_add_fusion.spots, bf16[512,1152]{1,0:T(8,128)(2,1)S(1)} %bitcast.44, bf16[128,1152]{1,0:T(8,128)(2,1)S(1)} %fusion.2.t0, ...), custom_call_target="tpu_custom_call" | custom-call | flops 1207959552 | bytes 4718624 | tf_op jit(solution)/shard_map/pair_own/pallas_call | solution.py:174
  84.1 3.1 %pair_other.1 = (bf16[512,1152]{1,0:T(8,128)(2,1)S(1)}, bf16[512,512]{1,0:T(8,128)(2,1)S(1)}, f32[8,8,128]{2,1,0:T(8,128)S(1)}) custom-call(f32[2]{0:T(128)S(1)} %pad_maximum_fusion.1.scales, s32[2]{0:T(128)S(1)} %pad_add_fusion.spots, bf16[512,1152]{1,0:T(8,128)(2,1)S(1)} %collective-permute-done.3.left.second, bf16[128,1152]{1,0:T(8,128)(2,1)S(1)} %fusion.2.t0, ...), custom_call_target="tpu_custom_call" | custom-call | flops 1207959552 | bytes 4743200 | tf_op jit(solution)/shard_map/pair_other/pallas_call | solution.py:174
  87.3 1.9 %collective-permute-start.4 = (bf16[512,1152]{1,0:T(8,128)(2,1)S(1)}, bf16[512,1152]{1,0:T(8,128)(2,1)S(1)}, u32[]{:S(2)}, u32[]{:S(2)}) collective-permute-start(bf16[512,1152]{1,0:T(8,128)(2,1)S(1)} %get-tuple-element.19), channel_id=1, source_target_pairs={{0,4},{4,0},{1,5},{5,1},{2,6},{6,2},{3,7},{7,3},{8,12},{12,8},{9,1... | collective-permute-start | bytes 3538952 | tf_op jit(solution)/shard_map/ppermute | solution.py:286
  89.2 2.3 %text_back.1 = (bf16[128,1152]{1,0:T(8,128)(2,1)S(1)}, bf16[128,1152]{1,0:T(8,128)(2,1)}, bf16[128,1152]{1,0:T(8,128)(2,1)}, bf16[128,1152]{1,0:T(8,128)(2,1)S(1)}) custom-call(bf16[512,512]{1,0:T(8,128)(2,1)S(1)} %get-tuple-element.23.first_weights, bf16[512,512]{1,0:T(8,128)(2,1)S(1)} %get-tuple-element.24.second_weights, bf16[512,1152]{1,0:T(8,128)(2,1)S(1)} %bitcast.45, ...), custom_call_target="tpu_custom_call" | custom-call | flops 1207959552 | bytes 4587520 | tf_op jit(solution)/shard_map/text_back/pallas_call | solution.py:26
  91.5 4.5 %collective-permute-start.5 = (bf16[128,1152]{1,0:T(8,128)(2,1)}, bf16[128,1152]{1,0:T(8,128)(2,1)S(1)}, u32[]{:S(2)}, u32[]{:S(2)}) collective-permute-start(bf16[128,1152]{1,0:T(8,128)(2,1)} %get-tuple-element.26), channel_id=1, source_target_pairs={{0,24},{8,0},{16,8},{24,16},{1,25},{9,1},{17,9},{25,17},{2,26},{10... | collective-permute-start | bytes 884744 | tf_op jit(solution)/shard_map/ppermute | solution.py:291
  96.0 3.8 %collective-permute-start.6 = (bf16[128,1152]{1,0:T(8,128)(2,1)}, bf16[128,1152]{1,0:T(8,128)(2,1)S(1)}, u32[]{:S(2)}, u32[]{:S(2)}) collective-permute-start(bf16[128,1152]{1,0:T(8,128)(2,1)} %get-tuple-element.27), channel_id=1, source_target_pairs={{0,16},{8,24},{16,0},{24,8},{1,17},{9,25},{17,1},{25,9},{2,18},{10... | collective-permute-start | bytes 884744 | tf_op jit(solution)/shard_map/ppermute | solution.py:291
  99.9 1.9 %collective-permute-start.7 = (bf16[128,1152]{1,0:T(8,128)(2,1)S(1)}, bf16[128,1152]{1,0:T(8,128)(2,1)S(1)}, u32[]{:S(2)}, u32[]{:S(2)}) collective-permute-start(bf16[128,1152]{1,0:T(8,128)(2,1)S(1)} %get-tuple-element.28), channel_id=1, source_target_pairs={{0,8},{8,16},{16,24},{24,0},{1,9},{9,17},{17,25},{25,1},{2,10},{10... | collective-permute-start | bytes 884744 | tf_op jit(solution)/shard_map/ppermute | solution.py:291
  101.8 13.7 %all_to_all.26.sums = f32[8,8,128]{2,1,0:T(8,128)S(1)} all-to-all(f32[8,8,128]{2,1,0:T(8,128)S(1)} %get-tuple-element.20), channel_id=1, replica_groups=mesh['zh'=4,'x'=4,'y'=4,'core'=2,'zl'=4] {'y','core'}, dimensions={0} | all-to-all | bytes 65536 | tf_op jit(solution)/shard_map/all_to_all | solution.py:328
  115.5 1.3 combine.1
  116.8 4.7 %all-to-all-start.3 = ((bf16[4,1184,128]{2,1,0:T(8,128)(2,1)}), bf16[4,1184,128]{2,1,0:T(8,128)(2,1)S(1)}, u32[]{:S(2)}, u32[]{:S(2)}) async-start(bf16[4,1184,128]{2,1,0:T(8,128)(2,1)} %combine.1), calls=%async_computation.3 | async-start | bytes 2424832 | tf_op jit(solution)/shard_map/all_to_all | solution.py:339
  121.6 0.0 collective-permute-done.7
  121.6 0.3 fusion.3
  121.9 0.3 fusion.6
  122.2 14.9 %all-to-all-done.3.backs = bf16[4,1184,128]{2,1,0:T(8,128)(2,1)S(1)} async-done(((bf16[4,1184,128]{2,1,0:T(8,128)(2,1)}), bf16[4,1184,128]{2,1,0:T(8,128)(2,1)S(1)}, u32[]{:S(2)}, u32[]{:S(2)}) %all-to-all-start.3) | async-done | bytes 1212448 | tf_op jit(solution)/shard_map/all_to_all | solution.py:339
  137.1 1.2 finish.1
  138.3 7.2 %all-to-all-start.4 = ((bf16[16,80,128]{2,1,0:T(8,128)(2,1)}), bf16[16,80,128]{2,1,0:T(8,128)(2,1)S(1)}, u32[]{:S(2)}, u32[]{:S(2)}) async-start(bf16[16,80,128]{2,1,0:T(8,128)(2,1)} %finish.1), calls=%async_computation.4 | async-start | bytes 655360 | tf_op jit(solution)/shard_map/all_to_all | solution.py:343
  145.4 0.1 fusion.12
  145.6 0.1 pad_maximum_fusion
  145.8 5.6 %collective-permute-start.10 = (bf16[128,288]{1,0:T(8,128)(2,1)S(1)}, bf16[128,288]{1,0:T(8,128)(2,1)S(1)}, u32[]{:S(2)}, u32[]{:S(2)}) collective-permute-start(bf16[128,288]{1,0:T(8,128)(2,1)S(1)} %get-tuple-element.35), channel_id=1, source_target_pairs={{0,3},{1,0},{2,1},{3,2},{4,7},{5,4},{6,5},{7,6},{8,11},{9,8},{10,9... | collective-permute-start | bytes 221192 | tf_op jit(solution)/shard_map/ppermute | solution.py:291
  151.4 1.9 %collective-permute-start.8 = (bf16[128,288]{1,0:T(8,128)(2,1)S(1)}, bf16[128,288]{1,0:T(8,128)(2,1)S(1)}, u32[]{:S(2)}, u32[]{:S(2)}) collective-permute-start(bf16[128,288]{1,0:T(8,128)(2,1)S(1)} %get-tuple-element.34), channel_id=1, source_target_pairs={{0,1},{1,2},{2,3},{3,0},{4,5},{5,6},{6,7},{7,4},{8,9},{9,10},{10,1... | collective-permute-start | bytes 221192 | tf_op jit(solution)/shard_map/ppermute | solution.py:291
  153.3 3.0 %collective-permute-start.9 = (bf16[128,288]{1,0:T(8,128)(2,1)S(1)}, bf16[128,288]{1,0:T(8,128)(2,1)S(1)}, u32[]{:S(2)}, u32[]{:S(2)}) collective-permute-start(bf16[128,288]{1,0:T(8,128)(2,1)S(1)} %get-tuple-element.36), channel_id=1, source_target_pairs={{0,2},{1,3},{2,0},{3,1},{4,6},{5,7},{6,4},{7,5},{8,10},{9,11},{10,... | collective-permute-start | bytes 221192 | tf_op jit(solution)/shard_map/ppermute | solution.py:291
  156.4 7.8 %collective-permute-done.10 = bf16[128,288]{1,0:T(8,128)(2,1)S(1)} collective-permute-done((bf16[128,288]{1,0:T(8,128)(2,1)S(1)}, bf16[128,288]{1,0:T(8,128)(2,1)S(1)}, u32[]{:S(2)}, u32[]{:S(2)}) %collective-permute-start.10) | collective-permute-done | bytes 73760 | tf_op jit(solution)/shard_map/ppermute | solution.py:291
  164.2 4.3 %collective-permute-done.8 = bf16[128,288]{1,0:T(8,128)(2,1)S(1)} collective-permute-done((bf16[128,288]{1,0:T(8,128)(2,1)S(1)}, bf16[128,288]{1,0:T(8,128)(2,1)S(1)}, u32[]{:S(2)}, u32[]{:S(2)}) %collective-permute-start.8) | collective-permute-done | bytes 73760 | tf_op jit(solution)/shard_map/ppermute | solution.py:291
  168.4 2.0 %collective-permute-done.9 = bf16[128,288]{1,0:T(8,128)(2,1)S(1)} collective-permute-done((bf16[128,288]{1,0:T(8,128)(2,1)S(1)}, bf16[128,288]{1,0:T(8,128)(2,1)S(1)}, u32[]{:S(2)}, u32[]{:S(2)}) %collective-permute-start.9) | collective-permute-done | bytes 73760 | tf_op jit(solution)/shard_map/ppermute | solution.py:291
  170.4 0.1 fusion.10
  170.5 0.7 copy.12
  171.2 0.1 last.1
  171.3 0.7 copy.11
  172.1 0.5 fusion.13
  (19 shorter events, 0.2 us)
Async XLA Ops:
  37.4 5.0 %copy-start.2 = (bf16[128,288]{0,1:T(8,128)(2,1)S(1)}, bf16[128,288]{0,1:T(8,128)(2,1)}, u32[]{:S(2)}) copy-start(bf16[128,288]{0,1:T(8,128)(2,1)} %param.5) | copy-start | bytes 221188
  37.4 19.6 %all-to-all-start.1 = ((bf16[4,128,1152]{2,1,0:T(8,128)(2,1)}), bf16[4,128,1152]{2,1,0:T(8,128)(2,1)S(1)}, u32[]{:S(2)}, u32[]{:S(2)}) async-start(bf16[4,128,1152]{2,1,0:T(8,128)(2,1)} %unit.1), calls=%async_computation.1 | async-start | bytes 2359296 | tf_op jit(solution)/shard_map/all_to_all | solution.py:320
  57.0 2.1 %copy-start = (bf16[128,1152]{1,0:T(8,128)(2,1)}, bf16[128,1152]{1,0:T(8,128)(2,1)S(1)}, u32[]{:S(2)}) copy-start(bf16[128,1152]{1,0:T(8,128)(2,1)S(1)} %concatenate.15) | copy-start | bytes 884740
  57.0 27.1 %collective-permute-start.3 = (bf16[512,1152]{1,0:T(8,128)(2,1)S(1)}, bf16[512,1152]{1,0:T(8,128)(2,1)S(1)}, u32[]{:S(2)}, u32[]{:S(2)}) collective-permute-start(bf16[512,1152]{1,0:T(8,128)(2,1)S(1)} %bitcast.43), channel_id=1, source_target_pairs={{0,4},{4,0},{1,5},{5,1},{2,6},{6,2},{3,7},{7,3},{8,12},{12,8},{9,1... | collective-permute-start | bytes 3538952 | tf_op jit(solution)/shard_map/ppermute | solution.py:286
  59.2 13.1 %collective-permute-start = (bf16[128,1152]{1,0:T(8,128)(2,1)S(1)}, bf16[128,1152]{1,0:T(8,128)(2,1)S(1)}, u32[]{:S(2)}, u32[]{:S(2)}) collective-permute-start(bf16[128,1152]{1,0:T(8,128)(2,1)S(1)} %fusion.2.t0), channel_id=1, source_target_pairs={{0,8},{8,16},{16,24},{24,0},{1,9},{9,17},{17,25},{25,1},{2,10},{10... | collective-permute-start | bytes 884744 | tf_op jit(solution)/shard_map/ppermute | solution.py:291
  62.7 16.7 %collective-permute-start.1 = (bf16[128,1152]{1,0:T(8,128)(2,1)S(1)}, bf16[128,1152]{1,0:T(8,128)(2,1)}, u32[]{:S(2)}, u32[]{:S(2)}) collective-permute-start(bf16[128,1152]{1,0:T(8,128)(2,1)S(1)} %fusion.2.t0), channel_id=1, source_target_pairs={{0,16},{8,24},{16,0},{24,8},{1,17},{9,25},{17,1},{25,9},{2,18},{10... | collective-permute-start | bytes 884744 | tf_op jit(solution)/shard_map/ppermute | solution.py:291
  67.5 13.2 %collective-permute-start.2 = (bf16[128,1152]{1,0:T(8,128)(2,1)S(1)}, bf16[128,1152]{1,0:T(8,128)(2,1)}, u32[]{:S(2)}, u32[]{:S(2)}) collective-permute-start(bf16[128,1152]{1,0:T(8,128)(2,1)S(1)} %fusion.2.t0), channel_id=1, source_target_pairs={{0,24},{8,0},{16,8},{24,16},{1,25},{9,1},{17,9},{25,17},{2,26},{10... | collective-permute-start | bytes 884744 | tf_op jit(solution)/shard_map/ppermute | solution.py:291
  87.3 28.2 %collective-permute-start.4 = (bf16[512,1152]{1,0:T(8,128)(2,1)S(1)}, bf16[512,1152]{1,0:T(8,128)(2,1)S(1)}, u32[]{:S(2)}, u32[]{:S(2)}) collective-permute-start(bf16[512,1152]{1,0:T(8,128)(2,1)S(1)} %get-tuple-element.19), channel_id=1, source_target_pairs={{0,4},{4,0},{1,5},{5,1},{2,6},{6,2},{3,7},{7,3},{8,12},{12,8},{9,1... | collective-permute-start | bytes 3538952 | tf_op jit(solution)/shard_map/ppermute | solution.py:286
  91.5 30.1 %collective-permute-start.5 = (bf16[128,1152]{1,0:T(8,128)(2,1)}, bf16[128,1152]{1,0:T(8,128)(2,1)S(1)}, u32[]{:S(2)}, u32[]{:S(2)}) collective-permute-start(bf16[128,1152]{1,0:T(8,128)(2,1)} %get-tuple-element.26), channel_id=1, source_target_pairs={{0,24},{8,0},{16,8},{24,16},{1,25},{9,1},{17,9},{25,17},{2,26},{10... | collective-permute-start | bytes 884744 | tf_op jit(solution)/shard_map/ppermute | solution.py:291
  96.0 25.5 %collective-permute-start.6 = (bf16[128,1152]{1,0:T(8,128)(2,1)}, bf16[128,1152]{1,0:T(8,128)(2,1)S(1)}, u32[]{:S(2)}, u32[]{:S(2)}) collective-permute-start(bf16[128,1152]{1,0:T(8,128)(2,1)} %get-tuple-element.27), channel_id=1, source_target_pairs={{0,16},{8,24},{16,0},{24,8},{1,17},{9,25},{17,1},{25,9},{2,18},{10... | collective-permute-start | bytes 884744 | tf_op jit(solution)/shard_map/ppermute | solution.py:291
  99.9 21.7 %collective-permute-start.7 = (bf16[128,1152]{1,0:T(8,128)(2,1)S(1)}, bf16[128,1152]{1,0:T(8,128)(2,1)S(1)}, u32[]{:S(2)}, u32[]{:S(2)}) collective-permute-start(bf16[128,1152]{1,0:T(8,128)(2,1)S(1)} %get-tuple-element.28), channel_id=1, source_target_pairs={{0,8},{8,16},{16,24},{24,0},{1,9},{9,17},{17,25},{25,1},{2,10},{10... | collective-permute-start | bytes 884744 | tf_op jit(solution)/shard_map/ppermute | solution.py:291
  116.8 4.8 %copy-start.1 = (bf16[128,1152]{1,0:T(8,128)(2,1)S(1)}, bf16[128,1152]{1,0:T(8,128)(2,1)}, u32[]{:S(2)}) copy-start(bf16[128,1152]{1,0:T(8,128)(2,1)} %copy-done) | copy-start | bytes 884740
  116.8 20.2 %all-to-all-start.3 = ((bf16[4,1184,128]{2,1,0:T(8,128)(2,1)}), bf16[4,1184,128]{2,1,0:T(8,128)(2,1)S(1)}, u32[]{:S(2)}, u32[]{:S(2)}) async-start(bf16[4,1184,128]{2,1,0:T(8,128)(2,1)} %combine.1), calls=%async_computation.3 | async-start | bytes 2424832 | tf_op jit(solution)/shard_map/all_to_all | solution.py:339
  138.3 33.0 %all-to-all-start.4 = ((bf16[16,80,128]{2,1,0:T(8,128)(2,1)}), bf16[16,80,128]{2,1,0:T(8,128)(2,1)S(1)}, u32[]{:S(2)}, u32[]{:S(2)}) async-start(bf16[16,80,128]{2,1,0:T(8,128)(2,1)} %finish.1), calls=%async_computation.4 | async-start | bytes 655360 | tf_op jit(solution)/shard_map/all_to_all | solution.py:343
  145.8 18.4 %collective-permute-start.10 = (bf16[128,288]{1,0:T(8,128)(2,1)S(1)}, bf16[128,288]{1,0:T(8,128)(2,1)S(1)}, u32[]{:S(2)}, u32[]{:S(2)}) collective-permute-start(bf16[128,288]{1,0:T(8,128)(2,1)S(1)} %get-tuple-element.35), channel_id=1, source_target_pairs={{0,3},{1,0},{2,1},{3,2},{4,7},{5,4},{6,5},{7,6},{8,11},{9,8},{10,9... | collective-permute-start | bytes 221192 | tf_op jit(solution)/shard_map/ppermute | solution.py:291
  151.4 17.0 %collective-permute-start.8 = (bf16[128,288]{1,0:T(8,128)(2,1)S(1)}, bf16[128,288]{1,0:T(8,128)(2,1)S(1)}, u32[]{:S(2)}, u32[]{:S(2)}) collective-permute-start(bf16[128,288]{1,0:T(8,128)(2,1)S(1)} %get-tuple-element.34), channel_id=1, source_target_pairs={{0,1},{1,2},{2,3},{3,0},{4,5},{5,6},{6,7},{7,4},{8,9},{9,10},{10,1... | collective-permute-start | bytes 221192 | tf_op jit(solution)/shard_map/ppermute | solution.py:291
  153.3 17.1 %collective-permute-start.9 = (bf16[128,288]{1,0:T(8,128)(2,1)S(1)}, bf16[128,288]{1,0:T(8,128)(2,1)S(1)}, u32[]{:S(2)}, u32[]{:S(2)}) collective-permute-start(bf16[128,288]{1,0:T(8,128)(2,1)S(1)} %get-tuple-element.36), channel_id=1, source_target_pairs={{0,2},{1,3},{2,0},{3,1},{4,6},{5,7},{6,4},{7,5},{8,10},{9,11},{10,... | collective-permute-start | bytes 221192 | tf_op jit(solution)/shard_map/ppermute | solution.py:291

commit v3 on v0

v3 whole, which is shorter than its diff:
```python
import functools

import jax
import jax.numpy as jnp
from jax import lax
from jax.experimental import pallas as pl
from jax.experimental.pallas import tpu as pltpu
from jax.sharding import Mesh, PartitionSpec as P

epsilon = 1e-06
lanes = 128
piece = 32
half = 64
strips = 4
rest = 32
chunk_rows = 72
carry_rows = 16
tiles = 9
vmem = pl.BlockSpec(memory_space=pltpu.VMEM)
smem = pl.BlockSpec(memory_space=pltpu.SMEM)
anywhere = pl.BlockSpec(memory_space=pl.ANY)
limits = pltpu.CompilerParams(vmem_limit_bytes=40 * 1024 * 1024)


def shape(dims, dtype=jnp.bfloat16):
    return jax.ShapeDtypeStruct(tuple(dims), dtype)


def call(kernel, out_shape, name, operands, scalars=(), after=(), flops=0, special=0):
    out_shape = tuple(out_shape)
    scalars, operands, after = tuple(scalars), tuple(operands), tuple(after)
    inputs = len(scalars) + len(operands)
    moved = sum(a.size * a.dtype.itemsize for a in operands + out_shape)

    def body(*refs):
        kernel(*refs[:inputs], *refs[inputs + len(after) :])

    return pl.pallas_call(
        body,
        out_shape=out_shape,
        in_specs=[smem] * len(scalars) + [vmem] * len(operands) + [anywhere] * len(after),
        out_specs=(vmem,) * len(out_shape),
        compiler_params=limits,
        cost_estimate=pl.CostEstimate(flops=flops, bytes_accessed=moved, transcendentals=special),
        name=name,
    )(*scalars, *operands, *after)


def total(values):
    return functools.reduce(lambda a, b: a + b, values)


def wide(ref, *index):
    return ref[index].astype(jnp.float32)


def lane_group():
    return lax.broadcasted_iota(jnp.int32, (8, lanes), 1) // rest


def pack_kernel(image, text, out):
    chunks = []
    for ref in (image, text):
        found = []
        for k in range(4):
            rows = wide(ref, pl.ds(k * piece, piece), slice(None))
            last = rows[:, 2 * lanes :]
            last = jnp.concatenate([last[8 * g : 8 * g + 8] for g in range(4)], axis=1)
            found.append(jnp.concatenate([rows[:, :lanes], rows[:, lanes : 2 * lanes], last], axis=0))
        chunks.append(found)
    for d in range(strips):
        a, b = d // 2, d % 2
        parts = chunks[0][2 * a : 2 * a + 2] + chunks[1][2 * b : 2 * b + 2]
        out[d] = jnp.concatenate(parts, axis=0).astype(jnp.bfloat16)


def unpack_rows(chunks, group):
    found = []
    lasts = []
    for chunk in chunks:
        found += [chunk[:piece], chunk[piece : 2 * piece]]
        lasts.append(chunk[2 * piece :])
    last = []
    for g in range(4):
        value = jnp.zeros((8, lanes), jnp.float32)
        for s in range(strips):
            turn = rest * (s - g) % lanes
            moved = pltpu.roll(lasts[s], turn, 1) if turn else lasts[s]
            value = jnp.where(group == s, moved, value)
        last.append(value)
    found.append(jnp.concatenate(last, axis=0))
    return found


def unit_tiles(arrived, c, group):
    chunks = [arrived[s][c * chunk_rows : (c + 1) * chunk_rows] for s in range(strips)]
    found = unpack_rows(chunks, group)
    inverse = lax.rsqrt(jnp.sum(total([t * t for t in found]), axis=1, keepdims=True) + epsilon)
    return [t * inverse for t in found], inverse


def unit_kernel(arrived, image, text):
    group = lane_group()
    values = [wide(arrived, s) for s in range(strips)]
    for c in range(4):
        units, _ = unit_tiles(values, c, group)
        out = image if c < 2 else text
        for t in range(tiles):
            out[(c % 2) * piece : (c % 2 + 1) * piece, t * lanes : (t + 1) * lanes] = units[
                t
            ].astype(jnp.bfloat16)


def join_kernel(image_own, image_near, text_own, text_near, image, text):
    for k in range(image.shape[0]):
        image[k, :half, :] = image_own[...]
        image[k, half:, :] = image_near[...]
    text[:half, :] = text_own[...]
    text[half:, :] = text_near[...]


def fold(values):
    rows, columns = values.shape
    part = jnp.sum(values.reshape(rows // 8, 8, columns), axis=0)
    return total([part[:, c : c + lanes] for c in range(0, columns, lanes)])


def pair_terms(left, right, scale, bias, same=None):
    product = lax.dot_general(
        left, right, (((1,), (1,)), ((), ())), preferred_element_type=jnp.float32
    )
    logits = scale * product + bias
    if same is None:
        grown = jnp.exp(logits)
        slope = grown / (1.0 + grown)
    else:
        grown = jnp.exp(jnp.where(same, -logits, logits))
        share = grown / (1.0 + grown)
        slope = jnp.where(same, -share, share)
    quarter = left.shape[0] // 4
    a, b, c, d = (grown[k * quarter : (k + 1) * quarter, :] for k in range(4))
    ab = a + (b + a * b)
    cd = c + (d + c * d)
    sums = (fold(jnp.log1p(ab + (cd + ab * cd))), fold(slope * product), fold(slope))
    return (scale * slope).astype(jnp.bfloat16), sums


def write_sums(out, sums, before=None):
    for k in range(3):
        value = total([found[k] for found in sums])
        if before is not None:
            value = value + before[8 * k : 8 * k + 8, :]
        out[8 * k : 8 * k + 8, :] = value


tile = 256


def home_kernel(scales, spot, left, right, weights, sums_out):
    rows, columns = left.shape[0], right.shape[0]
    sums = []
    for start in range(0, rows, tile):
        here = pl.ds(start, tile)
        row = lax.broadcasted_iota(jnp.int32, (tile, 1), 0) + (start - spot[0])
        row = jnp.where((row >= 0) & (row < half), row, -1)
        same = row == lax.broadcasted_iota(jnp.int32, (1, columns), 1)
        weights[here, :], found = pair_terms(
            left[here, :], right[...], scales[0], scales[1], same
        )
        sums.append(found)
    write_sums(sums_out, sums)


def own_kernel(scales, left, t0, t1, t2, t3, home, home_sums, back, weights, right, sums_out):
    rows, part = left.shape[0], t0.shape[0]
    for k, ref in enumerate((t0, t1, t2, t3)):
        right[k * part : (k + 1) * part, :] = ref[...]
    sums = []
    for start in range(0, rows, tile):
        here = pl.ds(start, tile)
        value, found = pair_terms(left[here, :], right[part:, :], scales[0], scales[1])
        weights[here, :part] = home[here, :]
        weights[here, part:] = value
        back[here, :] = jnp.dot(
            weights[here, :], right[...], preferred_element_type=jnp.float32
        ).astype(jnp.bfloat16)
        sums.append(found)
    write_sums(sums_out, sums, home_sums)


def other_kernel(scales, left, right, own_sums, back, weights, sums_out):
    sums = []
    for start in range(0, left.shape[0], tile):
        here = pl.ds(start, tile)
        value, found = pair_terms(left[here, :], right[...], scales[0], scales[1])
        weights[here, :] = value
        back[here, :] = jnp.dot(
            value, right[...], preferred_element_type=jnp.float32
        ).astype(jnp.bfloat16)
        sums.append(found)
    row = lax.broadcasted_iota(jnp.int32, (8, lanes), 0)
    value = jnp.zeros((8, lanes), jnp.float32)
    for k in range(3):
        found = total([s[k] for s in sums]) + own_sums[8 * k : 8 * k + 8, :]
        value = jnp.where(row == k, jnp.sum(found, axis=0, keepdims=True), value)
    for k in range(sums_out.shape[0]):
        sums_out[k] = value


def text_kernel(first_weights, second_weights, first, second, *backs):
    contract = (((0,), (0,)), ((), ()))
    part = backs[0].shape[0]
    value = lax.dot_general(
        first_weights[...], first[...], contract, preferred_element_type=jnp.float32
    ) + lax.dot_general(
        second_weights[...], second[...], contract, preferred_element_type=jnp.float32
    )
    for k, back in enumerate(backs):
        back[...] = value[k * part : (k + 1) * part].astype(jnp.bfloat16)


def three_parts(value):
    high = value.astype(jnp.bfloat16).astype(jnp.float32)
    middle = (value - high).astype(jnp.bfloat16).astype(jnp.float32)
    return high, middle, value - high - middle


def carry_of(value):
    parts = three_parts(jnp.sum(value, axis=1, keepdims=True))
    lane = lax.broadcasted_iota(jnp.int32, (8, lanes), 1)
    carry = jnp.zeros((8, lanes), jnp.float32)
    for k in range(3):
        carry = jnp.where(lane == k, parts[k], carry)
    return jnp.concatenate([carry, jnp.zeros((8, lanes), jnp.float32)], axis=0)


def combine_kernel(own, given, sums, out):
    count, all_rows, _ = out.shape
    block = own.shape[0] // count
    carry = carry_of(total([sums[k] for k in range(sums.shape[0])])).astype(jnp.bfloat16)
    for k in range(count):
        rows = pl.ds(k * block, block)
        for t in range(tiles):
            columns = pl.ds(t * lanes, lanes)
            value = wide(own, rows, columns) + wide(given, rows, columns)
            out[k, t * block : (t + 1) * block, :] = value.astype(jnp.bfloat16)
        out[k, tiles * block : all_rows, :] = carry


def image_sum_kernel(backs, kept, sent, carry_out):
    count = backs.shape[0]
    block = 2 * half
    tail = tiles * block
    for t in range(tiles):
        rows = total([wide(backs, k, pl.ds(t * block, block), slice(None)) for k in range(count)])
        kept[t * half : (t + 1) * half, :] = rows[:half]
        sent[t * half : (t + 1) * half, :] = rows[half:].astype(jnp.bfloat16)
    carried = total([wide(backs, k, pl.ds(tail, carry_rows), slice(None)) for k in range(count)])
    carry = carry_of(carried[:8])
    sent[tiles * half :, :] = carry.astype(jnp.bfloat16)
    carry_out[...] = carry.astype(jnp.bfloat16)


def text_sum_kernel(b0, b1, b2, b3, carry, kept, sent):
    for t in range(tiles):
        columns = pl.ds(t * lanes, lanes)
        rows = total([wide(b, slice(None), columns) for b in (b0, b1, b2, b3)])
        kept[t * half : (t + 1) * half, :] = rows[:half]
        sent[t * half : (t + 1) * half, :] = rows[half:].astype(jnp.bfloat16)
    sent[tiles * half :, :] = carry[...]


def finish_kernel(arrived, image_kept, image_given, text_kept, text_given, carry, far, out):
    group = lane_group()
    tail = pl.ds(tiles * half, carry_rows)
    carried = total(
        [
            wide(carry, slice(None)),
            wide(far, slice(None)),
            wide(image_given, tail, slice(None)),
            wide(text_given, tail, slice(None)),
        ]
    )
    carry_now = carry_of(carried[:8]).astype(jnp.bfloat16)
    values = [wide(arrived, s) for s in range(strips)]
    for c in range(4):
        units, inverse = unit_tiles(values, c, group)
        kept, given = (image_kept, image_given) if c < 2 else (text_kept, text_given)
        grads = []
        for t in range(tiles):
            rows = pl.ds(t * half + (c % 2) * piece, piece)
            grads.append(kept[rows, :] + wide(given, rows, slice(None)))
        along = jnp.sum(total([u * g for u, g in zip(units, grads)]), axis=1, keepdims=True)
        final = [(g - u * along) * inverse for u, g in zip(units, grads)]
        if c % 2 == 0:
            chunks = [[] for _ in range(strips)]
        for s in range(strips):
            last = jnp.zeros((8, lanes), jnp.float32)
            for g in range(4):
                turn = rest * (g - s) % lanes
                rows = final[tiles - 1][8 * g : 8 * g + 8]
                moved = pltpu.roll(rows, turn, 1) if turn else rows
                last = jnp.where(group == g, moved, last)
            chunks[s] += [final[2 * s], final[2 * s + 1], last]
            if c % 2 == 1:
                start = (c // 2) * 2 * chunk_rows
                value = jnp.concatenate(chunks[s], axis=0).astype(jnp.bfloat16)
                out[s, start : start + 2 * chunk_rows, :] = value
    for s in range(strips):
        out[s, 4 * chunk_rows :, :] = carry_now


def last_kernel(arrived, image, text, sums_out):
    values = [wide(arrived, s) for s in range(strips)]
    for which, out in enumerate((image, text)):
        for k in range(4):
            c = 2 * which + k % 2
            h = k // 2
            sources = (2 * h, 2 * h + 1) if which == 0 else (h, 2 + h)
            chunk = total([values[s][c * chunk_rows : (c + 1) * chunk_rows] for s in sources])
            rows = pl.ds(k * piece, piece)
            out[rows, 0:lanes] = chunk[:piece].astype(jnp.bfloat16)
            out[rows, lanes : 2 * lanes] = chunk[piece : 2 * piece].astype(jnp.bfloat16)
            last = chunk[2 * piece :]
            groups = [last] + [pltpu.roll(last, lanes - rest * g, 1) for g in range(1, 4)]
            value = jnp.concatenate(groups, axis=0)[:, :rest]
            out[rows, 2 * lanes : 2 * lanes + rest] = value.astype(jnp.bfloat16)
    sums = total([v[4 * chunk_rows : 4 * chunk_rows + 8] for v in values])
    sums_out[...] = jnp.broadcast_to(jnp.sum(sums, axis=1, keepdims=True), sums.shape)


def swap_core(value):
    return lax.ppermute(value, "core", [(0, 1), (1, 0)])


def shift(value, axis, k):
    count = lax.axis_size(axis)
    return lax.ppermute(value, axis, [(i, (i + k) % count) for i in range(count)])


def swap_image(value):
    return lax.ppermute(value, "zh", [(0, 1), (1, 0), (2, 3), (3, 2)])


def swap_text(value):
    return lax.ppermute(value, "zh", [(0, 3), (3, 0), (1, 2), (2, 1)])


def shards(image, text, log_temp, bias):
    rows, strip = image.shape
    x_count, y_count = (lax.axis_size(name) for name in ("x", "y"))
    width = strip * strips
    block = 2 * half
    count = x_count * block
    x, zl = (lax.axis_index(name) for name in ("x", "zl"))
    scale = jnp.exp(log_temp)
    scales = jnp.stack([scale, bias])
    spot = jnp.where(zl // 2 == zl % 2, x * block, -count).astype(jnp.int32).reshape(1)
    f32 = jnp.float32

    (packed,) = call(pack_kernel, [shape((strips, 4 * chunk_rows, lanes))], "pack", [image, text])
    arrived = lax.all_to_all(packed, "zl", 0, 0)
    image_unit, text_unit = call(unit_kernel, [shape((half, width))] * 2, "unit", [arrived])
    image_near = swap_image(image_unit)
    text_near = swap_text(text_unit)
    joined, home_text = call(
        join_kernel,
        [shape((x_count, block, width)), shape((block, width))],
        "join",
        [image_unit, image_near, text_unit, text_near],
    )
    image_rows = lax.all_to_all(joined, "x", 0, 0).reshape(count, width)
    texts = [home_text] + [shift(home_text, "y", k) for k in range(1, y_count)]
    other_rows = swap_core(image_rows)

    columns = y_count * block
    area = count * columns
    home_weights, home_sums = call(
        home_kernel,
        [shape((count, block)), shape((24, lanes), f32)],
        "home",
        [image_rows, home_text],
        scalars=[scales, spot],
        flops=200 * count * block * width,
    )
    own_back, own_weights, right, own_sums = call(
        own_kernel,
        [
            shape((count, width)),
            shape((count, columns)),
            shape((columns, width)),
            shape((24, lanes), f32),
        ],
        "own",
        [image_rows] + texts + [home_weights, home_sums],
        scalars=[scales],
        flops=4 * area * width,
        special=2 * area,
    )
    other_back, other_weights, sums = call(
        other_kernel,
        [shape((count, width)), shape((count, columns)), shape((y_count * 2, 8, lanes), f32)],
        "other",
        [other_rows, right, own_sums],
        scalars=[scales],
        flops=4 * area * width,
        special=2 * area,
    )
    given_back = swap_core(other_back)
    sums = lax.all_to_all(sums, ("y", "core"), 0, 0)
    text_backs = call(
        text_kernel,
        [shape((block, width))] * y_count,
        "text_back",
        [own_weights, other_weights, image_rows, other_rows],
        flops=4 * area * width,
    )
    (combined,) = call(
        combine_kernel,
        [shape((x_count, tiles * block + carry_rows, lanes))],
        "combine",
        [own_back, given_back, sums],
    )
    combined = lax.all_to_all(combined, "x", 0, 0)
    part = [shape((tiles * half, lanes), f32), shape((tiles * half + carry_rows, lanes))]
    image_kept, image_sent, carry = call(
        image_sum_kernel, part + [shape((carry_rows, lanes))], "image_sum", [combined]
    )
    image_given = swap_image(image_sent)
    far = shift(carry, "zh", 2)
    moved = [text_backs[0]] + [shift(text_backs[k], "y", -k) for k in range(1, y_count)]
    text_kept, text_sent = call(text_sum_kernel, part, "text_sum", moved + [carry])
    text_given = swap_text(text_sent)
    (finished,) = call(
        finish_kernel,
        [shape((strips, 4 * chunk_rows + carry_rows, lanes))],
        "finish",
        [arrived, image_kept, image_given, text_kept, text_given, carry, far],
    )
    finished = lax.all_to_all(finished, "zl", 0, 0)
    grad_image, grad_text, sums = call(
        last_kernel, [shape((rows, strip))] * 2 + [shape((8, lanes), f32)], "last", [finished]
    )
    pairs_count = rows * 4 * x_count * y_count * 2
    return (
        sums[0, 0] / pairs_count,
        grad_image,
        grad_text,
        scale * sums[1, 0] / pairs_count,
        sums[2, 0] / pairs_count,
    )


def solution(mesh):
    fine = Mesh(mesh.devices.reshape(4, 4, 4, 2, 4), ("zh", "x", "y", "core", "zl"))
    whole = P(("zh", "x", "y", "core"), "zl")
    return jax.shard_map(
        shards,
        mesh=fine,
        in_specs=(whole, whole, P(), P()),
        out_specs=(P(), whole, whole, P(), P()),
        check_vma=False,
    )
```

time: 455 us -> 167 us (0.37)
  the two profiles are of different devices: /device:TPU:1 before, /device:TPU:2 now
where the time goes in v3:
time: 167 us; the launch traced here: 166 us
  starting transfers between devices  68.3 us (41%)
  blocking collectives  44.3 us (27%)
  waiting for transfers between devices  24.7 us (15%)
  Pallas kernels  12.2 us (7%)
  local copies, waits for them, and re-layouts  8.95 us (5%)
  between operations  7.55 us (5%)
    ppermute x7, starting transfers between devices, shift(): lax.ppermute(value, axis, [(i, (i + k) % count) for i in range(count)])  30 us
    all_to_all x1, blocking collectives, shards(): finished = lax.all_to_all(finished, 'zl', 0, 0)  21.2 us
    ppermute x2, starting transfers between devices, swap_image(): return lax.ppermute(value, 'zh', [(0, 1), (1, 0), (2, 3), (3, 2)])  15.8 us
    all_to_all x1, blocking collectives, shards(): arrived = lax.all_to_all(packed, 'zl', 0, 0)  15.3 us
    pallas_call x12, Pallas kernels, call(): pl.pallas_call(body, out_shape=out_shape, in_specs=[smem] * len(scalars)...  12.2 us
    ppermute x7, waiting for transfers between devices, shift(): lax.ppermute(value, axis, [(i, (i + k) % count) for i in range(count)])  11.9 us
    ppermute x2, starting transfers between devices, swap_text(): return lax.ppermute(value, 'zh', [(0, 3), (3, 0), (1, 2), (2, 1)])  9.07 us
    unnamed x16, local copies, waits for them, and re-layouts  8.42 us
  transfers between devices with their start and end apart: 15, of which 7 were waited for; matrix products, arithmetic and copies ran while one was open for 0% of the time, Pallas kernels for 4%

profile of v3, /device:TPU:2, one launch (start us, length us, event | category | flops | bytes accessed | tf_op | source)
XLA Modules:
  0.0 166.1 jit_solution(487259457188057925)
XLA Ops:
  0.6 1.0 copy.9.refs_0_
  1.6 1.0 copy.10.refs_1_
  2.6 0.1 pack.1
  2.7 15.3 %all_to_all.25.refs_0_ = bf16[4,288,128]{2,1,0:T(8,128)(2,1)S(1)} all-to-all(bf16[4,288,128]{2,1,0:T(8,128)(2,1)S(1)} %pack.1), channel_id=1, replica_groups=mesh['zh'=4,'x'=4,'y'=4,'core'=2,'zl'=4] {'zl'}, dimensions={0} | all-to-all | bytes 589824 | tf_op jit(solution)/shard_map/all_to_all | solution.py:362
  18.0 0.2 unit.1
  18.2 9.1 %collective-permute-start = (bf16[64,1152]{1,0:T(8,128)(2,1)S(1)}, bf16[64,1152]{1,0:T(8,128)(2,1)S(1)}, u32[]{:S(2)}, u32[]{:S(2)}) collective-permute-start(bf16[64,1152]{1,0:T(8,128)(2,1)S(1)} %get-tuple-element.30.refs_0_), channel_id=1, source_target_pairs={{0,128},{128,0},{256,384},{384,256},{1,129},{129,1},{257,385},{385... | collective-permute-start | bytes 442376 | tf_op jit(solution)/shard_map/ppermute | solution.py:342
  27.3 6.4 %collective-permute-start.1 = (bf16[64,1152]{1,0:T(8,128)(2,1)S(1)}, bf16[64,1152]{1,0:T(8,128)(2,1)S(1)}, u32[]{:S(2)}, u32[]{:S(2)}) collective-permute-start(bf16[64,1152]{1,0:T(8,128)(2,1)S(1)} %get-tuple-element.31.refs_2_), channel_id=1, source_target_pairs={{0,384},{384,0},{128,256},{256,128},{1,385},{385,1},{129,257},{257... | collective-permute-start | bytes 442376 | tf_op jit(solution)/shard_map/ppermute | solution.py:346
  33.8 5.1 %collective-permute-done.refs_1_ = bf16[64,1152]{1,0:T(8,128)(2,1)S(1)} collective-permute-done((bf16[64,1152]{1,0:T(8,128)(2,1)S(1)}, bf16[64,1152]{1,0:T(8,128)(2,1)S(1)}, u32[]{:S(2)}, u32[]{:S(2)}) %collective-permute-start) | collective-permute-done | bytes 147488 | tf_op jit(solution)/shard_map/ppermute | solution.py:342
  38.8 6.5 %collective-permute-done.1.refs_3_ = bf16[64,1152]{1,0:T(8,128)(2,1)S(1)} collective-permute-done((bf16[64,1152]{1,0:T(8,128)(2,1)S(1)}, bf16[64,1152]{1,0:T(8,128)(2,1)S(1)}, u32[]{:S(2)}, u32[]{:S(2)}) %collective-permute-start.1) | collective-permute-done | bytes 147488 | tf_op jit(solution)/shard_map/ppermute | solution.py:346
  45.3 1.1 join.1
  46.5 4.8 %all-to-all-start.1 = ((bf16[4,128,1152]{2,1,0:T(8,128)(2,1)}), bf16[4,128,1152]{2,1,0:T(8,128)(2,1)S(1)}, u32[]{:S(2)}, u32[]{:S(2)}) async-start(bf16[4,128,1152]{2,1,0:T(8,128)(2,1)} %get-tuple-element.32), calls=%async_computation.1 | async-start | bytes 2359296 | tf_op jit(solution)/shard_map/all_to_all | solution.py:372
  52.6 0.1 pad_maximum_fusion.refs_0_
  52.7 4.9 %collective-permute-start.4 = (bf16[128,1152]{1,0:T(8,128)(2,1)S(1)}, bf16[128,1152]{1,0:T(8,128)(2,1)S(1)}, u32[]{:S(2)}, u32[]{:S(2)}) collective-permute-start(bf16[128,1152]{1,0:T(8,128)(2,1)S(1)} %get-tuple-element.33.refs_3_.refs_2_), channel_id=1, source_target_pairs={{0,24},{8,0},{16,8},{24,16},{1,25},{9,1},{17,9},{25,17},{2,26},{10... | collective-permute-start | bytes 884744 | tf_op jit(solution)/shard_map/ppermute | solution.py:338
  57.6 2.5 %collective-permute-start.3 = (bf16[128,1152]{1,0:T(8,128)(2,1)S(1)}, bf16[128,1152]{1,0:T(8,128)(2,1)S(1)}, u32[]{:S(2)}, u32[]{:S(2)}) collective-permute-start(bf16[128,1152]{1,0:T(8,128)(2,1)S(1)} %get-tuple-element.33.refs_3_.refs_2_), channel_id=1, source_target_pairs={{0,16},{8,24},{16,0},{24,8},{1,17},{9,25},{17,1},{25,9},{2,18},{10... | collective-permute-start | bytes 884744 | tf_op jit(solution)/shard_map/ppermute | solution.py:338
  60.2 2.9 %collective-permute-start.2 = (bf16[128,1152]{1,0:T(8,128)(2,1)S(1)}, bf16[128,1152]{1,0:T(8,128)(2,1)S(1)}, u32[]{:S(2)}, u32[]{:S(2)}) collective-permute-start(bf16[128,1152]{1,0:T(8,128)(2,1)S(1)} %get-tuple-element.33.refs_3_.refs_2_), channel_id=1, source_target_pairs={{0,8},{8,16},{16,24},{24,0},{1,9},{9,17},{17,25},{25,1},{2,10},{10... | collective-permute-start | bytes 884744 | tf_op jit(solution)/shard_map/ppermute | solution.py:338
  63.1 1.9 %collective-permute-start.5 = (bf16[512,1152]{1,0:T(8,128)(2,1)S(1)}, bf16[512,1152]{1,0:T(8,128)(2,1)S(1)}, u32[]{:S(2)}, u32[]{:S(2)}) collective-permute-start(bf16[512,1152]{1,0:T(8,128)(2,1)S(1)} %bitcast.8), channel_id=1, source_target_pairs={{0,4},{4,0},{1,5},{5,1},{2,6},{6,2},{3,7},{7,3},{8,12},{12,8},{9,1... | collective-permute-start | bytes 3538952 | tf_op jit(solution)/shard_map/ppermute | solution.py:333
  65.0 1.1 home.1
  66.2 1.7 %collective-permute-done.3.refs_4_ = bf16[128,1152]{1,0:T(8,128)(2,1)S(1)} collective-permute-done((bf16[128,1152]{1,0:T(8,128)(2,1)S(1)}, bf16[128,1152]{1,0:T(8,128)(2,1)S(1)}, u32[]{:S(2)}, u32[]{:S(2)}) %collective-permute-start.3) | collective-permute-done | bytes 294944 | tf_op jit(solution)/shard_map/ppermute | solution.py:338
  67.8 3.1 %collective-permute-done.2.refs_3_ = bf16[128,1152]{1,0:T(8,128)(2,1)S(1)} collective-permute-done((bf16[128,1152]{1,0:T(8,128)(2,1)S(1)}, bf16[128,1152]{1,0:T(8,128)(2,1)S(1)}, u32[]{:S(2)}, u32[]{:S(2)}) %collective-permute-start.2) | collective-permute-done | bytes 294944 | tf_op jit(solution)/shard_map/ppermute | solution.py:338
  70.9 2.6 %own.1 = (bf16[512,1152]{1,0:T(8,128)(2,1)S(1)}, bf16[512,512]{1,0:T(8,128)(2,1)S(1)}, bf16[512,1152]{1,0:T(8,128)(2,1)S(1)}, f32[24,128]{1,0:T(8,128)S(1)}) custom-call(f32[2]{0:T(128)S(1)} %pad_maximum_fusion.refs_0_, bf16[512,1152]{1,0:T(8,128)(2,1)S(1)} %bitcast.10, bf16[128,1152]{1,0:T(8,128)(2,1)S(1)} %get-tuple-element.33.refs_3_.refs_2_, ...), custom_call_target="tpu_custom_call" | custom-call | flops 1207959552 | bytes 5398528 | tf_op jit(solution)/shard_map/own/pallas_call | solution.py:38
  73.5 0.8 copy-done.2
  74.3 2.6 %other.1 = (bf16[512,1152]{1,0:T(8,128)(2,1)S(1)}, bf16[512,512]{1,0:T(8,128)(2,1)S(1)}, f32[8,8,128]{2,1,0:T(8,128)S(1)}) custom-call(f32[2]{0:T(128)S(1)} %pad_maximum_fusion.refs_0_, bf16[512,1152]{1,0:T(8,128)(2,1)S(1)} %collective-permute-done.5.refs_1_.refs_3_, bf16[512,1152]{1,0:T(8,128)(2,1)S(1)} %get-tuple-element.37.refs_2_, ...), custom_call_target="tpu_custom_call" | custom-call | flops 1207959552 | bytes 4108288 | tf_op jit(solution)/shard_map/other/pallas_call | solution.py:38
  76.9 0.8 copy-done.4
  77.7 1.9 %collective-permute-start.6 = (bf16[512,1152]{1,0:T(8,128)(2,1)S(1)}, bf16[512,1152]{1,0:T(8,128)(2,1)S(1)}, u32[]{:S(2)}, u32[]{:S(2)}) collective-permute-start(bf16[512,1152]{1,0:T(8,128)(2,1)S(1)} %get-tuple-element.39), channel_id=1, source_target_pairs={{0,4},{4,0},{1,5},{5,1},{2,6},{6,2},{3,7},{7,3},{8,12},{12,8},{9,1... | collective-permute-start | bytes 3538952 | tf_op jit(solution)/shard_map/ppermute | solution.py:333
  79.6 7.8 %all_to_all.26.refs_2_ = f32[8,8,128]{2,1,0:T(8,128)S(1)} all-to-all(f32[8,8,128]{2,1,0:T(8,128)S(1)} %get-tuple-element.40), channel_id=1, replica_groups=mesh['zh'=4,'x'=4,'y'=4,'core'=2,'zl'=4] {'y','core'}, dimensions={0} | all-to-all | bytes 65536 | tf_op jit(solution)/shard_map/all_to_all | solution.py:410
  87.4 1.4 combine.1
  88.8 4.8 %all-to-all-start.3 = ((bf16[4,1168,128]{2,1,0:T(8,128)(2,1)}), bf16[4,1168,128]{2,1,0:T(8,128)(2,1)S(1)}, u32[]{:S(2)}, u32[]{:S(2)}) async-start(bf16[4,1168,128]{2,1,0:T(8,128)(2,1)} %combine.1), calls=%async_computation.3 | async-start | bytes 2392064 | tf_op jit(solution)/shard_map/all_to_all | solution.py:424
  93.6 1.3 copy-done.1
  94.9 1.0 copy-done.3
  95.9 1.0 copy-done.5
  97.0 2.2 %text_back.1 = (bf16[128,1152]{1,0:T(8,128)(2,1)S(1)}, bf16[128,1152]{1,0:T(8,128)(2,1)}, bf16[128,1152]{1,0:T(8,128)(2,1)S(1)}, bf16[128,1152]{1,0:T(8,128)(2,1)S(1)}) custom-call(bf16[512,512]{1,0:T(8,128)(2,1)S(1)} %copy-done.3, bf16[512,512]{1,0:T(8,128)(2,1)S(1)} %copy-done.5, bf16[512,1152]{1,0:T(8,128)(2,1)S(1)} %bitcast.11, ...), custom_call_target="tpu_custom_call" | custom-call | flops 1207959552 | bytes 4587520 | tf_op jit(solution)/shard_map/text_back/pallas_call | solution.py:38
  99.2 3.1 %collective-permute-start.8 = (bf16[128,1152]{1,0:T(8,128)(2,1)}, bf16[128,1152]{1,0:T(8,128)(2,1)S(1)}, u32[]{:S(2)}, u32[]{:S(2)}) collective-permute-start(bf16[128,1152]{1,0:T(8,128)(2,1)} %get-tuple-element.46), channel_id=1, source_target_pairs={{0,24},{8,0},{16,8},{24,16},{1,25},{9,1},{17,9},{25,17},{2,26},{10... | collective-permute-start | bytes 884744 | tf_op jit(solution)/shard_map/ppermute | solution.py:338
  102.2 3.4 %collective-permute-start.9 = (bf16[128,1152]{1,0:T(8,128)(2,1)S(1)}, bf16[128,1152]{1,0:T(8,128)(2,1)S(1)}, u32[]{:S(2)}, u32[]{:S(2)}) collective-permute-start(bf16[128,1152]{1,0:T(8,128)(2,1)S(1)} %get-tuple-element.47), channel_id=1, source_target_pairs={{0,16},{8,24},{16,0},{24,8},{1,17},{9,25},{17,1},{25,9},{2,18},{10... | collective-permute-start | bytes 884744 | tf_op jit(solution)/shard_map/ppermute | solution.py:338
  105.6 1.9 %collective-permute-start.10 = (bf16[128,1152]{1,0:T(8,128)(2,1)S(1)}, bf16[128,1152]{1,0:T(8,128)(2,1)S(1)}, u32[]{:S(2)}, u32[]{:S(2)}) collective-permute-start(bf16[128,1152]{1,0:T(8,128)(2,1)S(1)} %get-tuple-element.48), channel_id=1, source_target_pairs={{0,8},{8,16},{16,24},{24,0},{1,9},{9,17},{17,25},{25,1},{2,10},{10... | collective-permute-start | bytes 884744 | tf_op jit(solution)/shard_map/ppermute | solution.py:338
  107.5 1.2 all-to-all-done.3.refs_0_
  108.8 0.2 image_sum.1
  109.0 6.7 %collective-permute-start.7 = (bf16[592,128]{1,0:T(8,128)(2,1)S(1)}, bf16[592,128]{1,0:T(8,128)(2,1)S(1)}, u32[]{:S(2)}, u32[]{:S(2)}) collective-permute-start(bf16[592,128]{1,0:T(8,128)(2,1)S(1)} %get-tuple-element.42), channel_id=1, source_target_pairs={{0,128},{128,0},{256,384},{384,256},{1,129},{129,1},{257,385},{385... | collective-permute-start | bytes 454664 | tf_op jit(solution)/shard_map/ppermute | solution.py:342
  115.7 4.1 %collective-permute-done.10.refs_3_ = bf16[128,1152]{1,0:T(8,128)(2,1)S(1)} collective-permute-done((bf16[128,1152]{1,0:T(8,128)(2,1)S(1)}, bf16[128,1152]{1,0:T(8,128)(2,1)S(1)}, u32[]{:S(2)}, u32[]{:S(2)}) %collective-permute-start.10) | collective-permute-done | bytes 294944 | tf_op jit(solution)/shard_map/ppermute | solution.py:338
  119.8 0.1 text_sum.1
  119.9 2.7 %collective-permute-start.11 = (bf16[592,128]{1,0:T(8,128)(2,1)S(1)}, bf16[592,128]{1,0:T(8,128)(2,1)S(1)}, u32[]{:S(2)}, u32[]{:S(2)}) collective-permute-start(bf16[592,128]{1,0:T(8,128)(2,1)S(1)} %get-tuple-element.51), channel_id=1, source_target_pairs={{0,384},{384,0},{128,256},{256,128},{1,385},{385,1},{129,257},{257... | collective-permute-start | bytes 454664 | tf_op jit(solution)/shard_map/ppermute | solution.py:346
  122.6 11.3 %collective-permute-start.12 = (bf16[16,128]{1,0:T(8,128)(2,1)S(1)}, bf16[16,128]{1,0:T(8,128)(2,1)S(1)}, u32[]{:S(2)}, u32[]{:S(2)}) collective-permute-start(bf16[16,128]{1,0:T(8,128)(2,1)S(1)} %get-tuple-element.49.refs_4_.refs_5_), channel_id=1, source_target_pairs={{0,256},{128,384},{256,0},{384,128},{1,257},{129,385},{257,1},{385... | collective-permute-start | bytes 12296 | tf_op jit(solution)/shard_map/ppermute | solution.py:338
  133.9 3.0 %collective-permute-done.12.refs_6_ = bf16[16,128]{1,0:T(8,128)(2,1)S(1)} collective-permute-done((bf16[16,128]{1,0:T(8,128)(2,1)S(1)}, bf16[16,128]{1,0:T(8,128)(2,1)S(1)}, u32[]{:S(2)}, u32[]{:S(2)}) %collective-permute-start.12) | collective-permute-done | bytes 4128 | tf_op jit(solution)/shard_map/ppermute | solution.py:338
  136.9 0.4 finish.1
  137.4 21.2 %all_to_all.27.refs_0_ = bf16[4,304,128]{2,1,0:T(8,128)(2,1)S(1)} all-to-all(bf16[4,304,128]{2,1,0:T(8,128)(2,1)S(1)} %finish.1), channel_id=1, replica_groups=mesh['zh'=4,'x'=4,'y'=4,'core'=2,'zl'=4] {'zl'}, dimensions={0} | all-to-all | bytes 622592 | tf_op jit(solution)/shard_map/all_to_all | solution.py:440
  158.6 0.1 last.1
  158.7 0.5 fusion
  161.2 0.7 copy.11
  161.9 0.7 copy.12
  (15 shorter events, 0.0 us)
Async XLA Ops:
  18.2 20.6 %collective-permute-start = (bf16[64,1152]{1,0:T(8,128)(2,1)S(1)}, bf16[64,1152]{1,0:T(8,128)(2,1)S(1)}, u32[]{:S(2)}, u32[]{:S(2)}) collective-permute-start(bf16[64,1152]{1,0:T(8,128)(2,1)S(1)} %get-tuple-element.30.refs_0_), channel_id=1, source_target_pairs={{0,128},{128,0},{256,384},{384,256},{1,129},{129,1},{257,385},{385... | collective-permute-start | bytes 442376 | tf_op jit(solution)/shard_map/ppermute | solution.py:342
  27.3 18.0 %collective-permute-start.1 = (bf16[64,1152]{1,0:T(8,128)(2,1)S(1)}, bf16[64,1152]{1,0:T(8,128)(2,1)S(1)}, u32[]{:S(2)}, u32[]{:S(2)}) collective-permute-start(bf16[64,1152]{1,0:T(8,128)(2,1)S(1)} %get-tuple-element.31.refs_2_), channel_id=1, source_target_pairs={{0,384},{384,0},{128,256},{256,128},{1,385},{385,1},{129,257},{257... | collective-permute-start | bytes 442376 | tf_op jit(solution)/shard_map/ppermute | solution.py:346
  46.5 16.6 %all-to-all-start.1 = ((bf16[4,128,1152]{2,1,0:T(8,128)(2,1)}), bf16[4,128,1152]{2,1,0:T(8,128)(2,1)S(1)}, u32[]{:S(2)}, u32[]{:S(2)}) async-start(bf16[4,128,1152]{2,1,0:T(8,128)(2,1)} %get-tuple-element.32), calls=%async_computation.1 | async-start | bytes 2359296 | tf_op jit(solution)/shard_map/all_to_all | solution.py:372
  52.7 13.4 %collective-permute-start.4 = (bf16[128,1152]{1,0:T(8,128)(2,1)S(1)}, bf16[128,1152]{1,0:T(8,128)(2,1)S(1)}, u32[]{:S(2)}, u32[]{:S(2)}) collective-permute-start(bf16[128,1152]{1,0:T(8,128)(2,1)S(1)} %get-tuple-element.33.refs_3_.refs_2_), channel_id=1, source_target_pairs={{0,24},{8,0},{16,8},{24,16},{1,25},{9,1},{17,9},{25,17},{2,26},{10... | collective-permute-start | bytes 884744 | tf_op jit(solution)/shard_map/ppermute | solution.py:338
  57.6 10.2 %collective-permute-start.3 = (bf16[128,1152]{1,0:T(8,128)(2,1)S(1)}, bf16[128,1152]{1,0:T(8,128)(2,1)S(1)}, u32[]{:S(2)}, u32[]{:S(2)}) collective-permute-start(bf16[128,1152]{1,0:T(8,128)(2,1)S(1)} %get-tuple-element.33.refs_3_.refs_2_), channel_id=1, source_target_pairs={{0,16},{8,24},{16,0},{24,8},{1,17},{9,25},{17,1},{25,9},{2,18},{10... | collective-permute-start | bytes 884744 | tf_op jit(solution)/shard_map/ppermute | solution.py:338
  60.2 10.7 %collective-permute-start.2 = (bf16[128,1152]{1,0:T(8,128)(2,1)S(1)}, bf16[128,1152]{1,0:T(8,128)(2,1)S(1)}, u32[]{:S(2)}, u32[]{:S(2)}) collective-permute-start(bf16[128,1152]{1,0:T(8,128)(2,1)S(1)} %get-tuple-element.33.refs_3_.refs_2_), channel_id=1, source_target_pairs={{0,8},{8,16},{16,24},{24,0},{1,9},{9,17},{17,25},{25,1},{2,10},{10... | collective-permute-start | bytes 884744 | tf_op jit(solution)/shard_map/ppermute | solution.py:338
  63.1 11.2 %collective-permute-start.5 = (bf16[512,1152]{1,0:T(8,128)(2,1)S(1)}, bf16[512,1152]{1,0:T(8,128)(2,1)S(1)}, u32[]{:S(2)}, u32[]{:S(2)}) collective-permute-start(bf16[512,1152]{1,0:T(8,128)(2,1)S(1)} %bitcast.8), channel_id=1, source_target_pairs={{0,4},{4,0},{1,5},{5,1},{2,6},{6,2},{3,7},{7,3},{8,12},{12,8},{9,1... | collective-permute-start | bytes 3538952 | tf_op jit(solution)/shard_map/ppermute | solution.py:333
  73.5 0.8 copy-start.2
  74.3 2.6 %copy-start = (bf16[512,1152]{1,0:T(8,128)(2,1)}, bf16[512,1152]{1,0:T(8,128)(2,1)S(1)}, u32[]{:S(2)}) copy-start(bf16[512,1152]{1,0:T(8,128)(2,1)S(1)} %collective-permute-done.5.refs_1_.refs_3_) | copy-start | bytes 3538948
  76.9 0.8 copy-start.4
  77.7 9.7 %collective-permute-start.6 = (bf16[512,1152]{1,0:T(8,128)(2,1)S(1)}, bf16[512,1152]{1,0:T(8,128)(2,1)S(1)}, u32[]{:S(2)}, u32[]{:S(2)}) collective-permute-start(bf16[512,1152]{1,0:T(8,128)(2,1)S(1)} %get-tuple-element.39), channel_id=1, source_target_pairs={{0,4},{4,0},{1,5},{5,1},{2,6},{6,2},{3,7},{7,3},{8,12},{12,8},{9,1... | collective-permute-start | bytes 3538952 | tf_op jit(solution)/shard_map/ppermute | solution.py:333
  88.8 19.9 %all-to-all-start.3 = ((bf16[4,1168,128]{2,1,0:T(8,128)(2,1)}), bf16[4,1168,128]{2,1,0:T(8,128)(2,1)S(1)}, u32[]{:S(2)}, u32[]{:S(2)}) async-start(bf16[4,1168,128]{2,1,0:T(8,128)(2,1)} %combine.1), calls=%async_computation.3 | async-start | bytes 2392064 | tf_op jit(solution)/shard_map/all_to_all | solution.py:424
  93.6 1.3 copy-start.1
  94.9 1.0 copy-start.3
  95.9 1.0 copy-start.5
  99.2 16.5 %collective-permute-start.8 = (bf16[128,1152]{1,0:T(8,128)(2,1)}, bf16[128,1152]{1,0:T(8,128)(2,1)S(1)}, u32[]{:S(2)}, u32[]{:S(2)}) collective-permute-start(bf16[128,1152]{1,0:T(8,128)(2,1)} %get-tuple-element.46), channel_id=1, source_target_pairs={{0,24},{8,0},{16,8},{24,16},{1,25},{9,1},{17,9},{25,17},{2,26},{10... | collective-permute-start | bytes 884744 | tf_op jit(solution)/shard_map/ppermute | solution.py:338
  102.2 13.5 %collective-permute-start.9 = (bf16[128,1152]{1,0:T(8,128)(2,1)S(1)}, bf16[128,1152]{1,0:T(8,128)(2,1)S(1)}, u32[]{:S(2)}, u32[]{:S(2)}) collective-permute-start(bf16[128,1152]{1,0:T(8,128)(2,1)S(1)} %get-tuple-element.47), channel_id=1, source_target_pairs={{0,16},{8,24},{16,0},{24,8},{1,17},{9,25},{17,1},{25,9},{2,18},{10... | collective-permute-start | bytes 884744 | tf_op jit(solution)/shard_map/ppermute | solution.py:338
  105.6 14.2 %collective-permute-start.10 = (bf16[128,1152]{1,0:T(8,128)(2,1)S(1)}, bf16[128,1152]{1,0:T(8,128)(2,1)S(1)}, u32[]{:S(2)}, u32[]{:S(2)}) collective-permute-start(bf16[128,1152]{1,0:T(8,128)(2,1)S(1)} %get-tuple-element.48), channel_id=1, source_target_pairs={{0,8},{8,16},{16,24},{24,0},{1,9},{9,17},{17,25},{25,1},{2,10},{10... | collective-permute-start | bytes 884744 | tf_op jit(solution)/shard_map/ppermute | solution.py:338
  109.0 28.0 %collective-permute-start.7 = (bf16[592,128]{1,0:T(8,128)(2,1)S(1)}, bf16[592,128]{1,0:T(8,128)(2,1)S(1)}, u32[]{:S(2)}, u32[]{:S(2)}) collective-permute-start(bf16[592,128]{1,0:T(8,128)(2,1)S(1)} %get-tuple-element.42), channel_id=1, source_target_pairs={{0,128},{128,0},{256,384},{384,256},{1,129},{129,1},{257,385},{385... | collective-permute-start | bytes 454664 | tf_op jit(solution)/shard_map/ppermute | solution.py:342
  119.9 17.0 %collective-permute-start.11 = (bf16[592,128]{1,0:T(8,128)(2,1)S(1)}, bf16[592,128]{1,0:T(8,128)(2,1)S(1)}, u32[]{:S(2)}, u32[]{:S(2)}) collective-permute-start(bf16[592,128]{1,0:T(8,128)(2,1)S(1)} %get-tuple-element.51), channel_id=1, source_target_pairs={{0,384},{384,0},{128,256},{256,128},{1,385},{385,1},{129,257},{257... | collective-permute-start | bytes 454664 | tf_op jit(solution)/shard_map/ppermute | solution.py:346
  122.6 14.3 %collective-permute-start.12 = (bf16[16,128]{1,0:T(8,128)(2,1)S(1)}, bf16[16,128]{1,0:T(8,128)(2,1)S(1)}, u32[]{:S(2)}, u32[]{:S(2)}) collective-permute-start(bf16[16,128]{1,0:T(8,128)(2,1)S(1)} %get-tuple-element.49.refs_4_.refs_5_), channel_id=1, source_target_pairs={{0,256},{128,384},{256,0},{384,128},{1,257},{129,385},{257,1},{385... | collective-permute-start | bytes 12296 | tf_op jit(solution)/shard_map/ppermute | solution.py:338

commit v4 on v3

--- a/solution.py
+++ b/solution.py
@@ -10,10 +10,10 @@
 epsilon = 1e-06
 lanes = 128
 piece = 32
-half = 64
 strips = 4
 rest = 32
 chunk_rows = 72
+part_rows = 2 * chunk_rows
 carry_rows = 16
 tiles = 9
 vmem = pl.BlockSpec(memory_space=pltpu.VMEM)
@@ -62,16 +62,16 @@
     chunks = []
     for ref in (image, text):
         found = []
+        whole = wide(ref, slice(None)).T
         for k in range(4):
-            rows = wide(ref, pl.ds(k * piece, piece), slice(None))
+            rows = whole[k * piece : (k + 1) * piece]
             last = rows[:, 2 * lanes :]
             last = jnp.concatenate([last[8 * g : 8 * g + 8] for g in range(4)], axis=1)
             found.append(jnp.concatenate([rows[:, :lanes], rows[:, lanes : 2 * lanes], last], axis=0))
         chunks.append(found)
-    for d in range(strips):
-        a, b = d // 2, d % 2
-        parts = chunks[0][2 * a : 2 * a + 2] + chunks[1][2 * b : 2 * b + 2]
-        out[d] = jnp.concatenate(parts, axis=0).astype(jnp.bfloat16)
+    for d in range(out.shape[0]):
+        both = [chunks[0][d % strips], chunks[1][d // strips]]
+        out[d] = jnp.concatenate(both, axis=0).astype(jnp.bfloat16)
 
 
 def unpack_rows(chunks, group):
@@ -92,31 +92,27 @@
     return found
 
 
-def unit_tiles(arrived, c, group):
-    chunks = [arrived[s][c * chunk_rows : (c + 1) * chunk_rows] for s in range(strips)]
-    found = unpack_rows(chunks, group)
+def unit_tiles(arrived, h, which, group):
+    rows = pl.ds(which * chunk_rows, chunk_rows)
+    found = unpack_rows([wide(arrived, h * strips + s, rows) for s in range(strips)], group)
     inverse = lax.rsqrt(jnp.sum(total([t * t for t in found]), axis=1, keepdims=True) + epsilon)
     return [t * inverse for t in found], inverse
 
 
 def unit_kernel(arrived, image, text):
     group = lane_group()
-    values = [wide(arrived, s) for s in range(strips)]
-    for c in range(4):
-        units, _ = unit_tiles(values, c, group)
-        out = image if c < 2 else text
-        for t in range(tiles):
-            out[(c % 2) * piece : (c % 2 + 1) * piece, t * lanes : (t + 1) * lanes] = units[
-                t
-            ].astype(jnp.bfloat16)
-
-
-def join_kernel(image_own, image_near, text_own, text_near, image, text):
-    for k in range(image.shape[0]):
-        image[k, :half, :] = image_own[...]
-        image[k, half:, :] = image_near[...]
-    text[:half, :] = text_own[...]
-    text[half:, :] = text_near[...]
+    for h in range(arrived.shape[0] // strips):
+        rows = pl.ds(h * piece, piece)
+        for which in range(2):
+            units, _ = unit_tiles(arrived, h, which, group)
+            for t in range(tiles):
+                columns = pl.ds(t * lanes, lanes)
+                value = units[t].astype(jnp.bfloat16)
+                if which:
+                    text[rows, columns] = value
+                else:
+                    for k in range(image.shape[0]):
+                        image[k, rows, columns] = value
 
 
 def fold(values):
@@ -162,7 +158,7 @@
     for start in range(0, rows, tile):
         here = pl.ds(start, tile)
         row = lax.broadcasted_iota(jnp.int32, (tile, 1), 0) + (start - spot[0])
-        row = jnp.where((row >= 0) & (row < half), row, -1)
+        row = jnp.where((row >= 0) & (row < columns), row, -1)
         same = row == lax.broadcasted_iota(jnp.int32, (1, columns), 1)
         weights[here, :], found = pair_terms(
             left[here, :], right[...], scales[0], scales[1], same
@@ -247,85 +243,72 @@
         out[k, tiles * block : all_rows, :] = carry
 
 
-def image_sum_kernel(backs, kept, sent, carry_out):
+def pack_grads(units, inverse, grads, group):
+    along = jnp.sum(total([u * g for u, g in zip(units, grads)]), axis=1, keepdims=True)
+    final = [(g - u * along) * inverse for u, g in zip(units, grads)]
+    chunks = []
+    for s in range(strips):
+        last = jnp.zeros((8, lanes), jnp.float32)
+        for g in range(4):
+            turn = rest * (g - s) % lanes
+            rows = final[tiles - 1][8 * g : 8 * g + 8]
+            moved = pltpu.roll(rows, turn, 1) if turn else rows
+            last = jnp.where(group == g, moved, last)
+        chunks.append(jnp.concatenate([final[2 * s], final[2 * s + 1], last], axis=0))
+    return chunks
+
+
+def image_finish_kernel(arrived, backs, out):
+    group = lane_group()
     count = backs.shape[0]
-    block = 2 * half
-    tail = tiles * block
-    for t in range(tiles):
-        rows = total([wide(backs, k, pl.ds(t * block, block), slice(None)) for k in range(count)])
-        kept[t * half : (t + 1) * half, :] = rows[:half]
-        sent[t * half : (t + 1) * half, :] = rows[half:].astype(jnp.bfloat16)
-    carried = total([wide(backs, k, pl.ds(tail, carry_rows), slice(None)) for k in range(count)])
-    carry = carry_of(carried[:8])
-    sent[tiles * half :, :] = carry.astype(jnp.bfloat16)
-    carry_out[...] = carry.astype(jnp.bfloat16)
-
-
-def text_sum_kernel(b0, b1, b2, b3, carry, kept, sent):
-    for t in range(tiles):
-        columns = pl.ds(t * lanes, lanes)
-        rows = total([wide(b, slice(None), columns) for b in (b0, b1, b2, b3)])
-        kept[t * half : (t + 1) * half, :] = rows[:half]
-        sent[t * half : (t + 1) * half, :] = rows[half:].astype(jnp.bfloat16)
-    sent[tiles * half :, :] = carry[...]
-
-
-def finish_kernel(arrived, image_kept, image_given, text_kept, text_given, carry, far, out):
-    group = lane_group()
-    tail = pl.ds(tiles * half, carry_rows)
-    carried = total(
-        [
-            wide(carry, slice(None)),
-            wide(far, slice(None)),
-            wide(image_given, tail, slice(None)),
-            wide(text_given, tail, slice(None)),
-        ]
-    )
-    carry_now = carry_of(carried[:8]).astype(jnp.bfloat16)
-    values = [wide(arrived, s) for s in range(strips)]
-    for c in range(4):
-        units, inverse = unit_tiles(values, c, group)
-        kept, given = (image_kept, image_given) if c < 2 else (text_kept, text_given)
+    heads = arrived.shape[0] // strips
+    block = heads * piece
+    tail = pl.ds(tiles * block, carry_rows)
+    carry = carry_of(total([wide(backs, k, tail) for k in range(count)])[:8])
+    for h in range(heads):
+        units, inverse = unit_tiles(arrived, h, 0, group)
         grads = []
         for t in range(tiles):
-            rows = pl.ds(t * half + (c % 2) * piece, piece)
-            grads.append(kept[rows, :] + wide(given, rows, slice(None)))
-        along = jnp.sum(total([u * g for u, g in zip(units, grads)]), axis=1, keepdims=True)
-        final = [(g - u * along) * inverse for u, g in zip(units, grads)]
-        if c % 2 == 0:
-            chunks = [[] for _ in range(strips)]
-        for s in range(strips):
-            last = jnp.zeros((8, lanes), jnp.float32)
-            for g in range(4):
-                turn = rest * (g - s) % lanes
-                rows = final[tiles - 1][8 * g : 8 * g + 8]
-                moved = pltpu.roll(rows, turn, 1) if turn else rows
-                last = jnp.where(group == g, moved, last)
-            chunks[s] += [final[2 * s], final[2 * s + 1], last]
-            if c % 2 == 1:
-                start = (c // 2) * 2 * chunk_rows
-                value = jnp.concatenate(chunks[s], axis=0).astype(jnp.bfloat16)
-                out[s, start : start + 2 * chunk_rows, :] = value
-    for s in range(strips):
-        out[s, 4 * chunk_rows :, :] = carry_now
+            rows = pl.ds(t * block + h * piece, piece)
+            grads.append(total([wide(backs, k, rows) for k in range(count)]))
+        for s, chunk in enumerate(pack_grads(units, inverse, grads, group)):
+            out[h * strips + s] = jnp.concatenate([carry, chunk], axis=0)
+
+
+def text_finish_kernel(arrived, image, b0, b1, b2, b3, out):
+    group = lane_group()
+    for h in range(arrived.shape[0] // strips):
+        units, inverse = unit_tiles(arrived, h, 1, group)
+        grads = []
+        for t in range(tiles):
+            rows, columns = pl.ds(h * piece, piece), pl.ds(t * lanes, lanes)
+            grads.append(total([wide(b, rows, columns) for b in (b0, b1, b2, b3)]))
+        for s, chunk in enumerate(pack_grads(units, inverse, grads, group)):
+            d = h * strips + s
+            out[d] = jnp.concatenate([image[d], chunk], axis=0).astype(jnp.bfloat16)
 
 
 def last_kernel(arrived, image, text, sums_out):
-    values = [wide(arrived, s) for s in range(strips)]
+    values = [wide(arrived, d) for d in range(arrived.shape[0])]
+    heads = len(values) // strips
     for which, out in enumerate((image, text)):
+        start = carry_rows + which * chunk_rows
+        found = []
         for k in range(4):
-            c = 2 * which + k % 2
-            h = k // 2
-            sources = (2 * h, 2 * h + 1) if which == 0 else (h, 2 + h)
-            chunk = total([values[s][c * chunk_rows : (c + 1) * chunk_rows] for s in sources])
-            rows = pl.ds(k * piece, piece)
-            out[rows, 0:lanes] = chunk[:piece].astype(jnp.bfloat16)
-            out[rows, lanes : 2 * lanes] = chunk[piece : 2 * piece].astype(jnp.bfloat16)
+            if which:
+                sources = [k * strips + s for s in range(strips)]
+            else:
+                sources = [h * strips + k for h in range(heads)]
+            chunk = total([values[d][start : start + chunk_rows] for d in sources])
             last = chunk[2 * piece :]
             groups = [last] + [pltpu.roll(last, lanes - rest * g, 1) for g in range(1, 4)]
-            value = jnp.concatenate(groups, axis=0)[:, :rest]
-            out[rows, 2 * lanes : 2 * lanes + rest] = value.astype(jnp.bfloat16)
-    sums = total([v[4 * chunk_rows : 4 * chunk_rows + 8] for v in values])
+            last = jnp.concatenate(groups, axis=0)
+            found.append((chunk[:piece], chunk[piece : 2 * piece], last))
+        for t in range(3):
+            rows = jnp.concatenate([f[t] for f in found], axis=0).T
+            count = lanes if t < 2 else rest
+            out[t * lanes : t * lanes + count, :] = rows[:count].astype(jnp.bfloat16)
+    sums = total([v[:8] for v in values])
     sums_out[...] = jnp.broadcast_to(jnp.sum(sums, axis=1, keepdims=True), sums.shape)
 
 
@@ -338,38 +321,25 @@
     return lax.ppermute(value, axis, [(i, (i + k) % count) for i in range(count)])
 
 
-def swap_image(value):
-    return lax.ppermute(value, "zh", [(0, 1), (1, 0), (2, 3), (3, 2)])
-
-
-def swap_text(value):
-    return lax.ppermute(value, "zh", [(0, 3), (3, 0), (1, 2), (2, 1)])
-
-
 def shards(image, text, log_temp, bias):
     rows, strip = image.shape
-    x_count, y_count = (lax.axis_size(name) for name in ("x", "y"))
+    x_count, y_count, zh_count = (lax.axis_size(name) for name in ("x", "y", "zh"))
+    z_count = zh_count * strips
     width = strip * strips
-    block = 2 * half
+    block = zh_count * piece
     count = x_count * block
-    x, zl = (lax.axis_index(name) for name in ("x", "zl"))
+    zh, x, zl = (lax.axis_index(name) for name in ("zh", "x", "zl"))
     scale = jnp.exp(log_temp)
     scales = jnp.stack([scale, bias])
-    spot = jnp.where(zl // 2 == zl % 2, x * block, -count).astype(jnp.int32).reshape(1)
+    spot = jnp.where(zh == zl, x * block, -count).astype(jnp.int32).reshape(1)
     f32 = jnp.float32
 
-    (packed,) = call(pack_kernel, [shape((strips, 4 * chunk_rows, lanes))], "pack", [image, text])
-    arrived = lax.all_to_all(packed, "zl", 0, 0)
-    image_unit, text_unit = call(unit_kernel, [shape((half, width))] * 2, "unit", [arrived])
-    image_near = swap_image(image_unit)
-    text_near = swap_text(text_unit)
-    joined, home_text = call(
-        join_kernel,
-        [shape((x_count, block, width)), shape((block, width))],
-        "join",
-        [image_unit, image_near, text_unit, text_near],
-    )
-    image_rows = lax.all_to_all(joined, "x", 0, 0).reshape(count, width)
+    (packed,) = call(pack_kernel, [shape((z_count, part_rows, lanes))], "pack", [image.T, text.T])
+    arrived = lax.all_to_all(packed, ("zh", "zl"), 0, 0)
+    units, home_text = call(
+        unit_kernel, [shape((x_count, block, width)), shape((block, width))], "unit", [arrived]
+    )
+    image_rows = lax.all_to_all(units, "x", 0, 0).reshape(count, width)
     texts = [home_text] + [shift(home_text, "y", k) for k in range(1, y_count)]
     other_rows = swap_core(image_rows)
 
@@ -420,32 +390,32 @@
         [shape((x_count, tiles * block + carry_rows, lanes))],
         "combine",
         [own_back, given_back, sums],
+        after=text_backs[:1],
     )
     combined = lax.all_to_all(combined, "x", 0, 0)
-    part = [shape((tiles * half, lanes), f32), shape((tiles * half + carry_rows, lanes))]
-    image_kept, image_sent, carry = call(
-        image_sum_kernel, part + [shape((carry_rows, lanes))], "image_sum", [combined]
-    )
-    image_given = swap_image(image_sent)
-    far = shift(carry, "zh", 2)
+    (finished,) = call(
+        image_finish_kernel,
+        [shape((z_count, carry_rows + chunk_rows, lanes), f32)],
+        "image_finish",
+        [arrived, combined],
+        flops=200 * count * block * width,
+    )
     moved = [text_backs[0]] + [shift(text_backs[k], "y", -k) for k in range(1, y_count)]
-    text_kept, text_sent = call(text_sum_kernel, part, "text_sum", moved + [carry])
-    text_given = swap_text(text_sent)
     (finished,) = call(
-        finish_kernel,
-        [shape((strips, 4 * chunk_rows + carry_rows, lanes))],
-        "finish",
-        [arrived, image_kept, image_given, text_kept, text_given, carry, far],
-    )
-    finished = lax.all_to_all(finished, "zl", 0, 0)
+        text_finish_kernel,
+        [shape((z_count, carry_rows + part_rows, lanes))],
+        "text_finish",
+        [arrived, finished] + moved,
+    )
+    finished = lax.all_to_all(finished, ("zh", "zl"), 0, 0)
     grad_image, grad_text, sums = call(
-        last_kernel, [shape((rows, strip))] * 2 + [shape((8, lanes), f32)], "last", [finished]
-    )
-    pairs_count = rows * 4 * x_count * y_count * 2
+        last_kernel, [shape((strip, rows))] * 2 + [shape((8, lanes), f32)], "last", [finished]
+    )
+    pairs_count = rows * zh_count * x_count * y_count * 2
     return (
         sums[0, 0] / pairs_count,
-        grad_image,
-        grad_text,
+        grad_image.T,
+        grad_text.T,
         scale * sums[1, 0] / pairs_count,
         sums[2, 0] / pairs_count,
     )

time: 167 us -> 184 us (1.10)
  the two profiles are of different devices: /device:TPU:2 before, /device:TPU:34 now
where the time goes in v4:
time: 184 us; the launch traced here: 183 us
  blocking collectives  92 us (50%)
  starting transfers between devices  37.7 us (20%)
  waiting for transfers between devices  18.7 us (10%)
  Pallas kernels  16.9 us (9%)
  local copies, waits for them, and re-layouts  10.6 us (6%)
  between operations  7.37 us (4%)
    all_to_all x1, blocking collectives, shards(): arrived = lax.all_to_all(packed, ('zh', 'zl'), 0, 0)  49.4 us
    all_to_all x1, blocking collectives, shards(): finished = lax.all_to_all(finished, ('zh', 'zl'), 0, 0)  42.6 us
    ppermute x6, starting transfers between devices, shift(): lax.ppermute(value, axis, [(i, (i + k) % count) for i in range(count)])  20.9 us
    pallas_call x10, Pallas kernels, call(): pl.pallas_call(body, out_shape=out_shape, in_specs=[smem] * len(scalars)...  16.9 us
    ppermute x6, waiting for transfers between devices, shift(): lax.ppermute(value, axis, [(i, (i + k) % count) for i in range(count)])  12.2 us
    unnamed x24, local copies, waits for them, and re-layouts  10.1 us
    all_to_all x1, waiting for transfers between devices, shards(): combined = lax.all_to_all(combined, 'x', 0, 0)  5.23 us
    all_to_all x1, starting transfers between devices, shards(): image_rows = lax.all_to_all(units, 'x', 0, 0).reshape(count, width)  4.82 us
  transfers between devices with their start and end apart: 11, of which 8 were waited for; matrix products, arithmetic and copies ran while one was open for 0% of the time, Pallas kernels for 4%

profile of v4, /device:TPU:34, one launch (start us, length us, event | category | flops | bytes accessed | tf_op | source)
XLA Modules:
  0.0 183.3 jit_solution(16864285260197780141)
XLA Ops:
  0.6 0.9 copy-done
  1.5 0.9 copy-done.1
  2.4 0.2 pack.1
  2.6 49.4 %all_to_all.25.refs_0_ = bf16[16,144,128]{2,1,0:T(8,128)(2,1)S(1)} all-to-all(bf16[16,144,128]{2,1,0:T(8,128)(2,1)S(1)} %pack.1), channel_id=1, replica_groups=mesh['zh'=4,'x'=4,'y'=4,'core'=2,'zl'=4] {'zh','zl'}, dimensions={0} | all-to-all | bytes 1179648 | tf_op jit(solution)/shard_map/all_to_all | solution.py:338
  52.0 1.6 unit.1
  53.6 4.8 %all-to-all-start.1 = ((bf16[4,128,1152]{2,1,0:T(8,128)(2,1)}), bf16[4,128,1152]{2,1,0:T(8,128)(2,1)S(1)}, u32[]{:S(2)}, u32[]{:S(2)}) async-start(bf16[4,128,1152]{2,1,0:T(8,128)(2,1)} %get-tuple-element.23), calls=%async_computation.1 | async-start | bytes 2359296 | tf_op jit(solution)/shard_map/all_to_all | solution.py:342
  59.7 0.1 pad_maximum_fusion.refs_0_
  59.8 4.9 %collective-permute-start.2 = (bf16[128,1152]{1,0:T(8,128)(2,1)S(1)}, bf16[128,1152]{1,0:T(8,128)(2,1)S(1)}, u32[]{:S(2)}, u32[]{:S(2)}) collective-permute-start(bf16[128,1152]{1,0:T(8,128)(2,1)S(1)} %get-tuple-element.24.refs_3_.refs_2_), channel_id=1, source_target_pairs={{0,24},{8,0},{16,8},{24,16},{1,25},{9,1},{17,9},{25,17},{2,26},{10... | collective-permute-start | bytes 884744 | tf_op jit(solution)/shard_map/ppermute | solution.py:321
  64.7 2.5 %collective-permute-start.1 = (bf16[128,1152]{1,0:T(8,128)(2,1)S(1)}, bf16[128,1152]{1,0:T(8,128)(2,1)S(1)}, u32[]{:S(2)}, u32[]{:S(2)}) collective-permute-start(bf16[128,1152]{1,0:T(8,128)(2,1)S(1)} %get-tuple-element.24.refs_3_.refs_2_), channel_id=1, source_target_pairs={{0,16},{8,24},{16,0},{24,8},{1,17},{9,25},{17,1},{25,9},{2,18},{10... | collective-permute-start | bytes 884744 | tf_op jit(solution)/shard_map/ppermute | solution.py:321
  67.3 2.9 %collective-permute-start = (bf16[128,1152]{1,0:T(8,128)(2,1)S(1)}, bf16[128,1152]{1,0:T(8,128)(2,1)S(1)}, u32[]{:S(2)}, u32[]{:S(2)}) collective-permute-start(bf16[128,1152]{1,0:T(8,128)(2,1)S(1)} %get-tuple-element.24.refs_3_.refs_2_), channel_id=1, source_target_pairs={{0,8},{8,16},{16,24},{24,0},{1,9},{9,17},{17,25},{25,1},{2,10},{10... | collective-permute-start | bytes 884744 | tf_op jit(solution)/shard_map/ppermute | solution.py:321
  70.2 1.3 all-to-all-done.1
  71.4 1.9 %collective-permute-start.3 = (bf16[512,1152]{1,0:T(8,128)(2,1)S(1)}, bf16[512,1152]{1,0:T(8,128)(2,1)S(1)}, u32[]{:S(2)}, u32[]{:S(2)}) collective-permute-start(bf16[512,1152]{1,0:T(8,128)(2,1)S(1)} %bitcast.12), channel_id=1, source_target_pairs={{0,4},{4,0},{1,5},{5,1},{2,6},{6,2},{3,7},{7,3},{8,12},{12,8},{9,1... | collective-permute-start | bytes 3538952 | tf_op jit(solution)/shard_map/ppermute | solution.py:316
  73.4 1.1 home.1
  74.5 0.3 collective-permute-done.2.refs_5_
  74.8 2.5 %collective-permute-done.1.refs_4_ = bf16[128,1152]{1,0:T(8,128)(2,1)S(1)} collective-permute-done((bf16[128,1152]{1,0:T(8,128)(2,1)S(1)}, bf16[128,1152]{1,0:T(8,128)(2,1)S(1)}, u32[]{:S(2)}, u32[]{:S(2)}) %collective-permute-start.1) | collective-permute-done | bytes 294944 | tf_op jit(solution)/shard_map/ppermute | solution.py:321
  77.3 0.7 copy-done.4
  78.0 2.4 %collective-permute-done.refs_3_ = bf16[128,1152]{1,0:T(8,128)(2,1)S(1)} collective-permute-done((bf16[128,1152]{1,0:T(8,128)(2,1)S(1)}, bf16[128,1152]{1,0:T(8,128)(2,1)S(1)}, u32[]{:S(2)}, u32[]{:S(2)}) %collective-permute-start) | collective-permute-done | bytes 294944 | tf_op jit(solution)/shard_map/ppermute | solution.py:321
  80.4 0.7 copy-done.6
  81.1 1.0 copy-done.5
  82.0 1.0 copy-done.7
  83.0 2.6 %own.1 = (bf16[512,1152]{1,0:T(8,128)(2,1)S(1)}, bf16[512,512]{1,0:T(8,128)(2,1)S(1)}, bf16[512,1152]{1,0:T(8,128)(2,1)S(1)}, f32[24,128]{1,0:T(8,128)S(1)}) custom-call(f32[2]{0:T(128)S(1)} %pad_maximum_fusion.refs_0_, bf16[512,1152]{1,0:T(8,128)(2,1)S(1)} %bitcast.14, bf16[128,1152]{1,0:T(8,128)(2,1)S(1)} %get-tuple-element.24.refs_3_.refs_2_, ...), custom_call_target="tpu_custom_call" | custom-call | flops 1207959552 | bytes 5398528 | tf_op jit(solution)/shard_map/own/pallas_call | solution.py:38
  85.6 0.0 copy-start.8
  85.6 0.8 copy-done.8
  86.4 0.0 collective-permute-done.3.refs_1_.refs_3_
  86.4 3.6 %other.1 = (bf16[512,1152]{1,0:T(8,128)(2,1)}, bf16[512,512]{1,0:T(8,128)(2,1)S(1)}, f32[8,8,128]{2,1,0:T(8,128)}) custom-call(f32[2]{0:T(128)S(1)} %pad_maximum_fusion.refs_0_, bf16[512,1152]{1,0:T(8,128)(2,1)S(1)} %collective-permute-done.3.refs_1_.refs_3_, bf16[512,1152]{1,0:T(8,128)(2,1)S(1)} %get-tuple-element.28.refs_2_, ...), custom_call_target="tpu_custom_call" | custom-call | flops 1207959552 | bytes 4108288 | tf_op jit(solution)/shard_map/other/pallas_call | solution.py:38
  90.0 0.8 copy-done.10
  90.8 1.9 %collective-permute-start.4 = (bf16[512,1152]{1,0:T(8,128)(2,1)}, bf16[512,1152]{1,0:T(8,128)(2,1)}, u32[]{:S(2)}, u32[]{:S(2)}) collective-permute-start(bf16[512,1152]{1,0:T(8,128)(2,1)} %get-tuple-element.30), channel_id=1, source_target_pairs={{0,4},{4,0},{1,5},{5,1},{2,6},{6,2},{3,7},{7,3},{8,12},{12,8},{9,1... | collective-permute-start | bytes 3538952 | tf_op jit(solution)/shard_map/ppermute | solution.py:316
  92.7 3.4 %all-to-all-start.2 = ((f32[8,8,128]{2,1,0:T(8,128)}), f32[8,8,128]{2,1,0:T(8,128)S(1)}, u32[]{:S(2)}, u32[]{:S(2)}) async-start(f32[8,8,128]{2,1,0:T(8,128)} %get-tuple-element.31), calls=%async_computation.2 | async-start | bytes 65536 | tf_op jit(solution)/shard_map/all_to_all | solution.py:380
  96.1 1.3 copy-done.3
  97.4 1.0 copy-done.9
  98.4 1.0 copy-done.11
  99.5 2.4 %text_back.1 = (bf16[128,1152]{1,0:T(8,128)(2,1)S(1)}, bf16[128,1152]{1,0:T(8,128)(2,1)}, bf16[128,1152]{1,0:T(8,128)(2,1)}, bf16[128,1152]{1,0:T(8,128)(2,1)}) custom-call(bf16[512,512]{1,0:T(8,128)(2,1)S(1)} %copy-done.9, bf16[512,512]{1,0:T(8,128)(2,1)S(1)} %copy-done.11, bf16[512,1152]{1,0:T(8,128)(2,1)S(1)} %bitcast.15, bf16[512,1152]{1,0:T(8,128)(2,1)S(1)} %copy-done.3), custom_call_target="tpu_custom_call" | custom-call | flops 1207959552 | bytes 4587520 | tf_op jit(solution)/shard_map/text_back/pallas_call | solution.py:38
  101.9 0.0 all-to-all-done.2.refs_2_
  101.9 0.0 collective-permute-done.4.refs_1_
  101.9 2.6 %combine.1 = bf16[4,1168,128]{2,1,0:T(8,128)(2,1)} custom-call(bf16[512,1152]{1,0:T(8,128)(2,1)S(1)} %get-tuple-element.27.refs_0_, bf16[512,1152]{1,0:T(8,128)(2,1)} %collective-permute-done.4.refs_1_, f32[8,8,128]{2,1,0:T(8,128)S(1)} %all-to-all-done.2.refs_2_, bf16[128,1152]{1,0:T(8,128)(2,1)S(1)} %get-tuple-element.34.refs_3_.refs_2_), custom_call_target="tpu_custom_call" | custom-call | bytes 3588096 | tf_op jit(solution)/shard_map/combine/pallas_call | solution.py:38
  104.5 4.8 %all-to-all-start.3 = ((bf16[4,1168,128]{2,1,0:T(8,128)(2,1)}), bf16[4,1168,128]{2,1,0:T(8,128)(2,1)S(1)}, u32[]{:S(2)}, u32[]{:S(2)}) async-start(bf16[4,1168,128]{2,1,0:T(8,128)(2,1)} %combine.1), calls=%async_computation.3 | async-start | bytes 2392064 | tf_op jit(solution)/shard_map/all_to_all | solution.py:395
  109.3 5.1 %collective-permute-start.5 = (bf16[128,1152]{1,0:T(8,128)(2,1)}, bf16[128,1152]{1,0:T(8,128)(2,1)S(1)}, u32[]{:S(2)}, u32[]{:S(2)}) collective-permute-start(bf16[128,1152]{1,0:T(8,128)(2,1)} %get-tuple-element.35), channel_id=1, source_target_pairs={{0,24},{8,0},{16,8},{24,16},{1,25},{9,1},{17,9},{25,17},{2,26},{10... | collective-permute-start | bytes 884744 | tf_op jit(solution)/shard_map/ppermute | solution.py:321
  114.4 2.7 %collective-permute-start.6 = (bf16[128,1152]{1,0:T(8,128)(2,1)}, bf16[128,1152]{1,0:T(8,128)(2,1)S(1)}, u32[]{:S(2)}, u32[]{:S(2)}) collective-permute-start(bf16[128,1152]{1,0:T(8,128)(2,1)} %get-tuple-element.36), channel_id=1, source_target_pairs={{0,16},{8,24},{16,0},{24,8},{1,17},{9,25},{17,1},{25,9},{2,18},{10... | collective-permute-start | bytes 884744 | tf_op jit(solution)/shard_map/ppermute | solution.py:321
  117.1 2.8 %collective-permute-start.7 = (bf16[128,1152]{1,0:T(8,128)(2,1)}, bf16[128,1152]{1,0:T(8,128)(2,1)}, u32[]{:S(2)}, u32[]{:S(2)}) collective-permute-start(bf16[128,1152]{1,0:T(8,128)(2,1)} %get-tuple-element.37), channel_id=1, source_target_pairs={{0,8},{8,16},{16,24},{24,0},{1,9},{9,17},{17,25},{25,1},{2,10},{10... | collective-permute-start | bytes 884744 | tf_op jit(solution)/shard_map/ppermute | solution.py:321
  119.9 5.2 %all-to-all-done.3.refs_1_ = bf16[4,1168,128]{2,1,0:T(8,128)(2,1)S(1)} async-done(((bf16[4,1168,128]{2,1,0:T(8,128)(2,1)}), bf16[4,1168,128]{2,1,0:T(8,128)(2,1)S(1)}, u32[]{:S(2)}, u32[]{:S(2)}) %all-to-all-start.3) | async-done | bytes 1196064 | tf_op jit(solution)/shard_map/all_to_all | solution.py:395
  125.1 0.5 image_finish.1.refs_1_
  125.6 1.4 collective-permute-done.5.refs_3_
  127.0 1.0 collective-permute-done.6.refs_4_
  128.0 4.7 %collective-permute-done.7.refs_5_ = bf16[128,1152]{1,0:T(8,128)(2,1)} collective-permute-done((bf16[128,1152]{1,0:T(8,128)(2,1)}, bf16[128,1152]{1,0:T(8,128)(2,1)}, u32[]{:S(2)}, u32[]{:S(2)}) %collective-permute-start.7) | collective-permute-done | bytes 294944 | tf_op jit(solution)/shard_map/ppermute | solution.py:321
  132.6 1.4 text_finish.1
  134.1 42.6 %all_to_all.26.refs_0_ = bf16[16,160,128]{2,1,0:T(8,128)(2,1)S(1)} all-to-all(bf16[16,160,128]{2,1,0:T(8,128)(2,1)S(1)} %text_finish.1), channel_id=1, replica_groups=mesh['zh'=4,'x'=4,'y'=4,'core'=2,'zl'=4] {'zh','zl'}, dimensions={0} | all-to-all | bytes 1310720 | tf_op jit(solution)/shard_map/all_to_all | solution.py:410
  176.7 0.8 last.1
  177.5 0.5 fusion
  (12 shorter events, 0.0 us)
Async XLA Ops:
  0.6 0.9 copy-start
  1.5 0.9 copy-start.1
  53.6 17.9 %all-to-all-start.1 = ((bf16[4,128,1152]{2,1,0:T(8,128)(2,1)}), bf16[4,128,1152]{2,1,0:T(8,128)(2,1)S(1)}, u32[]{:S(2)}, u32[]{:S(2)}) async-start(bf16[4,128,1152]{2,1,0:T(8,128)(2,1)} %get-tuple-element.23), calls=%async_computation.1 | async-start | bytes 2359296 | tf_op jit(solution)/shard_map/all_to_all | solution.py:342
  59.8 15.0 %collective-permute-start.2 = (bf16[128,1152]{1,0:T(8,128)(2,1)S(1)}, bf16[128,1152]{1,0:T(8,128)(2,1)S(1)}, u32[]{:S(2)}, u32[]{:S(2)}) collective-permute-start(bf16[128,1152]{1,0:T(8,128)(2,1)S(1)} %get-tuple-element.24.refs_3_.refs_2_), channel_id=1, source_target_pairs={{0,24},{8,0},{16,8},{24,16},{1,25},{9,1},{17,9},{25,17},{2,26},{10... | collective-permute-start | bytes 884744 | tf_op jit(solution)/shard_map/ppermute | solution.py:321
  64.7 12.5 %collective-permute-start.1 = (bf16[128,1152]{1,0:T(8,128)(2,1)S(1)}, bf16[128,1152]{1,0:T(8,128)(2,1)S(1)}, u32[]{:S(2)}, u32[]{:S(2)}) collective-permute-start(bf16[128,1152]{1,0:T(8,128)(2,1)S(1)} %get-tuple-element.24.refs_3_.refs_2_), channel_id=1, source_target_pairs={{0,16},{8,24},{16,0},{24,8},{1,17},{9,25},{17,1},{25,9},{2,18},{10... | collective-permute-start | bytes 884744 | tf_op jit(solution)/shard_map/ppermute | solution.py:321
  67.3 13.1 %collective-permute-start = (bf16[128,1152]{1,0:T(8,128)(2,1)S(1)}, bf16[128,1152]{1,0:T(8,128)(2,1)S(1)}, u32[]{:S(2)}, u32[]{:S(2)}) collective-permute-start(bf16[128,1152]{1,0:T(8,128)(2,1)S(1)} %get-tuple-element.24.refs_3_.refs_2_), channel_id=1, source_target_pairs={{0,8},{8,16},{16,24},{24,0},{1,9},{9,17},{17,25},{25,1},{2,10},{10... | collective-permute-start | bytes 884744 | tf_op jit(solution)/shard_map/ppermute | solution.py:321
  71.4 15.0 %collective-permute-start.3 = (bf16[512,1152]{1,0:T(8,128)(2,1)S(1)}, bf16[512,1152]{1,0:T(8,128)(2,1)S(1)}, u32[]{:S(2)}, u32[]{:S(2)}) collective-permute-start(bf16[512,1152]{1,0:T(8,128)(2,1)S(1)} %bitcast.12), channel_id=1, source_target_pairs={{0,4},{4,0},{1,5},{5,1},{2,6},{6,2},{3,7},{7,3},{8,12},{12,8},{9,1... | collective-permute-start | bytes 3538952 | tf_op jit(solution)/shard_map/ppermute | solution.py:316
  77.3 0.7 copy-start.4
  80.4 0.7 copy-start.6
  81.1 1.0 copy-start.5
  82.0 1.0 copy-start.7
  85.6 0.8 copy-start.8
  86.4 3.6 %copy-start.2 = (bf16[512,1152]{1,0:T(8,128)(2,1)}, bf16[512,1152]{1,0:T(8,128)(2,1)S(1)}, u32[]{:S(2)}) copy-start(bf16[512,1152]{1,0:T(8,128)(2,1)S(1)} %collective-permute-done.3.refs_1_.refs_3_) | copy-start | bytes 3538948
  90.0 0.8 copy-start.10
  90.8 11.1 %collective-permute-start.4 = (bf16[512,1152]{1,0:T(8,128)(2,1)}, bf16[512,1152]{1,0:T(8,128)(2,1)}, u32[]{:S(2)}, u32[]{:S(2)}) collective-permute-start(bf16[512,1152]{1,0:T(8,128)(2,1)} %get-tuple-element.30), channel_id=1, source_target_pairs={{0,4},{4,0},{1,5},{5,1},{2,6},{6,2},{3,7},{7,3},{8,12},{12,8},{9,1... | collective-permute-start | bytes 3538952 | tf_op jit(solution)/shard_map/ppermute | solution.py:316
  92.7 9.1 %all-to-all-start.2 = ((f32[8,8,128]{2,1,0:T(8,128)}), f32[8,8,128]{2,1,0:T(8,128)S(1)}, u32[]{:S(2)}, u32[]{:S(2)}) async-start(f32[8,8,128]{2,1,0:T(8,128)} %get-tuple-element.31), calls=%async_computation.2 | async-start | bytes 65536 | tf_op jit(solution)/shard_map/all_to_all | solution.py:380
  96.1 1.3 copy-start.3
  97.4 1.0 copy-start.9
  98.4 1.0 copy-start.11
  104.5 20.6 %all-to-all-start.3 = ((bf16[4,1168,128]{2,1,0:T(8,128)(2,1)}), bf16[4,1168,128]{2,1,0:T(8,128)(2,1)S(1)}, u32[]{:S(2)}, u32[]{:S(2)}) async-start(bf16[4,1168,128]{2,1,0:T(8,128)(2,1)} %combine.1), calls=%async_computation.3 | async-start | bytes 2392064 | tf_op jit(solution)/shard_map/all_to_all | solution.py:395
  109.3 17.7 %collective-permute-start.5 = (bf16[128,1152]{1,0:T(8,128)(2,1)}, bf16[128,1152]{1,0:T(8,128)(2,1)S(1)}, u32[]{:S(2)}, u32[]{:S(2)}) collective-permute-start(bf16[128,1152]{1,0:T(8,128)(2,1)} %get-tuple-element.35), channel_id=1, source_target_pairs={{0,24},{8,0},{16,8},{24,16},{1,25},{9,1},{17,9},{25,17},{2,26},{10... | collective-permute-start | bytes 884744 | tf_op jit(solution)/shard_map/ppermute | solution.py:321
  114.4 13.6 %collective-permute-start.6 = (bf16[128,1152]{1,0:T(8,128)(2,1)}, bf16[128,1152]{1,0:T(8,128)(2,1)S(1)}, u32[]{:S(2)}, u32[]{:S(2)}) collective-permute-start(bf16[128,1152]{1,0:T(8,128)(2,1)} %get-tuple-element.36), channel_id=1, source_target_pairs={{0,16},{8,24},{16,0},{24,8},{1,17},{9,25},{17,1},{25,9},{2,18},{10... | collective-permute-start | bytes 884744 | tf_op jit(solution)/shard_map/ppermute | solution.py:321
  117.1 15.5 %collective-permute-start.7 = (bf16[128,1152]{1,0:T(8,128)(2,1)}, bf16[128,1152]{1,0:T(8,128)(2,1)}, u32[]{:S(2)}, u32[]{:S(2)}) collective-permute-start(bf16[128,1152]{1,0:T(8,128)(2,1)} %get-tuple-element.37), channel_id=1, source_target_pairs={{0,8},{8,16},{16,24},{24,0},{1,9},{9,17},{17,25},{25,1},{2,10},{10... | collective-permute-start | bytes 884744 | tf_op jit(solution)/shard_map/ppermute | solution.py:321

commit v5 on v3

--- a/solution.py
+++ b/solution.py
@@ -19,14 +19,14 @@
 vmem = pl.BlockSpec(memory_space=pltpu.VMEM)
 smem = pl.BlockSpec(memory_space=pltpu.SMEM)
 anywhere = pl.BlockSpec(memory_space=pl.ANY)
-limits = pltpu.CompilerParams(vmem_limit_bytes=40 * 1024 * 1024)
+limits = pltpu.CompilerParams(vmem_limit_bytes=16 * 1024 * 1024)
 
 
 def shape(dims, dtype=jnp.bfloat16):
     return jax.ShapeDtypeStruct(tuple(dims), dtype)
 
 
-def call(kernel, out_shape, name, operands, scalars=(), after=(), flops=0, special=0):
+def call(kernel, out_shape, name, operands, scalars=(), after=(), flops=0, special=0, scratch=()):
     out_shape = tuple(out_shape)
     scalars, operands, after = tuple(scalars), tuple(operands), tuple(after)
     inputs = len(scalars) + len(operands)
@@ -40,6 +40,7 @@
         out_shape=out_shape,
         in_specs=[smem] * len(scalars) + [vmem] * len(operands) + [anywhere] * len(after),
         out_specs=(vmem,) * len(out_shape),
+        scratch_shapes=list(scratch),
         compiler_params=limits,
         cost_estimate=pl.CostEstimate(flops=flops, bytes_accessed=moved, transcendentals=special),
         name=name,
@@ -62,8 +63,9 @@
     chunks = []
     for ref in (image, text):
         found = []
+        whole = wide(ref, slice(None)).T
         for k in range(4):
-            rows = wide(ref, pl.ds(k * piece, piece), slice(None))
+            rows = whole[k * piece : (k + 1) * piece]
             last = rows[:, 2 * lanes :]
             last = jnp.concatenate([last[8 * g : 8 * g + 8] for g in range(4)], axis=1)
             found.append(jnp.concatenate([rows[:, :lanes], rows[:, lanes : 2 * lanes], last], axis=0))
@@ -156,7 +158,8 @@
 tile = 256
 
 
-def home_kernel(scales, spot, left, right, weights, sums_out):
+def home_kernel(scales, spot, left, right, weights, sums_out, kept):
+    kept[...] = right[...]
     rows, columns = left.shape[0], right.shape[0]
     sums = []
     for start in range(0, rows, tile):
@@ -188,7 +191,9 @@
     write_sums(sums_out, sums, home_sums)
 
 
-def other_kernel(scales, left, right, own_sums, back, weights, sums_out):
+def other_kernel(
+    scales, left, right, own_sums, own_weights, own_left, back, sums_out, b0, b1, b2, b3, weights
+):
     sums = []
     for start in range(0, left.shape[0], tile):
         here = pl.ds(start, tile)
@@ -205,18 +210,13 @@
         value = jnp.where(row == k, jnp.sum(found, axis=0, keepdims=True), value)
     for k in range(sums_out.shape[0]):
         sums_out[k] = value
-
-
-def text_kernel(first_weights, second_weights, first, second, *backs):
     contract = (((0,), (0,)), ((), ()))
-    part = backs[0].shape[0]
+    part = b0.shape[0]
     value = lax.dot_general(
-        first_weights[...], first[...], contract, preferred_element_type=jnp.float32
-    ) + lax.dot_general(
-        second_weights[...], second[...], contract, preferred_element_type=jnp.float32
-    )
-    for k, back in enumerate(backs):
-        back[...] = value[k * part : (k + 1) * part].astype(jnp.bfloat16)
+        own_weights[...], own_left[...], contract, preferred_element_type=jnp.float32
+    ) + lax.dot_general(weights[...], left[...], contract, preferred_element_type=jnp.float32)
+    for k, out in enumerate((b0, b1, b2, b3)):
+        out[...] = value[k * part : (k + 1) * part].astype(jnp.bfloat16)
 
 
 def three_parts(value):
@@ -247,40 +247,31 @@
         out[k, tiles * block : all_rows, :] = carry
 
 
-def image_sum_kernel(backs, kept, sent, carry_out):
+def image_sum_kernel(backs, kept, sent):
     count = backs.shape[0]
     block = 2 * half
-    tail = tiles * block
     for t in range(tiles):
         rows = total([wide(backs, k, pl.ds(t * block, block), slice(None)) for k in range(count)])
         kept[t * half : (t + 1) * half, :] = rows[:half]
         sent[t * half : (t + 1) * half, :] = rows[half:].astype(jnp.bfloat16)
-    carried = total([wide(backs, k, pl.ds(tail, carry_rows), slice(None)) for k in range(count)])
-    carry = carry_of(carried[:8])
+    tail = pl.ds(tiles * block, carry_rows)
+    carry = carry_of(total([wide(backs, k, tail, slice(None)) for k in range(count)])[:8])
+    kept[tiles * half :, :] = carry
     sent[tiles * half :, :] = carry.astype(jnp.bfloat16)
-    carry_out[...] = carry.astype(jnp.bfloat16)
-
-
-def text_sum_kernel(b0, b1, b2, b3, carry, kept, sent):
+
+
+def text_sum_kernel(b0, b1, b2, b3, kept, sent):
     for t in range(tiles):
         columns = pl.ds(t * lanes, lanes)
         rows = total([wide(b, slice(None), columns) for b in (b0, b1, b2, b3)])
         kept[t * half : (t + 1) * half, :] = rows[:half]
         sent[t * half : (t + 1) * half, :] = rows[half:].astype(jnp.bfloat16)
-    sent[tiles * half :, :] = carry[...]
-
-
-def finish_kernel(arrived, image_kept, image_given, text_kept, text_given, carry, far, out):
+
+
+def finish_kernel(arrived, image_kept, image_given, text_kept, text_given, out):
     group = lane_group()
     tail = pl.ds(tiles * half, carry_rows)
-    carried = total(
-        [
-            wide(carry, slice(None)),
-            wide(far, slice(None)),
-            wide(image_given, tail, slice(None)),
-            wide(text_given, tail, slice(None)),
-        ]
-    )
+    carried = image_kept[tail, :] + wide(image_given, tail, slice(None))
     carry_now = carry_of(carried[:8]).astype(jnp.bfloat16)
     values = [wide(arrived, s) for s in range(strips)]
     for c in range(4):
@@ -313,18 +304,20 @@
 def last_kernel(arrived, image, text, sums_out):
     values = [wide(arrived, s) for s in range(strips)]
     for which, out in enumerate((image, text)):
+        found = []
         for k in range(4):
             c = 2 * which + k % 2
             h = k // 2
-            sources = (2 * h, 2 * h + 1) if which == 0 else (h, 2 + h)
+            sources = (h, 2 + h) if which else (2 * h, 2 * h + 1)
             chunk = total([values[s][c * chunk_rows : (c + 1) * chunk_rows] for s in sources])
-            rows = pl.ds(k * piece, piece)
-            out[rows, 0:lanes] = chunk[:piece].astype(jnp.bfloat16)
-            out[rows, lanes : 2 * lanes] = chunk[piece : 2 * piece].astype(jnp.bfloat16)
             last = chunk[2 * piece :]
             groups = [last] + [pltpu.roll(last, lanes - rest * g, 1) for g in range(1, 4)]
-            value = jnp.concatenate(groups, axis=0)[:, :rest]
-            out[rows, 2 * lanes : 2 * lanes + rest] = value.astype(jnp.bfloat16)
+            last = jnp.concatenate(groups, axis=0)
+            found.append((chunk[:piece], chunk[piece : 2 * piece], last))
+        for t in range(3):
+            rows = jnp.concatenate([f[t] for f in found], axis=0).T
+            count = lanes if t < 2 else rest
+            out[t * lanes : t * lanes + count, :] = rows[:count].astype(jnp.bfloat16)
     sums = total([v[4 * chunk_rows : 4 * chunk_rows + 8] for v in values])
     sums_out[...] = jnp.broadcast_to(jnp.sum(sums, axis=1, keepdims=True), sums.shape)
 
@@ -339,11 +332,11 @@
 
 
 def swap_image(value):
-    return lax.ppermute(value, "zh", [(0, 1), (1, 0), (2, 3), (3, 2)])
+    return lax.ppermute(value, ("zh1", "zh0"), [(0, 3), (3, 0), (1, 2), (2, 1)])
 
 
 def swap_text(value):
-    return lax.ppermute(value, "zh", [(0, 3), (3, 0), (1, 2), (2, 1)])
+    return lax.ppermute(value, ("zh1", "zh0"), [(0, 1), (1, 0), (2, 3), (3, 2)])
 
 
 def shards(image, text, log_temp, bias):
@@ -358,7 +351,7 @@
     spot = jnp.where(zl // 2 == zl % 2, x * block, -count).astype(jnp.int32).reshape(1)
     f32 = jnp.float32
 
-    (packed,) = call(pack_kernel, [shape((strips, 4 * chunk_rows, lanes))], "pack", [image, text])
+    (packed,) = call(pack_kernel, [shape((strips, 4 * chunk_rows, lanes))], "pack", [image.T, text.T])
     arrived = lax.all_to_all(packed, "zl", 0, 0)
     image_unit, text_unit = call(unit_kernel, [shape((half, width))] * 2, "unit", [arrived])
     image_near = swap_image(image_unit)
@@ -370,14 +363,14 @@
         [image_unit, image_near, text_unit, text_near],
     )
     image_rows = lax.all_to_all(joined, "x", 0, 0).reshape(count, width)
-    texts = [home_text] + [shift(home_text, "y", k) for k in range(1, y_count)]
+    texts = [shift(home_text, "y", k) for k in range(1, y_count)]
     other_rows = swap_core(image_rows)
 
     columns = y_count * block
     area = count * columns
-    home_weights, home_sums = call(
+    home_weights, home_sums, home_text = call(
         home_kernel,
-        [shape((count, block)), shape((24, lanes), f32)],
+        [shape((count, block)), shape((24, lanes), f32), shape((block, width))],
         "home",
         [image_rows, home_text],
         scalars=[scales, spot],
@@ -392,29 +385,24 @@
             shape((24, lanes), f32),
         ],
         "own",
-        [image_rows] + texts + [home_weights, home_sums],
+        [image_rows, home_text] + texts + [home_weights, home_sums],
         scalars=[scales],
         flops=4 * area * width,
         special=2 * area,
     )
-    other_back, other_weights, sums = call(
+    other_back, sums, *text_backs = call(
         other_kernel,
-        [shape((count, width)), shape((count, columns)), shape((y_count * 2, 8, lanes), f32)],
+        [shape((count, width)), shape((y_count * 4, 8, lanes), f32)]
+        + [shape((block, width))] * y_count,
         "other",
-        [other_rows, right, own_sums],
+        [other_rows, right, own_sums, own_weights, image_rows],
         scalars=[scales],
-        flops=4 * area * width,
+        flops=8 * area * width,
         special=2 * area,
+        scratch=[pltpu.VMEM((count, columns), jnp.bfloat16)],
     )
     given_back = swap_core(other_back)
-    sums = lax.all_to_all(sums, ("y", "core"), 0, 0)
-    text_backs = call(
-        text_kernel,
-        [shape((block, width))] * y_count,
-        "text_back",
-        [own_weights, other_weights, image_rows, other_rows],
-        flops=4 * area * width,
-    )
+    sums = lax.all_to_all(sums, ("zh0", "y", "core"), 0, 0)
     (combined,) = call(
         combine_kernel,
         [shape((x_count, tiles * block + carry_rows, lanes))],
@@ -422,38 +410,45 @@
         [own_back, given_back, sums],
     )
     combined = lax.all_to_all(combined, "x", 0, 0)
-    part = [shape((tiles * half, lanes), f32), shape((tiles * half + carry_rows, lanes))]
-    image_kept, image_sent, carry = call(
-        image_sum_kernel, part + [shape((carry_rows, lanes))], "image_sum", [combined]
+    sums_rows = tiles * half + carry_rows
+    image_kept, image_sent = call(
+        image_sum_kernel,
+        [shape((sums_rows, lanes), f32), shape((sums_rows, lanes))],
+        "image_sum",
+        [combined],
     )
     image_given = swap_image(image_sent)
-    far = shift(carry, "zh", 2)
     moved = [text_backs[0]] + [shift(text_backs[k], "y", -k) for k in range(1, y_count)]
-    text_kept, text_sent = call(text_sum_kernel, part, "text_sum", moved + [carry])
+    text_kept, text_sent = call(
+        text_sum_kernel,
+        [shape((tiles * half, lanes), f32), shape((tiles * half, lanes))],
+        "text_sum",
+        moved,
+    )
     text_given = swap_text(text_sent)
     (finished,) = call(
         finish_kernel,
         [shape((strips, 4 * chunk_rows + carry_rows, lanes))],
         "finish",
-        [arrived, image_kept, image_given, text_kept, text_given, carry, far],
+        [arrived, image_kept, image_given, text_kept, text_given],
     )
     finished = lax.all_to_all(finished, "zl", 0, 0)
     grad_image, grad_text, sums = call(
-        last_kernel, [shape((rows, strip))] * 2 + [shape((8, lanes), f32)], "last", [finished]
+        last_kernel, [shape((strip, rows))] * 2 + [shape((8, lanes), f32)], "last", [finished]
     )
     pairs_count = rows * 4 * x_count * y_count * 2
     return (
         sums[0, 0] / pairs_count,
-        grad_image,
-        grad_text,
+        grad_image.T,
+        grad_text.T,
         scale * sums[1, 0] / pairs_count,
         sums[2, 0] / pairs_count,
     )
 
 
 def solution(mesh):
-    fine = Mesh(mesh.devices.reshape(4, 4, 4, 2, 4), ("zh", "x", "y", "core", "zl"))
-    whole = P(("zh", "x", "y", "core"), "zl")
+    fine = Mesh(mesh.devices.reshape(2, 2, 4, 4, 2, 4), ("zh1", "zh0", "x", "y", "core", "zl"))
+    whole = P(("zh1", "zh0", "x", "y", "core"), "zl")
     return jax.shard_map(
         shards,
         mesh=fine,

time: 167 us -> 167 us (level)
  the two profiles are of different devices: /device:TPU:2 before, /device:TPU:4 now
where the time goes in v5:
time: 167 us; the launch traced here: 166 us
  blocking collectives  52.7 us (32%)
  starting transfers between devices  51.4 us (31%)
  waiting for transfers between devices  39.8 us (24%)
  Pallas kernels  12.4 us (7%)
  between operations  7.41 us (4%)
  local copies, waits for them, and re-layouts  2.28 us (1%)
    all_to_all x1, blocking collectives, shards(): finished = lax.all_to_all(finished, 'zl', 0, 0)  21.6 us
    ppermute x6, starting transfers between devices, shift(): lax.ppermute(value, axis, [(i, (i + k) % count) for i in range(count)])  18.7 us
    all_to_all x1, blocking collectives, shards(): sums = lax.all_to_all(sums, ('zh0', 'y', 'core'), 0, 0)  15.9 us
    all_to_all x1, blocking collectives, shards(): arrived = lax.all_to_all(packed, 'zl', 0, 0)  15.3 us
    ppermute x2, waiting for transfers between devices, swap_text(): return lax.ppermute(value, ('zh1', 'zh0'), [(0, 1), (1, 0), (2, 3), (3, 2)])  14.9 us
    ppermute x6, waiting for transfers between devices, shift(): lax.ppermute(value, axis, [(i, (i + k) % count) for i in range(count)])  12.5 us
    pallas_call x11, Pallas kernels, call(): pl.pallas_call(body, out_shape=out_shape, in_specs=[smem] * len(scalars)...  12.4 us
    ppermute x2, starting transfers between devices, swap_image(): return lax.ppermute(value, ('zh1', 'zh0'), [(0, 3), (3, 0), (1, 2), (2, 1)])  11.9 us
  transfers between devices with their start and end apart: 14, of which 10 were waited for; matrix products, arithmetic and copies ran while one was open for 0% of the time, Pallas kernels for 2%

profile of v5, /device:TPU:4, one launch (start us, length us, event | category | flops | bytes accessed | tf_op | source)
XLA Modules:
  0.0 166.1 jit_solution(11928252135903445103)
XLA Ops:
  0.6 0.0 copy-start
  0.6 0.9 copy-done
  1.5 0.0 copy-start.1
  1.5 0.9 copy-done.1
  2.4 0.2 pack.1
  2.6 15.3 %all_to_all.25.refs_0_ = bf16[4,288,128]{2,1,0:T(8,128)(2,1)S(1)} all-to-all(bf16[4,288,128]{2,1,0:T(8,128)(2,1)S(1)} %pack.1), channel_id=1, replica_groups=mesh['zh1'=2,'zh0'=2,'x'=4,'y'=4,'core'=2,'zl'=4] {'zl'}, dimensions={0} | all-to-all | bytes 589824 | tf_op jit(solution)/shard_map/all_to_all | solution.py:355
  17.9 0.2 unit.1
  18.1 10.0 %collective-permute-start = (bf16[64,1152]{1,0:T(8,128)(2,1)S(1)}, bf16[64,1152]{1,0:T(8,128)(2,1)S(1)}, u32[]{:S(2)}, u32[]{:S(2)}) collective-permute-start(bf16[64,1152]{1,0:T(8,128)(2,1)S(1)} %get-tuple-element.29.refs_0_), channel_id=1, source_target_pairs={{0,384},{384,0},{128,256},{256,128},{1,385},{385,1},{129,257},{257... | collective-permute-start | bytes 442376 | tf_op jit(solution)/shard_map/ppermute | solution.py:335
  28.2 5.5 %collective-permute-start.1 = (bf16[64,1152]{1,0:T(8,128)(2,1)S(1)}, bf16[64,1152]{1,0:T(8,128)(2,1)S(1)}, u32[]{:S(2)}, u32[]{:S(2)}) collective-permute-start(bf16[64,1152]{1,0:T(8,128)(2,1)S(1)} %get-tuple-element.30.refs_2_), channel_id=1, source_target_pairs={{0,128},{128,0},{256,384},{384,256},{1,129},{129,1},{257,385},{385... | collective-permute-start | bytes 442376 | tf_op jit(solution)/shard_map/ppermute | solution.py:339
  33.6 5.1 %collective-permute-done.refs_1_ = bf16[64,1152]{1,0:T(8,128)(2,1)S(1)} collective-permute-done((bf16[64,1152]{1,0:T(8,128)(2,1)S(1)}, bf16[64,1152]{1,0:T(8,128)(2,1)S(1)}, u32[]{:S(2)}, u32[]{:S(2)}) %collective-permute-start) | collective-permute-done | bytes 147488 | tf_op jit(solution)/shard_map/ppermute | solution.py:335
  38.8 5.1 %collective-permute-done.1.refs_3_ = bf16[64,1152]{1,0:T(8,128)(2,1)S(1)} collective-permute-done((bf16[64,1152]{1,0:T(8,128)(2,1)S(1)}, bf16[64,1152]{1,0:T(8,128)(2,1)S(1)}, u32[]{:S(2)}, u32[]{:S(2)}) %collective-permute-start.1) | collective-permute-done | bytes 147488 | tf_op jit(solution)/shard_map/ppermute | solution.py:339
  43.9 1.2 join.1
  45.0 4.8 %all-to-all-start.1 = ((bf16[4,128,1152]{2,1,0:T(8,128)(2,1)}), bf16[4,128,1152]{2,1,0:T(8,128)(2,1)S(1)}, u32[]{:S(2)}, u32[]{:S(2)}) async-start(bf16[4,128,1152]{2,1,0:T(8,128)(2,1)} %get-tuple-element.31), calls=%async_computation.1 | async-start | bytes 2359296 | tf_op jit(solution)/shard_map/all_to_all | solution.py:365
  51.2 0.1 pad_maximum_fusion.refs_0_
  51.3 4.9 %collective-permute-start.4 = (bf16[128,1152]{1,0:T(8,128)(2,1)S(1)}, bf16[128,1152]{1,0:T(8,128)(2,1)S(1)}, u32[]{:S(2)}, u32[]{:S(2)}) collective-permute-start(bf16[128,1152]{1,0:T(8,128)(2,1)S(1)} %get-tuple-element.32.refs_3_), channel_id=1, source_target_pairs={{0,24},{8,0},{16,8},{24,16},{1,25},{9,1},{17,9},{25,17},{2,26},{10... | collective-permute-start | bytes 884744 | tf_op jit(solution)/shard_map/ppermute | solution.py:331
  56.2 2.5 %collective-permute-start.3 = (bf16[128,1152]{1,0:T(8,128)(2,1)S(1)}, bf16[128,1152]{1,0:T(8,128)(2,1)S(1)}, u32[]{:S(2)}, u32[]{:S(2)}) collective-permute-start(bf16[128,1152]{1,0:T(8,128)(2,1)S(1)} %get-tuple-element.32.refs_3_), channel_id=1, source_target_pairs={{0,16},{8,24},{16,0},{24,8},{1,17},{9,25},{17,1},{25,9},{2,18},{10... | collective-permute-start | bytes 884744 | tf_op jit(solution)/shard_map/ppermute | solution.py:331
  58.7 2.9 %collective-permute-start.2 = (bf16[128,1152]{1,0:T(8,128)(2,1)S(1)}, bf16[128,1152]{1,0:T(8,128)(2,1)S(1)}, u32[]{:S(2)}, u32[]{:S(2)}) collective-permute-start(bf16[128,1152]{1,0:T(8,128)(2,1)S(1)} %get-tuple-element.32.refs_3_), channel_id=1, source_target_pairs={{0,8},{8,16},{16,24},{24,0},{1,9},{9,17},{17,25},{25,1},{2,10},{10... | collective-permute-start | bytes 884744 | tf_op jit(solution)/shard_map/ppermute | solution.py:331
  61.6 1.8 %all-to-all-done.1 = bf16[4,128,1152]{2,1,0:T(8,128)(2,1)S(1)} async-done(((bf16[4,128,1152]{2,1,0:T(8,128)(2,1)}), bf16[4,128,1152]{2,1,0:T(8,128)(2,1)S(1)}, u32[]{:S(2)}, u32[]{:S(2)}) %all-to-all-start.1) | async-done | bytes 1179680 | tf_op jit(solution)/shard_map/all_to_all | solution.py:365
  63.4 1.9 %collective-permute-start.5 = (bf16[512,1152]{1,0:T(8,128)(2,1)S(1)}, bf16[512,1152]{1,0:T(8,128)(2,1)S(1)}, u32[]{:S(2)}, u32[]{:S(2)}) collective-permute-start(bf16[512,1152]{1,0:T(8,128)(2,1)S(1)} %bitcast.12), channel_id=1, source_target_pairs={{0,4},{4,0},{1,5},{5,1},{2,6},{6,2},{3,7},{7,3},{8,12},{12,8},{9,1... | collective-permute-start | bytes 3538952 | tf_op jit(solution)/shard_map/ppermute | solution.py:326
  65.3 1.1 home.1
  66.4 1.7 %collective-permute-done.4.refs_5_ = bf16[128,1152]{1,0:T(8,128)(2,1)S(1)} collective-permute-done((bf16[128,1152]{1,0:T(8,128)(2,1)S(1)}, bf16[128,1152]{1,0:T(8,128)(2,1)S(1)}, u32[]{:S(2)}, u32[]{:S(2)}) %collective-permute-start.4) | collective-permute-done | bytes 294944 | tf_op jit(solution)/shard_map/ppermute | solution.py:331
  68.2 1.4 collective-permute-done.3.refs_4_
  69.6 4.2 %collective-permute-done.2.refs_3_ = bf16[128,1152]{1,0:T(8,128)(2,1)S(1)} collective-permute-done((bf16[128,1152]{1,0:T(8,128)(2,1)S(1)}, bf16[128,1152]{1,0:T(8,128)(2,1)S(1)}, u32[]{:S(2)}, u32[]{:S(2)}) %collective-permute-start.2) | collective-permute-done | bytes 294944 | tf_op jit(solution)/shard_map/ppermute | solution.py:331
  73.8 2.6 %own.1 = (bf16[512,1152]{1,0:T(8,128)(2,1)S(1)}, bf16[512,512]{1,0:T(8,128)(2,1)S(1)}, bf16[512,1152]{1,0:T(8,128)(2,1)S(1)}, f32[24,128]{1,0:T(8,128)S(1)}) custom-call(f32[2]{0:T(128)S(1)} %pad_maximum_fusion.refs_0_, bf16[512,1152]{1,0:T(8,128)(2,1)S(1)} %bitcast.14, bf16[128,1152]{1,0:T(8,128)(2,1)S(1)} %get-tuple-element.33.refs_2_, ...), custom_call_target="tpu_custom_call" | custom-call | flops 1207959552 | bytes 5398528 | tf_op jit(solution)/shard_map/own/pallas_call | solution.py:38
  76.4 0.0 collective-permute-done.5.refs_1_
  76.4 4.1 %other.1 = (bf16[512,1152]{1,0:T(8,128)(2,1)S(1)}, f32[16,8,128]{2,1,0:T(8,128)S(1)}, bf16[128,1152]{1,0:T(8,128)(2,1)S(1)}, bf16[128,1152]{1,0:T(8,128)(2,1)S(1...) custom-call(f32[2]{0:T(128)S(1)} %pad_maximum_fusion.refs_0_, ...), custom_call_target="tpu_custom_call" | custom-call | flops 2415919104 | bytes 6500352 | tf_op jit(solution)/shard_map/other/pallas_call | solution.py:38
  80.5 1.9 %collective-permute-start.6 = (bf16[512,1152]{1,0:T(8,128)(2,1)S(1)}, bf16[512,1152]{1,0:T(8,128)(2,1)S(1)}, u32[]{:S(2)}, u32[]{:S(2)}) collective-permute-start(bf16[512,1152]{1,0:T(8,128)(2,1)S(1)} %get-tuple-element.40), channel_id=1, source_target_pairs={{0,4},{4,0},{1,5},{5,1},{2,6},{6,2},{3,7},{7,3},{8,12},{12,8},{9,1... | collective-permute-start | bytes 3538952 | tf_op jit(solution)/shard_map/ppermute | solution.py:326
  82.4 15.9 %all_to_all.26.refs_2_ = f32[16,8,128]{2,1,0:T(8,128)S(1)} all-to-all(f32[16,8,128]{2,1,0:T(8,128)S(1)} %get-tuple-element.41), channel_id=1, replica_groups=mesh['zh1'=2,'zh0'=2,'x'=4,'y'=4,'core'=2,'zl'=4] {'zh0','y','core'}, dimensions={0} | all-to-all | bytes 131072 | tf_op jit(solution)/shard_map/all_to_all | solution.py:405
  98.3 0.0 collective-permute-done.6.refs_1_
  98.3 1.4 combine.1
  99.7 4.8 %all-to-all-start.3 = ((bf16[4,1168,128]{2,1,0:T(8,128)(2,1)}), bf16[4,1168,128]{2,1,0:T(8,128)(2,1)S(1)}, u32[]{:S(2)}, u32[]{:S(2)}) async-start(bf16[4,1168,128]{2,1,0:T(8,128)(2,1)} %combine.1), calls=%async_computation.3 | async-start | bytes 2392064 | tf_op jit(solution)/shard_map/all_to_all | solution.py:412
  104.5 3.3 %collective-permute-start.8 = (bf16[128,1152]{1,0:T(8,128)(2,1)S(1)}, bf16[128,1152]{1,0:T(8,128)(2,1)S(1)}, u32[]{:S(2)}, u32[]{:S(2)}) collective-permute-start(bf16[128,1152]{1,0:T(8,128)(2,1)S(1)} %get-tuple-element.45), channel_id=1, source_target_pairs={{0,24},{8,0},{16,8},{24,16},{1,25},{9,1},{17,9},{25,17},{2,26},{10... | collective-permute-start | bytes 884744 | tf_op jit(solution)/shard_map/ppermute | solution.py:331
  107.8 3.1 %collective-permute-start.9 = (bf16[128,1152]{1,0:T(8,128)(2,1)S(1)}, bf16[128,1152]{1,0:T(8,128)(2,1)S(1)}, u32[]{:S(2)}, u32[]{:S(2)}) collective-permute-start(bf16[128,1152]{1,0:T(8,128)(2,1)S(1)} %get-tuple-element.46), channel_id=1, source_target_pairs={{0,16},{8,24},{16,0},{24,8},{1,17},{9,25},{17,1},{25,9},{2,18},{10... | collective-permute-start | bytes 884744 | tf_op jit(solution)/shard_map/ppermute | solution.py:331
  110.9 2.0 %collective-permute-start.10 = (bf16[128,1152]{1,0:T(8,128)(2,1)S(1)}, bf16[128,1152]{1,0:T(8,128)(2,1)S(1)}, u32[]{:S(2)}, u32[]{:S(2)}) collective-permute-start(bf16[128,1152]{1,0:T(8,128)(2,1)S(1)} %get-tuple-element.47), channel_id=1, source_target_pairs={{0,8},{8,16},{16,24},{24,0},{1,9},{9,17},{17,25},{25,1},{2,10},{10... | collective-permute-start | bytes 884744 | tf_op jit(solution)/shard_map/ppermute | solution.py:331
  112.8 5.6 %all-to-all-done.3.refs_0_ = bf16[4,1168,128]{2,1,0:T(8,128)(2,1)S(1)} async-done(((bf16[4,1168,128]{2,1,0:T(8,128)(2,1)}), bf16[4,1168,128]{2,1,0:T(8,128)(2,1)S(1)}, u32[]{:S(2)}, u32[]{:S(2)}) %all-to-all-start.3) | async-done | bytes 1196064 | tf_op jit(solution)/shard_map/all_to_all | solution.py:412
  118.4 0.2 image_sum.1
  118.6 1.9 %collective-permute-start.7 = (bf16[592,128]{1,0:T(8,128)(2,1)S(1)}, bf16[592,128]{1,0:T(8,128)(2,1)S(1)}, u32[]{:S(2)}, u32[]{:S(2)}) collective-permute-start(bf16[592,128]{1,0:T(8,128)(2,1)S(1)} %get-tuple-element.43), channel_id=1, source_target_pairs={{0,384},{384,0},{128,256},{256,128},{1,385},{385,1},{129,257},{257... | collective-permute-start | bytes 454664 | tf_op jit(solution)/shard_map/ppermute | solution.py:335
  120.6 0.0 collective-permute-done.8.refs_1_
  120.6 0.6 collective-permute-done.9.refs_2_
  121.2 4.5 %collective-permute-done.10.refs_3_ = bf16[128,1152]{1,0:T(8,128)(2,1)S(1)} collective-permute-done((bf16[128,1152]{1,0:T(8,128)(2,1)S(1)}, bf16[128,1152]{1,0:T(8,128)(2,1)S(1)}, u32[]{:S(2)}, u32[]{:S(2)}) %collective-permute-start.10) | collective-permute-done | bytes 294944 | tf_op jit(solution)/shard_map/ppermute | solution.py:331
  125.7 0.1 text_sum.1
  125.8 1.9 %collective-permute-start.11 = (bf16[576,128]{1,0:T(8,128)(2,1)S(1)}, bf16[576,128]{1,0:T(8,128)(2,1)S(1)}, u32[]{:S(2)}, u32[]{:S(2)}) collective-permute-start(bf16[576,128]{1,0:T(8,128)(2,1)S(1)} %get-tuple-element.49), channel_id=1, source_target_pairs={{0,128},{128,0},{256,384},{384,256},{1,129},{129,1},{257,385},{385... | collective-permute-start | bytes 442376 | tf_op jit(solution)/shard_map/ppermute | solution.py:339
  127.7 9.8 %collective-permute-done.11.refs_4_ = bf16[576,128]{1,0:T(8,128)(2,1)S(1)} collective-permute-done((bf16[576,128]{1,0:T(8,128)(2,1)S(1)}, bf16[576,128]{1,0:T(8,128)(2,1)S(1)}, u32[]{:S(2)}, u32[]{:S(2)}) %collective-permute-start.11) | collective-permute-done | bytes 147488 | tf_op jit(solution)/shard_map/ppermute | solution.py:339
  137.5 0.0 collective-permute-done.7.refs_2_
  137.5 0.4 finish.1
  137.9 21.6 %all_to_all.27.refs_0_ = bf16[4,304,128]{2,1,0:T(8,128)(2,1)S(1)} all-to-all(bf16[4,304,128]{2,1,0:T(8,128)(2,1)S(1)} %finish.1), channel_id=1, replica_groups=mesh['zh1'=2,'zh0'=2,'x'=4,'y'=4,'core'=2,'zl'=4] {'zl'}, dimensions={0} | all-to-all | bytes 622592 | tf_op jit(solution)/shard_map/all_to_all | solution.py:435
  159.5 0.8 last.1
  160.3 0.5 fusion
Async XLA Ops:
  0.6 0.9 copy-start
  1.5 0.9 copy-start.1
  18.1 20.7 %collective-permute-start = (bf16[64,1152]{1,0:T(8,128)(2,1)S(1)}, bf16[64,1152]{1,0:T(8,128)(2,1)S(1)}, u32[]{:S(2)}, u32[]{:S(2)}) collective-permute-start(bf16[64,1152]{1,0:T(8,128)(2,1)S(1)} %get-tuple-element.29.refs_0_), channel_id=1, source_target_pairs={{0,384},{384,0},{128,256},{256,128},{1,385},{385,1},{129,257},{257... | collective-permute-start | bytes 442376 | tf_op jit(solution)/shard_map/ppermute | solution.py:335
  28.2 15.7 %collective-permute-start.1 = (bf16[64,1152]{1,0:T(8,128)(2,1)S(1)}, bf16[64,1152]{1,0:T(8,128)(2,1)S(1)}, u32[]{:S(2)}, u32[]{:S(2)}) collective-permute-start(bf16[64,1152]{1,0:T(8,128)(2,1)S(1)} %get-tuple-element.30.refs_2_), channel_id=1, source_target_pairs={{0,128},{128,0},{256,384},{384,256},{1,129},{129,1},{257,385},{385... | collective-permute-start | bytes 442376 | tf_op jit(solution)/shard_map/ppermute | solution.py:339
  45.0 18.3 %all-to-all-start.1 = ((bf16[4,128,1152]{2,1,0:T(8,128)(2,1)}), bf16[4,128,1152]{2,1,0:T(8,128)(2,1)S(1)}, u32[]{:S(2)}, u32[]{:S(2)}) async-start(bf16[4,128,1152]{2,1,0:T(8,128)(2,1)} %get-tuple-element.31), calls=%async_computation.1 | async-start | bytes 2359296 | tf_op jit(solution)/shard_map/all_to_all | solution.py:365
  51.3 16.9 %collective-permute-start.4 = (bf16[128,1152]{1,0:T(8,128)(2,1)S(1)}, bf16[128,1152]{1,0:T(8,128)(2,1)S(1)}, u32[]{:S(2)}, u32[]{:S(2)}) collective-permute-start(bf16[128,1152]{1,0:T(8,128)(2,1)S(1)} %get-tuple-element.32.refs_3_), channel_id=1, source_target_pairs={{0,24},{8,0},{16,8},{24,16},{1,25},{9,1},{17,9},{25,17},{2,26},{10... | collective-permute-start | bytes 884744 | tf_op jit(solution)/shard_map/ppermute | solution.py:331
  56.2 13.4 %collective-permute-start.3 = (bf16[128,1152]{1,0:T(8,128)(2,1)S(1)}, bf16[128,1152]{1,0:T(8,128)(2,1)S(1)}, u32[]{:S(2)}, u32[]{:S(2)}) collective-permute-start(bf16[128,1152]{1,0:T(8,128)(2,1)S(1)} %get-tuple-element.32.refs_3_), channel_id=1, source_target_pairs={{0,16},{8,24},{16,0},{24,8},{1,17},{9,25},{17,1},{25,9},{2,18},{10... | collective-permute-start | bytes 884744 | tf_op jit(solution)/shard_map/ppermute | solution.py:331
  58.7 15.1 %collective-permute-start.2 = (bf16[128,1152]{1,0:T(8,128)(2,1)S(1)}, bf16[128,1152]{1,0:T(8,128)(2,1)S(1)}, u32[]{:S(2)}, u32[]{:S(2)}) collective-permute-start(bf16[128,1152]{1,0:T(8,128)(2,1)S(1)} %get-tuple-element.32.refs_3_), channel_id=1, source_target_pairs={{0,8},{8,16},{16,24},{24,0},{1,9},{9,17},{17,25},{25,1},{2,10},{10... | collective-permute-start | bytes 884744 | tf_op jit(solution)/shard_map/ppermute | solution.py:331
  63.4 13.0 %collective-permute-start.5 = (bf16[512,1152]{1,0:T(8,128)(2,1)S(1)}, bf16[512,1152]{1,0:T(8,128)(2,1)S(1)}, u32[]{:S(2)}, u32[]{:S(2)}) collective-permute-start(bf16[512,1152]{1,0:T(8,128)(2,1)S(1)} %bitcast.12), channel_id=1, source_target_pairs={{0,4},{4,0},{1,5},{5,1},{2,6},{6,2},{3,7},{7,3},{8,12},{12,8},{9,1... | collective-permute-start | bytes 3538952 | tf_op jit(solution)/shard_map/ppermute | solution.py:326
  80.5 17.8 %collective-permute-start.6 = (bf16[512,1152]{1,0:T(8,128)(2,1)S(1)}, bf16[512,1152]{1,0:T(8,128)(2,1)S(1)}, u32[]{:S(2)}, u32[]{:S(2)}) collective-permute-start(bf16[512,1152]{1,0:T(8,128)(2,1)S(1)} %get-tuple-element.40), channel_id=1, source_target_pairs={{0,4},{4,0},{1,5},{5,1},{2,6},{6,2},{3,7},{7,3},{8,12},{12,8},{9,1... | collective-permute-start | bytes 3538952 | tf_op jit(solution)/shard_map/ppermute | solution.py:326
  99.7 18.7 %all-to-all-start.3 = ((bf16[4,1168,128]{2,1,0:T(8,128)(2,1)}), bf16[4,1168,128]{2,1,0:T(8,128)(2,1)S(1)}, u32[]{:S(2)}, u32[]{:S(2)}) async-start(bf16[4,1168,128]{2,1,0:T(8,128)(2,1)} %combine.1), calls=%async_computation.3 | async-start | bytes 2392064 | tf_op jit(solution)/shard_map/all_to_all | solution.py:412
  104.5 16.1 %collective-permute-start.8 = (bf16[128,1152]{1,0:T(8,128)(2,1)S(1)}, bf16[128,1152]{1,0:T(8,128)(2,1)S(1)}, u32[]{:S(2)}, u32[]{:S(2)}) collective-permute-start(bf16[128,1152]{1,0:T(8,128)(2,1)S(1)} %get-tuple-element.45), channel_id=1, source_target_pairs={{0,24},{8,0},{16,8},{24,16},{1,25},{9,1},{17,9},{25,17},{2,26},{10... | collective-permute-start | bytes 884744 | tf_op jit(solution)/shard_map/ppermute | solution.py:331
  107.8 13.4 %collective-permute-start.9 = (bf16[128,1152]{1,0:T(8,128)(2,1)S(1)}, bf16[128,1152]{1,0:T(8,128)(2,1)S(1)}, u32[]{:S(2)}, u32[]{:S(2)}) collective-permute-start(bf16[128,1152]{1,0:T(8,128)(2,1)S(1)} %get-tuple-element.46), channel_id=1, source_target_pairs={{0,16},{8,24},{16,0},{24,8},{1,17},{9,25},{17,1},{25,9},{2,18},{10... | collective-permute-start | bytes 884744 | tf_op jit(solution)/shard_map/ppermute | solution.py:331
  110.9 14.8 %collective-permute-start.10 = (bf16[128,1152]{1,0:T(8,128)(2,1)S(1)}, bf16[128,1152]{1,0:T(8,128)(2,1)S(1)}, u32[]{:S(2)}, u32[]{:S(2)}) collective-permute-start(bf16[128,1152]{1,0:T(8,128)(2,1)S(1)} %get-tuple-element.47), channel_id=1, source_target_pairs={{0,8},{8,16},{16,24},{24,0},{1,9},{9,17},{17,25},{25,1},{2,10},{10... | collective-permute-start | bytes 884744 | tf_op jit(solution)/shard_map/ppermute | solution.py:331
  118.6 18.9 %collective-permute-start.7 = (bf16[592,128]{1,0:T(8,128)(2,1)S(1)}, bf16[592,128]{1,0:T(8,128)(2,1)S(1)}, u32[]{:S(2)}, u32[]{:S(2)}) collective-permute-start(bf16[592,128]{1,0:T(8,128)(2,1)S(1)} %get-tuple-element.43), channel_id=1, source_target_pairs={{0,384},{384,0},{128,256},{256,128},{1,385},{385,1},{129,257},{257... | collective-permute-start | bytes 454664 | tf_op jit(solution)/shard_map/ppermute | solution.py:335
  125.8 11.7 %collective-permute-start.11 = (bf16[576,128]{1,0:T(8,128)(2,1)S(1)}, bf16[576,128]{1,0:T(8,128)(2,1)S(1)}, u32[]{:S(2)}, u32[]{:S(2)}) collective-permute-start(bf16[576,128]{1,0:T(8,128)(2,1)S(1)} %get-tuple-element.49), channel_id=1, source_target_pairs={{0,128},{128,0},{256,384},{384,256},{1,129},{129,1},{257,385},{385... | collective-permute-start | bytes 442376 | tf_op jit(solution)/shard_map/ppermute | solution.py:339

commit v6 on v4

v6 whole, which is shorter than its diff:
```python
import functools

import jax
import jax.numpy as jnp
from jax import lax
from jax.experimental import pallas as pl
from jax.experimental.pallas import tpu as pltpu
from jax.sharding import Mesh, PartitionSpec as P

epsilon = 1e-06
lanes = 128
piece = 32
strips = 4
rest = 32
chunk_rows = 72
carry_rows = 16
sent_rows = 88
tiles = 9
vmem = pl.BlockSpec(memory_space=pltpu.VMEM)
smem = pl.BlockSpec(memory_space=pltpu.SMEM)
anywhere = pl.BlockSpec(memory_space=pl.ANY)
limits = pltpu.CompilerParams(vmem_limit_bytes=16 * 1024 * 1024)


def shape(dims, dtype=jnp.bfloat16):
    return jax.ShapeDtypeStruct(tuple(dims), dtype)


def call(kernel, out_shape, name, operands, scalars=(), after=(), flops=0, special=0, scratch=()):
    out_shape = tuple(out_shape)
    scalars, operands, after = tuple(scalars), tuple(operands), tuple(after)
    inputs = len(scalars) + len(operands)
    moved = sum(a.size * a.dtype.itemsize for a in operands + out_shape)

    def body(*refs):
        kernel(*refs[:inputs], *refs[inputs + len(after) :])

    return pl.pallas_call(
        body,
        out_shape=out_shape,
        in_specs=[smem] * len(scalars) + [vmem] * len(operands) + [anywhere] * len(after),
        out_specs=(vmem,) * len(out_shape),
        scratch_shapes=list(scratch),
        compiler_params=limits,
        cost_estimate=pl.CostEstimate(flops=flops, bytes_accessed=moved, transcendentals=special),
        name=name,
    )(*scalars, *operands, *after)


def hold(value, after):
    def body(*refs):
        del refs

    return pl.pallas_call(
        body,
        out_shape=shape(value.shape, value.dtype),
        in_specs=[anywhere] * (1 + len(after)),
        out_specs=anywhere,
        input_output_aliases={0: 0},
        compiler_params=limits,
        name="hold",
    )(value, *after)


def total(values):
    return functools.reduce(lambda a, b: a + b, values)


def wide(ref, *index):
    return ref[index].astype(jnp.float32)


def lane_group():
    return lax.broadcasted_iota(jnp.int32, (8, lanes), 1) // rest


def pack_kernel(image, out):
    whole = wide(image, slice(None)).T
    for k in range(4):
        rows = whole[k * piece : (k + 1) * piece]
        last = rows[:, 2 * lanes :]
        last = jnp.concatenate([last[8 * g : 8 * g + 8] for g in range(4)], axis=1)
        chunk = jnp.concatenate([rows[:, :lanes], rows[:, lanes : 2 * lanes], last], axis=0)
        chunk = chunk.astype(jnp.bfloat16)
        for h in range(out.shape[0] // strips):
            out[h * strips + k] = chunk


def unpack_rows(chunks, group):
    found = []
    lasts = []
    for chunk in chunks:
        found += [chunk[:piece], chunk[piece : 2 * piece]]
        lasts.append(chunk[2 * piece :])
    last = []
    for g in range(4):
        value = jnp.zeros((8, lanes), jnp.float32)
        for s in range(strips):
            turn = rest * (s - g) % lanes
            moved = pltpu.roll(lasts[s], turn, 1) if turn else lasts[s]
            value = jnp.where(group == s, moved, value)
        last.append(value)
    found.append(jnp.concatenate(last, axis=0))
    return found


def units_of(found):
    inverse = lax.rsqrt(jnp.sum(total([t * t for t in found]), axis=1, keepdims=True) + epsilon)
    return [t * inverse for t in found], inverse


def strip_at(place, k):
    return lax.rem(place[0] + (strips - k), strips)


def image_units(place, arrived, h, group):
    chunks = [wide(arrived, h * strips + strip_at(place, k)) for k in range(strips)]
    return units_of(unpack_rows(chunks, group))


def image_unit_kernel(place, arrived, out):
    group = lane_group()
    for h in range(arrived.shape[0] // strips):
        units, _ = image_units(place, arrived, h, group)
        for t in range(tiles):
            value = units[t].astype(jnp.bfloat16)
            for k in range(out.shape[0]):
                out[k, h * piece : (h + 1) * piece, t * lanes : (t + 1) * lanes] = value


def text_units(parts):
    rows = [wide(p, slice(None)).T for p in parts]
    found = []
    for r in rows:
        found += [r[:, :lanes], r[:, lanes : 2 * lanes]]
    found.append(jnp.concatenate([r[:, 2 * lanes :] for r in rows], axis=1))
    return units_of(found)


def text_unit_kernel(p0, p1, p2, p3, out):
    units, _ = text_units((p0, p1, p2, p3))
    for t in range(tiles):
        out[:, t * lanes : (t + 1) * lanes] = units[t].astype(jnp.bfloat16)


def fold(values):
    rows, columns = values.shape
    part = jnp.sum(values.reshape(rows // 8, 8, columns), axis=0)
    return total([part[:, c : c + lanes] for c in range(0, columns, lanes)])


def pair_terms(left, right, scale, bias, same=None):
    product = lax.dot_general(
        left, right, (((1,), (1,)), ((), ())), preferred_element_type=jnp.float32
    )
    logits = scale * product + bias
    if same is None:
        grown = jnp.exp(logits)
        slope = grown / (1.0 + grown)
    else:
        grown = jnp.exp(jnp.where(same, -logits, logits))
        share = grown / (1.0 + grown)
        slope = jnp.where(same, -share, share)
    quarter = left.shape[0] // 4
    a, b, c, d = (grown[k * quarter : (k + 1) * quarter, :] for k in range(4))
    ab = a + (b + a * b)
    cd = c + (d + c * d)
    sums = (fold(jnp.log1p(ab + (cd + ab * cd))), fold(slope * product), fold(slope))
    return (scale * slope).astype(jnp.bfloat16), sums


def write_sums(out, sums, before=None):
    for k in range(3):
        value = total([found[k] for found in sums])
        if before is not None:
            value = value + before[8 * k : 8 * k + 8, :]
        out[8 * k : 8 * k + 8, :] = value


tile = 256


def home_kernel(scales, spot, left, right, weights, sums_out, kept):
    kept[...] = right[...]
    rows, columns = left.shape[0], right.shape[0]
    sums = []
    for start in range(0, rows, tile):
        here = pl.ds(start, tile)
        row = lax.broadcasted_iota(jnp.int32, (tile, 1), 0) + (start - spot[0])
        row = jnp.where((row >= 0) & (row < piece), row, -1)
        column = lax.broadcasted_iota(jnp.int32, (1, columns), 1) - spot[1]
        same = row == jnp.where(column >= 0, column, -2)
        weights[here, :], found = pair_terms(
            left[here, :], right[...], scales[0], scales[1], same
        )
        sums.append(found)
    write_sums(sums_out, sums)


def own_kernel(scales, left, t0, t1, t2, t3, home, home_sums, back, weights, right, sums_out):
    rows, part = left.shape[0], t0.shape[0]
    for k, ref in enumerate((t0, t1, t2, t3)):
        right[k * part : (k + 1) * part, :] = ref[...]
    sums = []
    for start in range(0, rows, tile):
        here = pl.ds(start, tile)
        value, found = pair_terms(left[here, :], right[part:, :], scales[0], scales[1])
        weights[here, :part] = home[here, :]
        weights[here, part:] = value
        back[here, :] = jnp.dot(
            weights[here, :], right[...], preferred_element_type=jnp.float32
        ).astype(jnp.bfloat16)
        sums.append(found)
    write_sums(sums_out, sums, home_sums)


def other_kernel(
    scales, left, right, own_sums, own_weights, own_left, back, sums_out, b0, b1, b2, b3, weights
):
    sums = []
    for start in range(0, left.shape[0], tile):
        here = pl.ds(start, tile)
        value, found = pair_terms(left[here, :], right[...], scales[0], scales[1])
        weights[here, :] = value
        back[here, :] = jnp.dot(
            value, right[...], preferred_element_type=jnp.float32
        ).astype(jnp.bfloat16)
        sums.append(found)
    row = lax.broadcasted_iota(jnp.int32, (8, lanes), 0)
    value = jnp.zeros((8, lanes), jnp.float32)
    for k in range(3):
        found = total([s[k] for s in sums]) + own_sums[8 * k : 8 * k + 8, :]
        value = jnp.where(row == k, jnp.sum(found, axis=0, keepdims=True), value)
    for k in range(sums_out.shape[0]):
        sums_out[k] = value
    contract = (((0,), (0,)), ((), ()))
    part = b0.shape[0]
    value = lax.dot_general(
        own_weights[...], own_left[...], contract, preferred_element_type=jnp.float32
    ) + lax.dot_general(weights[...], left[...], contract, preferred_element_type=jnp.float32)
    for k, out in enumerate((b0, b1, b2, b3)):
        out[...] = value[k * part : (k + 1) * part].astype(jnp.bfloat16)


def three_parts(value):
    high = value.astype(jnp.bfloat16).astype(jnp.float32)
    middle = (value - high).astype(jnp.bfloat16).astype(jnp.float32)
    return high, middle, value - high - middle


def carry_of(value):
    parts = three_parts(jnp.sum(value, axis=1, keepdims=True))
    lane = lax.broadcasted_iota(jnp.int32, (8, lanes), 1)
    carry = jnp.zeros((8, lanes), jnp.float32)
    for k in range(3):
        carry = jnp.where(lane == k, parts[k], carry)
    return jnp.concatenate([carry, jnp.zeros((8, lanes), jnp.float32)], axis=0)


def combine_kernel(own, given, sums, out):
    count, all_rows, _ = out.shape
    block = own.shape[0] // count
    carry = carry_of(total([sums[k] for k in range(sums.shape[0])])).astype(jnp.bfloat16)
    for k in range(count):
        rows = pl.ds(k * block, block)
        for t in range(tiles):
            columns = pl.ds(t * lanes, lanes)
            value = wide(own, rows, columns) + wide(given, rows, columns)
            out[k, t * block : (t + 1) * block, :] = value.astype(jnp.bfloat16)
        out[k, tiles * block : all_rows, :] = carry


def grads_of(units, inverse, grads):
    along = jnp.sum(total([u * g for u, g in zip(units, grads)]), axis=1, keepdims=True)
    return [(g - u * along) * inverse for u, g in zip(units, grads)]


def image_finish_kernel(place, arrived, backs, out):
    group = lane_group()
    count = backs.shape[0]
    heads = arrived.shape[0] // strips
    block = heads * piece
    tail = pl.ds(tiles * block, carry_rows)
    carry = carry_of(total([wide(backs, k, tail, slice(None)) for k in range(count)])[:8])
    for h in range(heads):
        units, inverse = image_units(place, arrived, h, group)
        grads = []
        for t in range(tiles):
            rows = pl.ds(t * block + h * piece, piece)
            grads.append(total([wide(backs, k, rows, slice(None)) for k in range(count)]))
        final = grads_of(units, inverse, grads)
        for s in range(strips):
            last = jnp.zeros((8, lanes), jnp.float32)
            for g in range(4):
                turn = rest * (g - s) % lanes
                rows = final[tiles - 1][8 * g : 8 * g + 8]
                moved = pltpu.roll(rows, turn, 1) if turn else rows
                last = jnp.where(group == g, moved, last)
            chunk = jnp.concatenate([carry, final[2 * s], final[2 * s + 1], last], axis=0)
            out[h * strips + strip_at(place, s)] = chunk.astype(jnp.bfloat16)


def text_finish_kernel(p0, p1, p2, p3, b0, b1, b2, b3, *outs):
    units, inverse = text_units((p0, p1, p2, p3))
    grads = []
    for t in range(tiles):
        columns = pl.ds(t * lanes, lanes)
        grads.append(total([wide(b, slice(None), columns) for b in (b0, b1, b2, b3)]))
    final = grads_of(units, inverse, grads)
    last = final[tiles - 1].T.astype(jnp.bfloat16)
    for s, out in enumerate(outs):
        out[:lanes, :] = final[2 * s].T.astype(jnp.bfloat16)
        out[lanes : 2 * lanes, :] = final[2 * s + 1].T.astype(jnp.bfloat16)
        out[2 * lanes :, :] = last[s * rest : (s + 1) * rest]


def text_last_kernel(g0, g1, g2, g3, out):
    value = total([wide(g, slice(None)) for g in (g0, g1, g2, g3)])
    out[...] = value.astype(jnp.bfloat16)


def image_last_kernel(arrived, out, sums_out):
    values = [wide(arrived, d) for d in range(arrived.shape[0])]
    heads = len(values) // strips
    found = []
    for k in range(strips):
        chunk = total([values[h * strips + k][carry_rows:] for h in range(heads)])
        last = chunk[2 * piece :]
        groups = [last] + [pltpu.roll(last, lanes - rest * g, 1) for g in range(1, 4)]
        last = jnp.concatenate(groups, axis=0)
        found.append((chunk[:piece], chunk[piece : 2 * piece], last))
    for t in range(3):
        rows = jnp.concatenate([f[t] for f in found], axis=0).T
        count = lanes if t < 2 else rest
        out[t * lanes : t * lanes + count, :] = rows[:count].astype(jnp.bfloat16)
    sums = total([v[:8] for v in values])
    sums_out[...] = jnp.broadcast_to(jnp.sum(sums, axis=1, keepdims=True), sums.shape)


def swap_core(value):
    return lax.ppermute(value, "core", [(0, 1), (1, 0)])


def shift(value, axis, k):
    count = lax.axis_size(axis)
    return lax.ppermute(value, axis, [(i, (i + k) % count) for i in range(count)])


def shards(image, text, log_temp, bias):
    rows, strip = image.shape
    x_count, y_count, zh_count = (lax.axis_size(name) for name in ("x", "y", "zh"))
    z_count = zh_count * strips
    width = strip * strips
    block = zh_count * piece
    count = x_count * block
    zh, x, zl = (lax.axis_index(name).astype(jnp.int32) for name in ("zh", "x", "zl"))
    scale = jnp.exp(log_temp)
    scales = jnp.stack([scale, bias])
    place = zl.reshape(1)
    spot = jnp.stack([x * block + zh * piece, zl * piece])
    f32 = jnp.float32

    (packed,) = call(pack_kernel, [shape((z_count, chunk_rows, lanes))], "pack", [image.T])
    parts = [text.T] + [shift(text.T, "zl", k) for k in range(1, strips)]
    arrived = lax.all_to_all(hold(packed, parts[1:]), ("zh", "zl"), 0, 0)
    (home_text,) = call(text_unit_kernel, [shape((block, width))], "text_unit", parts)
    texts = [shift(home_text, "y", k) for k in range(1, y_count)]
    (units,) = call(
        image_unit_kernel,
        [shape((x_count, block, width))],
        "image_unit",
        [arrived],
        scalars=[place],
        after=texts,
    )
    image_rows = lax.all_to_all(units, "x", 0, 0).reshape(count, width)
    other_rows = swap_core(image_rows)

    columns = y_count * block
    area = count * columns
    home_weights, home_sums, home_text = call(
        home_kernel,
        [shape((count, block)), shape((24, lanes), f32), shape((block, width))],
        "home",
        [image_rows, home_text],
        scalars=[scales, spot],
        flops=200 * count * block * width,
    )
    own_back, own_weights, right, own_sums = call(
        own_kernel,
        [
            shape((count, width)),
            shape((count, columns)),
            shape((columns, width)),
            shape((24, lanes), f32),
        ],
        "own",
        [image_rows, home_text] + texts + [home_weights, home_sums],
        scalars=[scales],
        flops=4 * area * width,
        special=2 * area,
    )
    other_back, sums, *text_backs = call(
        other_kernel,
        [shape((count, width)), shape((y_count * 2, 8, lanes), f32)]
        + [shape((block, width))] * y_count,
        "other",
        [other_rows, right, own_sums, own_weights, image_rows],
        scalars=[scales],
        flops=8 * area * width,
        special=2 * area,
        scratch=[pltpu.VMEM((count, columns), jnp.bfloat16)],
    )
    given_back = swap_core(other_back)
    sums = lax.all_to_all(sums, ("y", "core"), 0, 0)
    (combined,) = call(
        combine_kernel,
        [shape((x_count, tiles * block + carry_rows, lanes))],
        "combine",
        [own_back, given_back, sums],
    )
    combined = lax.all_to_all(combined, "x", 0, 0)
    (finished,) = call(
        image_finish_kernel,
        [shape((z_count, sent_rows, lanes))],
        "image_finish",
        [arrived, combined],
        scalars=[place],
        flops=200 * count * block * width,
    )
    moved = [text_backs[0]] + [shift(text_backs[k], "y", -k) for k in range(1, y_count)]
    finished = hold(finished, moved[1:])
    finished = lax.all_to_all(finished, ("zh", "zl"), 0, 0)
    text_parts = call(
        text_finish_kernel, [shape((strip, rows))] * strips, "text_finish", parts + moved
    )
    given = [text_parts[0]] + [shift(text_parts[k], "zl", -k) for k in range(1, strips)]
    (grad_text,) = call(text_last_kernel, [shape((strip, rows))], "text_last", given)
    grad_image, sums = call(
        image_last_kernel, [shape((strip, rows)), shape((8, lanes), f32)], "image_last", [finished]
    )
    pairs_count = rows * 4 * x_count * y_count * 2
    return (
        sums[0, 0] / pairs_count,
        grad_image.T,
        grad_text.T,
        scale * sums[1, 0] / pairs_count,
        sums[2, 0] / pairs_count,
    )


def solution(mesh):
    fine = Mesh(mesh.devices.reshape(4, 4, 4, 2, 4), ("zh", "x", "y", "core", "zl"))
    whole = P(("zh", "x", "y", "core"), "zl")
    return jax.shard_map(
        shards,
        mesh=fine,
        in_specs=(whole, whole, P(), P()),
        out_specs=(P(), whole, whole, P(), P()),
        check_vma=False,
    )
```

time: 184 us -> 165 us (0.90)
  the two profiles are of different devices: /device:TPU:34 before, /device:TPU:2 now
where the time goes in v6:
time: 165 us; the launch traced here: 164 us
  starting transfers between devices  79 us (48%)
  waiting for transfers between devices  52.2 us (32%)
  Pallas kernels  15.7 us (10%)
  blocking collectives  7.82 us (5%)
  between operations  7.48 us (5%)
    ppermute x12, starting transfers between devices, shift(): lax.ppermute(value, axis, [(i, (i + k) % count) for i in range(count)])  40.4 us
    ppermute x12, waiting for transfers between devices, shift(): lax.ppermute(value, axis, [(i, (i + k) % count) for i in range(count)])  32.7 us
    pallas_call x11, Pallas kernels, call(): pl.pallas_call(body, out_shape=out_shape, in_specs=[smem] * len(scalars)...  15.7 us
    all_to_all x1, starting transfers between devices, shards(): arrived = lax.all_to_all(hold(packed, parts[1:]), ('zh', 'zl'), 0, 0)  13 us
    all_to_all x1, waiting for transfers between devices, shards(): image_rows = lax.all_to_all(units, 'x', 0, 0).reshape(count, width)  12.4 us
    all_to_all x1, starting transfers between devices, shards(): finished = lax.all_to_all(finished, ('zh', 'zl'), 0, 0)  11.5 us
    all_to_all x1, blocking collectives, shards(): sums = lax.all_to_all(sums, ('y', 'core'), 0, 0)  7.82 us
    all_to_all x1, waiting for transfers between devices, shards(): combined = lax.all_to_all(combined, 'x', 0, 0)  7.06 us
  transfers between devices with their start and end apart: 18, of which 10 were waited for; matrix products, arithmetic and copies ran while one was open for 0% of the time, Pallas kernels for 5%

profile of v6, /device:TPU:2, one launch (start us, length us, event | category | flops | bytes accessed | tf_op | source)
XLA Modules:
  0.0 163.7 jit_solution(9052673449916099800)
XLA Ops:
  0.6 6.7 %collective-permute-start.2 = (bf16[288,128]{1,0:T(8,128)(2,1)}, bf16[288,128]{1,0:T(8,128)(2,1)S(1)}, u32[]{:S(2)}, u32[]{:S(2)}) collective-permute-start(bf16[288,128]{1,0:T(8,128)(2,1)} %bitcast.18), channel_id=1, source_target_pairs={{0,3},{1,0},{2,1},{3,2},{4,7},{5,4},{6,5},{7,6},{8,11},{9,8},{10,9... | collective-permute-start | bytes 221192 | tf_op jit(solution)/shard_map/ppermute | solution.py:346
  7.3 1.9 %collective-permute-start.1 = (bf16[288,128]{1,0:T(8,128)(2,1)}, bf16[288,128]{1,0:T(8,128)(2,1)S(1)}, u32[]{:S(2)}, u32[]{:S(2)}) collective-permute-start(bf16[288,128]{1,0:T(8,128)(2,1)} %bitcast.19), channel_id=1, source_target_pairs={{0,2},{1,3},{2,0},{3,1},{4,6},{5,7},{6,4},{7,5},{8,10},{9,11},{10,... | collective-permute-start | bytes 221192 | tf_op jit(solution)/shard_map/ppermute | solution.py:346
  9.2 2.6 %collective-permute-start = (bf16[288,128]{1,0:T(8,128)(2,1)}, bf16[288,128]{1,0:T(8,128)(2,1)S(1)}, u32[]{:S(2)}, u32[]{:S(2)}) collective-permute-start(bf16[288,128]{1,0:T(8,128)(2,1)} %bitcast.20), channel_id=1, source_target_pairs={{0,1},{1,2},{2,3},{3,0},{4,5},{5,6},{6,7},{7,4},{8,9},{9,10},{10,1... | collective-permute-start | bytes 221192 | tf_op jit(solution)/shard_map/ppermute | solution.py:346
  11.8 0.9 copy-done.1
  12.7 0.9 pack.1.refs_0_
  13.6 1.1 collective-permute-done.1.refs_2_
  14.7 2.8 %collective-permute-done.refs_1_ = bf16[288,128]{1,0:T(8,128)(2,1)S(1)} collective-permute-done((bf16[288,128]{1,0:T(8,128)(2,1)}, bf16[288,128]{1,0:T(8,128)(2,1)S(1)}, u32[]{:S(2)}, u32[]{:S(2)}) %collective-permute-start) | collective-permute-done | bytes 73760 | tf_op jit(solution)/shard_map/ppermute | solution.py:346
  17.5 13.0 %all-to-all-start = ((bf16[16,72,128]{2,1,0:T(8,128)(2,1)}), bf16[16,72,128]{2,1,0:T(8,128)(2,1)S(1)}, u32[]{:S(2)}, u32[]{:S(2)}) async-start(bf16[16,72,128]{2,1,0:T(8,128)(2,1)} %hold.2), calls=%async_computation | async-start | bytes 589824 | tf_op jit(solution)/shard_map/all_to_all | solution.py:365
  30.6 0.4 text_unit.1.refs_3_
  30.9 4.9 %collective-permute-start.5 = (bf16[128,1152]{1,0:T(8,128)(2,1)S(1)}, bf16[128,1152]{1,0:T(8,128)(2,1)S(1)}, u32[]{:S(2)}, u32[]{:S(2)}) collective-permute-start(bf16[128,1152]{1,0:T(8,128)(2,1)S(1)} %text_unit.1.refs_3_), channel_id=1, source_target_pairs={{0,24},{8,0},{16,8},{24,16},{1,25},{9,1},{17,9},{25,17},{2,26},{10... | collective-permute-start | bytes 884744 | tf_op jit(solution)/shard_map/ppermute | solution.py:346
  35.9 2.5 %collective-permute-start.4 = (bf16[128,1152]{1,0:T(8,128)(2,1)S(1)}, bf16[128,1152]{1,0:T(8,128)(2,1)S(1)}, u32[]{:S(2)}, u32[]{:S(2)}) collective-permute-start(bf16[128,1152]{1,0:T(8,128)(2,1)S(1)} %text_unit.1.refs_3_), channel_id=1, source_target_pairs={{0,16},{8,24},{16,0},{24,8},{1,17},{9,25},{17,1},{25,9},{2,18},{10... | collective-permute-start | bytes 884744 | tf_op jit(solution)/shard_map/ppermute | solution.py:346
  38.4 2.9 %collective-permute-start.3 = (bf16[128,1152]{1,0:T(8,128)(2,1)S(1)}, bf16[128,1152]{1,0:T(8,128)(2,1)S(1)}, u32[]{:S(2)}, u32[]{:S(2)}) collective-permute-start(bf16[128,1152]{1,0:T(8,128)(2,1)S(1)} %text_unit.1.refs_3_), channel_id=1, source_target_pairs={{0,8},{8,16},{16,24},{24,0},{1,9},{9,17},{17,25},{25,1},{2,10},{10... | collective-permute-start | bytes 884744 | tf_op jit(solution)/shard_map/ppermute | solution.py:346
  41.3 5.1 %collective-permute-done.5.refs_4_.refs_5_ = bf16[128,1152]{1,0:T(8,128)(2,1)S(1)} collective-permute-done((bf16[128,1152]{1,0:T(8,128)(2,1)S(1)}, bf16[128,1152]{1,0:T(8,128)(2,1)S(1)}, u32[]{:S(2)}, u32[]{:S(2)}) %collective-permute-start.5) | collective-permute-done | bytes 294944 | tf_op jit(solution)/shard_map/ppermute | solution.py:346
  46.4 2.5 %collective-permute-done.4.refs_3_.refs_4_ = bf16[128,1152]{1,0:T(8,128)(2,1)S(1)} collective-permute-done((bf16[128,1152]{1,0:T(8,128)(2,1)S(1)}, bf16[128,1152]{1,0:T(8,128)(2,1)S(1)}, u32[]{:S(2)}, u32[]{:S(2)}) %collective-permute-start.4) | collective-permute-done | bytes 294944 | tf_op jit(solution)/shard_map/ppermute | solution.py:346
  48.9 3.1 %collective-permute-done.3.refs_2_.refs_3_ = bf16[128,1152]{1,0:T(8,128)(2,1)S(1)} collective-permute-done((bf16[128,1152]{1,0:T(8,128)(2,1)S(1)}, bf16[128,1152]{1,0:T(8,128)(2,1)S(1)}, u32[]{:S(2)}, u32[]{:S(2)}) %collective-permute-start.3) | collective-permute-done | bytes 294944 | tf_op jit(solution)/shard_map/ppermute | solution.py:346
  52.1 0.0 all-to-all-done.refs_1_
  52.1 1.4 image_unit.1
  53.4 4.8 %all-to-all-start.1 = ((bf16[4,128,1152]{2,1,0:T(8,128)(2,1)}), bf16[4,128,1152]{2,1,0:T(8,128)(2,1)S(1)}, u32[]{:S(2)}, u32[]{:S(2)}) async-start(bf16[4,128,1152]{2,1,0:T(8,128)(2,1)} %image_unit.1), calls=%async_computation.1 | async-start | bytes 2359296 | tf_op jit(solution)/shard_map/all_to_all | solution.py:376
  59.6 0.1 pad_add_fusion.refs_1_
  59.7 0.1 pad_maximum_fusion.refs_0_
  59.7 12.4 %all-to-all-done.1 = bf16[4,128,1152]{2,1,0:T(8,128)(2,1)S(1)} async-done(((bf16[4,128,1152]{2,1,0:T(8,128)(2,1)}), bf16[4,128,1152]{2,1,0:T(8,128)(2,1)S(1)}, u32[]{:S(2)}, u32[]{:S(2)}) %all-to-all-start.1) | async-done | bytes 1179680 | tf_op jit(solution)/shard_map/all_to_all | solution.py:376
  72.1 1.9 %collective-permute-start.6 = (bf16[512,1152]{1,0:T(8,128)(2,1)S(1)}, bf16[512,1152]{1,0:T(8,128)(2,1)S(1)}, u32[]{:S(2)}, u32[]{:S(2)}) collective-permute-start(bf16[512,1152]{1,0:T(8,128)(2,1)S(1)} %bitcast.14), channel_id=1, source_target_pairs={{0,4},{4,0},{1,5},{5,1},{2,6},{6,2},{3,7},{7,3},{8,12},{12,8},{9,1... | collective-permute-start | bytes 3538952 | tf_op jit(solution)/shard_map/ppermute | solution.py:341
  74.0 1.1 home.1
  75.2 2.6 %own.1 = (bf16[512,1152]{1,0:T(8,128)(2,1)S(1)}, bf16[512,512]{1,0:T(8,128)(2,1)S(1)}, bf16[512,1152]{1,0:T(8,128)(2,1)S(1)}, f32[24,128]{1,0:T(8,128)S(1)}) custom-call(f32[2]{0:T(128)S(1)} %pad_maximum_fusion.refs_0_, bf16[512,1152]{1,0:T(8,128)(2,1)S(1)} %bitcast.16, bf16[128,1152]{1,0:T(8,128)(2,1)S(1)} %get-tuple-element.24.refs_2_, ...), custom_call_target="tpu_custom_call" | custom-call | flops 1207959552 | bytes 5398528 | tf_op jit(solution)/shard_map/own/pallas_call | solution.py:38
  77.7 0.0 collective-permute-done.6.refs_1_
  77.7 4.7 %other.1 = (bf16[512,1152]{1,0:T(8,128)(2,1)S(1)}, f32[8,8,128]{2,1,0:T(8,128)S(1)}, bf16[128,1152]{1,0:T(8,128)(2,1)S(1)}, bf16[128,1152]{1,0:T(8,128)(2,1)}, b...) custom-call(f32[2]{0:T(128)S(1)} %pad_maximum_fusion.refs_0_, ...), custom_call_target="tpu_custom_call" | custom-call | flops 2415919104 | bytes 6467584 | tf_op jit(solution)/shard_map/other/pallas_call | solution.py:38
  82.4 2.4 %collective-permute-start.7 = (bf16[512,1152]{1,0:T(8,128)(2,1)S(1)}, bf16[512,1152]{1,0:T(8,128)(2,1)S(1)}, u32[]{:S(2)}, u32[]{:S(2)}) collective-permute-start(bf16[512,1152]{1,0:T(8,128)(2,1)S(1)} %get-tuple-element.31), channel_id=1, source_target_pairs={{0,4},{4,0},{1,5},{5,1},{2,6},{6,2},{3,7},{7,3},{8,12},{12,8},{9,1... | collective-permute-start | bytes 3538952 | tf_op jit(solution)/shard_map/ppermute | solution.py:341
  84.8 7.8 %all_to_all.25.refs_2_ = f32[8,8,128]{2,1,0:T(8,128)S(1)} all-to-all(f32[8,8,128]{2,1,0:T(8,128)S(1)} %get-tuple-element.32), channel_id=1, replica_groups=mesh['zh'=4,'x'=4,'y'=4,'core'=2,'zl'=4] {'y','core'}, dimensions={0} | all-to-all | bytes 65536 | tf_op jit(solution)/shard_map/all_to_all | solution.py:415
  92.6 1.3 combine.1
  94.0 5.0 %all-to-all-start.3 = ((bf16[4,1168,128]{2,1,0:T(8,128)(2,1)}), bf16[4,1168,128]{2,1,0:T(8,128)(2,1)S(1)}, u32[]{:S(2)}, u32[]{:S(2)}) async-start(bf16[4,1168,128]{2,1,0:T(8,128)(2,1)} %combine.1), calls=%async_computation.3 | async-start | bytes 2392064 | tf_op jit(solution)/shard_map/all_to_all | solution.py:422
  98.9 3.1 %collective-permute-start.8 = (bf16[128,1152]{1,0:T(8,128)(2,1)}, bf16[128,1152]{1,0:T(8,128)(2,1)S(1)}, u32[]{:S(2)}, u32[]{:S(2)}) collective-permute-start(bf16[128,1152]{1,0:T(8,128)(2,1)} %get-tuple-element.33), channel_id=1, source_target_pairs={{0,24},{8,0},{16,8},{24,16},{1,25},{9,1},{17,9},{25,17},{2,26},{10... | collective-permute-start | bytes 884744 | tf_op jit(solution)/shard_map/ppermute | solution.py:346
  102.0 3.4 %collective-permute-start.9 = (bf16[128,1152]{1,0:T(8,128)(2,1)S(1)}, bf16[128,1152]{1,0:T(8,128)(2,1)S(1)}, u32[]{:S(2)}, u32[]{:S(2)}) collective-permute-start(bf16[128,1152]{1,0:T(8,128)(2,1)S(1)} %get-tuple-element.34), channel_id=1, source_target_pairs={{0,16},{8,24},{16,0},{24,8},{1,17},{9,25},{17,1},{25,9},{2,18},{10... | collective-permute-start | bytes 884744 | tf_op jit(solution)/shard_map/ppermute | solution.py:346
  105.4 1.9 %collective-permute-start.10 = (bf16[128,1152]{1,0:T(8,128)(2,1)S(1)}, bf16[128,1152]{1,0:T(8,128)(2,1)S(1)}, u32[]{:S(2)}, u32[]{:S(2)}) collective-permute-start(bf16[128,1152]{1,0:T(8,128)(2,1)S(1)} %get-tuple-element.35), channel_id=1, source_target_pairs={{0,8},{8,16},{16,24},{24,0},{1,9},{9,17},{17,25},{25,1},{2,10},{10... | collective-permute-start | bytes 884744 | tf_op jit(solution)/shard_map/ppermute | solution.py:346
  107.3 7.1 %all-to-all-done.3.refs_2_ = bf16[4,1168,128]{2,1,0:T(8,128)(2,1)S(1)} async-done(((bf16[4,1168,128]{2,1,0:T(8,128)(2,1)}), bf16[4,1168,128]{2,1,0:T(8,128)(2,1)S(1)}, u32[]{:S(2)}, u32[]{:S(2)}) %all-to-all-start.3) | async-done | bytes 1196064 | tf_op jit(solution)/shard_map/all_to_all | solution.py:422
  114.4 1.2 image_finish.1.refs_0_
  115.6 0.0 collective-permute-done.8.refs_1_.refs_5_
  115.6 0.0 collective-permute-done.9.refs_2_.refs_6_
  115.6 4.3 %collective-permute-done.10.refs_3_.refs_7_ = bf16[128,1152]{1,0:T(8,128)(2,1)S(1)} collective-permute-done((bf16[128,1152]{1,0:T(8,128)(2,1)S(1)}, bf16[128,1152]{1,0:T(8,128)(2,1)S(1)}, u32[]{:S(2)}, u32[]{:S(2)}) %collective-permute-start.10) | collective-permute-done | bytes 294944 | tf_op jit(solution)/shard_map/ppermute | solution.py:346
  119.9 11.5 %all-to-all-start.4 = ((bf16[16,88,128]{2,1,0:T(8,128)(2,1)}), bf16[16,88,128]{2,1,0:T(8,128)(2,1)S(1)}, u32[]{:S(2)}, u32[]{:S(2)}) async-start(bf16[16,88,128]{2,1,0:T(8,128)(2,1)} %hold.3), calls=%async_computation.4 | async-start | bytes 720896 | tf_op jit(solution)/shard_map/all_to_all | solution.py:433
  131.3 0.7 text_finish.1
  132.0 5.6 %collective-permute-start.11 = (bf16[288,128]{1,0:T(8,128)(2,1)S(1)}, bf16[288,128]{1,0:T(8,128)(2,1)S(1)}, u32[]{:S(2)}, u32[]{:S(2)}) collective-permute-start(bf16[288,128]{1,0:T(8,128)(2,1)S(1)} %get-tuple-element.40), channel_id=1, source_target_pairs={{0,3},{1,0},{2,1},{3,2},{4,7},{5,4},{6,5},{7,6},{8,11},{9,8},{10,9... | collective-permute-start | bytes 221192 | tf_op jit(solution)/shard_map/ppermute | solution.py:346
  137.6 1.9 %collective-permute-start.12 = (bf16[288,128]{1,0:T(8,128)(2,1)S(1)}, bf16[288,128]{1,0:T(8,128)(2,1)S(1)}, u32[]{:S(2)}, u32[]{:S(2)}) collective-permute-start(bf16[288,128]{1,0:T(8,128)(2,1)S(1)} %get-tuple-element.41), channel_id=1, source_target_pairs={{0,2},{1,3},{2,0},{3,1},{4,6},{5,7},{6,4},{7,5},{8,10},{9,11},{10,... | collective-permute-start | bytes 221192 | tf_op jit(solution)/shard_map/ppermute | solution.py:346
  139.6 3.0 %collective-permute-start.13 = (bf16[288,128]{1,0:T(8,128)(2,1)S(1)}, bf16[288,128]{1,0:T(8,128)(2,1)S(1)}, u32[]{:S(2)}, u32[]{:S(2)}) collective-permute-start(bf16[288,128]{1,0:T(8,128)(2,1)S(1)} %get-tuple-element.42), channel_id=1, source_target_pairs={{0,1},{1,2},{2,3},{3,0},{4,5},{5,6},{6,7},{7,4},{8,9},{9,10},{10,1... | collective-permute-start | bytes 221192 | tf_op jit(solution)/shard_map/ppermute | solution.py:346
  142.6 8.3 %collective-permute-done.11.refs_1_ = bf16[288,128]{1,0:T(8,128)(2,1)S(1)} collective-permute-done((bf16[288,128]{1,0:T(8,128)(2,1)S(1)}, bf16[288,128]{1,0:T(8,128)(2,1)S(1)}, u32[]{:S(2)}, u32[]{:S(2)}) %collective-permute-start.11) | collective-permute-done | bytes 73760 | tf_op jit(solution)/shard_map/ppermute | solution.py:346
  150.9 5.6 %collective-permute-done.12.refs_2_ = bf16[288,128]{1,0:T(8,128)(2,1)S(1)} collective-permute-done((bf16[288,128]{1,0:T(8,128)(2,1)S(1)}, bf16[288,128]{1,0:T(8,128)(2,1)S(1)}, u32[]{:S(2)}, u32[]{:S(2)}) %collective-permute-start.12) | collective-permute-done | bytes 73760 | tf_op jit(solution)/shard_map/ppermute | solution.py:346
  156.4 0.7 text_last.1
  157.1 0.8 image_last.1
  157.9 0.5 fusion
  (9 shorter events, 0.0 us)
Async XLA Ops:
  0.6 29.9 %copy-start = (bf16[128,288]{0,1:T(8,128)(2,1)S(1)}, bf16[128,288]{0,1:T(8,128)(2,1)}, u32[]{:S(2)}) copy-start(bf16[128,288]{0,1:T(8,128)(2,1)} %param.5) | copy-start | bytes 221188
  0.6 13.0 %collective-permute-start.2 = (bf16[288,128]{1,0:T(8,128)(2,1)}, bf16[288,128]{1,0:T(8,128)(2,1)S(1)}, u32[]{:S(2)}, u32[]{:S(2)}) collective-permute-start(bf16[288,128]{1,0:T(8,128)(2,1)} %bitcast.18), channel_id=1, source_target_pairs={{0,3},{1,0},{2,1},{3,2},{4,7},{5,4},{6,5},{7,6},{8,11},{9,8},{10,9... | collective-permute-start | bytes 221192 | tf_op jit(solution)/shard_map/ppermute | solution.py:346
  7.3 7.4 %collective-permute-start.1 = (bf16[288,128]{1,0:T(8,128)(2,1)}, bf16[288,128]{1,0:T(8,128)(2,1)S(1)}, u32[]{:S(2)}, u32[]{:S(2)}) collective-permute-start(bf16[288,128]{1,0:T(8,128)(2,1)} %bitcast.19), channel_id=1, source_target_pairs={{0,2},{1,3},{2,0},{3,1},{4,6},{5,7},{6,4},{7,5},{8,10},{9,11},{10,... | collective-permute-start | bytes 221192 | tf_op jit(solution)/shard_map/ppermute | solution.py:346
  9.2 8.3 %collective-permute-start = (bf16[288,128]{1,0:T(8,128)(2,1)}, bf16[288,128]{1,0:T(8,128)(2,1)S(1)}, u32[]{:S(2)}, u32[]{:S(2)}) collective-permute-start(bf16[288,128]{1,0:T(8,128)(2,1)} %bitcast.20), channel_id=1, source_target_pairs={{0,1},{1,2},{2,3},{3,0},{4,5},{5,6},{6,7},{7,4},{8,9},{9,10},{10,1... | collective-permute-start | bytes 221192 | tf_op jit(solution)/shard_map/ppermute | solution.py:346
  11.8 0.9 copy-start.1
  17.5 34.6 %all-to-all-start = ((bf16[16,72,128]{2,1,0:T(8,128)(2,1)}), bf16[16,72,128]{2,1,0:T(8,128)(2,1)S(1)}, u32[]{:S(2)}, u32[]{:S(2)}) async-start(bf16[16,72,128]{2,1,0:T(8,128)(2,1)} %hold.2), calls=%async_computation | async-start | bytes 589824 | tf_op jit(solution)/shard_map/all_to_all | solution.py:365
  30.9 15.5 %collective-permute-start.5 = (bf16[128,1152]{1,0:T(8,128)(2,1)S(1)}, bf16[128,1152]{1,0:T(8,128)(2,1)S(1)}, u32[]{:S(2)}, u32[]{:S(2)}) collective-permute-start(bf16[128,1152]{1,0:T(8,128)(2,1)S(1)} %text_unit.1.refs_3_), channel_id=1, source_target_pairs={{0,24},{8,0},{16,8},{24,16},{1,25},{9,1},{17,9},{25,17},{2,26},{10... | collective-permute-start | bytes 884744 | tf_op jit(solution)/shard_map/ppermute | solution.py:346
  35.9 13.1 %collective-permute-start.4 = (bf16[128,1152]{1,0:T(8,128)(2,1)S(1)}, bf16[128,1152]{1,0:T(8,128)(2,1)S(1)}, u32[]{:S(2)}, u32[]{:S(2)}) collective-permute-start(bf16[128,1152]{1,0:T(8,128)(2,1)S(1)} %text_unit.1.refs_3_), channel_id=1, source_target_pairs={{0,16},{8,24},{16,0},{24,8},{1,17},{9,25},{17,1},{25,9},{2,18},{10... | collective-permute-start | bytes 884744 | tf_op jit(solution)/shard_map/ppermute | solution.py:346
  38.4 13.7 %collective-permute-start.3 = (bf16[128,1152]{1,0:T(8,128)(2,1)S(1)}, bf16[128,1152]{1,0:T(8,128)(2,1)S(1)}, u32[]{:S(2)}, u32[]{:S(2)}) collective-permute-start(bf16[128,1152]{1,0:T(8,128)(2,1)S(1)} %text_unit.1.refs_3_), channel_id=1, source_target_pairs={{0,8},{8,16},{16,24},{24,0},{1,9},{9,17},{17,25},{25,1},{2,10},{10... | collective-permute-start | bytes 884744 | tf_op jit(solution)/shard_map/ppermute | solution.py:346
  53.4 18.7 %all-to-all-start.1 = ((bf16[4,128,1152]{2,1,0:T(8,128)(2,1)}), bf16[4,128,1152]{2,1,0:T(8,128)(2,1)S(1)}, u32[]{:S(2)}, u32[]{:S(2)}) async-start(bf16[4,128,1152]{2,1,0:T(8,128)(2,1)} %image_unit.1), calls=%async_computation.1 | async-start | bytes 2359296 | tf_op jit(solution)/shard_map/all_to_all | solution.py:376
  72.1 5.6 %collective-permute-start.6 = (bf16[512,1152]{1,0:T(8,128)(2,1)S(1)}, bf16[512,1152]{1,0:T(8,128)(2,1)S(1)}, u32[]{:S(2)}, u32[]{:S(2)}) collective-permute-start(bf16[512,1152]{1,0:T(8,128)(2,1)S(1)} %bitcast.14), channel_id=1, source_target_pairs={{0,4},{4,0},{1,5},{5,1},{2,6},{6,2},{3,7},{7,3},{8,12},{12,8},{9,1... | collective-permute-start | bytes 3538952 | tf_op jit(solution)/shard_map/ppermute | solution.py:341
  82.4 10.2 %collective-permute-start.7 = (bf16[512,1152]{1,0:T(8,128)(2,1)S(1)}, bf16[512,1152]{1,0:T(8,128)(2,1)S(1)}, u32[]{:S(2)}, u32[]{:S(2)}) collective-permute-start(bf16[512,1152]{1,0:T(8,128)(2,1)S(1)} %get-tuple-element.31), channel_id=1, source_target_pairs={{0,4},{4,0},{1,5},{5,1},{2,6},{6,2},{3,7},{7,3},{8,12},{12,8},{9,1... | collective-permute-start | bytes 3538952 | tf_op jit(solution)/shard_map/ppermute | solution.py:341
  94.0 20.4 %all-to-all-start.3 = ((bf16[4,1168,128]{2,1,0:T(8,128)(2,1)}), bf16[4,1168,128]{2,1,0:T(8,128)(2,1)S(1)}, u32[]{:S(2)}, u32[]{:S(2)}) async-start(bf16[4,1168,128]{2,1,0:T(8,128)(2,1)} %combine.1), calls=%async_computation.3 | async-start | bytes 2392064 | tf_op jit(solution)/shard_map/all_to_all | solution.py:422
  98.9 16.7 %collective-permute-start.8 = (bf16[128,1152]{1,0:T(8,128)(2,1)}, bf16[128,1152]{1,0:T(8,128)(2,1)S(1)}, u32[]{:S(2)}, u32[]{:S(2)}) collective-permute-start(bf16[128,1152]{1,0:T(8,128)(2,1)} %get-tuple-element.33), channel_id=1, source_target_pairs={{0,24},{8,0},{16,8},{24,16},{1,25},{9,1},{17,9},{25,17},{2,26},{10... | collective-permute-start | bytes 884744 | tf_op jit(solution)/shard_map/ppermute | solution.py:346
  102.0 13.6 %collective-permute-start.9 = (bf16[128,1152]{1,0:T(8,128)(2,1)S(1)}, bf16[128,1152]{1,0:T(8,128)(2,1)S(1)}, u32[]{:S(2)}, u32[]{:S(2)}) collective-permute-start(bf16[128,1152]{1,0:T(8,128)(2,1)S(1)} %get-tuple-element.34), channel_id=1, source_target_pairs={{0,16},{8,24},{16,0},{24,8},{1,17},{9,25},{17,1},{25,9},{2,18},{10... | collective-permute-start | bytes 884744 | tf_op jit(solution)/shard_map/ppermute | solution.py:346
  105.4 14.5 %collective-permute-start.10 = (bf16[128,1152]{1,0:T(8,128)(2,1)S(1)}, bf16[128,1152]{1,0:T(8,128)(2,1)S(1)}, u32[]{:S(2)}, u32[]{:S(2)}) collective-permute-start(bf16[128,1152]{1,0:T(8,128)(2,1)S(1)} %get-tuple-element.35), channel_id=1, source_target_pairs={{0,8},{8,16},{16,24},{24,0},{1,9},{9,17},{17,25},{25,1},{2,10},{10... | collective-permute-start | bytes 884744 | tf_op jit(solution)/shard_map/ppermute | solution.py:346
  119.9 37.3 %all-to-all-start.4 = ((bf16[16,88,128]{2,1,0:T(8,128)(2,1)}), bf16[16,88,128]{2,1,0:T(8,128)(2,1)S(1)}, u32[]{:S(2)}, u32[]{:S(2)}) async-start(bf16[16,88,128]{2,1,0:T(8,128)(2,1)} %hold.3), calls=%async_computation.4 | async-start | bytes 720896 | tf_op jit(solution)/shard_map/all_to_all | solution.py:433
  132.0 18.9 %collective-permute-start.11 = (bf16[288,128]{1,0:T(8,128)(2,1)S(1)}, bf16[288,128]{1,0:T(8,128)(2,1)S(1)}, u32[]{:S(2)}, u32[]{:S(2)}) collective-permute-start(bf16[288,128]{1,0:T(8,128)(2,1)S(1)} %get-tuple-element.40), channel_id=1, source_target_pairs={{0,3},{1,0},{2,1},{3,2},{4,7},{5,4},{6,5},{7,6},{8,11},{9,8},{10,9... | collective-permute-start | bytes 221192 | tf_op jit(solution)/shard_map/ppermute | solution.py:346
  137.6 18.8 %collective-permute-start.12 = (bf16[288,128]{1,0:T(8,128)(2,1)S(1)}, bf16[288,128]{1,0:T(8,128)(2,1)S(1)}, u32[]{:S(2)}, u32[]{:S(2)}) collective-permute-start(bf16[288,128]{1,0:T(8,128)(2,1)S(1)} %get-tuple-element.41), channel_id=1, source_target_pairs={{0,2},{1,3},{2,0},{3,1},{4,6},{5,7},{6,4},{7,5},{8,10},{9,11},{10,... | collective-permute-start | bytes 221192 | tf_op jit(solution)/shard_map/ppermute | solution.py:346
  139.6 16.9 %collective-permute-start.13 = (bf16[288,128]{1,0:T(8,128)(2,1)S(1)}, bf16[288,128]{1,0:T(8,128)(2,1)S(1)}, u32[]{:S(2)}, u32[]{:S(2)}) collective-permute-start(bf16[288,128]{1,0:T(8,128)(2,1)S(1)} %get-tuple-element.42), channel_id=1, source_target_pairs={{0,1},{1,2},{2,3},{3,0},{4,5},{5,6},{6,7},{7,4},{8,9},{9,10},{10,1... | collective-permute-start | bytes 221192 | tf_op jit(solution)/shard_map/ppermute | solution.py:346

commit v7 on v5

v7 whole, which is shorter than its diff:
```python
import functools

import jax
import jax.numpy as jnp
from jax import lax
from jax.experimental import pallas as pl
from jax.experimental.pallas import tpu as pltpu
from jax.sharding import Mesh, PartitionSpec as P

epsilon = 1e-06
lanes = 128
piece = 32
strips = 4
rest = 32
chunk_rows = 72
carry_rows = 16
in_rows = 368
out_rows = 384
tiles = 9
vmem = pl.BlockSpec(memory_space=pltpu.VMEM)
smem = pl.BlockSpec(memory_space=pltpu.SMEM)
anywhere = pl.BlockSpec(memory_space=pl.ANY)
limits = pltpu.CompilerParams(vmem_limit_bytes=24 * 1024 * 1024)


def shape(dims, dtype=jnp.bfloat16):
    return jax.ShapeDtypeStruct(tuple(dims), dtype)


def call(kernel, out_shape, name, operands, scalars=(), after=(), flops=0, special=0, scratch=()):
    out_shape = tuple(out_shape)
    scalars, operands, after = tuple(scalars), tuple(operands), tuple(after)
    inputs = len(scalars) + len(operands)
    moved = sum(a.size * a.dtype.itemsize for a in operands + out_shape)

    def body(*refs):
        kernel(*refs[:inputs], *refs[inputs + len(after) :])

    return pl.pallas_call(
        body,
        out_shape=out_shape,
        in_specs=[smem] * len(scalars) + [vmem] * len(operands) + [anywhere] * len(after),
        out_specs=(vmem,) * len(out_shape),
        scratch_shapes=list(scratch),
        compiler_params=limits,
        cost_estimate=pl.CostEstimate(flops=flops, bytes_accessed=moved, transcendentals=special),
        name=name,
    )(*scalars, *operands, *after)


def total(values):
    return functools.reduce(lambda a, b: a + b, values)


def wide(ref, *index):
    return ref[index].astype(jnp.float32)


def lane_group():
    return lax.broadcasted_iota(jnp.int32, (8, lanes), 1) // rest


def pack_kernel(image, text, out):
    chunks = []
    for ref in (image, text):
        found = []
        whole = wide(ref, slice(None)).T
        for k in range(4):
            rows = whole[k * piece : (k + 1) * piece]
            last = rows[:, 2 * lanes :]
            last = jnp.concatenate([last[8 * g : 8 * g + 8] for g in range(4)], axis=1)
            found.append(jnp.concatenate([rows[:, :lanes], rows[:, lanes : 2 * lanes], last], axis=0))
        chunks.append(found)
    spare = jnp.zeros((in_rows - 5 * chunk_rows, lanes), jnp.float32)
    for d in range(strips):
        parts = [chunks[0][d]] + chunks[1] + [spare]
        out[d] = jnp.concatenate(parts, axis=0).astype(jnp.bfloat16)


def unpack_rows(chunks, group):
    found = []
    lasts = []
    for chunk in chunks:
        found += [chunk[:piece], chunk[piece : 2 * piece]]
        lasts.append(chunk[2 * piece :])
    last = []
    for g in range(4):
        value = jnp.zeros((8, lanes), jnp.float32)
        for s in range(strips):
            turn = rest * (s - g) % lanes
            moved = pltpu.roll(lasts[s], turn, 1) if turn else lasts[s]
            value = jnp.where(group == s, moved, value)
        last.append(value)
    found.append(jnp.concatenate(last, axis=0))
    return found


def unit_tiles(arrived, c, group):
    chunks = [arrived[s][c * chunk_rows : (c + 1) * chunk_rows] for s in range(strips)]
    found = unpack_rows(chunks, group)
    inverse = lax.rsqrt(jnp.sum(total([t * t for t in found]), axis=1, keepdims=True) + epsilon)
    return [t * inverse for t in found], inverse


def unit_kernel(arrived, image, text):
    group = lane_group()
    values = [wide(arrived, s) for s in range(strips)]
    for c in range(5):
        units, _ = unit_tiles(values, c, group)
        for t in range(tiles):
            columns = pl.ds(t * lanes, lanes)
            if c == 0:
                image[:, columns] = units[t].astype(jnp.bfloat16)
            else:
                text[(c - 1) * piece : c * piece, columns] = units[t].astype(jnp.bfloat16)


def join_image_kernel(own, near, out):
    for k in range(out.shape[0]):
        out[k, :piece, :] = own[...]
        out[k, piece:, :] = near[...]


def join_text_kernel(own, near, out):
    rows = own.shape[0]
    out[:rows, :] = own[...]
    out[rows:, :] = near[...]


def fold(values):
    rows, columns = values.shape
    part = jnp.sum(values.reshape(rows // 8, 8, columns), axis=0)
    return total([part[:, c : c + lanes] for c in range(0, columns, lanes)])


tile = 256


def pair_kernel(scales, spot, left, first, second, out, weights_out, right):
    scale = scales[0]
    bias = scales[1]
    count, block, _ = left.shape
    part = first.shape[0]
    right[:part, :] = first[...]
    right[part:, :] = second[...]
    per_tile = tile // block
    sums = [jnp.zeros((8, lanes), jnp.float32) for _ in range(3)]
    for start in range(0, count, per_tile):
        rows = jnp.concatenate([left[start + k] for k in range(per_tile)], axis=0)
        product = lax.dot_general(
            rows, right[...], (((1,), (1,)), ((), ())), preferred_element_type=jnp.float32
        )
        logits = scale * product + bias
        row = lax.broadcasted_iota(jnp.int32, (tile, 1), 0) + (start * block - spot[0])
        row = jnp.where((row >= 0) & (row < piece), row, -1)
        column = lax.broadcasted_iota(jnp.int32, (1, lanes), 1) - spot[1]
        same = row == jnp.where(column >= 0, column, -2)
        home = logits[:, :lanes]
        grown = jnp.exp(jnp.concatenate([jnp.where(same, -home, home), logits[:, lanes:]], axis=1))
        slope = grown / (1.0 + grown)
        home = slope[:, :lanes]
        slope = jnp.concatenate([jnp.where(same, -home, home), slope[:, lanes:]], axis=1)
        weights = (scale * slope).astype(jnp.bfloat16)
        weights_out[start * block : start * block + tile, :] = weights
        back = jnp.dot(weights, right[...], preferred_element_type=jnp.float32)
        for k in range(per_tile):
            for t in range(tiles):
                out[start + k, t * block : (t + 1) * block, :] = back[
                    k * block : (k + 1) * block, t * lanes : (t + 1) * lanes
                ].astype(jnp.bfloat16)
        quarter = tile // 4
        a, b, c, d = (grown[k * quarter : (k + 1) * quarter, :] for k in range(4))
        ab = a + (b + a * b)
        cd = c + (d + c * d)
        sums[0] += fold(jnp.log1p(ab + (cd + ab * cd)))
        sums[1] += fold(slope * product)
        sums[2] += fold(slope)
    row = lax.broadcasted_iota(jnp.int32, (8, lanes), 0)
    value = jnp.zeros((8, lanes), jnp.float32)
    for k in range(3):
        value = jnp.where(row == k, jnp.sum(sums[k], axis=0, keepdims=True), value)
    carry = carry_of(value).astype(jnp.bfloat16)
    for k in range(count):
        out[k, tiles * block :, :] = carry


def text_kernel(weights, left, own, other):
    count, block, width = left.shape
    part = own.shape[0]
    contract = (((0,), (0,)), ((), ()))
    value = lax.dot_general(
        weights[...], left[...].reshape(count * block, width), contract,
        preferred_element_type=jnp.float32,
    )
    own[...] = value[:part]
    other[...] = value[part:].astype(jnp.bfloat16)


def text_sum_kernel(own, given, kept, sent):
    rows = kept.shape[0]
    kept[...] = own[:rows, :] + wide(given, pl.ds(0, rows), slice(None))
    value = own[rows:, :] + wide(given, pl.ds(rows, rows), slice(None))
    sent[...] = value.astype(jnp.bfloat16)


def three_parts(value):
    high = value.astype(jnp.bfloat16).astype(jnp.float32)
    middle = (value - high).astype(jnp.bfloat16).astype(jnp.float32)
    return high, middle, value - high - middle


def carry_of(value):
    parts = three_parts(jnp.sum(value, axis=1, keepdims=True))
    lane = lax.broadcasted_iota(jnp.int32, (8, lanes), 1)
    carry = jnp.zeros((8, lanes), jnp.float32)
    for k in range(3):
        carry = jnp.where(lane == k, parts[k], carry)
    return jnp.concatenate([carry, jnp.zeros((8, lanes), jnp.float32)], axis=0)


def pack_grads(units, inverse, grads, group):
    along = jnp.sum(total([u * g for u, g in zip(units, grads)]), axis=1, keepdims=True)
    final = [(g - u * along) * inverse for u, g in zip(units, grads)]
    chunks = []
    for s in range(strips):
        last = jnp.zeros((8, lanes), jnp.float32)
        for g in range(4):
            turn = rest * (g - s) % lanes
            rows = final[tiles - 1][8 * g : 8 * g + 8]
            moved = pltpu.roll(rows, turn, 1) if turn else rows
            last = jnp.where(group == g, moved, last)
        chunks.append(jnp.concatenate([final[2 * s], final[2 * s + 1], last], axis=0))
    return chunks


def image_sum_kernel(backs, kept, sent):
    count = backs.shape[0]
    block = 2 * piece
    for t in range(tiles):
        rows = total([wide(backs, k, pl.ds(t * block, block), slice(None)) for k in range(count)])
        kept[t * piece : (t + 1) * piece, :] = rows[:piece]
        sent[t * piece : (t + 1) * piece, :] = rows[piece:].astype(jnp.bfloat16)
    tail = pl.ds(tiles * block, carry_rows)
    carry = carry_of(total([wide(backs, k, tail, slice(None)) for k in range(count)])[:8])
    kept[tiles * piece :, :] = carry
    sent[tiles * piece :, :] = carry.astype(jnp.bfloat16)


def finish_kernel(arrived, image_kept, image_given, text_kept, text_given, near, far, out):
    group = lane_group()
    values = [wide(arrived, s) for s in range(strips)]
    tail = pl.ds(tiles * piece, carry_rows)
    carried = image_kept[tail, :] + wide(image_given, tail, slice(None))
    carry = carry_of((carried + wide(near, slice(None)) + wide(far, slice(None)))[:8])
    spare = jnp.zeros((out_rows - 5 * chunk_rows - carry_rows, lanes), jnp.float32)
    chunks = [[] for _ in range(strips)]
    for c in range(5):
        units, inverse = unit_tiles(values, c, group)
        grads = []
        for t in range(tiles):
            if c == 0:
                rows = pl.ds(t * piece, piece)
                grads.append(image_kept[rows, :] + wide(image_given, rows, slice(None)))
            else:
                rows, columns = pl.ds((c - 1) * piece, piece), pl.ds(t * lanes, lanes)
                grads.append(text_kept[rows, columns] + wide(text_given, rows, columns))
        for s, chunk in enumerate(pack_grads(units, inverse, grads, group)):
            chunks[s].append(chunk)
    for s in range(strips):
        out[s] = jnp.concatenate([carry] + chunks[s] + [spare], axis=0).astype(jnp.bfloat16)


def last_kernel(arrived, image, text, sums_out):
    values = [wide(arrived, s) for s in range(strips)]
    for which, out in enumerate((image, text)):
        found = []
        for k in range(4):
            if which:
                first = carry_rows + (1 + k) * chunk_rows
                chunk = total([v[first : first + chunk_rows] for v in values])
            else:
                chunk = values[k][carry_rows : carry_rows + chunk_rows]
            last = chunk[2 * piece :]
            groups = [last] + [pltpu.roll(last, lanes - rest * g, 1) for g in range(1, 4)]
            last = jnp.concatenate(groups, axis=0)
            found.append((chunk[:piece], chunk[piece : 2 * piece], last))
        for t in range(3):
            rows = jnp.concatenate([f[t] for f in found], axis=0).T
            size = lanes if t < 2 else rest
            out[t * lanes : t * lanes + size, :] = rows[:size].astype(jnp.bfloat16)
    sums = jnp.sum(total([v[:8] for v in values]), axis=1, keepdims=True)
    sums_out[...] = jnp.broadcast_to(sums, sums_out.shape)


def swap_core(value):
    return lax.ppermute(value, "core", [(0, 1), (1, 0)])


def shift(value, axis, k):
    count = lax.axis_size(axis)
    return lax.ppermute(value, axis, [(i, (i + k) % count) for i in range(count)])


def swap_image(value):
    return lax.ppermute(value, "zh", [(0, 3), (3, 0), (1, 2), (2, 1)])


def swap_text(value):
    return lax.ppermute(value, "zh", [(0, 1), (1, 0), (2, 3), (3, 2)])


def shards(image, text, log_temp, bias):
    rows, strip = image.shape
    x_count, y_count, zh_count = (lax.axis_size(name) for name in ("x", "y", "zh"))
    width = strip * strips
    block = 2 * piece
    blocks = x_count * y_count
    count = blocks * block
    columns = 4 * rows
    area = count * columns
    x, y, zl = (lax.axis_index(name).astype(jnp.int32) for name in ("x", "y", "zl"))
    scale = jnp.exp(log_temp)
    scales = jnp.stack([scale, bias])
    spot = jnp.stack([(x * y_count + y) * block, zl * piece])
    f32 = jnp.float32

    (packed,) = call(pack_kernel, [shape((strips, in_rows, lanes))], "pack", [image.T, text.T])
    arrived = lax.all_to_all(packed, "zl", 0, 0)
    image_own, text_own = call(
        unit_kernel, [shape((piece, width)), shape((rows, width))], "unit", [arrived]
    )
    image_near = swap_image(image_own)
    text_near = swap_text(text_own)
    (joined,) = call(
        join_image_kernel, [shape((blocks, block, width))], "join_image", [image_own, image_near]
    )
    image_rows = lax.all_to_all(joined, ("x", "y"), 0, 0)
    (text_rows,) = call(
        join_text_kernel, [shape((2 * rows, width))], "join_text", [text_own, text_near]
    )
    text_other = swap_core(text_rows)

    back, weights = call(
        pair_kernel,
        [shape((blocks, tiles * block + carry_rows, lanes)), shape((count, columns))],
        "pair",
        [image_rows, text_rows, text_other],
        scalars=[scales, spot],
        flops=4 * area * width,
        special=2 * area,
        scratch=[pltpu.VMEM((columns, width), jnp.bfloat16)],
    )
    back = lax.all_to_all(back, ("x", "y"), 0, 0)
    text_kept, text_sent = call(
        text_kernel,
        [shape((2 * rows, width), f32), shape((2 * rows, width))],
        "text_back",
        [weights, image_rows],
        flops=2 * area * width,
    )
    text_given = swap_core(text_sent)
    text_kept, text_sent = call(
        text_sum_kernel,
        [shape((rows, width), f32), shape((rows, width))],
        "text_sum",
        [text_kept, text_given],
    )
    text_given = swap_text(text_sent)
    sums_rows = tiles * piece + carry_rows
    image_kept, image_sent = call(
        image_sum_kernel,
        [shape((sums_rows, lanes), f32), shape((sums_rows, lanes))],
        "image_sum",
        [back],
    )
    image_given = swap_image(image_sent)
    carry = image_sent[tiles * piece :]
    near = swap_text(carry)
    far = shift(carry, "zh", 2)
    (finished,) = call(
        finish_kernel,
        [shape((strips, out_rows, lanes))],
        "finish",
        [arrived, image_kept, image_given, text_kept, text_given, near, far],
    )
    finished = lax.all_to_all(finished, "zl", 0, 0)
    grad_image, grad_text, sums = call(
        last_kernel, [shape((strip, rows))] * 2 + [shape((8, lanes), f32)], "last", [finished]
    )
    sums = (sums + swap_core(sums))[:, 0]
    pairs_count = rows * zh_count * blocks * 2
    return (
        sums[0] / pairs_count,
        grad_image.T,
        grad_text.T,
        scale * sums[1] / pairs_count,
        sums[2] / pairs_count,
    )


def solution(mesh):
    fine = Mesh(mesh.devices.reshape(4, 4, 4, 2, 4), ("zh", "x", "y", "core", "zl"))
    whole = P(("zh", "x", "y", "core"), "zl")
    return jax.shard_map(
        shards,
        mesh=fine,
        in_specs=(whole, whole, P(), P()),
        out_specs=(P(), whole, whole, P(), P()),
        check_vma=False,
    )
```

time: 167 us -> 175 us (1.048)
  the two profiles are of different devices: /device:TPU:4 before, /device:TPU:1 now
where the time goes in v7:
time: 175 us; the launch traced here: 174 us
  starting transfers between devices  62.5 us (36%)
  waiting for transfers between devices  56.1 us (32%)
  blocking collectives  26.1 us (15%)
  Pallas kernels  12.6 us (7%)
  local copies, waits for them, and re-layouts  8.66 us (5%)
  between operations  7.55 us (4%)
    ppermute x3, waiting for transfers between devices, swap_text(): return lax.ppermute(value, 'zh', [(0, 1), (1, 0), (2, 3), (3, 2)])  28.9 us
    all_to_all x1, waiting for transfers between devices, shards(): back = lax.all_to_all(back, ('x', 'y'), 0, 0)  21.2 us
    ppermute x2, starting transfers between devices, swap_image(): return lax.ppermute(value, 'zh', [(0, 3), (3, 0), (1, 2), (2, 1)])  16.6 us
    all_to_all x1, blocking collectives, shards(): arrived = lax.all_to_all(packed, 'zl', 0, 0)  14 us
    ppermute x3, starting transfers between devices, swap_text(): return lax.ppermute(value, 'zh', [(0, 1), (1, 0), (2, 3), (3, 2)])  12.7 us
    pallas_call x10, Pallas kernels, call(): pl.pallas_call(body, out_shape=out_shape, in_specs=[smem] * len(scalars)...  12.6 us
    all_to_all x1, blocking collectives, shards(): finished = lax.all_to_all(finished, 'zl', 0, 0)  12.1 us
    ppermute x3, starting transfers between devices, swap_core(): return lax.ppermute(value, 'core', [(0, 1), (1, 0)])  12.1 us
  transfers between devices with their start and end apart: 11, of which 8 were waited for; matrix products, arithmetic and copies ran while one was open for 0% of the time, Pallas kernels for 2%

profile of v7, /device:TPU:1, one launch (start us, length us, event | category | flops | bytes accessed | tf_op | source)
XLA Modules:
  0.0 173.7 jit_solution(13888811420102727568)
XLA Ops:
  0.6 0.0 copy-start.5
  0.6 0.9 copy-done.5
  1.5 0.9 copy-done.6
  2.4 0.2 pack.1
  2.6 14.0 %all_to_all.20.refs_0_ = bf16[4,368,128]{2,1,0:T(8,128)(2,1)S(1)} all-to-all(bf16[4,368,128]{2,1,0:T(8,128)(2,1)S(1)} %pack.1), channel_id=1, replica_groups=mesh['zh'=4,'x'=4,'y'=4,'core'=2,'zl'=4] {'zl'}, dimensions={0} | all-to-all | bytes 753664 | tf_op jit(solution)/shard_map/all_to_all | solution.py:328
  16.6 0.3 unit.1
  16.9 0.0 copy-start.3
  16.9 12.2 %collective-permute-start = (bf16[32,1152]{1,0:T(8,128)(2,1)S(1)}, bf16[32,1152]{1,0:T(8,128)(2,1)S(1)}, u32[]{:S(2)}, u32[]{:S(2)}) collective-permute-start(bf16[32,1152]{1,0:T(8,128)(2,1)S(1)} %get-tuple-element.18.refs_0_), channel_id=1, source_target_pairs={{0,384},{384,0},{128,256},{256,128},{1,385},{385,1},{129,257},{257... | collective-permute-start | bytes 221192 | tf_op jit(solution)/shard_map/ppermute | solution.py:305
  29.1 2.1 %collective-permute-done.refs_1_ = bf16[32,1152]{1,0:T(8,128)(2,1)S(1)} collective-permute-done((bf16[32,1152]{1,0:T(8,128)(2,1)S(1)}, bf16[32,1152]{1,0:T(8,128)(2,1)S(1)}, u32[]{:S(2)}, u32[]{:S(2)}) %collective-permute-start) | collective-permute-done | bytes 73760 | tf_op jit(solution)/shard_map/ppermute | solution.py:305
  31.2 1.6 join_image.1
  32.8 6.8 %all-to-all-start.1 = ((bf16[16,64,1152]{2,1,0:T(8,128)(2,1)}), bf16[16,64,1152]{2,1,0:T(8,128)(2,1)S(1)}, u32[]{:S(2)}, u32[]{:S(2)}) async-start(bf16[16,64,1152]{2,1,0:T(8,128)(2,1)} %join_image.1), calls=%async_computation.1 | async-start | bytes 4718592 | tf_op jit(solution)/shard_map/all_to_all | solution.py:337
  39.6 0.0 copy-done.3
  39.6 6.8 %collective-permute-start.1 = (bf16[128,1152]{1,0:T(8,128)(2,1)S(1)}, bf16[128,1152]{1,0:T(8,128)(2,1)S(1)}, u32[]{:S(2)}, u32[]{:S(2)}) collective-permute-start(bf16[128,1152]{1,0:T(8,128)(2,1)S(1)} %get-tuple-element.19.refs_0_), channel_id=1, source_target_pairs={{0,128},{128,0},{256,384},{384,256},{1,129},{129,1},{257,385},{385... | collective-permute-start | bytes 884744 | tf_op jit(solution)/shard_map/ppermute | solution.py:309
  46.4 25.7 %collective-permute-done.1.refs_1_ = bf16[128,1152]{1,0:T(8,128)(2,1)S(1)} collective-permute-done((bf16[128,1152]{1,0:T(8,128)(2,1)S(1)}, bf16[128,1152]{1,0:T(8,128)(2,1)S(1)}, u32[]{:S(2)}, u32[]{:S(2)}) %collective-permute-start.1) | collective-permute-done | bytes 294944 | tf_op jit(solution)/shard_map/ppermute | solution.py:309
  72.0 1.0 copy-done.4
  73.0 2.4 %collective-permute-start.2 = (bf16[256,1152]{1,0:T(8,128)(2,1)S(1)}, bf16[256,1152]{1,0:T(8,128)(2,1)}, u32[]{:S(2)}, u32[]{:S(2)}) collective-permute-start(bf16[256,1152]{1,0:T(8,128)(2,1)S(1)} %join_text.1.refs_3_), channel_id=1, source_target_pairs={{0,4},{4,0},{1,5},{5,1},{2,6},{6,2},{3,7},{7,3},{8,12},{12,8},{9,1... | collective-permute-start | bytes 1769480 | tf_op jit(solution)/shard_map/ppermute | solution.py:296
  76.8 0.1 pad_add_fusion.refs_1_
  76.9 0.1 pad_maximum_fusion.refs_0_
  76.9 0.2 collective-permute-done.2.refs_4_
  77.2 0.0 all-to-all-done.1.refs_2_.refs_1_
  77.2 5.4 %pair.1 = (bf16[16,592,128]{2,1,0:T(8,128)(2,1)S(1)}, bf16[1024,512]{1,0:T(8,128)(2,1)S(1)}) custom-call(f32[2]{0:T(128)S(1)} %pad_maximum_fusion.refs_0_, s32[2]{0:T(128)S(1)} %pad_add_fusion.refs_1_, bf16[16,64,1152]{2,1,0:T(8,128)(2,1)S(1)} %all-to-all-done.1.refs_2_.refs_1_, bf16[256,1152]{1,0:T(8,128)(2,1)S(1)} %join_text.1.refs_3_, ...), custom_call_target="tpu_custom_call" | custom-call | flops 2415919104 | bytes 7012352 | tf_op jit(solution)/shard_map/pair/pallas_call | solution.py:39
  82.6 0.0 copy-done.1
  82.6 0.0 copy-start
  82.6 1.4 copy-done
  84.0 1.0 copy-done.7
  85.1 6.7 %all-to-all-start.2 = ((bf16[16,592,128]{2,1,0:T(8,128)(2,1)}), bf16[16,592,128]{2,1,0:T(8,128)(2,1)S(1)}, u32[]{:S(2)}, u32[]{:S(2)}) async-start(bf16[16,592,128]{2,1,0:T(8,128)(2,1)} %copy-done), calls=%async_computation.2 | async-start | bytes 4849664 | tf_op jit(solution)/shard_map/all_to_all | solution.py:353
  91.7 1.7 copy-done.2
  93.4 1.2 copy-done.8
  94.6 1.6 text_back.1
  96.2 2.6 %collective-permute-start.4 = (bf16[256,1152]{1,0:T(8,128)(2,1)S(1)}, bf16[256,1152]{1,0:T(8,128)(2,1)S(1)}, u32[]{:S(2)}, u32[]{:S(2)}) collective-permute-start(bf16[256,1152]{1,0:T(8,128)(2,1)S(1)} %get-tuple-element.25), channel_id=1, source_target_pairs={{0,4},{4,0},{1,5},{5,1},{2,6},{6,2},{3,7},{7,3},{8,12},{12,8},{9,1... | collective-permute-start | bytes 1769480 | tf_op jit(solution)/shard_map/ppermute | solution.py:296
  98.7 1.6 collective-permute-done.4.refs_1_
  100.3 0.8 text_sum.1
  101.2 1.9 %collective-permute-start.5 = (bf16[128,1152]{1,0:T(8,128)(2,1)}, bf16[128,1152]{1,0:T(8,128)(2,1)}, u32[]{:S(2)}, u32[]{:S(2)}) collective-permute-start(bf16[128,1152]{1,0:T(8,128)(2,1)} %get-tuple-element.27), channel_id=1, source_target_pairs={{0,128},{128,0},{256,384},{384,256},{1,129},{129,1},{257,385},{385... | collective-permute-start | bytes 884744 | tf_op jit(solution)/shard_map/ppermute | solution.py:309
  103.1 21.2 %all-to-all-done.2.refs_0_ = bf16[16,592,128]{2,1,0:T(8,128)(2,1)S(1)} async-done(((bf16[16,592,128]{2,1,0:T(8,128)(2,1)}), bf16[16,592,128]{2,1,0:T(8,128)(2,1)S(1)}, u32[]{:S(2)}, u32[]{:S(2)}) %all-to-all-start.2) | async-done | bytes 2424864 | tf_op jit(solution)/shard_map/all_to_all | solution.py:353
  124.3 0.4 image_sum.1
  124.8 4.4 %collective-permute-start.3 = (bf16[304,128]{1,0:T(8,128)(2,1)S(1)}, bf16[304,128]{1,0:T(8,128)(2,1)S(1)}, u32[]{:S(2)}, u32[]{:S(2)}) collective-permute-start(bf16[304,128]{1,0:T(8,128)(2,1)S(1)} %get-tuple-element.22), channel_id=1, source_target_pairs={{0,384},{384,0},{128,256},{256,128},{1,385},{385,1},{129,257},{257... | collective-permute-start | bytes 233480 | tf_op jit(solution)/shard_map/ppermute | solution.py:305
  129.2 7.7 %collective-permute-start.7 = (bf16[16,128]{1,0:T(8,128)(2,1)S(1)}, bf16[16,128]{1,0:T(8,128)(2,1)S(1)}, u32[]{:S(2)}, u32[]{:S(2)}) collective-permute-start(bf16[16,128]{1,0:T(8,128)(2,1)S(1)} %slice.19), channel_id=1, source_target_pairs={{0,256},{128,384},{256,0},{384,128},{1,257},{129,385},{257,1},{385... | collective-permute-start | bytes 12296 | tf_op jit(solution)/shard_map/ppermute | solution.py:301
  136.9 4.0 %collective-permute-start.6 = (bf16[16,128]{1,0:T(8,128)(2,1)S(1)}, bf16[16,128]{1,0:T(8,128)(2,1)S(1)}, u32[]{:S(2)}, u32[]{:S(2)}) collective-permute-start(bf16[16,128]{1,0:T(8,128)(2,1)S(1)} %slice.19), channel_id=1, source_target_pairs={{0,128},{128,0},{256,384},{384,256},{1,129},{129,1},{257,385},{385... | collective-permute-start | bytes 12296 | tf_op jit(solution)/shard_map/ppermute | solution.py:309
  141.0 0.0 collective-permute-done.5.refs_4_
  141.0 1.3 collective-permute-done.7.refs_6_
  142.2 3.2 %collective-permute-done.6.refs_5_ = bf16[16,128]{1,0:T(8,128)(2,1)S(1)} collective-permute-done((bf16[16,128]{1,0:T(8,128)(2,1)S(1)}, bf16[16,128]{1,0:T(8,128)(2,1)S(1)}, u32[]{:S(2)}, u32[]{:S(2)}) %collective-permute-start.6) | collective-permute-done | bytes 4128 | tf_op jit(solution)/shard_map/ppermute | solution.py:309
  145.5 0.0 collective-permute-done.3.refs_2_
  145.5 1.4 finish.1
  146.9 12.1 %all_to_all.21.refs_0_ = bf16[4,384,128]{2,1,0:T(8,128)(2,1)S(1)} all-to-all(bf16[4,384,128]{2,1,0:T(8,128)(2,1)S(1)} %finish.1), channel_id=1, replica_groups=mesh['zh'=4,'x'=4,'y'=4,'core'=2,'zl'=4] {'zl'}, dimensions={0} | all-to-all | bytes 786432 | tf_op jit(solution)/shard_map/all_to_all | solution.py:386
  159.0 0.8 last.1
  159.8 7.1 %collective-permute-start.8 = (f32[8,128]{1,0:T(8,128)S(1)}, f32[8,128]{1,0:T(8,128)S(1)}, u32[]{:S(2)}, u32[]{:S(2)}) collective-permute-start(f32[8,128]{1,0:T(8,128)S(1)} %get-tuple-element.28), channel_id=1, source_target_pairs={{0,4},{4,0},{1,5},{5,1},{2,6},{6,2},{3,7},{7,3},{8,12},{12,8},{9,1... | collective-permute-start | bytes 12296 | tf_op jit(solution)/shard_map/ppermute | solution.py:296
  166.9 0.8 collective-permute-done.8
  167.7 0.6 fusion
  (9 shorter events, 0.1 us)
Async XLA Ops:
  0.6 0.9 copy-start.5
  1.5 0.9 copy-start.6
  16.9 22.6 %copy-start.3 = (bf16[128,1152]{1,0:T(8,128)(2,1)}, bf16[128,1152]{1,0:T(8,128)(2,1)S(1)}, u32[]{:S(2)}) copy-start(bf16[128,1152]{1,0:T(8,128)(2,1)S(1)} %get-tuple-element.19.refs_0_) | copy-start | bytes 884740
  16.9 14.3 %collective-permute-start = (bf16[32,1152]{1,0:T(8,128)(2,1)S(1)}, bf16[32,1152]{1,0:T(8,128)(2,1)S(1)}, u32[]{:S(2)}, u32[]{:S(2)}) collective-permute-start(bf16[32,1152]{1,0:T(8,128)(2,1)S(1)} %get-tuple-element.18.refs_0_), channel_id=1, source_target_pairs={{0,384},{384,0},{128,256},{256,128},{1,385},{385,1},{129,257},{257... | collective-permute-start | bytes 221192 | tf_op jit(solution)/shard_map/ppermute | solution.py:305
  32.8 44.4 %all-to-all-start.1 = ((bf16[16,64,1152]{2,1,0:T(8,128)(2,1)}), bf16[16,64,1152]{2,1,0:T(8,128)(2,1)S(1)}, u32[]{:S(2)}, u32[]{:S(2)}) async-start(bf16[16,64,1152]{2,1,0:T(8,128)(2,1)} %join_image.1), calls=%async_computation.1 | async-start | bytes 4718592 | tf_op jit(solution)/shard_map/all_to_all | solution.py:337
  39.6 32.4 %collective-permute-start.1 = (bf16[128,1152]{1,0:T(8,128)(2,1)S(1)}, bf16[128,1152]{1,0:T(8,128)(2,1)S(1)}, u32[]{:S(2)}, u32[]{:S(2)}) collective-permute-start(bf16[128,1152]{1,0:T(8,128)(2,1)S(1)} %get-tuple-element.19.refs_0_), channel_id=1, source_target_pairs={{0,128},{128,0},{256,384},{384,256},{1,129},{129,1},{257,385},{385... | collective-permute-start | bytes 884744 | tf_op jit(solution)/shard_map/ppermute | solution.py:309
  72.0 1.0 copy-start.4
  73.0 4.2 %collective-permute-start.2 = (bf16[256,1152]{1,0:T(8,128)(2,1)S(1)}, bf16[256,1152]{1,0:T(8,128)(2,1)}, u32[]{:S(2)}, u32[]{:S(2)}) collective-permute-start(bf16[256,1152]{1,0:T(8,128)(2,1)S(1)} %join_text.1.refs_3_), channel_id=1, source_target_pairs={{0,4},{4,0},{1,5},{5,1},{2,6},{6,2},{3,7},{7,3},{8,12},{12,8},{9,1... | collective-permute-start | bytes 1769480 | tf_op jit(solution)/shard_map/ppermute | solution.py:296
  77.2 5.4 %copy-start.1 = (bf16[16,64,1152]{2,1,0:T(8,128)(2,1)}, bf16[16,64,1152]{2,1,0:T(8,128)(2,1)S(1)}, u32[]{:S(2)}) copy-start(bf16[16,64,1152]{2,1,0:T(8,128)(2,1)S(1)} %all-to-all-done.1.refs_2_.refs_1_) | copy-start | bytes 7077892
  82.6 1.4 copy-start
  84.0 1.0 copy-start.7
  85.1 39.3 %all-to-all-start.2 = ((bf16[16,592,128]{2,1,0:T(8,128)(2,1)}), bf16[16,592,128]{2,1,0:T(8,128)(2,1)S(1)}, u32[]{:S(2)}, u32[]{:S(2)}) async-start(bf16[16,592,128]{2,1,0:T(8,128)(2,1)} %copy-done), calls=%async_computation.2 | async-start | bytes 4849664 | tf_op jit(solution)/shard_map/all_to_all | solution.py:353
  91.7 1.7 copy-start.2
  93.4 1.2 copy-start.8
  96.2 4.2 %collective-permute-start.4 = (bf16[256,1152]{1,0:T(8,128)(2,1)S(1)}, bf16[256,1152]{1,0:T(8,128)(2,1)S(1)}, u32[]{:S(2)}, u32[]{:S(2)}) collective-permute-start(bf16[256,1152]{1,0:T(8,128)(2,1)S(1)} %get-tuple-element.25), channel_id=1, source_target_pairs={{0,4},{4,0},{1,5},{5,1},{2,6},{6,2},{3,7},{7,3},{8,12},{12,8},{9,1... | collective-permute-start | bytes 1769480 | tf_op jit(solution)/shard_map/ppermute | solution.py:296
  101.2 39.8 %collective-permute-start.5 = (bf16[128,1152]{1,0:T(8,128)(2,1)}, bf16[128,1152]{1,0:T(8,128)(2,1)}, u32[]{:S(2)}, u32[]{:S(2)}) collective-permute-start(bf16[128,1152]{1,0:T(8,128)(2,1)} %get-tuple-element.27), channel_id=1, source_target_pairs={{0,128},{128,0},{256,384},{384,256},{1,129},{129,1},{257,385},{385... | collective-permute-start | bytes 884744 | tf_op jit(solution)/shard_map/ppermute | solution.py:309
  124.8 20.7 %collective-permute-start.3 = (bf16[304,128]{1,0:T(8,128)(2,1)S(1)}, bf16[304,128]{1,0:T(8,128)(2,1)S(1)}, u32[]{:S(2)}, u32[]{:S(2)}) collective-permute-start(bf16[304,128]{1,0:T(8,128)(2,1)S(1)} %get-tuple-element.22), channel_id=1, source_target_pairs={{0,384},{384,0},{128,256},{256,128},{1,385},{385,1},{129,257},{257... | collective-permute-start | bytes 233480 | tf_op jit(solution)/shard_map/ppermute | solution.py:305
  129.2 13.1 %collective-permute-start.7 = (bf16[16,128]{1,0:T(8,128)(2,1)S(1)}, bf16[16,128]{1,0:T(8,128)(2,1)S(1)}, u32[]{:S(2)}, u32[]{:S(2)}) collective-permute-start(bf16[16,128]{1,0:T(8,128)(2,1)S(1)} %slice.19), channel_id=1, source_target_pairs={{0,256},{128,384},{256,0},{384,128},{1,257},{129,385},{257,1},{385... | collective-permute-start | bytes 12296 | tf_op jit(solution)/shard_map/ppermute | solution.py:301
  136.9 8.6 %collective-permute-start.6 = (bf16[16,128]{1,0:T(8,128)(2,1)S(1)}, bf16[16,128]{1,0:T(8,128)(2,1)S(1)}, u32[]{:S(2)}, u32[]{:S(2)}) collective-permute-start(bf16[16,128]{1,0:T(8,128)(2,1)S(1)} %slice.19), channel_id=1, source_target_pairs={{0,128},{128,0},{256,384},{384,256},{1,129},{129,1},{257,385},{385... | collective-permute-start | bytes 12296 | tf_op jit(solution)/shard_map/ppermute | solution.py:309
  159.8 7.9 %collective-permute-start.8 = (f32[8,128]{1,0:T(8,128)S(1)}, f32[8,128]{1,0:T(8,128)S(1)}, u32[]{:S(2)}, u32[]{:S(2)}) collective-permute-start(f32[8,128]{1,0:T(8,128)S(1)} %get-tuple-element.28), channel_id=1, source_target_pairs={{0,4},{4,0},{1,5},{5,1},{2,6},{6,2},{3,7},{7,3},{8,12},{12,8},{9,1... | collective-permute-start | bytes 12296 | tf_op jit(solution)/shard_map/ppermute | solution.py:296

commit v8 on v7

--- a/solution.py
+++ b/solution.py
@@ -14,20 +14,32 @@
 rest = 32
 chunk_rows = 72
 carry_rows = 16
-in_rows = 368
-out_rows = 384
+chunk_total = 368
+strip_rows = 304
 tiles = 9
 vmem = pl.BlockSpec(memory_space=pltpu.VMEM)
 smem = pl.BlockSpec(memory_space=pltpu.SMEM)
 anywhere = pl.BlockSpec(memory_space=pl.ANY)
-limits = pltpu.CompilerParams(vmem_limit_bytes=24 * 1024 * 1024)
+mebibyte = 1024 * 1024
 
 
 def shape(dims, dtype=jnp.bfloat16):
     return jax.ShapeDtypeStruct(tuple(dims), dtype)
 
 
-def call(kernel, out_shape, name, operands, scalars=(), after=(), flops=0, special=0, scratch=()):
+def call(
+    kernel,
+    out_shape,
+    name,
+    operands,
+    scalars=(),
+    after=(),
+    flops=0,
+    special=0,
+    scratch=(),
+    out_specs=None,
+    limit=24,
+):
     out_shape = tuple(out_shape)
     scalars, operands, after = tuple(scalars), tuple(operands), tuple(after)
     inputs = len(scalars) + len(operands)
@@ -40,9 +52,9 @@
         body,
         out_shape=out_shape,
         in_specs=[smem] * len(scalars) + [vmem] * len(operands) + [anywhere] * len(after),
-        out_specs=(vmem,) * len(out_shape),
+        out_specs=out_specs or (vmem,) * len(out_shape),
         scratch_shapes=list(scratch),
-        compiler_params=limits,
+        compiler_params=pltpu.CompilerParams(vmem_limit_bytes=limit * mebibyte),
         cost_estimate=pl.CostEstimate(flops=flops, bytes_accessed=moved, transcendentals=special),
         name=name,
     )(*scalars, *operands, *after)
@@ -71,7 +83,7 @@
             last = jnp.concatenate([last[8 * g : 8 * g + 8] for g in range(4)], axis=1)
             found.append(jnp.concatenate([rows[:, :lanes], rows[:, lanes : 2 * lanes], last], axis=0))
         chunks.append(found)
-    spare = jnp.zeros((in_rows - 5 * chunk_rows, lanes), jnp.float32)
+    spare = jnp.zeros((chunk_total - 5 * chunk_rows, lanes), jnp.float32)
     for d in range(strips):
         parts = [chunks[0][d]] + chunks[1] + [spare]
         out[d] = jnp.concatenate(parts, axis=0).astype(jnp.bfloat16)
@@ -95,16 +107,26 @@
     return found
 
 
-def unit_tiles(arrived, c, group):
-    chunks = [arrived[s][c * chunk_rows : (c + 1) * chunk_rows] for s in range(strips)]
-    found = unpack_rows(chunks, group)
+def units_of(found):
     inverse = lax.rsqrt(jnp.sum(total([t * t for t in found]), axis=1, keepdims=True) + epsilon)
     return [t * inverse for t in found], inverse
 
 
-def unit_kernel(arrived, image, text):
+def strip_at(place, k):
+    return lax.rem(place[0] + (strips - k), strips)
+
+
+def read_strips(place, arrived):
+    return [wide(arrived, strip_at(place, k)) for k in range(strips)]
+
+
+def unit_tiles(values, c, group):
+    return units_of(unpack_rows([v[c * chunk_rows : (c + 1) * chunk_rows] for v in values], group))
+
+
+def unit_kernel(place, arrived, image, text):
     group = lane_group()
-    values = [wide(arrived, s) for s in range(strips)]
+    values = read_strips(place, arrived)
     for c in range(5):
         units, _ = unit_tiles(values, c, group)
         for t in range(tiles):
@@ -115,18 +137,29 @@
                 text[(c - 1) * piece : c * piece, columns] = units[t].astype(jnp.bfloat16)
 
 
+def text_units(parts):
+    rows = [wide(p, slice(None)).T for p in parts]
+    found = []
+    for r in rows:
+        found += [r[:, :lanes], r[:, lanes : 2 * lanes]]
+    found.append(jnp.concatenate([r[:, 2 * lanes :] for r in rows], axis=1))
+    return units_of(found)
+
+
+def text_rows_kernel(own, p0, p1, p2, p3, out):
+    rows = own.shape[0]
+    out[:rows, :] = own[...]
+    units, _ = text_units((p0, p1, p2, p3))
+    for t in range(tiles):
+        out[rows:, t * lanes : (t + 1) * lanes] = units[t].astype(jnp.bfloat16)
+
+
 def join_image_kernel(own, near, out):
     for k in range(out.shape[0]):
         out[k, :piece, :] = own[...]
         out[k, piece:, :] = near[...]
 
 
-def join_text_kernel(own, near, out):
-    rows = own.shape[0]
-    out[:rows, :] = own[...]
-    out[rows:, :] = near[...]
-
-
 def fold(values):
     rows, columns = values.shape
     part = jnp.sum(values.reshape(rows // 8, 8, columns), axis=0)
@@ -136,7 +169,9 @@
 tile = 256
 
 
-def pair_kernel(scales, spot, left, first, second, out, weights_out, right):
+def pair_kernel(
+    scales, spot, left, first, second, out, weights_out, sums_out, right, buffer, semaphores
+):
     scale = scales[0]
     bias = scales[1]
     count, block, _ = left.shape
@@ -144,6 +179,7 @@
     right[:part, :] = first[...]
     right[part:, :] = second[...]
     per_tile = tile // block
+    copies = []
     sums = [jnp.zeros((8, lanes), jnp.float32) for _ in range(3)]
     for start in range(0, count, per_tile):
         rows = jnp.concatenate([left[start + k] for k in range(per_tile)], axis=0)
@@ -163,11 +199,20 @@
         weights = (scale * slope).astype(jnp.bfloat16)
         weights_out[start * block : start * block + tile, :] = weights
         back = jnp.dot(weights, right[...], preferred_element_type=jnp.float32)
+        slot = len(copies) % 2
+        if len(copies) > 1:
+            copies[-2].wait()
         for k in range(per_tile):
             for t in range(tiles):
-                out[start + k, t * block : (t + 1) * block, :] = back[
+                buffer[slot, k, t * block : (t + 1) * block, :] = back[
                     k * block : (k + 1) * block, t * lanes : (t + 1) * lanes
                 ].astype(jnp.bfloat16)
+        copies.append(
+            pltpu.make_async_copy(
+                buffer.at[slot], out.at[pl.ds(start, per_tile)], semaphores.at[slot]
+            )
+        )
+        copies[-1].start()
         quarter = tile // 4
         a, b, c, d = (grown[k * quarter : (k + 1) * quarter, :] for k in range(4))
         ab = a + (b + a * b)
@@ -179,28 +224,59 @@
     value = jnp.zeros((8, lanes), jnp.float32)
     for k in range(3):
         value = jnp.where(row == k, jnp.sum(sums[k], axis=0, keepdims=True), value)
-    carry = carry_of(value).astype(jnp.bfloat16)
-    for k in range(count):
-        out[k, tiles * block :, :] = carry
-
-
-def text_kernel(weights, left, own, other):
+    sums_out[...] = value
+    for copy in copies[-2:]:
+        copy.wait()
+
+
+def text_kernel(weights, left, sums, sums_given, own, other, sums_out):
     count, block, width = left.shape
     part = own.shape[0]
     contract = (((0,), (0,)), ((), ()))
     value = lax.dot_general(
-        weights[...], left[...].reshape(count * block, width), contract,
+        weights[...],
+        left[...].reshape(count * block, width),
+        contract,
         preferred_element_type=jnp.float32,
     )
     own[...] = value[:part]
-    other[...] = value[part:].astype(jnp.bfloat16)
-
-
-def text_sum_kernel(own, given, kept, sent):
+    other[:part, :] = value[part:].astype(jnp.bfloat16)
+    sums_now = carry_of(sums[...] + sums_given[...])
+    sums_out[...] = sums_now
+    other[part:, :lanes] = sums_now.astype(jnp.bfloat16)
+    other[part:, lanes:] = jnp.zeros((carry_rows, width - lanes), jnp.bfloat16)
+
+
+def text_sum_kernel(own, given, sums, p0, p1, p2, p3, kept, *outs):
     rows = kept.shape[0]
     kept[...] = own[:rows, :] + wide(given, pl.ds(0, rows), slice(None))
-    value = own[rows:, :] + wide(given, pl.ds(rows, rows), slice(None))
-    sent[...] = value.astype(jnp.bfloat16)
+    units, inverse = text_units((p0, p1, p2, p3))
+    here = pl.ds(rows, rows)
+    grads = []
+    for t in range(tiles):
+        columns = pl.ds(t * lanes, lanes)
+        grads.append(own[here, columns] + wide(given, here, columns))
+    final = grads_of(units, inverse, grads)
+    carry = sums[...] + wide(given, pl.ds(2 * rows, carry_rows), pl.ds(0, lanes))
+    carry = carry_of(carry[:8])
+    last = final[tiles - 1].T
+    for k, out in enumerate(outs):
+        parts = [final[2 * k].T, final[2 * k + 1].T, last[k * rest : (k + 1) * rest], carry]
+        out[...] = jnp.concatenate(parts, axis=0).astype(jnp.bfloat16)
+
+
+def strip_sum_kernel(g0, g1, g2, g3, out):
+    value = total([wide(g, slice(None)) for g in (g0, g1, g2, g3)])
+    strip = strip_rows - carry_rows
+    out[:strip, :] = value[:strip].astype(jnp.bfloat16)
+    out[strip:, :] = carry_of(value[strip : strip + 8]).astype(jnp.bfloat16)
+
+
+def sums_kernel(own, given, out):
+    tail = pl.ds(strip_rows - carry_rows, carry_rows)
+    value = (wide(own, tail, slice(None)) + wide(given, tail, slice(None)))[:8]
+    for k in range(out.shape[0]):
+        out[k] = value
 
 
 def three_parts(value):
@@ -218,9 +294,13 @@
     return jnp.concatenate([carry, jnp.zeros((8, lanes), jnp.float32)], axis=0)
 
 
+def grads_of(units, inverse, grads):
+    along = jnp.sum(total([u * g for u, g in zip(units, grads)]), axis=1, keepdims=True)
+    return [(g - u * along) * inverse for u, g in zip(units, grads)]
+
+
 def pack_grads(units, inverse, grads, group):
-    along = jnp.sum(total([u * g for u, g in zip(units, grads)]), axis=1, keepdims=True)
-    final = [(g - u * along) * inverse for u, g in zip(units, grads)]
+    final = grads_of(units, inverse, grads)
     chunks = []
     for s in range(strips):
         last = jnp.zeros((8, lanes), jnp.float32)
@@ -240,19 +320,12 @@
         rows = total([wide(backs, k, pl.ds(t * block, block), slice(None)) for k in range(count)])
         kept[t * piece : (t + 1) * piece, :] = rows[:piece]
         sent[t * piece : (t + 1) * piece, :] = rows[piece:].astype(jnp.bfloat16)
-    tail = pl.ds(tiles * block, carry_rows)
-    carry = carry_of(total([wide(backs, k, tail, slice(None)) for k in range(count)])[:8])
-    kept[tiles * piece :, :] = carry
-    sent[tiles * piece :, :] = carry.astype(jnp.bfloat16)
-
-
-def finish_kernel(arrived, image_kept, image_given, text_kept, text_given, near, far, out):
+
+
+def finish_kernel(place, arrived, image_kept, image_given, text_kept, out):
     group = lane_group()
-    values = [wide(arrived, s) for s in range(strips)]
-    tail = pl.ds(tiles * piece, carry_rows)
-    carried = image_kept[tail, :] + wide(image_given, tail, slice(None))
-    carry = carry_of((carried + wide(near, slice(None)) + wide(far, slice(None)))[:8])
-    spare = jnp.zeros((out_rows - 5 * chunk_rows - carry_rows, lanes), jnp.float32)
+    values = read_strips(place, arrived)
+    spare = jnp.zeros((chunk_total - 5 * chunk_rows, lanes), jnp.float32)
     chunks = [[] for _ in range(strips)]
     for c in range(5):
         units, inverse = unit_tiles(values, c, group)
@@ -263,33 +336,37 @@
                 grads.append(image_kept[rows, :] + wide(image_given, rows, slice(None)))
             else:
                 rows, columns = pl.ds((c - 1) * piece, piece), pl.ds(t * lanes, lanes)
-                grads.append(text_kept[rows, columns] + wide(text_given, rows, columns))
+                grads.append(text_kept[rows, columns])
         for s, chunk in enumerate(pack_grads(units, inverse, grads, group)):
             chunks[s].append(chunk)
     for s in range(strips):
-        out[s] = jnp.concatenate([carry] + chunks[s] + [spare], axis=0).astype(jnp.bfloat16)
-
-
-def last_kernel(arrived, image, text, sums_out):
+        value = jnp.concatenate(chunks[s] + [spare], axis=0)
+        out[strip_at(place, s)] = value.astype(jnp.bfloat16)
+
+
+def last_kernel(arrived, text_given, sums, image, text, sums_out):
     values = [wide(arrived, s) for s in range(strips)]
     for which, out in enumerate((image, text)):
         found = []
         for k in range(4):
             if which:
-                first = carry_rows + (1 + k) * chunk_rows
+                first = (1 + k) * chunk_rows
                 chunk = total([v[first : first + chunk_rows] for v in values])
             else:
-                chunk = values[k][carry_rows : carry_rows + chunk_rows]
+                chunk = values[k][:chunk_rows]
             last = chunk[2 * piece :]
             groups = [last] + [pltpu.roll(last, lanes - rest * g, 1) for g in range(1, 4)]
             last = jnp.concatenate(groups, axis=0)
             found.append((chunk[:piece], chunk[piece : 2 * piece], last))
         for t in range(3):
             rows = jnp.concatenate([f[t] for f in found], axis=0).T
-            size = lanes if t < 2 else rest
-            out[t * lanes : t * lanes + size, :] = rows[:size].astype(jnp.bfloat16)
-    sums = jnp.sum(total([v[:8] for v in values]), axis=1, keepdims=True)
-    sums_out[...] = jnp.broadcast_to(sums, sums_out.shape)
+            here = pl.ds(t * lanes, lanes if t < 2 else rest)
+            rows = rows[: here.size]
+            if which:
+                rows = rows + wide(text_given, here, slice(None))
+            out[here, :] = rows.astype(jnp.bfloat16)
+    value = total([sums[k] for k in range(sums.shape[0])])
+    sums_out[...] = jnp.broadcast_to(jnp.sum(value, axis=1, keepdims=True), value.shape)
 
 
 def swap_core(value):
@@ -318,76 +395,113 @@
     count = blocks * block
     columns = 4 * rows
     area = count * columns
+    place = lax.axis_index("zl").astype(jnp.int32).reshape(1)
     x, y, zl = (lax.axis_index(name).astype(jnp.int32) for name in ("x", "y", "zl"))
     scale = jnp.exp(log_temp)
     scales = jnp.stack([scale, bias])
     spot = jnp.stack([(x * y_count + y) * block, zl * piece])
     f32 = jnp.float32
 
-    (packed,) = call(pack_kernel, [shape((strips, in_rows, lanes))], "pack", [image.T, text.T])
+    strip_near = swap_text(text.T)
+    (packed,) = call(pack_kernel, [shape((strips, chunk_total, lanes))], "pack", [image.T, text.T])
     arrived = lax.all_to_all(packed, "zl", 0, 0)
     image_own, text_own = call(
-        unit_kernel, [shape((piece, width)), shape((rows, width))], "unit", [arrived]
+        unit_kernel,
+        [shape((piece, width)), shape((rows, width))],
+        "unit",
+        [arrived],
+        scalars=[place],
+        after=[strip_near],
     )
     image_near = swap_image(image_own)
-    text_near = swap_text(text_own)
     (joined,) = call(
         join_image_kernel, [shape((blocks, block, width))], "join_image", [image_own, image_near]
     )
     image_rows = lax.all_to_all(joined, ("x", "y"), 0, 0)
+    parts = [strip_near] + [shift(strip_near, "zl", k) for k in range(1, strips)]
     (text_rows,) = call(
-        join_text_kernel, [shape((2 * rows, width))], "join_text", [text_own, text_near]
+        text_rows_kernel, [shape((2 * rows, width))], "text_rows", [text_own] + parts
     )
     text_other = swap_core(text_rows)
 
-    back, weights = call(
+    back, weights, sums = call(
         pair_kernel,
-        [shape((blocks, tiles * block + carry_rows, lanes)), shape((count, columns))],
+        [
+            shape((blocks, tiles * block, lanes)),
+            shape((count, columns)),
+            shape((8, lanes), f32),
+        ],
         "pair",
         [image_rows, text_rows, text_other],
         scalars=[scales, spot],
         flops=4 * area * width,
         special=2 * area,
-        scratch=[pltpu.VMEM((columns, width), jnp.bfloat16)],
+        scratch=[
+            pltpu.VMEM((columns, width), jnp.bfloat16),
+            pltpu.VMEM((2, tile // block, tiles * block, lanes), jnp.bfloat16),
+            pltpu.SemaphoreType.DMA((2,)),
+        ],
+        out_specs=(pl.BlockSpec(memory_space=pltpu.HBM), vmem, vmem),
+        limit=58,
     )
     back = lax.all_to_all(back, ("x", "y"), 0, 0)
-    text_kept, text_sent = call(
+    sums_given = swap_image(sums)
+    text_kept, text_sent, sums = call(
         text_kernel,
-        [shape((2 * rows, width), f32), shape((2 * rows, width))],
+        [
+            shape((2 * rows, width), f32),
+            shape((2 * rows + carry_rows, width)),
+            shape((carry_rows, lanes), f32),
+        ],
         "text_back",
-        [weights, image_rows],
+        [weights, image_rows, sums, sums_given],
         flops=2 * area * width,
     )
     text_given = swap_core(text_sent)
-    text_kept, text_sent = call(
+    text_kept, *near_strips = call(
         text_sum_kernel,
-        [shape((rows, width), f32), shape((rows, width))],
+        [shape((rows, width), f32)] + [shape((strip_rows, lanes))] * strips,
         "text_sum",
-        [text_kept, text_given],
-    )
-    text_given = swap_text(text_sent)
-    sums_rows = tiles * piece + carry_rows
+        [text_kept, text_given, sums] + parts,
+    )
+    near_strips = [near_strips[0]] + [
+        shift(near_strips[k], "zl", -k) for k in range(1, strips)
+    ]
+    (strip_sent,) = call(
+        strip_sum_kernel, [shape((strip_rows, lanes))], "strip_sum", near_strips
+    )
+    strip_given = swap_text(strip_sent)
     image_kept, image_sent = call(
         image_sum_kernel,
-        [shape((sums_rows, lanes), f32), shape((sums_rows, lanes))],
+        [shape((tiles * piece, lanes), f32), shape((tiles * piece, lanes))],
         "image_sum",
         [back],
     )
     image_given = swap_image(image_sent)
-    carry = image_sent[tiles * piece :]
-    near = swap_text(carry)
-    far = shift(carry, "zh", 2)
+    (sums,) = call(
+        sums_kernel,
+        [shape((blocks, 8, lanes), f32)],
+        "sums",
+        [strip_sent, strip_given],
+        after=[image_sent],
+    )
+    sums = lax.all_to_all(sums, ("x", "y"), 0, 0)
     (finished,) = call(
         finish_kernel,
-        [shape((strips, out_rows, lanes))],
+        [shape((strips, chunk_total, lanes))],
         "finish",
-        [arrived, image_kept, image_given, text_kept, text_given, near, far],
+        [arrived, image_kept, image_given, text_kept],
+        scalars=[place],
+        after=[sums],
     )
     finished = lax.all_to_all(finished, "zl", 0, 0)
     grad_image, grad_text, sums = call(
-        last_kernel, [shape((strip, rows))] * 2 + [shape((8, lanes), f32)], "last", [finished]
-    )
-    sums = (sums + swap_core(sums))[:, 0]
+        last_kernel,
+        [shape((strip, rows))] * 2 + [shape((8, lanes), f32)],
+        "last",
+        [finished, strip_given, sums],
+    )
+    sums = sums[:, 0]
     pairs_count = rows * zh_count * blocks * 2
     return (
         sums[0] / pairs_count,

time: 175 us -> 178 us (1.017)
  the two profiles are of different devices: /device:TPU:1 before, /device:TPU:2 now
where the time goes in v8:
time: 178 us; the launch traced here: 177 us
  starting transfers between devices  91.4 us (51%)
  blocking collectives  25.9 us (15%)
  waiting for transfers between devices  25.1 us (14%)
  Pallas kernels  15.4 us (9%)
  local copies, waits for them, and re-layouts  9.86 us (6%)
  between operations  7.57 us (4%)
    ppermute x6, starting transfers between devices, shift(): lax.ppermute(value, axis, [(i, (i + k) % count) for i in range(count)])  27.4 us
    ppermute x3, starting transfers between devices, swap_image(): return lax.ppermute(value, 'zh', [(0, 3), (3, 0), (1, 2), (2, 1)])  26.4 us
    pallas_call x12, Pallas kernels, call(): pl.pallas_call(body, out_shape=out_shape, in_specs=[smem] * len(scalars)...  15.4 us
    all_to_all x1, blocking collectives, shards(): sums = lax.all_to_all(sums, ('x', 'y'), 0, 0)  13.3 us
    ppermute x2, starting transfers between devices, swap_text(): return lax.ppermute(value, 'zh', [(0, 1), (1, 0), (2, 3), (3, 2)])  13 us
    all_to_all x1, blocking collectives, shards(): finished = lax.all_to_all(finished, 'zl', 0, 0)  12.7 us
    unnamed x22, local copies, waits for them, and re-layouts  9.27 us
    ppermute x3, waiting for transfers between devices, swap_image(): return lax.ppermute(value, 'zh', [(0, 3), (3, 0), (1, 2), (2, 1)])  7.78 us
  transfers between devices with their start and end apart: 16, of which 11 were waited for; matrix products, arithmetic and copies ran while one was open for 1% of the time, Pallas kernels for 2%

profile of v8, /device:TPU:2, one launch (start us, length us, event | category | flops | bytes accessed | tf_op | source)
XLA Modules:
  0.0 176.6 jit_solution(8615531514335990146)
XLA Ops:
  0.6 0.9 copy-done.7
  1.5 0.9 copy-done.8
  2.4 1.0 pack.1
  3.4 5.9 %all-to-all-start = ((bf16[4,368,128]{2,1,0:T(8,128)(2,1)}), bf16[4,368,128]{2,1,0:T(8,128)(2,1)S(1)}, u32[]{:S(2)}, u32[]{:S(2)}) async-start(bf16[4,368,128]{2,1,0:T(8,128)(2,1)} %pack.1), calls=%async_computation | async-start | bytes 753664 | tf_op jit(solution)/shard_map/all_to_all | solution.py:407
  9.3 9.1 %collective-permute-start = (bf16[288,128]{1,0:T(8,128)(2,1)}, bf16[288,128]{1,0:T(8,128)(2,1)S(1)}, u32[]{:S(2)}, u32[]{:S(2)}) collective-permute-start(bf16[288,128]{1,0:T(8,128)(2,1)} %bitcast.14), channel_id=1, source_target_pairs={{0,128},{128,0},{256,384},{384,256},{1,129},{129,1},{257,385},{385... | collective-permute-start | bytes 221192 | tf_op jit(solution)/shard_map/ppermute | solution.py:386
  18.4 2.5 %collective-permute-done.refs_2_.refs_1_.refs_3_ = bf16[288,128]{1,0:T(8,128)(2,1)S(1)} collective-permute-done((bf16[288,128]{1,0:T(8,128)(2,1)}, bf16[288,128]{1,0:T(8,128)(2,1)S(1)}, u32[]{:S(2)}, u32[]{:S(2)}) %collective-permute-start) | collective-permute-done | bytes 73760 | tf_op jit(solution)/shard_map/ppermute | solution.py:386
  20.9 1.5 all-to-all-done.refs_1_
  22.7 0.7 copy-done.5
  23.5 11.1 %collective-permute-start.1 = (bf16[32,1152]{1,0:T(8,128)(2,1)S(1)}, bf16[32,1152]{1,0:T(8,128)(2,1)S(1)}, u32[]{:S(2)}, u32[]{:S(2)}) collective-permute-start(bf16[32,1152]{1,0:T(8,128)(2,1)S(1)} %get-tuple-element.23.refs_0_), channel_id=1, source_target_pairs={{0,384},{384,0},{128,256},{256,128},{1,385},{385,1},{129,257},{257... | collective-permute-start | bytes 221192 | tf_op jit(solution)/shard_map/ppermute | solution.py:382
  34.6 5.8 %collective-permute-done.1.refs_1_ = bf16[32,1152]{1,0:T(8,128)(2,1)S(1)} collective-permute-done((bf16[32,1152]{1,0:T(8,128)(2,1)S(1)}, bf16[32,1152]{1,0:T(8,128)(2,1)S(1)}, u32[]{:S(2)}, u32[]{:S(2)}) %collective-permute-start.1) | collective-permute-done | bytes 73760 | tf_op jit(solution)/shard_map/ppermute | solution.py:382
  40.4 1.6 join_image.1
  42.0 7.5 %all-to-all-start.1 = ((bf16[16,64,1152]{2,1,0:T(8,128)(2,1)}), bf16[16,64,1152]{2,1,0:T(8,128)(2,1)S(1)}, u32[]{:S(2)}, u32[]{:S(2)}) async-start(bf16[16,64,1152]{2,1,0:T(8,128)(2,1)} %join_image.1), calls=%async_computation.1 | async-start | bytes 4718592 | tf_op jit(solution)/shard_map/all_to_all | solution.py:420
  49.5 2.1 %collective-permute-start.2 = (bf16[288,128]{1,0:T(8,128)(2,1)S(1)}, bf16[288,128]{1,0:T(8,128)(2,1)S(1)}, u32[]{:S(2)}, u32[]{:S(2)}) collective-permute-start(bf16[288,128]{1,0:T(8,128)(2,1)S(1)} %collective-permute-done.refs_2_.refs_1_.refs_3_), channel_id=1, source_target_pairs={{0,1},{1,2},{2,3},{3,0},{4,5},{5,6},{6,7},{7,4},{8,9},{9,10},{10,1... | collective-permute-start | bytes 221192 | tf_op jit(solution)/shard_map/ppermute | solution.py:378
  51.6 5.5 %collective-permute-start.3 = (bf16[288,128]{1,0:T(8,128)(2,1)S(1)}, bf16[288,128]{1,0:T(8,128)(2,1)S(1)}, u32[]{:S(2)}, u32[]{:S(2)}) collective-permute-start(bf16[288,128]{1,0:T(8,128)(2,1)S(1)} %collective-permute-done.refs_2_.refs_1_.refs_3_), channel_id=1, source_target_pairs={{0,2},{1,3},{2,0},{3,1},{4,6},{5,7},{6,4},{7,5},{8,10},{9,11},{10,... | collective-permute-start | bytes 221192 | tf_op jit(solution)/shard_map/ppermute | solution.py:378
  57.1 3.1 %collective-permute-start.4 = (bf16[288,128]{1,0:T(8,128)(2,1)S(1)}, bf16[288,128]{1,0:T(8,128)(2,1)S(1)}, u32[]{:S(2)}, u32[]{:S(2)}) collective-permute-start(bf16[288,128]{1,0:T(8,128)(2,1)S(1)} %collective-permute-done.refs_2_.refs_1_.refs_3_), channel_id=1, source_target_pairs={{0,3},{1,0},{2,1},{3,2},{4,7},{5,4},{6,5},{7,6},{8,11},{9,8},{10,9... | collective-permute-start | bytes 221192 | tf_op jit(solution)/shard_map/ppermute | solution.py:378
  60.5 2.9 %collective-permute-done.4.refs_4_.refs_6_ = bf16[288,128]{1,0:T(8,128)(2,1)S(1)} collective-permute-done((bf16[288,128]{1,0:T(8,128)(2,1)S(1)}, bf16[288,128]{1,0:T(8,128)(2,1)S(1)}, u32[]{:S(2)}, u32[]{:S(2)}) %collective-permute-start.4) | collective-permute-done | bytes 73760 | tf_op jit(solution)/shard_map/ppermute | solution.py:378
  63.4 1.0 copy-done.6
  64.3 0.4 text_rows.1.refs_3_
  64.7 0.6 copy-done.3
  65.4 1.9 %collective-permute-start.5 = (bf16[256,1152]{1,0:T(8,128)(2,1)S(1)}, bf16[256,1152]{1,0:T(8,128)(2,1)}, u32[]{:S(2)}, u32[]{:S(2)}) collective-permute-start(bf16[256,1152]{1,0:T(8,128)(2,1)S(1)} %text_rows.1.refs_3_), channel_id=1, source_target_pairs={{0,4},{4,0},{1,5},{5,1},{2,6},{6,2},{3,7},{7,3},{8,12},{12,8},{9,1... | collective-permute-start | bytes 1769480 | tf_op jit(solution)/shard_map/ppermute | solution.py:373
  68.6 0.6 pad_add_fusion.refs_1_
  69.3 0.7 pad_maximum_fusion.refs_0_
  69.9 4.0 %all-to-all-done.1.refs_2_.refs_1_ = bf16[16,64,1152]{2,1,0:T(8,128)(2,1)S(1)} async-done(((bf16[16,64,1152]{2,1,0:T(8,128)(2,1)}), bf16[16,64,1152]{2,1,0:T(8,128)(2,1)S(1)}, u32[]{:S(2)}, u32[]{:S(2)}) %all-to-all-start.1) | async-done | bytes 2359328 | tf_op jit(solution)/shard_map/all_to_all | solution.py:420
  74.0 1.4 copy-done
  75.4 8.2 %pair.1 = (bf16[16,576,128]{2,1,0:T(8,128)(2,1)}, bf16[1024,512]{1,0:T(8,128)(2,1)}, f32[8,128]{1,0:T(8,128)}) custom-call(f32[2]{0:T(128)} %pad_maximum_fusion.refs_0_, s32[2]{0:T(128)} %pad_add_fusion.refs_1_, bf16[16,64,1152]{2,1,0:T(8,128)(2,1)} %copy-done, bf16[256,1152]{1,0:T(8,128)(2,1)} %copy-done.2, bf16[256,1152]{1,0:T(8,128)(2,1)} %collective-permute-done.5.refs_4_), custom_call_target="tpu_custom_call" | custom-call | flops 2415919104 | bytes 6950912 | tf_op jit(solution)/shard_map/pair/pallas_call | solution.py:51
  83.6 7.3 %all-to-all-start.2 = ((bf16[16,576,128]{2,1,0:T(8,128)(2,1)}), bf16[16,576,128]{2,1,0:T(8,128)(2,1)S(1)}, u32[]{:S(2)}, u32[]{:S(2)}) async-start(bf16[16,576,128]{2,1,0:T(8,128)(2,1)} %get-tuple-element.25), calls=%async_computation.2 | async-start | bytes 4718592 | tf_op jit(solution)/shard_map/all_to_all | solution.py:447
  90.9 7.5 %collective-permute-start.7 = (f32[8,128]{1,0:T(8,128)S(1)}, f32[8,128]{1,0:T(8,128)S(1)}, u32[]{:S(2)}, u32[]{:S(2)}) collective-permute-start(f32[8,128]{1,0:T(8,128)S(1)} %copy-done.9), channel_id=1, source_target_pairs={{0,384},{384,0},{128,256},{256,128},{1,385},{385,1},{129,257},{257... | collective-permute-start | bytes 12296 | tf_op jit(solution)/shard_map/ppermute | solution.py:382
  98.4 1.9 %collective-permute-done.7.refs_3_ = f32[8,128]{1,0:T(8,128)S(1)} collective-permute-done((f32[8,128]{1,0:T(8,128)S(1)}, f32[8,128]{1,0:T(8,128)S(1)}, u32[]{:S(2)}, u32[]{:S(2)}) %collective-permute-start.7) | collective-permute-done | bytes 4128 | tf_op jit(solution)/shard_map/ppermute | solution.py:382
  100.4 1.7 copy-done.1
  102.0 1.2 copy-done.10
  103.2 1.6 text_back.1
  104.8 1.9 %collective-permute-start.8 = (bf16[272,1152]{1,0:T(8,128)(2,1)S(1)}, bf16[272,1152]{1,0:T(8,128)(2,1)S(1)}, u32[]{:S(2)}, u32[]{:S(2)}) collective-permute-start(bf16[272,1152]{1,0:T(8,128)(2,1)S(1)} %get-tuple-element.31), channel_id=1, source_target_pairs={{0,4},{4,0},{1,5},{5,1},{2,6},{6,2},{3,7},{7,3},{8,12},{12,8},{9,1... | collective-permute-start | bytes 1880072 | tf_op jit(solution)/shard_map/ppermute | solution.py:373
  106.7 2.0 %collective-permute-done.8.refs_1_ = bf16[272,1152]{1,0:T(8,128)(2,1)S(1)} collective-permute-done((bf16[272,1152]{1,0:T(8,128)(2,1)S(1)}, bf16[272,1152]{1,0:T(8,128)(2,1)S(1)}, u32[]{:S(2)}, u32[]{:S(2)}) %collective-permute-start.8) | collective-permute-done | bytes 626720 | tf_op jit(solution)/shard_map/ppermute | solution.py:373
  108.8 0.9 copy-done.4
  109.6 0.6 text_sum.1
  110.3 9.1 %collective-permute-start.10 = (bf16[304,128]{1,0:T(8,128)(2,1)S(1)}, bf16[304,128]{1,0:T(8,128)(2,1)S(1)}, u32[]{:S(2)}, u32[]{:S(2)}) collective-permute-start(bf16[304,128]{1,0:T(8,128)(2,1)S(1)} %get-tuple-element.36), channel_id=1, source_target_pairs={{0,2},{1,3},{2,0},{3,1},{4,6},{5,7},{6,4},{7,5},{8,10},{9,11},{10,... | collective-permute-start | bytes 233480 | tf_op jit(solution)/shard_map/ppermute | solution.py:378
  119.4 1.9 %collective-permute-start.11 = (bf16[304,128]{1,0:T(8,128)(2,1)S(1)}, bf16[304,128]{1,0:T(8,128)(2,1)S(1)}, u32[]{:S(2)}, u32[]{:S(2)}) collective-permute-start(bf16[304,128]{1,0:T(8,128)(2,1)S(1)} %get-tuple-element.37), channel_id=1, source_target_pairs={{0,1},{1,2},{2,3},{3,0},{4,5},{5,6},{6,7},{7,4},{8,9},{9,10},{10,1... | collective-permute-start | bytes 233480 | tf_op jit(solution)/shard_map/ppermute | solution.py:378
  121.3 5.7 %collective-permute-start.9 = (bf16[304,128]{1,0:T(8,128)(2,1)S(1)}, bf16[304,128]{1,0:T(8,128)(2,1)S(1)}, u32[]{:S(2)}, u32[]{:S(2)}) collective-permute-start(bf16[304,128]{1,0:T(8,128)(2,1)S(1)} %get-tuple-element.35), channel_id=1, source_target_pairs={{0,3},{1,0},{2,1},{3,2},{4,7},{5,4},{6,5},{7,6},{8,11},{9,8},{10,9... | collective-permute-start | bytes 233480 | tf_op jit(solution)/shard_map/ppermute | solution.py:378
  127.0 0.5 collective-permute-done.11.refs_3_
  127.6 1.5 collective-permute-done.9.refs_1_
  129.2 3.9 %collective-permute-start.12 = (bf16[304,128]{1,0:T(8,128)(2,1)S(1)}, bf16[304,128]{1,0:T(8,128)(2,1)S(1)}, u32[]{:S(2)}, u32[]{:S(2)}) collective-permute-start(bf16[304,128]{1,0:T(8,128)(2,1)S(1)} %strip_sum.1.refs_0_), channel_id=1, source_target_pairs={{0,128},{128,0},{256,384},{384,256},{1,129},{129,1},{257,385},{385... | collective-permute-start | bytes 233480 | tf_op jit(solution)/shard_map/ppermute | solution.py:386
  133.4 7.8 %collective-permute-start.6 = (bf16[288,128]{1,0:T(8,128)(2,1)S(1)}, bf16[288,128]{1,0:T(8,128)(2,1)S(1)}, u32[]{:S(2)}, u32[]{:S(2)}) collective-permute-start(bf16[288,128]{1,0:T(8,128)(2,1)S(1)} %get-tuple-element.27.refs_2_), channel_id=1, source_target_pairs={{0,384},{384,0},{128,256},{256,128},{1,385},{385,1},{129,257},{257... | collective-permute-start | bytes 221192 | tf_op jit(solution)/shard_map/ppermute | solution.py:382
  141.3 2.1 %collective-permute-done.12.refs_1_ = bf16[304,128]{1,0:T(8,128)(2,1)S(1)} collective-permute-done((bf16[304,128]{1,0:T(8,128)(2,1)S(1)}, bf16[304,128]{1,0:T(8,128)(2,1)S(1)}, u32[]{:S(2)}, u32[]{:S(2)}) %collective-permute-start.12) | collective-permute-done | bytes 77856 | tf_op jit(solution)/shard_map/ppermute | solution.py:386
  143.4 13.3 %all_to_all.25.refs_5_.refs_2_ = f32[16,8,128]{2,1,0:T(8,128)S(1)} all-to-all(f32[16,8,128]{2,1,0:T(8,128)S(1)} %sums.1), channel_id=1, replica_groups=mesh['zh'=4,'x'=4,'y'=4,'core'=2,'zl'=4] {'x','y'}, dimensions={0} | all-to-all | bytes 131072 | tf_op jit(solution)/shard_map/all_to_all | solution.py:488
  156.6 0.5 finish.1
  157.1 12.7 %all_to_all.26.refs_0_ = bf16[4,368,128]{2,1,0:T(8,128)(2,1)S(1)} all-to-all(bf16[4,368,128]{2,1,0:T(8,128)(2,1)S(1)} %finish.1), channel_id=1, replica_groups=mesh['zh'=4,'x'=4,'y'=4,'core'=2,'zl'=4] {'zl'}, dimensions={0} | all-to-all | bytes 753664 | tf_op jit(solution)/shard_map/all_to_all | solution.py:497
  169.8 0.8 last.1
  170.6 0.6 fusion
  (23 shorter events, 1.1 us)
Async XLA Ops:
  0.6 0.9 copy-start.7
  1.5 0.9 copy-start.8
  3.4 19.0 %all-to-all-start = ((bf16[4,368,128]{2,1,0:T(8,128)(2,1)}), bf16[4,368,128]{2,1,0:T(8,128)(2,1)S(1)}, u32[]{:S(2)}, u32[]{:S(2)}) async-start(bf16[4,368,128]{2,1,0:T(8,128)(2,1)} %pack.1), calls=%async_computation | async-start | bytes 753664 | tf_op jit(solution)/shard_map/all_to_all | solution.py:407
  9.3 11.6 %collective-permute-start = (bf16[288,128]{1,0:T(8,128)(2,1)}, bf16[288,128]{1,0:T(8,128)(2,1)S(1)}, u32[]{:S(2)}, u32[]{:S(2)}) collective-permute-start(bf16[288,128]{1,0:T(8,128)(2,1)} %bitcast.14), channel_id=1, source_target_pairs={{0,128},{128,0},{256,384},{384,256},{1,129},{129,1},{257,385},{385... | collective-permute-start | bytes 221192 | tf_op jit(solution)/shard_map/ppermute | solution.py:386
  22.7 0.7 copy-start.5
  23.5 16.9 %collective-permute-start.1 = (bf16[32,1152]{1,0:T(8,128)(2,1)S(1)}, bf16[32,1152]{1,0:T(8,128)(2,1)S(1)}, u32[]{:S(2)}, u32[]{:S(2)}) collective-permute-start(bf16[32,1152]{1,0:T(8,128)(2,1)S(1)} %get-tuple-element.23.refs_0_), channel_id=1, source_target_pairs={{0,384},{384,0},{128,256},{256,128},{1,385},{385,1},{129,257},{257... | collective-permute-start | bytes 221192 | tf_op jit(solution)/shard_map/ppermute | solution.py:382
  42.0 32.0 %all-to-all-start.1 = ((bf16[16,64,1152]{2,1,0:T(8,128)(2,1)}), bf16[16,64,1152]{2,1,0:T(8,128)(2,1)S(1)}, u32[]{:S(2)}, u32[]{:S(2)}) async-start(bf16[16,64,1152]{2,1,0:T(8,128)(2,1)} %join_image.1), calls=%async_computation.1 | async-start | bytes 4718592 | tf_op jit(solution)/shard_map/all_to_all | solution.py:420
  49.5 10.8 %collective-permute-start.2 = (bf16[288,128]{1,0:T(8,128)(2,1)S(1)}, bf16[288,128]{1,0:T(8,128)(2,1)S(1)}, u32[]{:S(2)}, u32[]{:S(2)}) collective-permute-start(bf16[288,128]{1,0:T(8,128)(2,1)S(1)} %collective-permute-done.refs_2_.refs_1_.refs_3_), channel_id=1, source_target_pairs={{0,1},{1,2},{2,3},{3,0},{4,5},{5,6},{6,7},{7,4},{8,9},{9,10},{10,1... | collective-permute-start | bytes 221192 | tf_op jit(solution)/shard_map/ppermute | solution.py:378
  51.6 8.9 %collective-permute-start.3 = (bf16[288,128]{1,0:T(8,128)(2,1)S(1)}, bf16[288,128]{1,0:T(8,128)(2,1)S(1)}, u32[]{:S(2)}, u32[]{:S(2)}) collective-permute-start(bf16[288,128]{1,0:T(8,128)(2,1)S(1)} %collective-permute-done.refs_2_.refs_1_.refs_3_), channel_id=1, source_target_pairs={{0,2},{1,3},{2,0},{3,1},{4,6},{5,7},{6,4},{7,5},{8,10},{9,11},{10,... | collective-permute-start | bytes 221192 | tf_op jit(solution)/shard_map/ppermute | solution.py:378
  57.1 6.2 %collective-permute-start.4 = (bf16[288,128]{1,0:T(8,128)(2,1)S(1)}, bf16[288,128]{1,0:T(8,128)(2,1)S(1)}, u32[]{:S(2)}, u32[]{:S(2)}) collective-permute-start(bf16[288,128]{1,0:T(8,128)(2,1)S(1)} %collective-permute-done.refs_2_.refs_1_.refs_3_), channel_id=1, source_target_pairs={{0,3},{1,0},{2,1},{3,2},{4,7},{5,4},{6,5},{7,6},{8,11},{9,8},{10,9... | collective-permute-start | bytes 221192 | tf_op jit(solution)/shard_map/ppermute | solution.py:378
  63.4 1.0 copy-start.6
  64.7 0.6 copy-start.3
  65.4 8.6 %copy-start.2 = (bf16[256,1152]{1,0:T(8,128)(2,1)}, bf16[256,1152]{1,0:T(8,128)(2,1)S(1)}, u32[]{:S(2)}) copy-start(bf16[256,1152]{1,0:T(8,128)(2,1)S(1)} %text_rows.1.refs_3_) | copy-start | bytes 1769476
  65.4 4.6 %collective-permute-start.5 = (bf16[256,1152]{1,0:T(8,128)(2,1)S(1)}, bf16[256,1152]{1,0:T(8,128)(2,1)}, u32[]{:S(2)}, u32[]{:S(2)}) collective-permute-start(bf16[256,1152]{1,0:T(8,128)(2,1)S(1)} %text_rows.1.refs_3_), channel_id=1, source_target_pairs={{0,4},{4,0},{1,5},{5,1},{2,6},{6,2},{3,7},{7,3},{8,12},{12,8},{9,1... | collective-permute-start | bytes 1769480 | tf_op jit(solution)/shard_map/ppermute | solution.py:373
  73.9 1.4 copy-start
  83.6 7.4 %copy-start.9 = (f32[8,128]{1,0:T(8,128)S(1)}, f32[8,128]{1,0:T(8,128)}, u32[]{:S(2)}) copy-start(f32[8,128]{1,0:T(8,128)} %get-tuple-element.29.refs_2_) | copy-start | bytes 12292
  83.6 49.5 %all-to-all-start.2 = ((bf16[16,576,128]{2,1,0:T(8,128)(2,1)}), bf16[16,576,128]{2,1,0:T(8,128)(2,1)S(1)}, u32[]{:S(2)}, u32[]{:S(2)}) async-start(bf16[16,576,128]{2,1,0:T(8,128)(2,1)} %get-tuple-element.25), calls=%async_computation.2 | async-start | bytes 4718592 | tf_op jit(solution)/shard_map/all_to_all | solution.py:447
  90.9 9.4 %collective-permute-start.7 = (f32[8,128]{1,0:T(8,128)S(1)}, f32[8,128]{1,0:T(8,128)S(1)}, u32[]{:S(2)}, u32[]{:S(2)}) collective-permute-start(f32[8,128]{1,0:T(8,128)S(1)} %copy-done.9), channel_id=1, source_target_pairs={{0,384},{384,0},{128,256},{256,128},{1,385},{385,1},{129,257},{257... | collective-permute-start | bytes 12296 | tf_op jit(solution)/shard_map/ppermute | solution.py:382
  100.4 1.7 copy-start.1
  102.0 1.2 copy-start.10
  104.8 4.0 %collective-permute-start.8 = (bf16[272,1152]{1,0:T(8,128)(2,1)S(1)}, bf16[272,1152]{1,0:T(8,128)(2,1)S(1)}, u32[]{:S(2)}, u32[]{:S(2)}) collective-permute-start(bf16[272,1152]{1,0:T(8,128)(2,1)S(1)} %get-tuple-element.31), channel_id=1, source_target_pairs={{0,4},{4,0},{1,5},{5,1},{2,6},{6,2},{3,7},{7,3},{8,12},{12,8},{9,1... | collective-permute-start | bytes 1880072 | tf_op jit(solution)/shard_map/ppermute | solution.py:373
  108.8 0.9 copy-start.4
  110.3 16.7 %collective-permute-start.10 = (bf16[304,128]{1,0:T(8,128)(2,1)S(1)}, bf16[304,128]{1,0:T(8,128)(2,1)S(1)}, u32[]{:S(2)}, u32[]{:S(2)}) collective-permute-start(bf16[304,128]{1,0:T(8,128)(2,1)S(1)} %get-tuple-element.36), channel_id=1, source_target_pairs={{0,2},{1,3},{2,0},{3,1},{4,6},{5,7},{6,4},{7,5},{8,10},{9,11},{10,... | collective-permute-start | bytes 233480 | tf_op jit(solution)/shard_map/ppermute | solution.py:378
  119.4 8.2 %collective-permute-start.11 = (bf16[304,128]{1,0:T(8,128)(2,1)S(1)}, bf16[304,128]{1,0:T(8,128)(2,1)S(1)}, u32[]{:S(2)}, u32[]{:S(2)}) collective-permute-start(bf16[304,128]{1,0:T(8,128)(2,1)S(1)} %get-tuple-element.37), channel_id=1, source_target_pairs={{0,1},{1,2},{2,3},{3,0},{4,5},{5,6},{6,7},{7,4},{8,9},{9,10},{10,1... | collective-permute-start | bytes 233480 | tf_op jit(solution)/shard_map/ppermute | solution.py:378
  121.3 7.7 %collective-permute-start.9 = (bf16[304,128]{1,0:T(8,128)(2,1)S(1)}, bf16[304,128]{1,0:T(8,128)(2,1)S(1)}, u32[]{:S(2)}, u32[]{:S(2)}) collective-permute-start(bf16[304,128]{1,0:T(8,128)(2,1)S(1)} %get-tuple-element.35), channel_id=1, source_target_pairs={{0,3},{1,0},{2,1},{3,2},{4,7},{5,4},{6,5},{7,6},{8,11},{9,8},{10,9... | collective-permute-start | bytes 233480 | tf_op jit(solution)/shard_map/ppermute | solution.py:378
  129.2 14.2 %collective-permute-start.12 = (bf16[304,128]{1,0:T(8,128)(2,1)S(1)}, bf16[304,128]{1,0:T(8,128)(2,1)S(1)}, u32[]{:S(2)}, u32[]{:S(2)}) collective-permute-start(bf16[304,128]{1,0:T(8,128)(2,1)S(1)} %strip_sum.1.refs_0_), channel_id=1, source_target_pairs={{0,128},{128,0},{256,384},{384,256},{1,129},{129,1},{257,385},{385... | collective-permute-start | bytes 233480 | tf_op jit(solution)/shard_map/ppermute | solution.py:386
  133.4 23.2 %collective-permute-start.6 = (bf16[288,128]{1,0:T(8,128)(2,1)S(1)}, bf16[288,128]{1,0:T(8,128)(2,1)S(1)}, u32[]{:S(2)}, u32[]{:S(2)}) collective-permute-start(bf16[288,128]{1,0:T(8,128)(2,1)S(1)} %get-tuple-element.27.refs_2_), channel_id=1, source_target_pairs={{0,384},{384,0},{128,256},{256,128},{1,385},{385,1},{129,257},{257... | collective-permute-start | bytes 221192 | tf_op jit(solution)/shard_map/ppermute | solution.py:382

commit v9 on v6

--- a/solution.py
+++ b/solution.py
@@ -362,7 +362,7 @@
 
     (packed,) = call(pack_kernel, [shape((z_count, chunk_rows, lanes))], "pack", [image.T])
     parts = [text.T] + [shift(text.T, "zl", k) for k in range(1, strips)]
-    arrived = lax.all_to_all(hold(packed, parts[1:]), ("zh", "zl"), 0, 0)
+    arrived = lax.all_to_all(packed, ("zh", "zl"), 0, 0)
     (home_text,) = call(text_unit_kernel, [shape((block, width))], "text_unit", parts)
     texts = [shift(home_text, "y", k) for k in range(1, y_count)]
     (units,) = call(
@@ -371,7 +371,7 @@
         "image_unit",
         [arrived],
         scalars=[place],
-        after=texts,
+        after=[home_text],
     )
     image_rows = lax.all_to_all(units, "x", 0, 0).reshape(count, width)
     other_rows = swap_core(image_rows)
@@ -429,7 +429,7 @@
         flops=200 * count * block * width,
     )
     moved = [text_backs[0]] + [shift(text_backs[k], "y", -k) for k in range(1, y_count)]
-    finished = hold(finished, moved[1:])
+    finished = hold(finished, moved[1:3])
     finished = lax.all_to_all(finished, ("zh", "zl"), 0, 0)
     text_parts = call(
         text_finish_kernel, [shape((strip, rows))] * strips, "text_finish", parts + moved

time: 165 us -> 155 us (0.939)
  waiting for transfers between devices: 52.2 us -> 40.6 us
    all_to_all x1, waiting for transfers between devices: 12.4 us -> 1.52 us  [shards(): image_rows = lax.all_to_all(units, 'x', 0, 0).reshape(count, width)]
    ppermute x12, waiting for transfers between devices: 32.7 us -> 30.4 us  [shift(): lax.ppermute(value, axis, [(i, (i + k) % count) for i in range(count)])]
    all_to_all x1, starting transfers between devices: 13 us -> 15.2 us  [shards(): arrived = lax.all_to_all(packed, ('zh', 'zl'), 0, 0)]
  transfers between devices with their start and end apart: 18 -> 18, of which waited for: 10 -> 10; matrix products, arithmetic and copies ran while one was open for 0% -> 0% of each run, Pallas kernels for 5% -> 4%
where the time goes in v9:
time: 155 us; the launch traced here: 154 us
  starting transfers between devices  80.4 us (52%)
  waiting for transfers between devices  40.6 us (26%)
  Pallas kernels  15.1 us (10%)
  blocking collectives  7.82 us (5%)
  between operations  7.48 us (5%)
  local copies, waits for them, and re-layouts  2.32 us (1%)
    ppermute x12, starting transfers between devices, shift(): lax.ppermute(value, axis, [(i, (i + k) % count) for i in range(count)])  40.1 us
    ppermute x12, waiting for transfers between devices, shift(): lax.ppermute(value, axis, [(i, (i + k) % count) for i in range(count)])  30.4 us
    all_to_all x1, starting transfers between devices, shards(): arrived = lax.all_to_all(packed, ('zh', 'zl'), 0, 0)  15.2 us
    pallas_call x11, Pallas kernels, call(): pl.pallas_call(body, out_shape=out_shape, in_specs=[smem] * len(scalars)...  15.1 us
    all_to_all x1, starting transfers between devices, shards(): finished = lax.all_to_all(finished, ('zh', 'zl'), 0, 0)  11.7 us
    all_to_all x1, waiting for transfers between devices, shards(): combined = lax.all_to_all(combined, 'x', 0, 0)  8.7 us
    all_to_all x1, blocking collectives, shards(): sums = lax.all_to_all(sums, ('y', 'core'), 0, 0)  7.82 us
    all_to_all x1, starting transfers between devices, shards(): image_rows = lax.all_to_all(units, 'x', 0, 0).reshape(count, width)  4.82 us
  transfers between devices with their start and end apart: 18, of which 10 were waited for; matrix products, arithmetic and copies ran while one was open for 0% of the time, Pallas kernels for 4%

profile of v9, /device:TPU:2, one launch (start us, length us, event | category | flops | bytes accessed | tf_op | source)
XLA Modules:
  0.0 153.9 jit_solution(15508362423821611801)
XLA Ops:
  0.6 0.9 copy-done.2
  1.5 0.9 pack.1
  2.4 15.2 %all-to-all-start = ((bf16[16,72,128]{2,1,0:T(8,128)(2,1)}), bf16[16,72,128]{2,1,0:T(8,128)(2,1)S(1)}, u32[]{:S(2)}, u32[]{:S(2)}) async-start(bf16[16,72,128]{2,1,0:T(8,128)(2,1)} %pack.1), calls=%async_computation | async-start | bytes 589824 | tf_op jit(solution)/shard_map/all_to_all | solution.py:365
  17.6 5.6 %collective-permute-start.2 = (bf16[288,128]{1,0:T(8,128)(2,1)}, bf16[288,128]{1,0:T(8,128)(2,1)S(1)}, u32[]{:S(2)}, u32[]{:S(2)}) collective-permute-start(bf16[288,128]{1,0:T(8,128)(2,1)} %bitcast.18), channel_id=1, source_target_pairs={{0,3},{1,0},{2,1},{3,2},{4,7},{5,4},{6,5},{7,6},{8,11},{9,8},{10,9... | collective-permute-start | bytes 221192 | tf_op jit(solution)/shard_map/ppermute | solution.py:346
  23.2 1.9 %collective-permute-start.1 = (bf16[288,128]{1,0:T(8,128)(2,1)}, bf16[288,128]{1,0:T(8,128)(2,1)S(1)}, u32[]{:S(2)}, u32[]{:S(2)}) collective-permute-start(bf16[288,128]{1,0:T(8,128)(2,1)} %bitcast.19), channel_id=1, source_target_pairs={{0,2},{1,3},{2,0},{3,1},{4,6},{5,7},{6,4},{7,5},{8,10},{9,11},{10,... | collective-permute-start | bytes 221192 | tf_op jit(solution)/shard_map/ppermute | solution.py:346
  25.2 3.0 %collective-permute-start = (bf16[288,128]{1,0:T(8,128)(2,1)}, bf16[288,128]{1,0:T(8,128)(2,1)S(1)}, u32[]{:S(2)}, u32[]{:S(2)}) collective-permute-start(bf16[288,128]{1,0:T(8,128)(2,1)} %bitcast.20), channel_id=1, source_target_pairs={{0,1},{1,2},{2,3},{3,0},{4,5},{5,6},{6,7},{7,4},{8,9},{9,10},{10,1... | collective-permute-start | bytes 221192 | tf_op jit(solution)/shard_map/ppermute | solution.py:346
  28.2 6.0 %collective-permute-done.2.refs_3_ = bf16[288,128]{1,0:T(8,128)(2,1)S(1)} collective-permute-done((bf16[288,128]{1,0:T(8,128)(2,1)}, bf16[288,128]{1,0:T(8,128)(2,1)S(1)}, u32[]{:S(2)}, u32[]{:S(2)}) %collective-permute-start.2) | collective-permute-done | bytes 73760 | tf_op jit(solution)/shard_map/ppermute | solution.py:346
  34.2 5.6 %collective-permute-done.1.refs_2_ = bf16[288,128]{1,0:T(8,128)(2,1)S(1)} collective-permute-done((bf16[288,128]{1,0:T(8,128)(2,1)}, bf16[288,128]{1,0:T(8,128)(2,1)S(1)}, u32[]{:S(2)}, u32[]{:S(2)}) %collective-permute-start.1) | collective-permute-done | bytes 73760 | tf_op jit(solution)/shard_map/ppermute | solution.py:346
  39.8 0.0 collective-permute-done.refs_1_
  39.8 0.9 copy-done
  40.7 0.4 text_unit.1.refs_2_.refs_3_
  41.1 0.0 all-to-all-done.refs_1_
  41.1 1.4 image_unit.1
  42.4 4.8 %all-to-all-start.1 = ((bf16[4,128,1152]{2,1,0:T(8,128)(2,1)}), bf16[4,128,1152]{2,1,0:T(8,128)(2,1)S(1)}, u32[]{:S(2)}, u32[]{:S(2)}) async-start(bf16[4,128,1152]{2,1,0:T(8,128)(2,1)} %image_unit.1), calls=%async_computation.1 | async-start | bytes 2359296 | tf_op jit(solution)/shard_map/all_to_all | solution.py:376
  48.6 0.1 pad_add_fusion.refs_1_
  48.7 0.1 pad_maximum_fusion.refs_0_
  48.8 4.9 %collective-permute-start.5 = (bf16[128,1152]{1,0:T(8,128)(2,1)S(1)}, bf16[128,1152]{1,0:T(8,128)(2,1)S(1)}, u32[]{:S(2)}, u32[]{:S(2)}) collective-permute-start(bf16[128,1152]{1,0:T(8,128)(2,1)S(1)} %text_unit.1.refs_2_.refs_3_), channel_id=1, source_target_pairs={{0,24},{8,0},{16,8},{24,16},{1,25},{9,1},{17,9},{25,17},{2,26},{10... | collective-permute-start | bytes 884744 | tf_op jit(solution)/shard_map/ppermute | solution.py:346
  53.7 2.5 %collective-permute-start.4 = (bf16[128,1152]{1,0:T(8,128)(2,1)S(1)}, bf16[128,1152]{1,0:T(8,128)(2,1)S(1)}, u32[]{:S(2)}, u32[]{:S(2)}) collective-permute-start(bf16[128,1152]{1,0:T(8,128)(2,1)S(1)} %text_unit.1.refs_2_.refs_3_), channel_id=1, source_target_pairs={{0,16},{8,24},{16,0},{24,8},{1,17},{9,25},{17,1},{25,9},{2,18},{10... | collective-permute-start | bytes 884744 | tf_op jit(solution)/shard_map/ppermute | solution.py:346
  56.2 2.9 %collective-permute-start.3 = (bf16[128,1152]{1,0:T(8,128)(2,1)S(1)}, bf16[128,1152]{1,0:T(8,128)(2,1)S(1)}, u32[]{:S(2)}, u32[]{:S(2)}) collective-permute-start(bf16[128,1152]{1,0:T(8,128)(2,1)S(1)} %text_unit.1.refs_2_.refs_3_), channel_id=1, source_target_pairs={{0,8},{8,16},{16,24},{24,0},{1,9},{9,17},{17,25},{25,1},{2,10},{10... | collective-permute-start | bytes 884744 | tf_op jit(solution)/shard_map/ppermute | solution.py:346
  59.1 1.5 all-to-all-done.1
  60.6 1.9 %collective-permute-start.6 = (bf16[512,1152]{1,0:T(8,128)(2,1)S(1)}, bf16[512,1152]{1,0:T(8,128)(2,1)S(1)}, u32[]{:S(2)}, u32[]{:S(2)}) collective-permute-start(bf16[512,1152]{1,0:T(8,128)(2,1)S(1)} %bitcast.14), channel_id=1, source_target_pairs={{0,4},{4,0},{1,5},{5,1},{2,6},{6,2},{3,7},{7,3},{8,12},{12,8},{9,1... | collective-permute-start | bytes 3538952 | tf_op jit(solution)/shard_map/ppermute | solution.py:341
  62.5 1.1 home.1
  63.7 0.3 collective-permute-done.5.refs_5_
  64.0 2.5 %collective-permute-done.4.refs_4_ = bf16[128,1152]{1,0:T(8,128)(2,1)S(1)} collective-permute-done((bf16[128,1152]{1,0:T(8,128)(2,1)S(1)}, bf16[128,1152]{1,0:T(8,128)(2,1)S(1)}, u32[]{:S(2)}, u32[]{:S(2)}) %collective-permute-start.4) | collective-permute-done | bytes 294944 | tf_op jit(solution)/shard_map/ppermute | solution.py:346
  66.5 3.1 %collective-permute-done.3.refs_3_ = bf16[128,1152]{1,0:T(8,128)(2,1)S(1)} collective-permute-done((bf16[128,1152]{1,0:T(8,128)(2,1)S(1)}, bf16[128,1152]{1,0:T(8,128)(2,1)S(1)}, u32[]{:S(2)}, u32[]{:S(2)}) %collective-permute-start.3) | collective-permute-done | bytes 294944 | tf_op jit(solution)/shard_map/ppermute | solution.py:346
  69.6 2.6 %own.1 = (bf16[512,1152]{1,0:T(8,128)(2,1)S(1)}, bf16[512,512]{1,0:T(8,128)(2,1)S(1)}, bf16[512,1152]{1,0:T(8,128)(2,1)S(1)}, f32[24,128]{1,0:T(8,128)S(1)}) custom-call(f32[2]{0:T(128)S(1)} %pad_maximum_fusion.refs_0_, bf16[512,1152]{1,0:T(8,128)(2,1)S(1)} %bitcast.16, bf16[128,1152]{1,0:T(8,128)(2,1)S(1)} %get-tuple-element.24.refs_2_, ...), custom_call_target="tpu_custom_call" | custom-call | flops 1207959552 | bytes 5398528 | tf_op jit(solution)/shard_map/own/pallas_call | solution.py:38
  72.2 0.0 collective-permute-done.6.refs_1_
  72.2 4.1 %other.1 = (bf16[512,1152]{1,0:T(8,128)(2,1)S(1)}, f32[8,8,128]{2,1,0:T(8,128)S(1)}, bf16[128,1152]{1,0:T(8,128)(2,1)S(1)}, bf16[128,1152]{1,0:T(8,128)(2,1)S(1)...) custom-call(f32[2]{0:T(128)S(1)} %pad_maximum_fusion.refs_0_, ...), custom_call_target="tpu_custom_call" | custom-call | flops 2415919104 | bytes 6467584 | tf_op jit(solution)/shard_map/other/pallas_call | solution.py:38
  76.3 1.9 %collective-permute-start.7 = (bf16[512,1152]{1,0:T(8,128)(2,1)S(1)}, bf16[512,1152]{1,0:T(8,128)(2,1)S(1)}, u32[]{:S(2)}, u32[]{:S(2)}) collective-permute-start(bf16[512,1152]{1,0:T(8,128)(2,1)S(1)} %get-tuple-element.31), channel_id=1, source_target_pairs={{0,4},{4,0},{1,5},{5,1},{2,6},{6,2},{3,7},{7,3},{8,12},{12,8},{9,1... | collective-permute-start | bytes 3538952 | tf_op jit(solution)/shard_map/ppermute | solution.py:341
  78.2 7.8 %all_to_all.25.refs_2_ = f32[8,8,128]{2,1,0:T(8,128)S(1)} all-to-all(f32[8,8,128]{2,1,0:T(8,128)S(1)} %get-tuple-element.32), channel_id=1, replica_groups=mesh['zh'=4,'x'=4,'y'=4,'core'=2,'zl'=4] {'y','core'}, dimensions={0} | all-to-all | bytes 65536 | tf_op jit(solution)/shard_map/all_to_all | solution.py:415
  86.0 1.3 combine.1
  87.4 4.8 %all-to-all-start.3 = ((bf16[4,1168,128]{2,1,0:T(8,128)(2,1)}), bf16[4,1168,128]{2,1,0:T(8,128)(2,1)S(1)}, u32[]{:S(2)}, u32[]{:S(2)}) async-start(bf16[4,1168,128]{2,1,0:T(8,128)(2,1)} %combine.1), calls=%async_computation.3 | async-start | bytes 2392064 | tf_op jit(solution)/shard_map/all_to_all | solution.py:422
  92.2 3.1 %collective-permute-start.8 = (bf16[128,1152]{1,0:T(8,128)(2,1)S(1)}, bf16[128,1152]{1,0:T(8,128)(2,1)S(1)}, u32[]{:S(2)}, u32[]{:S(2)}) collective-permute-start(bf16[128,1152]{1,0:T(8,128)(2,1)S(1)} %get-tuple-element.33), channel_id=1, source_target_pairs={{0,24},{8,0},{16,8},{24,16},{1,25},{9,1},{17,9},{25,17},{2,26},{10... | collective-permute-start | bytes 884744 | tf_op jit(solution)/shard_map/ppermute | solution.py:346
  95.2 3.4 %collective-permute-start.9 = (bf16[128,1152]{1,0:T(8,128)(2,1)S(1)}, bf16[128,1152]{1,0:T(8,128)(2,1)S(1)}, u32[]{:S(2)}, u32[]{:S(2)}) collective-permute-start(bf16[128,1152]{1,0:T(8,128)(2,1)S(1)} %get-tuple-element.34), channel_id=1, source_target_pairs={{0,16},{8,24},{16,0},{24,8},{1,17},{9,25},{17,1},{25,9},{2,18},{10... | collective-permute-start | bytes 884744 | tf_op jit(solution)/shard_map/ppermute | solution.py:346
  98.6 8.7 %all-to-all-done.3.refs_2_ = bf16[4,1168,128]{2,1,0:T(8,128)(2,1)S(1)} async-done(((bf16[4,1168,128]{2,1,0:T(8,128)(2,1)}), bf16[4,1168,128]{2,1,0:T(8,128)(2,1)S(1)}, u32[]{:S(2)}, u32[]{:S(2)}) %all-to-all-start.3) | async-done | bytes 1196064 | tf_op jit(solution)/shard_map/all_to_all | solution.py:422
  107.3 1.2 image_finish.1.refs_0_
  108.6 11.7 %all-to-all-start.4 = ((bf16[16,88,128]{2,1,0:T(8,128)(2,1)}), bf16[16,88,128]{2,1,0:T(8,128)(2,1)S(1)}, u32[]{:S(2)}, u32[]{:S(2)}) async-start(bf16[16,88,128]{2,1,0:T(8,128)(2,1)} %hold.1), calls=%async_computation.4 | async-start | bytes 720896 | tf_op jit(solution)/shard_map/all_to_all | solution.py:433
  120.2 2.5 %collective-permute-start.10 = (bf16[128,1152]{1,0:T(8,128)(2,1)S(1)}, bf16[128,1152]{1,0:T(8,128)(2,1)S(1)}, u32[]{:S(2)}, u32[]{:S(2)}) collective-permute-start(bf16[128,1152]{1,0:T(8,128)(2,1)S(1)} %get-tuple-element.38), channel_id=1, source_target_pairs={{0,8},{8,16},{16,24},{24,0},{1,9},{9,17},{17,25},{25,1},{2,10},{10... | collective-permute-start | bytes 884744 | tf_op jit(solution)/shard_map/ppermute | solution.py:346
  122.7 7.8 %collective-permute-done.10.refs_7_ = bf16[128,1152]{1,0:T(8,128)(2,1)S(1)} collective-permute-done((bf16[128,1152]{1,0:T(8,128)(2,1)S(1)}, bf16[128,1152]{1,0:T(8,128)(2,1)S(1)}, u32[]{:S(2)}, u32[]{:S(2)}) %collective-permute-start.10) | collective-permute-done | bytes 294944 | tf_op jit(solution)/shard_map/ppermute | solution.py:346
  130.6 0.7 text_finish.1
  131.2 5.3 %collective-permute-start.11 = (bf16[288,128]{1,0:T(8,128)(2,1)S(1)}, bf16[288,128]{1,0:T(8,128)(2,1)S(1)}, u32[]{:S(2)}, u32[]{:S(2)}) collective-permute-start(bf16[288,128]{1,0:T(8,128)(2,1)S(1)} %get-tuple-element.40), channel_id=1, source_target_pairs={{0,3},{1,0},{2,1},{3,2},{4,7},{5,4},{6,5},{7,6},{8,11},{9,8},{10,9... | collective-permute-start | bytes 221192 | tf_op jit(solution)/shard_map/ppermute | solution.py:346
  136.6 1.9 %collective-permute-start.12 = (bf16[288,128]{1,0:T(8,128)(2,1)S(1)}, bf16[288,128]{1,0:T(8,128)(2,1)S(1)}, u32[]{:S(2)}, u32[]{:S(2)}) collective-permute-start(bf16[288,128]{1,0:T(8,128)(2,1)S(1)} %get-tuple-element.41), channel_id=1, source_target_pairs={{0,2},{1,3},{2,0},{3,1},{4,6},{5,7},{6,4},{7,5},{8,10},{9,11},{10,... | collective-permute-start | bytes 221192 | tf_op jit(solution)/shard_map/ppermute | solution.py:346
  138.5 3.0 %collective-permute-start.13 = (bf16[288,128]{1,0:T(8,128)(2,1)S(1)}, bf16[288,128]{1,0:T(8,128)(2,1)S(1)}, u32[]{:S(2)}, u32[]{:S(2)}) collective-permute-start(bf16[288,128]{1,0:T(8,128)(2,1)S(1)} %get-tuple-element.42), channel_id=1, source_target_pairs={{0,1},{1,2},{2,3},{3,0},{4,5},{5,6},{6,7},{7,4},{8,9},{9,10},{10,1... | collective-permute-start | bytes 221192 | tf_op jit(solution)/shard_map/ppermute | solution.py:346
  141.6 2.2 %collective-permute-done.12.refs_2_ = bf16[288,128]{1,0:T(8,128)(2,1)S(1)} collective-permute-done((bf16[288,128]{1,0:T(8,128)(2,1)S(1)}, bf16[288,128]{1,0:T(8,128)(2,1)S(1)}, u32[]{:S(2)}, u32[]{:S(2)}) %collective-permute-start.12) | collective-permute-done | bytes 73760 | tf_op jit(solution)/shard_map/ppermute | solution.py:346
  143.7 2.8 %collective-permute-done.13.refs_3_ = bf16[288,128]{1,0:T(8,128)(2,1)S(1)} collective-permute-done((bf16[288,128]{1,0:T(8,128)(2,1)S(1)}, bf16[288,128]{1,0:T(8,128)(2,1)S(1)}, u32[]{:S(2)}, u32[]{:S(2)}) %collective-permute-start.13) | collective-permute-done | bytes 73760 | tf_op jit(solution)/shard_map/ppermute | solution.py:346
  146.6 0.7 text_last.1
  147.2 0.8 image_last.1
  148.0 0.6 fusion
  (10 shorter events, 0.0 us)
Async XLA Ops:
  0.6 0.9 copy-start.2
  2.4 38.7 %all-to-all-start = ((bf16[16,72,128]{2,1,0:T(8,128)(2,1)}), bf16[16,72,128]{2,1,0:T(8,128)(2,1)S(1)}, u32[]{:S(2)}, u32[]{:S(2)}) async-start(bf16[16,72,128]{2,1,0:T(8,128)(2,1)} %pack.1), calls=%async_computation | async-start | bytes 589824 | tf_op jit(solution)/shard_map/all_to_all | solution.py:365
  17.6 16.6 %collective-permute-start.2 = (bf16[288,128]{1,0:T(8,128)(2,1)}, bf16[288,128]{1,0:T(8,128)(2,1)S(1)}, u32[]{:S(2)}, u32[]{:S(2)}) collective-permute-start(bf16[288,128]{1,0:T(8,128)(2,1)} %bitcast.18), channel_id=1, source_target_pairs={{0,3},{1,0},{2,1},{3,2},{4,7},{5,4},{6,5},{7,6},{8,11},{9,8},{10,9... | collective-permute-start | bytes 221192 | tf_op jit(solution)/shard_map/ppermute | solution.py:346
  23.2 16.6 %collective-permute-start.1 = (bf16[288,128]{1,0:T(8,128)(2,1)}, bf16[288,128]{1,0:T(8,128)(2,1)S(1)}, u32[]{:S(2)}, u32[]{:S(2)}) collective-permute-start(bf16[288,128]{1,0:T(8,128)(2,1)} %bitcast.19), channel_id=1, source_target_pairs={{0,2},{1,3},{2,0},{3,1},{4,6},{5,7},{6,4},{7,5},{8,10},{9,11},{10,... | collective-permute-start | bytes 221192 | tf_op jit(solution)/shard_map/ppermute | solution.py:346
  25.2 14.6 %collective-permute-start = (bf16[288,128]{1,0:T(8,128)(2,1)}, bf16[288,128]{1,0:T(8,128)(2,1)S(1)}, u32[]{:S(2)}, u32[]{:S(2)}) collective-permute-start(bf16[288,128]{1,0:T(8,128)(2,1)} %bitcast.20), channel_id=1, source_target_pairs={{0,1},{1,2},{2,3},{3,0},{4,5},{5,6},{6,7},{7,4},{8,9},{9,10},{10,1... | collective-permute-start | bytes 221192 | tf_op jit(solution)/shard_map/ppermute | solution.py:346
  39.8 0.9 copy-start
  42.4 18.2 %all-to-all-start.1 = ((bf16[4,128,1152]{2,1,0:T(8,128)(2,1)}), bf16[4,128,1152]{2,1,0:T(8,128)(2,1)S(1)}, u32[]{:S(2)}, u32[]{:S(2)}) async-start(bf16[4,128,1152]{2,1,0:T(8,128)(2,1)} %image_unit.1), calls=%async_computation.1 | async-start | bytes 2359296 | tf_op jit(solution)/shard_map/all_to_all | solution.py:376
  48.8 15.2 %collective-permute-start.5 = (bf16[128,1152]{1,0:T(8,128)(2,1)S(1)}, bf16[128,1152]{1,0:T(8,128)(2,1)S(1)}, u32[]{:S(2)}, u32[]{:S(2)}) collective-permute-start(bf16[128,1152]{1,0:T(8,128)(2,1)S(1)} %text_unit.1.refs_2_.refs_3_), channel_id=1, source_target_pairs={{0,24},{8,0},{16,8},{24,16},{1,25},{9,1},{17,9},{25,17},{2,26},{10... | collective-permute-start | bytes 884744 | tf_op jit(solution)/shard_map/ppermute | solution.py:346
  53.7 12.8 %collective-permute-start.4 = (bf16[128,1152]{1,0:T(8,128)(2,1)S(1)}, bf16[128,1152]{1,0:T(8,128)(2,1)S(1)}, u32[]{:S(2)}, u32[]{:S(2)}) collective-permute-start(bf16[128,1152]{1,0:T(8,128)(2,1)S(1)} %text_unit.1.refs_2_.refs_3_), channel_id=1, source_target_pairs={{0,16},{8,24},{16,0},{24,8},{1,17},{9,25},{17,1},{25,9},{2,18},{10... | collective-permute-start | bytes 884744 | tf_op jit(solution)/shard_map/ppermute | solution.py:346
  56.2 13.4 %collective-permute-start.3 = (bf16[128,1152]{1,0:T(8,128)(2,1)S(1)}, bf16[128,1152]{1,0:T(8,128)(2,1)S(1)}, u32[]{:S(2)}, u32[]{:S(2)}) collective-permute-start(bf16[128,1152]{1,0:T(8,128)(2,1)S(1)} %text_unit.1.refs_2_.refs_3_), channel_id=1, source_target_pairs={{0,8},{8,16},{16,24},{24,0},{1,9},{9,17},{17,25},{25,1},{2,10},{10... | collective-permute-start | bytes 884744 | tf_op jit(solution)/shard_map/ppermute | solution.py:346
  60.6 11.6 %collective-permute-start.6 = (bf16[512,1152]{1,0:T(8,128)(2,1)S(1)}, bf16[512,1152]{1,0:T(8,128)(2,1)S(1)}, u32[]{:S(2)}, u32[]{:S(2)}) collective-permute-start(bf16[512,1152]{1,0:T(8,128)(2,1)S(1)} %bitcast.14), channel_id=1, source_target_pairs={{0,4},{4,0},{1,5},{5,1},{2,6},{6,2},{3,7},{7,3},{8,12},{12,8},{9,1... | collective-permute-start | bytes 3538952 | tf_op jit(solution)/shard_map/ppermute | solution.py:341
  76.3 9.7 %collective-permute-start.7 = (bf16[512,1152]{1,0:T(8,128)(2,1)S(1)}, bf16[512,1152]{1,0:T(8,128)(2,1)S(1)}, u32[]{:S(2)}, u32[]{:S(2)}) collective-permute-start(bf16[512,1152]{1,0:T(8,128)(2,1)S(1)} %get-tuple-element.31), channel_id=1, source_target_pairs={{0,4},{4,0},{1,5},{5,1},{2,6},{6,2},{3,7},{7,3},{8,12},{12,8},{9,1... | collective-permute-start | bytes 3538952 | tf_op jit(solution)/shard_map/ppermute | solution.py:341
  87.4 20.0 %all-to-all-start.3 = ((bf16[4,1168,128]{2,1,0:T(8,128)(2,1)}), bf16[4,1168,128]{2,1,0:T(8,128)(2,1)S(1)}, u32[]{:S(2)}, u32[]{:S(2)}) async-start(bf16[4,1168,128]{2,1,0:T(8,128)(2,1)} %combine.1), calls=%async_computation.3 | async-start | bytes 2392064 | tf_op jit(solution)/shard_map/all_to_all | solution.py:422
  92.2 16.4 %collective-permute-start.8 = (bf16[128,1152]{1,0:T(8,128)(2,1)S(1)}, bf16[128,1152]{1,0:T(8,128)(2,1)S(1)}, u32[]{:S(2)}, u32[]{:S(2)}) collective-permute-start(bf16[128,1152]{1,0:T(8,128)(2,1)S(1)} %get-tuple-element.33), channel_id=1, source_target_pairs={{0,24},{8,0},{16,8},{24,16},{1,25},{9,1},{17,9},{25,17},{2,26},{10... | collective-permute-start | bytes 884744 | tf_op jit(solution)/shard_map/ppermute | solution.py:346
  95.2 13.3 %collective-permute-start.9 = (bf16[128,1152]{1,0:T(8,128)(2,1)S(1)}, bf16[128,1152]{1,0:T(8,128)(2,1)S(1)}, u32[]{:S(2)}, u32[]{:S(2)}) collective-permute-start(bf16[128,1152]{1,0:T(8,128)(2,1)S(1)} %get-tuple-element.34), channel_id=1, source_target_pairs={{0,16},{8,24},{16,0},{24,8},{1,17},{9,25},{17,1},{25,9},{2,18},{10... | collective-permute-start | bytes 884744 | tf_op jit(solution)/shard_map/ppermute | solution.py:346
  108.5 22.0 %copy-start.1 = (bf16[128,288]{0,1:T(8,128)(2,1)S(1)}, bf16[128,288]{0,1:T(8,128)(2,1)}, u32[]{:S(2)}) copy-start(bf16[128,288]{0,1:T(8,128)(2,1)} %param.5) | copy-start | bytes 221188
  108.6 38.7 %all-to-all-start.4 = ((bf16[16,88,128]{2,1,0:T(8,128)(2,1)}), bf16[16,88,128]{2,1,0:T(8,128)(2,1)S(1)}, u32[]{:S(2)}, u32[]{:S(2)}) async-start(bf16[16,88,128]{2,1,0:T(8,128)(2,1)} %hold.1), calls=%async_computation.4 | async-start | bytes 720896 | tf_op jit(solution)/shard_map/all_to_all | solution.py:433
  120.2 10.3 %collective-permute-start.10 = (bf16[128,1152]{1,0:T(8,128)(2,1)S(1)}, bf16[128,1152]{1,0:T(8,128)(2,1)S(1)}, u32[]{:S(2)}, u32[]{:S(2)}) collective-permute-start(bf16[128,1152]{1,0:T(8,128)(2,1)S(1)} %get-tuple-element.38), channel_id=1, source_target_pairs={{0,8},{8,16},{16,24},{24,0},{1,9},{9,17},{17,25},{25,1},{2,10},{10... | collective-permute-start | bytes 884744 | tf_op jit(solution)/shard_map/ppermute | solution.py:346
  131.2 10.3 %collective-permute-start.11 = (bf16[288,128]{1,0:T(8,128)(2,1)S(1)}, bf16[288,128]{1,0:T(8,128)(2,1)S(1)}, u32[]{:S(2)}, u32[]{:S(2)}) collective-permute-start(bf16[288,128]{1,0:T(8,128)(2,1)S(1)} %get-tuple-element.40), channel_id=1, source_target_pairs={{0,3},{1,0},{2,1},{3,2},{4,7},{5,4},{6,5},{7,6},{8,11},{9,8},{10,9... | collective-permute-start | bytes 221192 | tf_op jit(solution)/shard_map/ppermute | solution.py:346
  136.6 7.1 %collective-permute-start.12 = (bf16[288,128]{1,0:T(8,128)(2,1)S(1)}, bf16[288,128]{1,0:T(8,128)(2,1)S(1)}, u32[]{:S(2)}, u32[]{:S(2)}) collective-permute-start(bf16[288,128]{1,0:T(8,128)(2,1)S(1)} %get-tuple-element.41), channel_id=1, source_target_pairs={{0,2},{1,3},{2,0},{3,1},{4,6},{5,7},{6,4},{7,5},{8,10},{9,11},{10,... | collective-permute-start | bytes 221192 | tf_op jit(solution)/shard_map/ppermute | solution.py:346
  138.5 8.0 %collective-permute-start.13 = (bf16[288,128]{1,0:T(8,128)(2,1)S(1)}, bf16[288,128]{1,0:T(8,128)(2,1)S(1)}, u32[]{:S(2)}, u32[]{:S(2)}) collective-permute-start(bf16[288,128]{1,0:T(8,128)(2,1)S(1)} %get-tuple-element.42), channel_id=1, source_target_pairs={{0,1},{1,2},{2,3},{3,0},{4,5},{5,6},{6,7},{7,4},{8,9},{9,10},{10,1... | collective-permute-start | bytes 221192 | tf_op jit(solution)/shard_map/ppermute | solution.py:346

commit v10 on v9

--- a/solution.py
+++ b/solution.py
@@ -14,7 +14,7 @@
 rest = 32
 chunk_rows = 72
 carry_rows = 16
-sent_rows = 88
+sent_rows = 80
 tiles = 9
 vmem = pl.BlockSpec(memory_space=pltpu.VMEM)
 smem = pl.BlockSpec(memory_space=pltpu.SMEM)
@@ -214,9 +214,7 @@
     write_sums(sums_out, sums, home_sums)
 
 
-def other_kernel(
-    scales, left, right, own_sums, own_weights, own_left, back, sums_out, b0, b1, b2, b3, weights
-):
+def other_kernel(scales, left, right, own_sums, back, weights, sums_out):
     sums = []
     for start in range(0, left.shape[0], tile):
         here = pl.ds(start, tile)
@@ -231,14 +229,22 @@
     for k in range(3):
         found = total([s[k] for s in sums]) + own_sums[8 * k : 8 * k + 8, :]
         value = jnp.where(row == k, jnp.sum(found, axis=0, keepdims=True), value)
-    for k in range(sums_out.shape[0]):
-        sums_out[k] = value
+    carry = carry_of(value)
+    sums_out[...] = carry
+    rows = left.shape[0]
+    back[rows:, :lanes] = carry.astype(jnp.bfloat16)
+    back[rows:, lanes:] = jnp.zeros((carry_rows, back.shape[1] - lanes), jnp.bfloat16)
+
+
+def text_kernel(own_weights, other_weights, own_left, other_left, *backs):
     contract = (((0,), (0,)), ((), ()))
-    part = b0.shape[0]
+    part = backs[0].shape[0]
     value = lax.dot_general(
         own_weights[...], own_left[...], contract, preferred_element_type=jnp.float32
-    ) + lax.dot_general(weights[...], left[...], contract, preferred_element_type=jnp.float32)
-    for k, out in enumerate((b0, b1, b2, b3)):
+    ) + lax.dot_general(
+        other_weights[...], other_left[...], contract, preferred_element_type=jnp.float32
+    )
+    for k, out in enumerate(backs):
         out[...] = value[k * part : (k + 1) * part].astype(jnp.bfloat16)
 
 
@@ -260,7 +266,8 @@
 def combine_kernel(own, given, sums, out):
     count, all_rows, _ = out.shape
     block = own.shape[0] // count
-    carry = carry_of(total([sums[k] for k in range(sums.shape[0])])).astype(jnp.bfloat16)
+    carry = sums[...] + wide(given, pl.ds(own.shape[0], carry_rows), pl.ds(0, lanes))
+    carry = carry_of(carry[:8]).astype(jnp.bfloat16)
     for k in range(count):
         rows = pl.ds(k * block, block)
         for t in range(tiles):
@@ -281,7 +288,7 @@
     heads = arrived.shape[0] // strips
     block = heads * piece
     tail = pl.ds(tiles * block, carry_rows)
-    carry = carry_of(total([wide(backs, k, tail, slice(None)) for k in range(count)])[:8])
+    carry = carry_of(total([wide(backs, k, tail, slice(None)) for k in range(count)])[:8])[:8]
     for h in range(heads):
         units, inverse = image_units(place, arrived, h, group)
         grads = []
@@ -324,7 +331,7 @@
     heads = len(values) // strips
     found = []
     for k in range(strips):
-        chunk = total([values[h * strips + k][carry_rows:] for h in range(heads)])
+        chunk = total([values[h * strips + k][8:] for h in range(heads)])
         last = chunk[2 * piece :]
         groups = [last] + [pltpu.roll(last, lanes - rest * g, 1) for g in range(1, 4)]
         last = jnp.concatenate(groups, axis=0)
@@ -333,8 +340,9 @@
         rows = jnp.concatenate([f[t] for f in found], axis=0).T
         count = lanes if t < 2 else rest
         out[t * lanes : t * lanes + count, :] = rows[:count].astype(jnp.bfloat16)
-    sums = total([v[:8] for v in values])
-    sums_out[...] = jnp.broadcast_to(jnp.sum(sums, axis=1, keepdims=True), sums.shape)
+    sums = jnp.sum(total([v[:8] for v in values]), axis=1, keepdims=True)
+    for k in range(sums_out.shape[0]):
+        sums_out[k] = jnp.broadcast_to(sums, sums_out.shape[1:])
 
 
 def swap_core(value):
@@ -371,7 +379,7 @@
         "image_unit",
         [arrived],
         scalars=[place],
-        after=[home_text],
+        after=parts[1:] + [scales, spot],
     )
     image_rows = lax.all_to_all(units, "x", 0, 0).reshape(count, width)
     other_rows = swap_core(image_rows)
@@ -400,24 +408,33 @@
         flops=4 * area * width,
         special=2 * area,
     )
-    other_back, sums, *text_backs = call(
+    other_back, other_weights, sums = call(
         other_kernel,
-        [shape((count, width)), shape((y_count * 2, 8, lanes), f32)]
-        + [shape((block, width))] * y_count,
+        [
+            shape((count + carry_rows, width)),
+            shape((count, columns)),
+            shape((carry_rows, lanes), f32),
+        ],
         "other",
-        [other_rows, right, own_sums, own_weights, image_rows],
+        [other_rows, right, own_sums],
         scalars=[scales],
-        flops=8 * area * width,
+        flops=4 * area * width,
         special=2 * area,
-        scratch=[pltpu.VMEM((count, columns), jnp.bfloat16)],
     )
     given_back = swap_core(other_back)
-    sums = lax.all_to_all(sums, ("y", "core"), 0, 0)
+    text_backs = call(
+        text_kernel,
+        [shape((block, width))] * y_count,
+        "text_back",
+        [own_weights, other_weights, image_rows, other_rows],
+        flops=4 * area * width,
+    )
     (combined,) = call(
         combine_kernel,
         [shape((x_count, tiles * block + carry_rows, lanes))],
         "combine",
         [own_back, given_back, sums],
+        after=text_backs[:1],
     )
     combined = lax.all_to_all(combined, "x", 0, 0)
     (finished,) = call(
@@ -432,13 +449,17 @@
     finished = hold(finished, moved[1:3])
     finished = lax.all_to_all(finished, ("zh", "zl"), 0, 0)
     text_parts = call(
-        text_finish_kernel, [shape((strip, rows))] * strips, "text_finish", parts + moved
+        text_finish_kernel, [shape((strip, rows))] * strips, "text_finish", parts + moved, flops=200 * count * block * width
     )
     given = [text_parts[0]] + [shift(text_parts[k], "zl", -k) for k in range(1, strips)]
     (grad_text,) = call(text_last_kernel, [shape((strip, rows))], "text_last", given)
     grad_image, sums = call(
-        image_last_kernel, [shape((strip, rows)), shape((8, lanes), f32)], "image_last", [finished]
-    )
+        image_last_kernel,
+        [shape((strip, rows)), shape((y_count, 8, lanes), f32)],
+        "image_last",
+        [finished],
+    )
+    sums = jnp.sum(lax.all_to_all(sums, "y", 0, 0), axis=0)
     pairs_count = rows * 4 * x_count * y_count * 2
     return (
         sums[0, 0] / pairs_count,

time: 155 us -> 151 us (0.974)
  blocking collectives: 7.82 us -> 0 us
  starting transfers between devices: 80.4 us -> 83.8 us
    ppermute x12, waiting for transfers between devices: 30.4 us -> 15 us  [shift(): lax.ppermute(value, axis, [(i, (i + k) % count) for i in range(count)])]
    all_to_all x1, waiting for transfers between devices: 0.01 us -> 10.1 us  [shards(): finished = lax.all_to_all(finished, ('zh', 'zl'), 0, 0)]
    all_to_all x1 -> x0, blocking collectives: 7.82 us -> none  [shards(): sums = lax.all_to_all(sums, ('y', 'core'), 0, 0)]
    all_to_all x0 -> x1, waiting for transfers between devices: none -> 4.67 us  [shards(): sums = jnp.sum(lax.all_to_all(sums, 'y', 0, 0), axis=0)]
    all_to_all x0 -> x1, starting transfers between devices: none -> 4.19 us  [shards(): sums = jnp.sum(lax.all_to_all(sums, 'y', 0, 0), axis=0)]
    pallas_call x11 -> x12, Pallas kernels: 15.1 us -> 16.1 us  [call(): pl.pallas_call(body, out_shape=out_shape, in_specs=[smem] * len(scalars)...]
  transfers between devices with their start and end apart: 18 -> 19, of which waited for: 10 -> 9; matrix products, arithmetic and copies ran while one was open for 0% -> 0% of each run, Pallas kernels for 4% -> 7%
where the time goes in v10:
time: 151 us; the launch traced here: 150 us
  starting transfers between devices  83.8 us (55%)
  waiting for transfers between devices  41.4 us (27%)
  Pallas kernels  16.1 us (11%)
  between operations  7.48 us (5%)
    ppermute x12, starting transfers between devices, shift(): lax.ppermute(value, axis, [(i, (i + k) % count) for i in range(count)])  39.3 us
    pallas_call x12, Pallas kernels, call(): pl.pallas_call(body, out_shape=out_shape, in_specs=[smem] * len(scalars)...  16.1 us
    all_to_all x1, starting transfers between devices, shards(): arrived = lax.all_to_all(packed, ('zh', 'zl'), 0, 0)  15.2 us
    ppermute x12, waiting for transfers between devices, shift(): lax.ppermute(value, axis, [(i, (i + k) % count) for i in range(count)])  15 us
    all_to_all x1, starting transfers between devices, shards(): finished = lax.all_to_all(finished, ('zh', 'zl'), 0, 0)  11.5 us
    all_to_all x1, waiting for transfers between devices, shards(): finished = lax.all_to_all(finished, ('zh', 'zl'), 0, 0)  10.1 us
    all_to_all x1, waiting for transfers between devices, shards(): combined = lax.all_to_all(combined, 'x', 0, 0)  7.72 us
    all_to_all x1, starting transfers between devices, shards(): image_rows = lax.all_to_all(units, 'x', 0, 0).reshape(count, width)  4.96 us
  transfers between devices with their start and end apart: 19, of which 9 were waited for; matrix products, arithmetic and copies ran while one was open for 0% of the time, Pallas kernels for 7%

profile of v10, /device:TPU:2, one launch (start us, length us, event | category | flops | bytes accessed | tf_op | source)
XLA Modules:
  0.0 150.3 jit_solution(5468308771804270345)
XLA Ops:
  0.6 0.9 copy-done.1
  1.5 0.9 pack.1
  2.4 15.2 %all-to-all-start = ((bf16[16,72,128]{2,1,0:T(8,128)(2,1)}), bf16[16,72,128]{2,1,0:T(8,128)(2,1)S(1)}, u32[]{:S(2)}, u32[]{:S(2)}) async-start(bf16[16,72,128]{2,1,0:T(8,128)(2,1)} %pack.1), calls=%async_computation | async-start | bytes 589824 | tf_op jit(solution)/shard_map/all_to_all | solution.py:373
  17.6 5.6 %collective-permute-start.2 = (bf16[288,128]{1,0:T(8,128)(2,1)}, bf16[288,128]{1,0:T(8,128)(2,1)S(1)}, u32[]{:S(2)}, u32[]{:S(2)}) collective-permute-start(bf16[288,128]{1,0:T(8,128)(2,1)} %bitcast.18), channel_id=1, source_target_pairs={{0,3},{1,0},{2,1},{3,2},{4,7},{5,4},{6,5},{7,6},{8,11},{9,8},{10,9... | collective-permute-start | bytes 221192 | tf_op jit(solution)/shard_map/ppermute | solution.py:354
  23.2 1.9 %collective-permute-start.1 = (bf16[288,128]{1,0:T(8,128)(2,1)}, bf16[288,128]{1,0:T(8,128)(2,1)S(1)}, u32[]{:S(2)}, u32[]{:S(2)}) collective-permute-start(bf16[288,128]{1,0:T(8,128)(2,1)} %bitcast.19), channel_id=1, source_target_pairs={{0,2},{1,3},{2,0},{3,1},{4,6},{5,7},{6,4},{7,5},{8,10},{9,11},{10,... | collective-permute-start | bytes 221192 | tf_op jit(solution)/shard_map/ppermute | solution.py:354
  25.2 3.0 %collective-permute-start = (bf16[288,128]{1,0:T(8,128)(2,1)}, bf16[288,128]{1,0:T(8,128)(2,1)S(1)}, u32[]{:S(2)}, u32[]{:S(2)}) collective-permute-start(bf16[288,128]{1,0:T(8,128)(2,1)} %bitcast.20), channel_id=1, source_target_pairs={{0,1},{1,2},{2,3},{3,0},{4,5},{5,6},{6,7},{7,4},{8,9},{9,10},{10,1... | collective-permute-start | bytes 221192 | tf_op jit(solution)/shard_map/ppermute | solution.py:354
  29.5 0.1 pad_add_fusion.refs_6_.refs_1_
  29.6 0.1 pad_maximum_fusion.refs_5_.refs_0_
  29.7 4.5 %collective-permute-done.2.refs_4_.refs_3_ = bf16[288,128]{1,0:T(8,128)(2,1)S(1)} collective-permute-done((bf16[288,128]{1,0:T(8,128)(2,1)}, bf16[288,128]{1,0:T(8,128)(2,1)S(1)}, u32[]{:S(2)}, u32[]{:S(2)}) %collective-permute-start.2) | collective-permute-done | bytes 73760 | tf_op jit(solution)/shard_map/ppermute | solution.py:354
  34.2 5.6 %collective-permute-done.1.refs_3_.refs_2_ = bf16[288,128]{1,0:T(8,128)(2,1)S(1)} collective-permute-done((bf16[288,128]{1,0:T(8,128)(2,1)}, bf16[288,128]{1,0:T(8,128)(2,1)S(1)}, u32[]{:S(2)}, u32[]{:S(2)}) %collective-permute-start.1) | collective-permute-done | bytes 73760 | tf_op jit(solution)/shard_map/ppermute | solution.py:354
  39.8 0.0 collective-permute-done.refs_2_.refs_1_
  39.8 0.0 all-to-all-done.refs_1_
  39.8 1.4 image_unit.1
  41.2 5.0 %all-to-all-start.1 = ((bf16[4,128,1152]{2,1,0:T(8,128)(2,1)}), bf16[4,128,1152]{2,1,0:T(8,128)(2,1)S(1)}, u32[]{:S(2)}, u32[]{:S(2)}) async-start(bf16[4,128,1152]{2,1,0:T(8,128)(2,1)} %image_unit.1), calls=%async_computation.1 | async-start | bytes 2359296 | tf_op jit(solution)/shard_map/all_to_all | solution.py:384
  46.1 0.4 text_unit.1.refs_3_
  46.5 4.9 %collective-permute-start.5 = (bf16[128,1152]{1,0:T(8,128)(2,1)S(1)}, bf16[128,1152]{1,0:T(8,128)(2,1)S(1)}, u32[]{:S(2)}, u32[]{:S(2)}) collective-permute-start(bf16[128,1152]{1,0:T(8,128)(2,1)S(1)} %text_unit.1.refs_3_), channel_id=1, source_target_pairs={{0,24},{8,0},{16,8},{24,16},{1,25},{9,1},{17,9},{25,17},{2,26},{10... | collective-permute-start | bytes 884744 | tf_op jit(solution)/shard_map/ppermute | solution.py:354
  51.4 2.5 %collective-permute-start.4 = (bf16[128,1152]{1,0:T(8,128)(2,1)S(1)}, bf16[128,1152]{1,0:T(8,128)(2,1)S(1)}, u32[]{:S(2)}, u32[]{:S(2)}) collective-permute-start(bf16[128,1152]{1,0:T(8,128)(2,1)S(1)} %text_unit.1.refs_3_), channel_id=1, source_target_pairs={{0,16},{8,24},{16,0},{24,8},{1,17},{9,25},{17,1},{25,9},{2,18},{10... | collective-permute-start | bytes 884744 | tf_op jit(solution)/shard_map/ppermute | solution.py:354
  54.0 2.9 %collective-permute-start.3 = (bf16[128,1152]{1,0:T(8,128)(2,1)S(1)}, bf16[128,1152]{1,0:T(8,128)(2,1)S(1)}, u32[]{:S(2)}, u32[]{:S(2)}) collective-permute-start(bf16[128,1152]{1,0:T(8,128)(2,1)S(1)} %text_unit.1.refs_3_), channel_id=1, source_target_pairs={{0,8},{8,16},{16,24},{24,0},{1,9},{9,17},{17,25},{25,1},{2,10},{10... | collective-permute-start | bytes 884744 | tf_op jit(solution)/shard_map/ppermute | solution.py:354
  56.9 2.6 %all-to-all-done.1 = bf16[4,128,1152]{2,1,0:T(8,128)(2,1)S(1)} async-done(((bf16[4,128,1152]{2,1,0:T(8,128)(2,1)}), bf16[4,128,1152]{2,1,0:T(8,128)(2,1)S(1)}, u32[]{:S(2)}, u32[]{:S(2)}) %all-to-all-start.1) | async-done | bytes 1179680 | tf_op jit(solution)/shard_map/all_to_all | solution.py:384
  59.5 1.9 %collective-permute-start.6 = (bf16[512,1152]{1,0:T(8,128)(2,1)S(1)}, bf16[512,1152]{1,0:T(8,128)(2,1)S(1)}, u32[]{:S(2)}, u32[]{:S(2)}) collective-permute-start(bf16[512,1152]{1,0:T(8,128)(2,1)S(1)} %bitcast.14), channel_id=1, source_target_pairs={{0,4},{4,0},{1,5},{5,1},{2,6},{6,2},{3,7},{7,3},{8,12},{12,8},{9,1... | collective-permute-start | bytes 3538952 | tf_op jit(solution)/shard_map/ppermute | solution.py:349
  61.4 1.1 home.1
  62.6 1.7 %collective-permute-done.4.refs_4_ = bf16[128,1152]{1,0:T(8,128)(2,1)S(1)} collective-permute-done((bf16[128,1152]{1,0:T(8,128)(2,1)S(1)}, bf16[128,1152]{1,0:T(8,128)(2,1)S(1)}, u32[]{:S(2)}, u32[]{:S(2)}) %collective-permute-start.4) | collective-permute-done | bytes 294944 | tf_op jit(solution)/shard_map/ppermute | solution.py:354
  64.3 3.1 %collective-permute-done.3.refs_3_ = bf16[128,1152]{1,0:T(8,128)(2,1)S(1)} collective-permute-done((bf16[128,1152]{1,0:T(8,128)(2,1)S(1)}, bf16[128,1152]{1,0:T(8,128)(2,1)S(1)}, u32[]{:S(2)}, u32[]{:S(2)}) %collective-permute-start.3) | collective-permute-done | bytes 294944 | tf_op jit(solution)/shard_map/ppermute | solution.py:354
  67.4 2.6 %own.1 = (bf16[512,1152]{1,0:T(8,128)(2,1)S(1)}, bf16[512,512]{1,0:T(8,128)(2,1)S(1)}, bf16[512,1152]{1,0:T(8,128)(2,1)S(1)}, f32[24,128]{1,0:T(8,128)S(1)}) custom-call(f32[2]{0:T(128)S(1)} %pad_maximum_fusion.refs_5_.refs_0_, bf16[512,1152]{1,0:T(8,128)(2,1)S(1)} %bitcast.16, bf16[128,1152]{1,0:T(8,128)(2,1)S(1)} %get-tuple-element.25.refs_2_, ...), custom_call_target="tpu_custom_call" | custom-call | flops 1207959552 | bytes 5398528 | tf_op jit(solution)/shard_map/own/pallas_call | solution.py:38
  70.0 0.0 collective-permute-done.6.refs_1_.refs_3_
  70.0 2.6 %other.1 = (bf16[528,1152]{1,0:T(8,128)(2,1)S(1)}, bf16[512,512]{1,0:T(8,128)(2,1)S(1)}, f32[16,128]{1,0:T(8,128)S(1)}) custom-call(f32[2]{0:T(128)S(1)} %pad_maximum_fusion.refs_5_.refs_0_, bf16[512,1152]{1,0:T(8,128)(2,1)S(1)} %collective-permute-done.6.refs_1_.refs_3_, bf16[512,1152]{1,0:T(8,128)(2,1)S(1)} %get-tuple-element.29.refs_2_, ...), custom_call_target="tpu_custom_call" | custom-call | flops 1207959552 | bytes 4120576 | tf_op jit(solution)/shard_map/other/pallas_call | solution.py:38
  72.6 1.9 %collective-permute-start.7 = (bf16[528,1152]{1,0:T(8,128)(2,1)S(1)}, bf16[528,1152]{1,0:T(8,128)(2,1)S(1)}, u32[]{:S(2)}, u32[]{:S(2)}) collective-permute-start(bf16[528,1152]{1,0:T(8,128)(2,1)S(1)} %get-tuple-element.31), channel_id=1, source_target_pairs={{0,4},{4,0},{1,5},{5,1},{2,6},{6,2},{3,7},{7,3},{8,12},{12,8},{9,1... | collective-permute-start | bytes 3649544 | tf_op jit(solution)/shard_map/ppermute | solution.py:349
  74.5 1.6 %text_back.1 = (bf16[128,1152]{1,0:T(8,128)(2,1)S(1)}, bf16[128,1152]{1,0:T(8,128)(2,1)S(1)}, bf16[128,1152]{1,0:T(8,128)(2,1)S(1)}, bf16[128,1152]{1,0:T(8,128)(2,1)S(1)}) custom-call(bf16[512,512]{1,0:T(8,128)(2,1)S(1)} %get-tuple-element.33.refs_0_, bf16[512,512]{1,0:T(8,128)(2,1)S(1)} %get-tuple-element.34.refs_1_, bf16[512,1152]{1,0:T(8,128)(2,1)S(1)} %bitcast.17, ...), custom_call_target="tpu_custom_call" | custom-call | flops 1207959552 | bytes 4587520 | tf_op jit(solution)/shard_map/text_back/pallas_call | solution.py:38
  76.1 1.3 collective-permute-done.7.refs_1_
  77.4 1.4 combine.1
  78.7 4.8 %all-to-all-start.2 = ((bf16[4,1168,128]{2,1,0:T(8,128)(2,1)}), bf16[4,1168,128]{2,1,0:T(8,128)(2,1)S(1)}, u32[]{:S(2)}, u32[]{:S(2)}) async-start(bf16[4,1168,128]{2,1,0:T(8,128)(2,1)} %combine.1), calls=%async_computation.2 | async-start | bytes 2392064 | tf_op jit(solution)/shard_map/all_to_all | solution.py:439
  83.5 2.5 %collective-permute-start.8 = (bf16[128,1152]{1,0:T(8,128)(2,1)S(1)}, bf16[128,1152]{1,0:T(8,128)(2,1)S(1)}, u32[]{:S(2)}, u32[]{:S(2)}) collective-permute-start(bf16[128,1152]{1,0:T(8,128)(2,1)S(1)} %get-tuple-element.36), channel_id=1, source_target_pairs={{0,24},{8,0},{16,8},{24,16},{1,25},{9,1},{17,9},{25,17},{2,26},{10... | collective-permute-start | bytes 884744 | tf_op jit(solution)/shard_map/ppermute | solution.py:354
  86.0 2.5 %collective-permute-start.9 = (bf16[128,1152]{1,0:T(8,128)(2,1)S(1)}, bf16[128,1152]{1,0:T(8,128)(2,1)S(1)}, u32[]{:S(2)}, u32[]{:S(2)}) collective-permute-start(bf16[128,1152]{1,0:T(8,128)(2,1)S(1)} %get-tuple-element.37), channel_id=1, source_target_pairs={{0,16},{8,24},{16,0},{24,8},{1,17},{9,25},{17,1},{25,9},{2,18},{10... | collective-permute-start | bytes 884744 | tf_op jit(solution)/shard_map/ppermute | solution.py:354
  88.5 2.8 %collective-permute-start.10 = (bf16[128,1152]{1,0:T(8,128)(2,1)S(1)}, bf16[128,1152]{1,0:T(8,128)(2,1)}, u32[]{:S(2)}, u32[]{:S(2)}) collective-permute-start(bf16[128,1152]{1,0:T(8,128)(2,1)S(1)} %get-tuple-element.40), channel_id=1, source_target_pairs={{0,8},{8,16},{16,24},{24,0},{1,9},{9,17},{17,25},{25,1},{2,10},{10... | collective-permute-start | bytes 884744 | tf_op jit(solution)/shard_map/ppermute | solution.py:354
  91.3 7.7 %all-to-all-done.2.refs_2_ = bf16[4,1168,128]{2,1,0:T(8,128)(2,1)S(1)} async-done(((bf16[4,1168,128]{2,1,0:T(8,128)(2,1)}), bf16[4,1168,128]{2,1,0:T(8,128)(2,1)S(1)}, u32[]{:S(2)}, u32[]{:S(2)}) %all-to-all-start.2) | async-done | bytes 1196064 | tf_op jit(solution)/shard_map/all_to_all | solution.py:439
  99.0 1.2 image_finish.1.refs_0_
  100.2 11.5 %all-to-all-start.3 = ((bf16[16,80,128]{2,1,0:T(8,128)(2,1)}), bf16[16,80,128]{2,1,0:T(8,128)(2,1)S(1)}, u32[]{:S(2)}, u32[]{:S(2)}) async-start(bf16[16,80,128]{2,1,0:T(8,128)(2,1)} %hold.1), calls=%async_computation.3 | async-start | bytes 655360 | tf_op jit(solution)/shard_map/all_to_all | solution.py:450
  111.8 1.6 %text_finish.1 = (bf16[288,128]{1,0:T(8,128)(2,1)S(1)}, bf16[288,128]{1,0:T(8,128)(2,1)S(1)}, bf16[288,128]{1,0:T(8,128)(2,1)S(1)}, bf16[288,128]{1,0:T(8,128)(2,1)S(1)}) custom-call(bf16[288,128]{1,0:T(8,128)(2,1)S(1)} %bitcast.22, bf16[288,128]{1,0:T(8,128)(2,1)S(1)} %collective-permute-done.refs_2_.refs_1_, ...), custom_call_target="tpu_custom_call" | custom-call | flops 15099494400 | bytes 1769472 | tf_op jit(solution)/shard_map/text_finish/pallas_call | solution.py:38
  113.4 5.6 %collective-permute-start.11 = (bf16[288,128]{1,0:T(8,128)(2,1)S(1)}, bf16[288,128]{1,0:T(8,128)(2,1)S(1)}, u32[]{:S(2)}, u32[]{:S(2)}) collective-permute-start(bf16[288,128]{1,0:T(8,128)(2,1)S(1)} %get-tuple-element.42), channel_id=1, source_target_pairs={{0,3},{1,0},{2,1},{3,2},{4,7},{5,4},{6,5},{7,6},{8,11},{9,8},{10,9... | collective-permute-start | bytes 221192 | tf_op jit(solution)/shard_map/ppermute | solution.py:354
  119.1 1.9 %collective-permute-start.12 = (bf16[288,128]{1,0:T(8,128)(2,1)S(1)}, bf16[288,128]{1,0:T(8,128)(2,1)S(1)}, u32[]{:S(2)}, u32[]{:S(2)}) collective-permute-start(bf16[288,128]{1,0:T(8,128)(2,1)S(1)} %get-tuple-element.43), channel_id=1, source_target_pairs={{0,2},{1,3},{2,0},{3,1},{4,6},{5,7},{6,4},{7,5},{8,10},{9,11},{10,... | collective-permute-start | bytes 221192 | tf_op jit(solution)/shard_map/ppermute | solution.py:354
  121.0 3.0 %collective-permute-start.13 = (bf16[288,128]{1,0:T(8,128)(2,1)S(1)}, bf16[288,128]{1,0:T(8,128)(2,1)S(1)}, u32[]{:S(2)}, u32[]{:S(2)}) collective-permute-start(bf16[288,128]{1,0:T(8,128)(2,1)S(1)} %get-tuple-element.44), channel_id=1, source_target_pairs={{0,1},{1,2},{2,3},{3,0},{4,5},{5,6},{6,7},{7,4},{8,9},{9,10},{10,1... | collective-permute-start | bytes 221192 | tf_op jit(solution)/shard_map/ppermute | solution.py:354
  124.0 10.1 %all-to-all-done.3.refs_0_ = bf16[16,80,128]{2,1,0:T(8,128)(2,1)S(1)} async-done(((bf16[16,80,128]{2,1,0:T(8,128)(2,1)}), bf16[16,80,128]{2,1,0:T(8,128)(2,1)S(1)}, u32[]{:S(2)}, u32[]{:S(2)}) %all-to-all-start.3) | async-done | bytes 327712 | tf_op jit(solution)/shard_map/all_to_all | solution.py:450
  134.1 0.8 image_last.1
  134.9 4.2 %all-to-all-start.4 = ((f32[4,8,128]{2,1,0:T(8,128)}), f32[4,8,128]{2,1,0:T(8,128)S(1)}, u32[]{:S(2)}, u32[]{:S(2)}) async-start(f32[4,8,128]{2,1,0:T(8,128)} %get-tuple-element.38), calls=%async_computation.4 | async-start | bytes 32768 | tf_op jit(solution)/shard_map/all_to_all | solution.py:462
  139.1 0.0 collective-permute-done.11.refs_1_
  139.1 0.7 text_last.1
  139.8 4.7 %all-to-all-done.4 = f32[4,8,128]{2,1,0:T(8,128)S(1)} async-done(((f32[4,8,128]{2,1,0:T(8,128)}), f32[4,8,128]{2,1,0:T(8,128)S(1)}, u32[]{:S(2)}, u32[]{:S(2)}) %all-to-all-start.4) | async-done | bytes 16416 | tf_op jit(solution)/shard_map/all_to_all | solution.py:462
  144.5 0.6 fusion
  (11 shorter events, 0.0 us)
Async XLA Ops:
  0.6 0.9 copy-start.1
  2.4 37.4 %all-to-all-start = ((bf16[16,72,128]{2,1,0:T(8,128)(2,1)}), bf16[16,72,128]{2,1,0:T(8,128)(2,1)S(1)}, u32[]{:S(2)}, u32[]{:S(2)}) async-start(bf16[16,72,128]{2,1,0:T(8,128)(2,1)} %pack.1), calls=%async_computation | async-start | bytes 589824 | tf_op jit(solution)/shard_map/all_to_all | solution.py:373
  17.6 16.6 %collective-permute-start.2 = (bf16[288,128]{1,0:T(8,128)(2,1)}, bf16[288,128]{1,0:T(8,128)(2,1)S(1)}, u32[]{:S(2)}, u32[]{:S(2)}) collective-permute-start(bf16[288,128]{1,0:T(8,128)(2,1)} %bitcast.18), channel_id=1, source_target_pairs={{0,3},{1,0},{2,1},{3,2},{4,7},{5,4},{6,5},{7,6},{8,11},{9,8},{10,9... | collective-permute-start | bytes 221192 | tf_op jit(solution)/shard_map/ppermute | solution.py:354
  23.2 16.6 %collective-permute-start.1 = (bf16[288,128]{1,0:T(8,128)(2,1)}, bf16[288,128]{1,0:T(8,128)(2,1)S(1)}, u32[]{:S(2)}, u32[]{:S(2)}) collective-permute-start(bf16[288,128]{1,0:T(8,128)(2,1)} %bitcast.19), channel_id=1, source_target_pairs={{0,2},{1,3},{2,0},{3,1},{4,6},{5,7},{6,4},{7,5},{8,10},{9,11},{10,... | collective-permute-start | bytes 221192 | tf_op jit(solution)/shard_map/ppermute | solution.py:354
  25.2 14.6 %collective-permute-start = (bf16[288,128]{1,0:T(8,128)(2,1)}, bf16[288,128]{1,0:T(8,128)(2,1)S(1)}, u32[]{:S(2)}, u32[]{:S(2)}) collective-permute-start(bf16[288,128]{1,0:T(8,128)(2,1)} %bitcast.20), channel_id=1, source_target_pairs={{0,1},{1,2},{2,3},{3,0},{4,5},{5,6},{6,7},{7,4},{8,9},{9,10},{10,1... | collective-permute-start | bytes 221192 | tf_op jit(solution)/shard_map/ppermute | solution.py:354
  41.2 5.0 %copy-start = (bf16[128,288]{0,1:T(8,128)(2,1)S(1)}, bf16[128,288]{0,1:T(8,128)(2,1)}, u32[]{:S(2)}) copy-start(bf16[128,288]{0,1:T(8,128)(2,1)} %param.5) | copy-start | bytes 221188
  41.2 18.3 %all-to-all-start.1 = ((bf16[4,128,1152]{2,1,0:T(8,128)(2,1)}), bf16[4,128,1152]{2,1,0:T(8,128)(2,1)S(1)}, u32[]{:S(2)}, u32[]{:S(2)}) async-start(bf16[4,128,1152]{2,1,0:T(8,128)(2,1)} %image_unit.1), calls=%async_computation.1 | async-start | bytes 2359296 | tf_op jit(solution)/shard_map/all_to_all | solution.py:384
  46.5 16.1 %collective-permute-start.5 = (bf16[128,1152]{1,0:T(8,128)(2,1)S(1)}, bf16[128,1152]{1,0:T(8,128)(2,1)S(1)}, u32[]{:S(2)}, u32[]{:S(2)}) collective-permute-start(bf16[128,1152]{1,0:T(8,128)(2,1)S(1)} %text_unit.1.refs_3_), channel_id=1, source_target_pairs={{0,24},{8,0},{16,8},{24,16},{1,25},{9,1},{17,9},{25,17},{2,26},{10... | collective-permute-start | bytes 884744 | tf_op jit(solution)/shard_map/ppermute | solution.py:354
  51.4 12.8 %collective-permute-start.4 = (bf16[128,1152]{1,0:T(8,128)(2,1)S(1)}, bf16[128,1152]{1,0:T(8,128)(2,1)S(1)}, u32[]{:S(2)}, u32[]{:S(2)}) collective-permute-start(bf16[128,1152]{1,0:T(8,128)(2,1)S(1)} %text_unit.1.refs_3_), channel_id=1, source_target_pairs={{0,16},{8,24},{16,0},{24,8},{1,17},{9,25},{17,1},{25,9},{2,18},{10... | collective-permute-start | bytes 884744 | tf_op jit(solution)/shard_map/ppermute | solution.py:354
  54.0 13.4 %collective-permute-start.3 = (bf16[128,1152]{1,0:T(8,128)(2,1)S(1)}, bf16[128,1152]{1,0:T(8,128)(2,1)S(1)}, u32[]{:S(2)}, u32[]{:S(2)}) collective-permute-start(bf16[128,1152]{1,0:T(8,128)(2,1)S(1)} %text_unit.1.refs_3_), channel_id=1, source_target_pairs={{0,8},{8,16},{16,24},{24,0},{1,9},{9,17},{17,25},{25,1},{2,10},{10... | collective-permute-start | bytes 884744 | tf_op jit(solution)/shard_map/ppermute | solution.py:354
  59.5 10.5 %collective-permute-start.6 = (bf16[512,1152]{1,0:T(8,128)(2,1)S(1)}, bf16[512,1152]{1,0:T(8,128)(2,1)S(1)}, u32[]{:S(2)}, u32[]{:S(2)}) collective-permute-start(bf16[512,1152]{1,0:T(8,128)(2,1)S(1)} %bitcast.14), channel_id=1, source_target_pairs={{0,4},{4,0},{1,5},{5,1},{2,6},{6,2},{3,7},{7,3},{8,12},{12,8},{9,1... | collective-permute-start | bytes 3538952 | tf_op jit(solution)/shard_map/ppermute | solution.py:349
  72.6 4.8 %collective-permute-start.7 = (bf16[528,1152]{1,0:T(8,128)(2,1)S(1)}, bf16[528,1152]{1,0:T(8,128)(2,1)S(1)}, u32[]{:S(2)}, u32[]{:S(2)}) collective-permute-start(bf16[528,1152]{1,0:T(8,128)(2,1)S(1)} %get-tuple-element.31), channel_id=1, source_target_pairs={{0,4},{4,0},{1,5},{5,1},{2,6},{6,2},{3,7},{7,3},{8,12},{12,8},{9,1... | collective-permute-start | bytes 3649544 | tf_op jit(solution)/shard_map/ppermute | solution.py:349
  78.7 20.3 %all-to-all-start.2 = ((bf16[4,1168,128]{2,1,0:T(8,128)(2,1)}), bf16[4,1168,128]{2,1,0:T(8,128)(2,1)S(1)}, u32[]{:S(2)}, u32[]{:S(2)}) async-start(bf16[4,1168,128]{2,1,0:T(8,128)(2,1)} %combine.1), calls=%async_computation.2 | async-start | bytes 2392064 | tf_op jit(solution)/shard_map/all_to_all | solution.py:439
  83.5 16.7 %collective-permute-start.8 = (bf16[128,1152]{1,0:T(8,128)(2,1)S(1)}, bf16[128,1152]{1,0:T(8,128)(2,1)S(1)}, u32[]{:S(2)}, u32[]{:S(2)}) collective-permute-start(bf16[128,1152]{1,0:T(8,128)(2,1)S(1)} %get-tuple-element.36), channel_id=1, source_target_pairs={{0,24},{8,0},{16,8},{24,16},{1,25},{9,1},{17,9},{25,17},{2,26},{10... | collective-permute-start | bytes 884744 | tf_op jit(solution)/shard_map/ppermute | solution.py:354
  86.0 14.2 %collective-permute-start.9 = (bf16[128,1152]{1,0:T(8,128)(2,1)S(1)}, bf16[128,1152]{1,0:T(8,128)(2,1)S(1)}, u32[]{:S(2)}, u32[]{:S(2)}) collective-permute-start(bf16[128,1152]{1,0:T(8,128)(2,1)S(1)} %get-tuple-element.37), channel_id=1, source_target_pairs={{0,16},{8,24},{16,0},{24,8},{1,17},{9,25},{17,1},{25,9},{2,18},{10... | collective-permute-start | bytes 884744 | tf_op jit(solution)/shard_map/ppermute | solution.py:354
  88.5 23.2 %collective-permute-start.10 = (bf16[128,1152]{1,0:T(8,128)(2,1)S(1)}, bf16[128,1152]{1,0:T(8,128)(2,1)}, u32[]{:S(2)}, u32[]{:S(2)}) collective-permute-start(bf16[128,1152]{1,0:T(8,128)(2,1)S(1)} %get-tuple-element.40), channel_id=1, source_target_pairs={{0,8},{8,16},{16,24},{24,0},{1,9},{9,17},{17,25},{25,1},{2,10},{10... | collective-permute-start | bytes 884744 | tf_op jit(solution)/shard_map/ppermute | solution.py:354
  100.2 33.9 %all-to-all-start.3 = ((bf16[16,80,128]{2,1,0:T(8,128)(2,1)}), bf16[16,80,128]{2,1,0:T(8,128)(2,1)S(1)}, u32[]{:S(2)}, u32[]{:S(2)}) async-start(bf16[16,80,128]{2,1,0:T(8,128)(2,1)} %hold.1), calls=%async_computation.3 | async-start | bytes 655360 | tf_op jit(solution)/shard_map/all_to_all | solution.py:450
  113.4 25.7 %collective-permute-start.11 = (bf16[288,128]{1,0:T(8,128)(2,1)S(1)}, bf16[288,128]{1,0:T(8,128)(2,1)S(1)}, u32[]{:S(2)}, u32[]{:S(2)}) collective-permute-start(bf16[288,128]{1,0:T(8,128)(2,1)S(1)} %get-tuple-element.42), channel_id=1, source_target_pairs={{0,3},{1,0},{2,1},{3,2},{4,7},{5,4},{6,5},{7,6},{8,11},{9,8},{10,9... | collective-permute-start | bytes 221192 | tf_op jit(solution)/shard_map/ppermute | solution.py:354
  119.1 20.0 %collective-permute-start.12 = (bf16[288,128]{1,0:T(8,128)(2,1)S(1)}, bf16[288,128]{1,0:T(8,128)(2,1)S(1)}, u32[]{:S(2)}, u32[]{:S(2)}) collective-permute-start(bf16[288,128]{1,0:T(8,128)(2,1)S(1)} %get-tuple-element.43), channel_id=1, source_target_pairs={{0,2},{1,3},{2,0},{3,1},{4,6},{5,7},{6,4},{7,5},{8,10},{9,11},{10,... | collective-permute-start | bytes 221192 | tf_op jit(solution)/shard_map/ppermute | solution.py:354
  121.0 18.1 %collective-permute-start.13 = (bf16[288,128]{1,0:T(8,128)(2,1)S(1)}, bf16[288,128]{1,0:T(8,128)(2,1)S(1)}, u32[]{:S(2)}, u32[]{:S(2)}) collective-permute-start(bf16[288,128]{1,0:T(8,128)(2,1)S(1)} %get-tuple-element.44), channel_id=1, source_target_pairs={{0,1},{1,2},{2,3},{3,0},{4,5},{5,6},{6,7},{7,4},{8,9},{9,10},{10,1... | collective-permute-start | bytes 221192 | tf_op jit(solution)/shard_map/ppermute | solution.py:354
  134.9 9.6 %all-to-all-start.4 = ((f32[4,8,128]{2,1,0:T(8,128)}), f32[4,8,128]{2,1,0:T(8,128)S(1)}, u32[]{:S(2)}, u32[]{:S(2)}) async-start(f32[4,8,128]{2,1,0:T(8,128)} %get-tuple-element.38), calls=%async_computation.4 | async-start | bytes 32768 | tf_op jit(solution)/shard_map/all_to_all | solution.py:462

commit v11 on v10

--- a/solution.py
+++ b/solution.py
@@ -149,10 +149,13 @@
     return total([part[:, c : c + lanes] for c in range(0, columns, lanes)])
 
 
-def pair_terms(left, right, scale, bias, same=None):
-    product = lax.dot_general(
+def pair_product(left, right):
+    return lax.dot_general(
         left, right, (((1,), (1,)), ((), ())), preferred_element_type=jnp.float32
     )
+
+
+def pair_terms(product, scale, bias, same=None):
     logits = scale * product + bias
     if same is None:
         grown = jnp.exp(logits)
@@ -161,7 +164,7 @@
         grown = jnp.exp(jnp.where(same, -logits, logits))
         share = grown / (1.0 + grown)
         slope = jnp.where(same, -share, share)
-    quarter = left.shape[0] // 4
+    quarter = product.shape[0] // 4
     a, b, c, d = (grown[k * quarter : (k + 1) * quarter, :] for k in range(4))
     ab = a + (b + a * b)
     cd = c + (d + c * d)
@@ -190,9 +193,8 @@
         row = jnp.where((row >= 0) & (row < piece), row, -1)
         column = lax.broadcasted_iota(jnp.int32, (1, columns), 1) - spot[1]
         same = row == jnp.where(column >= 0, column, -2)
-        weights[here, :], found = pair_terms(
-            left[here, :], right[...], scales[0], scales[1], same
-        )
+        product = pair_product(left[here, :], right[...])
+        weights[here, :], found = pair_terms(product, scales[0], scales[1], same)
         sums.append(found)
     write_sums(sums_out, sums)
 
@@ -202,9 +204,10 @@
     for k, ref in enumerate((t0, t1, t2, t3)):
         right[k * part : (k + 1) * part, :] = ref[...]
     sums = []
+    products = [pair_product(left[k : k + tile, :], right[part:, :]) for k in range(0, rows, tile)]
     for start in range(0, rows, tile):
         here = pl.ds(start, tile)
-        value, found = pair_terms(left[here, :], right[part:, :], scales[0], scales[1])
+        value, found = pair_terms(products[start // tile], scales[0], scales[1])
         weights[here, :part] = home[here, :]
         weights[here, part:] = value
         back[here, :] = jnp.dot(
@@ -216,9 +219,11 @@
 
 def other_kernel(scales, left, right, own_sums, back, weights, sums_out):
     sums = []
-    for start in range(0, left.shape[0], tile):
+    rows = left.shape[0]
+    products = [pair_product(left[k : k + tile, :], right[...]) for k in range(0, rows, tile)]
+    for start in range(0, rows, tile):
         here = pl.ds(start, tile)
-        value, found = pair_terms(left[here, :], right[...], scales[0], scales[1])
+        value, found = pair_terms(products[start // tile], scales[0], scales[1])
         weights[here, :] = value
         back[here, :] = jnp.dot(
             value, right[...], preferred_element_type=jnp.float32
@@ -231,7 +236,6 @@
         value = jnp.where(row == k, jnp.sum(found, axis=0, keepdims=True), value)
     carry = carry_of(value)
     sums_out[...] = carry
-    rows = left.shape[0]
     back[rows:, :lanes] = carry.astype(jnp.bfloat16)
     back[rows:, lanes:] = jnp.zeros((carry_rows, back.shape[1] - lanes), jnp.bfloat16)
 
@@ -326,7 +330,7 @@
     out[...] = value.astype(jnp.bfloat16)
 
 
-def image_last_kernel(arrived, out, sums_out):
+def image_last_kernel(arrived, out):
     values = [wide(arrived, d) for d in range(arrived.shape[0])]
     heads = len(values) // strips
     found = []
@@ -340,9 +344,13 @@
         rows = jnp.concatenate([f[t] for f in found], axis=0).T
         count = lanes if t < 2 else rest
         out[t * lanes : t * lanes + count, :] = rows[:count].astype(jnp.bfloat16)
-    sums = jnp.sum(total([v[:8] for v in values]), axis=1, keepdims=True)
-    for k in range(sums_out.shape[0]):
-        sums_out[k] = jnp.broadcast_to(sums, sums_out.shape[1:])
+
+
+def sums_kernel(arrived, out):
+    value = total([arrived[d].astype(jnp.float32)[:8] for d in range(arrived.shape[0])])
+    value = jnp.sum(value, axis=1, keepdims=True)
+    for k in range(out.shape[0]):
+        out[k] = jnp.broadcast_to(value, out.shape[1:])
 
 
 def swap_core(value):
@@ -371,7 +379,7 @@
     (packed,) = call(pack_kernel, [shape((z_count, chunk_rows, lanes))], "pack", [image.T])
     parts = [text.T] + [shift(text.T, "zl", k) for k in range(1, strips)]
     arrived = lax.all_to_all(packed, ("zh", "zl"), 0, 0)
-    (home_text,) = call(text_unit_kernel, [shape((block, width))], "text_unit", parts)
+    (home_text,) = call(text_unit_kernel, [shape((block, width))], "text_unit", parts, flops=400 * count * block * width)
     texts = [shift(home_text, "y", k) for k in range(1, y_count)]
     (units,) = call(
         image_unit_kernel,
@@ -379,7 +387,7 @@
         "image_unit",
         [arrived],
         scalars=[place],
-        after=parts[1:] + [scales, spot],
+        after=[scales, spot],
     )
     image_rows = lax.all_to_all(units, "x", 0, 0).reshape(count, width)
     other_rows = swap_core(image_rows)
@@ -446,19 +454,14 @@
         flops=200 * count * block * width,
     )
     moved = [text_backs[0]] + [shift(text_backs[k], "y", -k) for k in range(1, y_count)]
-    finished = hold(finished, moved[1:3])
     finished = lax.all_to_all(finished, ("zh", "zl"), 0, 0)
     text_parts = call(
         text_finish_kernel, [shape((strip, rows))] * strips, "text_finish", parts + moved, flops=200 * count * block * width
     )
     given = [text_parts[0]] + [shift(text_parts[k], "zl", -k) for k in range(1, strips)]
     (grad_text,) = call(text_last_kernel, [shape((strip, rows))], "text_last", given)
-    grad_image, sums = call(
-        image_last_kernel,
-        [shape((strip, rows)), shape((y_count, 8, lanes), f32)],
-        "image_last",
-        [finished],
-    )
+    (sums,) = call(sums_kernel, [shape((y_count, 8, lanes), f32)], "sums", [finished])
+    (grad_image,) = call(image_last_kernel, [shape((strip, rows))], "image_last", [finished], after=[sums])
     sums = jnp.sum(lax.all_to_all(sums, "y", 0, 0), axis=0)
     pairs_count = rows * 4 * x_count * y_count * 2
     return (

time: 151 us -> 146 us (0.967)
  waiting for transfers between devices: 41.4 us -> 34.4 us
  local copies, waits for them, and re-layouts: 1.44 us -> 6.89 us
  starting transfers between devices: 83.8 us -> 80.4 us
    ppermute x12, waiting for transfers between devices: 15 us -> 4.77 us  [shift(): lax.ppermute(value, axis, [(i, (i + k) % count) for i in range(count)])]
    all_to_all x1, waiting for transfers between devices: 0.01 us -> 9.56 us  [shards(): arrived = lax.all_to_all(packed, ('zh', 'zl'), 0, 0)]
    unnamed x4 -> x18, local copies, waits for them, and re-layouts: 0.88 us -> 6.3 us
    all_to_all x1, waiting for transfers between devices: 10.1 us -> 7.31 us  [shards(): finished = lax.all_to_all(finished, ('zh', 'zl'), 0, 0)]
    all_to_all x1, waiting for transfers between devices: 2.62 us -> 0.01 us  [shards(): image_rows = lax.all_to_all(units, 'x', 0, 0).reshape(count, width)]
    all_to_all x1, starting transfers between devices: 11.5 us -> 9.03 us  [shards(): finished = lax.all_to_all(finished, ('zh', 'zl'), 0, 0)]
    pallas_call x12 -> x13, Pallas kernels: 16.1 us -> 15.4 us  [call(): pl.pallas_call(body, out_shape=out_shape, in_specs=[smem] * len(scalars)...]
  transfers between devices with their start and end apart: 19 -> 19, of which waited for: 9 -> 7; matrix products, arithmetic and copies ran while one was open for 0% -> 0% of each run, Pallas kernels for 7% -> 7%
where the time goes in v11:
time: 146 us; the launch traced here: 145 us
  starting transfers between devices  80.4 us (55%)
  waiting for transfers between devices  34.4 us (24%)
  Pallas kernels  15.4 us (11%)
  between operations  7.62 us (5%)
  local copies, waits for them, and re-layouts  6.89 us (5%)
    ppermute x12, starting transfers between devices, shift(): lax.ppermute(value, axis, [(i, (i + k) % count) for i in range(count)])  39.4 us
    pallas_call x13, Pallas kernels, call(): pl.pallas_call(body, out_shape=out_shape, in_specs=[smem] * len(scalars)...  15.4 us
    all_to_all x1, starting transfers between devices, shards(): arrived = lax.all_to_all(packed, ('zh', 'zl'), 0, 0)  15.2 us
    all_to_all x1, waiting for transfers between devices, shards(): arrived = lax.all_to_all(packed, ('zh', 'zl'), 0, 0)  9.56 us
    all_to_all x1, starting transfers between devices, shards(): finished = lax.all_to_all(finished, ('zh', 'zl'), 0, 0)  9.03 us
    all_to_all x1, waiting for transfers between devices, shards(): combined = lax.all_to_all(combined, 'x', 0, 0)  7.57 us
    all_to_all x1, waiting for transfers between devices, shards(): finished = lax.all_to_all(finished, ('zh', 'zl'), 0, 0)  7.31 us
    unnamed x18, local copies, waits for them, and re-layouts  6.3 us
  transfers between devices with their start and end apart: 19, of which 7 were waited for; matrix products, arithmetic and copies ran while one was open for 0% of the time, Pallas kernels for 7%

profile of v11, /device:TPU:2, one launch (start us, length us, event | category | flops | bytes accessed | tf_op | source)
XLA Modules:
  0.0 144.9 jit_solution(849791350695518860)
XLA Ops:
  0.6 0.9 copy-done
  1.5 0.9 pack.1
  2.4 15.2 %all-to-all-start = ((bf16[16,72,128]{2,1,0:T(8,128)(2,1)}), bf16[16,72,128]{2,1,0:T(8,128)(2,1)S(1)}, u32[]{:S(2)}, u32[]{:S(2)}) async-start(bf16[16,72,128]{2,1,0:T(8,128)(2,1)} %pack.1), calls=%async_computation | async-start | bytes 589824 | tf_op jit(solution)/shard_map/all_to_all | solution.py:381
  17.6 5.6 %collective-permute-start.2 = (bf16[288,128]{1,0:T(8,128)(2,1)}, bf16[288,128]{1,0:T(8,128)(2,1)S(1)}, u32[]{:S(2)}, u32[]{:S(2)}) collective-permute-start(bf16[288,128]{1,0:T(8,128)(2,1)} %bitcast.19), channel_id=1, source_target_pairs={{0,3},{1,0},{2,1},{3,2},{4,7},{5,4},{6,5},{7,6},{8,11},{9,8},{10,9... | collective-permute-start | bytes 221192 | tf_op jit(solution)/shard_map/ppermute | solution.py:362
  23.3 1.9 %collective-permute-start.1 = (bf16[288,128]{1,0:T(8,128)(2,1)}, bf16[288,128]{1,0:T(8,128)(2,1)S(1)}, u32[]{:S(2)}, u32[]{:S(2)}) collective-permute-start(bf16[288,128]{1,0:T(8,128)(2,1)} %bitcast.20), channel_id=1, source_target_pairs={{0,2},{1,3},{2,0},{3,1},{4,6},{5,7},{6,4},{7,5},{8,10},{9,11},{10,... | collective-permute-start | bytes 221192 | tf_op jit(solution)/shard_map/ppermute | solution.py:362
  25.2 3.0 %collective-permute-start = (bf16[288,128]{1,0:T(8,128)(2,1)}, bf16[288,128]{1,0:T(8,128)(2,1)S(1)}, u32[]{:S(2)}, u32[]{:S(2)}) collective-permute-start(bf16[288,128]{1,0:T(8,128)(2,1)} %bitcast.21), channel_id=1, source_target_pairs={{0,1},{1,2},{2,3},{3,0},{4,5},{5,6},{6,7},{7,4},{8,9},{9,10},{10,1... | collective-permute-start | bytes 221192 | tf_op jit(solution)/shard_map/ppermute | solution.py:362
  29.7 9.6 %all-to-all-done.refs_1_ = bf16[16,72,128]{2,1,0:T(8,128)(2,1)S(1)} async-done(((bf16[16,72,128]{2,1,0:T(8,128)(2,1)}), bf16[16,72,128]{2,1,0:T(8,128)(2,1)S(1)}, u32[]{:S(2)}, u32[]{:S(2)}) %all-to-all-start) | async-done | bytes 294944 | tf_op jit(solution)/shard_map/all_to_all | solution.py:381
  39.3 1.4 image_unit.1
  40.6 5.0 %all-to-all-start.1 = ((bf16[4,128,1152]{2,1,0:T(8,128)(2,1)}), bf16[4,128,1152]{2,1,0:T(8,128)(2,1)S(1)}, u32[]{:S(2)}, u32[]{:S(2)}) async-start(bf16[4,128,1152]{2,1,0:T(8,128)(2,1)} %image_unit.1), calls=%async_computation.1 | async-start | bytes 2359296 | tf_op jit(solution)/shard_map/all_to_all | solution.py:392
  45.6 0.4 text_unit.1.refs_3_
  46.0 0.6 copy-done.3
  46.6 0.6 copy-done.5
  47.2 0.6 copy-done.7
  47.9 4.9 %collective-permute-start.5 = (bf16[128,1152]{1,0:T(8,128)(2,1)S(1)}, bf16[128,1152]{1,0:T(8,128)(2,1)S(1)}, u32[]{:S(2)}, u32[]{:S(2)}) collective-permute-start(bf16[128,1152]{1,0:T(8,128)(2,1)S(1)} %text_unit.1.refs_3_), channel_id=1, source_target_pairs={{0,24},{8,0},{16,8},{24,16},{1,25},{9,1},{17,9},{25,17},{2,26},{10... | collective-permute-start | bytes 884744 | tf_op jit(solution)/shard_map/ppermute | solution.py:362
  52.8 2.5 %collective-permute-start.4 = (bf16[128,1152]{1,0:T(8,128)(2,1)S(1)}, bf16[128,1152]{1,0:T(8,128)(2,1)S(1)}, u32[]{:S(2)}, u32[]{:S(2)}) collective-permute-start(bf16[128,1152]{1,0:T(8,128)(2,1)S(1)} %text_unit.1.refs_3_), channel_id=1, source_target_pairs={{0,16},{8,24},{16,0},{24,8},{1,17},{9,25},{17,1},{25,9},{2,18},{10... | collective-permute-start | bytes 884744 | tf_op jit(solution)/shard_map/ppermute | solution.py:362
  55.3 2.9 %collective-permute-start.3 = (bf16[128,1152]{1,0:T(8,128)(2,1)S(1)}, bf16[128,1152]{1,0:T(8,128)(2,1)S(1)}, u32[]{:S(2)}, u32[]{:S(2)}) collective-permute-start(bf16[128,1152]{1,0:T(8,128)(2,1)S(1)} %text_unit.1.refs_3_), channel_id=1, source_target_pairs={{0,8},{8,16},{16,24},{24,0},{1,9},{9,17},{17,25},{25,1},{2,10},{10... | collective-permute-start | bytes 884744 | tf_op jit(solution)/shard_map/ppermute | solution.py:362
  58.2 1.9 %collective-permute-start.6 = (bf16[512,1152]{1,0:T(8,128)(2,1)S(1)}, bf16[512,1152]{1,0:T(8,128)(2,1)S(1)}, u32[]{:S(2)}, u32[]{:S(2)}) collective-permute-start(bf16[512,1152]{1,0:T(8,128)(2,1)S(1)} %bitcast.14), channel_id=1, source_target_pairs={{0,4},{4,0},{1,5},{5,1},{2,6},{6,2},{3,7},{7,3},{8,12},{12,8},{9,1... | collective-permute-start | bytes 3538952 | tf_op jit(solution)/shard_map/ppermute | solution.py:357
  60.2 1.1 home.1
  61.3 1.7 %collective-permute-done.4.refs_4_ = bf16[128,1152]{1,0:T(8,128)(2,1)S(1)} collective-permute-done((bf16[128,1152]{1,0:T(8,128)(2,1)S(1)}, bf16[128,1152]{1,0:T(8,128)(2,1)S(1)}, u32[]{:S(2)}, u32[]{:S(2)}) %collective-permute-start.4) | collective-permute-done | bytes 294944 | tf_op jit(solution)/shard_map/ppermute | solution.py:362
  63.0 3.1 %collective-permute-done.3.refs_3_ = bf16[128,1152]{1,0:T(8,128)(2,1)S(1)} collective-permute-done((bf16[128,1152]{1,0:T(8,128)(2,1)S(1)}, bf16[128,1152]{1,0:T(8,128)(2,1)S(1)}, u32[]{:S(2)}, u32[]{:S(2)}) %collective-permute-start.3) | collective-permute-done | bytes 294944 | tf_op jit(solution)/shard_map/ppermute | solution.py:362
  66.1 2.2 %own.1 = (bf16[512,1152]{1,0:T(8,128)(2,1)S(1)}, bf16[512,512]{1,0:T(8,128)(2,1)S(1)}, bf16[512,1152]{1,0:T(8,128)(2,1)S(1)}, f32[24,128]{1,0:T(8,128)S(1)}) custom-call(f32[2]{0:T(128)S(1)} %pad_maximum_fusion.refs_2_.refs_0_, bf16[512,1152]{1,0:T(8,128)(2,1)S(1)} %bitcast.16, bf16[128,1152]{1,0:T(8,128)(2,1)S(1)} %get-tuple-element.23.refs_2_, ...), custom_call_target="tpu_custom_call" | custom-call | flops 1207959552 | bytes 5398528 | tf_op jit(solution)/shard_map/own/pallas_call | solution.py:38
  68.3 2.4 %other.1 = (bf16[528,1152]{1,0:T(8,128)(2,1)S(1)}, bf16[512,512]{1,0:T(8,128)(2,1)S(1)}, f32[16,128]{1,0:T(8,128)S(1)}) custom-call(f32[2]{0:T(128)S(1)} %pad_maximum_fusion.refs_2_.refs_0_, bf16[512,1152]{1,0:T(8,128)(2,1)S(1)} %collective-permute-done.6.refs_1_.refs_3_, bf16[512,1152]{1,0:T(8,128)(2,1)S(1)} %get-tuple-element.27.refs_2_, ...), custom_call_target="tpu_custom_call" | custom-call | flops 1207959552 | bytes 4120576 | tf_op jit(solution)/shard_map/other/pallas_call | solution.py:38
  70.8 1.9 %collective-permute-start.7 = (bf16[528,1152]{1,0:T(8,128)(2,1)S(1)}, bf16[528,1152]{1,0:T(8,128)(2,1)S(1)}, u32[]{:S(2)}, u32[]{:S(2)}) collective-permute-start(bf16[528,1152]{1,0:T(8,128)(2,1)S(1)} %get-tuple-element.29), channel_id=1, source_target_pairs={{0,4},{4,0},{1,5},{5,1},{2,6},{6,2},{3,7},{7,3},{8,12},{12,8},{9,1... | collective-permute-start | bytes 3649544 | tf_op jit(solution)/shard_map/ppermute | solution.py:357
  72.7 1.6 %text_back.1 = (bf16[128,1152]{1,0:T(8,128)(2,1)S(1)}, bf16[128,1152]{1,0:T(8,128)(2,1)S(1)}, bf16[128,1152]{1,0:T(8,128)(2,1)S(1)}, bf16[128,1152]{1,0:T(8,128)(2,1)S(1)}) custom-call(bf16[512,512]{1,0:T(8,128)(2,1)S(1)} %get-tuple-element.31.refs_0_, bf16[512,512]{1,0:T(8,128)(2,1)S(1)} %get-tuple-element.32.refs_1_, bf16[512,1152]{1,0:T(8,128)(2,1)S(1)} %bitcast.17, ...), custom_call_target="tpu_custom_call" | custom-call | flops 1207959552 | bytes 4587520 | tf_op jit(solution)/shard_map/text_back/pallas_call | solution.py:38
  74.3 1.3 collective-permute-done.7.refs_1_
  75.6 1.4 combine.1
  76.9 4.8 %all-to-all-start.2 = ((bf16[4,1168,128]{2,1,0:T(8,128)(2,1)}), bf16[4,1168,128]{2,1,0:T(8,128)(2,1)S(1)}, u32[]{:S(2)}, u32[]{:S(2)}) async-start(bf16[4,1168,128]{2,1,0:T(8,128)(2,1)} %combine.1), calls=%async_computation.2 | async-start | bytes 2392064 | tf_op jit(solution)/shard_map/all_to_all | solution.py:447
  81.7 2.5 %collective-permute-start.8 = (bf16[128,1152]{1,0:T(8,128)(2,1)S(1)}, bf16[128,1152]{1,0:T(8,128)(2,1)S(1)}, u32[]{:S(2)}, u32[]{:S(2)}) collective-permute-start(bf16[128,1152]{1,0:T(8,128)(2,1)S(1)} %get-tuple-element.34), channel_id=1, source_target_pairs={{0,24},{8,0},{16,8},{24,16},{1,25},{9,1},{17,9},{25,17},{2,26},{10... | collective-permute-start | bytes 884744 | tf_op jit(solution)/shard_map/ppermute | solution.py:362
  84.2 2.5 %collective-permute-start.9 = (bf16[128,1152]{1,0:T(8,128)(2,1)S(1)}, bf16[128,1152]{1,0:T(8,128)(2,1)S(1)}, u32[]{:S(2)}, u32[]{:S(2)}) collective-permute-start(bf16[128,1152]{1,0:T(8,128)(2,1)S(1)} %get-tuple-element.35), channel_id=1, source_target_pairs={{0,16},{8,24},{16,0},{24,8},{1,17},{9,25},{17,1},{25,9},{2,18},{10... | collective-permute-start | bytes 884744 | tf_op jit(solution)/shard_map/ppermute | solution.py:362
  86.7 2.9 %collective-permute-start.10 = (bf16[128,1152]{1,0:T(8,128)(2,1)S(1)}, bf16[128,1152]{1,0:T(8,128)(2,1)S(1)}, u32[]{:S(2)}, u32[]{:S(2)}) collective-permute-start(bf16[128,1152]{1,0:T(8,128)(2,1)S(1)} %get-tuple-element.36), channel_id=1, source_target_pairs={{0,8},{8,16},{16,24},{24,0},{1,9},{9,17},{17,25},{25,1},{2,10},{10... | collective-permute-start | bytes 884744 | tf_op jit(solution)/shard_map/ppermute | solution.py:362
  89.7 7.6 %all-to-all-done.2.refs_2_ = bf16[4,1168,128]{2,1,0:T(8,128)(2,1)S(1)} async-done(((bf16[4,1168,128]{2,1,0:T(8,128)(2,1)}), bf16[4,1168,128]{2,1,0:T(8,128)(2,1)S(1)}, u32[]{:S(2)}, u32[]{:S(2)}) %all-to-all-start.2) | async-done | bytes 1196064 | tf_op jit(solution)/shard_map/all_to_all | solution.py:447
  97.3 1.2 image_finish.1
  98.4 9.0 %all-to-all-start.3 = ((bf16[16,80,128]{2,1,0:T(8,128)(2,1)}), bf16[16,80,128]{2,1,0:T(8,128)(2,1)S(1)}, u32[]{:S(2)}, u32[]{:S(2)}) async-start(bf16[16,80,128]{2,1,0:T(8,128)(2,1)} %image_finish.1), calls=%async_computation.3 | async-start | bytes 655360 | tf_op jit(solution)/shard_map/all_to_all | solution.py:457
  107.5 0.9 copy-done.2
  108.4 0.9 copy-done.4
  109.3 0.9 copy-done.6
  110.2 0.9 copy-done.8
  111.1 0.7 text_finish.1
  111.7 5.6 %collective-permute-start.11 = (bf16[288,128]{1,0:T(8,128)(2,1)S(1)}, bf16[288,128]{1,0:T(8,128)(2,1)S(1)}, u32[]{:S(2)}, u32[]{:S(2)}) collective-permute-start(bf16[288,128]{1,0:T(8,128)(2,1)S(1)} %get-tuple-element.38), channel_id=1, source_target_pairs={{0,3},{1,0},{2,1},{3,2},{4,7},{5,4},{6,5},{7,6},{8,11},{9,8},{10,9... | collective-permute-start | bytes 221192 | tf_op jit(solution)/shard_map/ppermute | solution.py:362
  117.4 1.9 %collective-permute-start.12 = (bf16[288,128]{1,0:T(8,128)(2,1)S(1)}, bf16[288,128]{1,0:T(8,128)(2,1)S(1)}, u32[]{:S(2)}, u32[]{:S(2)}) collective-permute-start(bf16[288,128]{1,0:T(8,128)(2,1)S(1)} %get-tuple-element.39), channel_id=1, source_target_pairs={{0,2},{1,3},{2,0},{3,1},{4,6},{5,7},{6,4},{7,5},{8,10},{9,11},{10,... | collective-permute-start | bytes 221192 | tf_op jit(solution)/shard_map/ppermute | solution.py:362
  119.3 3.0 %collective-permute-start.13 = (bf16[288,128]{1,0:T(8,128)(2,1)S(1)}, bf16[288,128]{1,0:T(8,128)(2,1)S(1)}, u32[]{:S(2)}, u32[]{:S(2)}) collective-permute-start(bf16[288,128]{1,0:T(8,128)(2,1)S(1)} %get-tuple-element.40), channel_id=1, source_target_pairs={{0,1},{1,2},{2,3},{3,0},{4,5},{5,6},{6,7},{7,4},{8,9},{9,10},{10,1... | collective-permute-start | bytes 221192 | tf_op jit(solution)/shard_map/ppermute | solution.py:362
  122.3 7.3 %all-to-all-done.3.refs_0_ = bf16[16,80,128]{2,1,0:T(8,128)(2,1)S(1)} async-done(((bf16[16,80,128]{2,1,0:T(8,128)(2,1)}), bf16[16,80,128]{2,1,0:T(8,128)(2,1)S(1)}, u32[]{:S(2)}, u32[]{:S(2)}) %all-to-all-start.3) | async-done | bytes 327712 | tf_op jit(solution)/shard_map/all_to_all | solution.py:457
  129.6 0.7 sums.1.refs_1_
  130.3 3.2 %all-to-all-start.4 = ((f32[4,8,128]{2,1,0:T(8,128)}), f32[4,8,128]{2,1,0:T(8,128)S(1)}, u32[]{:S(2)}, u32[]{:S(2)}) async-start(f32[4,8,128]{2,1,0:T(8,128)} %sums.1.refs_1_), calls=%async_computation.4 | async-start | bytes 32768 | tf_op jit(solution)/shard_map/all_to_all | solution.py:465
  133.6 0.7 text_last.1
  134.3 0.8 image_last.1
  135.1 3.8 %all-to-all-done.4 = f32[4,8,128]{2,1,0:T(8,128)S(1)} async-done(((f32[4,8,128]{2,1,0:T(8,128)}), f32[4,8,128]{2,1,0:T(8,128)S(1)}, u32[]{:S(2)}, u32[]{:S(2)}) %all-to-all-start.4) | async-done | bytes 16416 | tf_op jit(solution)/shard_map/all_to_all | solution.py:465
  138.9 0.6 fusion
  (25 shorter events, 0.2 us)
Async XLA Ops:
  0.6 0.9 copy-start
  2.4 36.8 %all-to-all-start = ((bf16[16,72,128]{2,1,0:T(8,128)(2,1)}), bf16[16,72,128]{2,1,0:T(8,128)(2,1)S(1)}, u32[]{:S(2)}, u32[]{:S(2)}) async-start(bf16[16,72,128]{2,1,0:T(8,128)(2,1)} %pack.1), calls=%async_computation | async-start | bytes 589824 | tf_op jit(solution)/shard_map/all_to_all | solution.py:381
  17.6 28.0 %collective-permute-start.2 = (bf16[288,128]{1,0:T(8,128)(2,1)}, bf16[288,128]{1,0:T(8,128)(2,1)S(1)}, u32[]{:S(2)}, u32[]{:S(2)}) collective-permute-start(bf16[288,128]{1,0:T(8,128)(2,1)} %bitcast.19), channel_id=1, source_target_pairs={{0,3},{1,0},{2,1},{3,2},{4,7},{5,4},{6,5},{7,6},{8,11},{9,8},{10,9... | collective-permute-start | bytes 221192 | tf_op jit(solution)/shard_map/ppermute | solution.py:362
  23.3 22.3 %collective-permute-start.1 = (bf16[288,128]{1,0:T(8,128)(2,1)}, bf16[288,128]{1,0:T(8,128)(2,1)S(1)}, u32[]{:S(2)}, u32[]{:S(2)}) collective-permute-start(bf16[288,128]{1,0:T(8,128)(2,1)} %bitcast.20), channel_id=1, source_target_pairs={{0,2},{1,3},{2,0},{3,1},{4,6},{5,7},{6,4},{7,5},{8,10},{9,11},{10,... | collective-permute-start | bytes 221192 | tf_op jit(solution)/shard_map/ppermute | solution.py:362
  25.2 20.4 %collective-permute-start = (bf16[288,128]{1,0:T(8,128)(2,1)}, bf16[288,128]{1,0:T(8,128)(2,1)S(1)}, u32[]{:S(2)}, u32[]{:S(2)}) collective-permute-start(bf16[288,128]{1,0:T(8,128)(2,1)} %bitcast.21), channel_id=1, source_target_pairs={{0,1},{1,2},{2,3},{3,0},{4,5},{5,6},{6,7},{7,4},{8,9},{9,10},{10,1... | collective-permute-start | bytes 221192 | tf_op jit(solution)/shard_map/ppermute | solution.py:362
  40.6 5.0 %copy-start.1 = (bf16[128,288]{0,1:T(8,128)(2,1)S(1)}, bf16[128,288]{0,1:T(8,128)(2,1)}, u32[]{:S(2)}) copy-start(bf16[128,288]{0,1:T(8,128)(2,1)} %param.5) | copy-start | bytes 221188
  40.6 17.6 %all-to-all-start.1 = ((bf16[4,128,1152]{2,1,0:T(8,128)(2,1)}), bf16[4,128,1152]{2,1,0:T(8,128)(2,1)S(1)}, u32[]{:S(2)}, u32[]{:S(2)}) async-start(bf16[4,128,1152]{2,1,0:T(8,128)(2,1)} %image_unit.1), calls=%async_computation.1 | async-start | bytes 2359296 | tf_op jit(solution)/shard_map/all_to_all | solution.py:392
  46.0 0.6 copy-start.3
  46.6 0.6 copy-start.5
  47.2 0.6 copy-start.7
  47.9 13.4 %collective-permute-start.5 = (bf16[128,1152]{1,0:T(8,128)(2,1)S(1)}, bf16[128,1152]{1,0:T(8,128)(2,1)S(1)}, u32[]{:S(2)}, u32[]{:S(2)}) collective-permute-start(bf16[128,1152]{1,0:T(8,128)(2,1)S(1)} %text_unit.1.refs_3_), channel_id=1, source_target_pairs={{0,24},{8,0},{16,8},{24,16},{1,25},{9,1},{17,9},{25,17},{2,26},{10... | collective-permute-start | bytes 884744 | tf_op jit(solution)/shard_map/ppermute | solution.py:362
  52.8 10.2 %collective-permute-start.4 = (bf16[128,1152]{1,0:T(8,128)(2,1)S(1)}, bf16[128,1152]{1,0:T(8,128)(2,1)S(1)}, u32[]{:S(2)}, u32[]{:S(2)}) collective-permute-start(bf16[128,1152]{1,0:T(8,128)(2,1)S(1)} %text_unit.1.refs_3_), channel_id=1, source_target_pairs={{0,16},{8,24},{16,0},{24,8},{1,17},{9,25},{17,1},{25,9},{2,18},{10... | collective-permute-start | bytes 884744 | tf_op jit(solution)/shard_map/ppermute | solution.py:362
  55.3 10.7 %collective-permute-start.3 = (bf16[128,1152]{1,0:T(8,128)(2,1)S(1)}, bf16[128,1152]{1,0:T(8,128)(2,1)S(1)}, u32[]{:S(2)}, u32[]{:S(2)}) collective-permute-start(bf16[128,1152]{1,0:T(8,128)(2,1)S(1)} %text_unit.1.refs_3_), channel_id=1, source_target_pairs={{0,8},{8,16},{16,24},{24,0},{1,9},{9,17},{17,25},{25,1},{2,10},{10... | collective-permute-start | bytes 884744 | tf_op jit(solution)/shard_map/ppermute | solution.py:362
  58.2 10.1 %collective-permute-start.6 = (bf16[512,1152]{1,0:T(8,128)(2,1)S(1)}, bf16[512,1152]{1,0:T(8,128)(2,1)S(1)}, u32[]{:S(2)}, u32[]{:S(2)}) collective-permute-start(bf16[512,1152]{1,0:T(8,128)(2,1)S(1)} %bitcast.14), channel_id=1, source_target_pairs={{0,4},{4,0},{1,5},{5,1},{2,6},{6,2},{3,7},{7,3},{8,12},{12,8},{9,1... | collective-permute-start | bytes 3538952 | tf_op jit(solution)/shard_map/ppermute | solution.py:357
  70.8 4.8 %collective-permute-start.7 = (bf16[528,1152]{1,0:T(8,128)(2,1)S(1)}, bf16[528,1152]{1,0:T(8,128)(2,1)S(1)}, u32[]{:S(2)}, u32[]{:S(2)}) collective-permute-start(bf16[528,1152]{1,0:T(8,128)(2,1)S(1)} %get-tuple-element.29), channel_id=1, source_target_pairs={{0,4},{4,0},{1,5},{5,1},{2,6},{6,2},{3,7},{7,3},{8,12},{12,8},{9,1... | collective-permute-start | bytes 3649544 | tf_op jit(solution)/shard_map/ppermute | solution.py:357
  76.9 20.3 %all-to-all-start.2 = ((bf16[4,1168,128]{2,1,0:T(8,128)(2,1)}), bf16[4,1168,128]{2,1,0:T(8,128)(2,1)S(1)}, u32[]{:S(2)}, u32[]{:S(2)}) async-start(bf16[4,1168,128]{2,1,0:T(8,128)(2,1)} %combine.1), calls=%async_computation.2 | async-start | bytes 2392064 | tf_op jit(solution)/shard_map/all_to_all | solution.py:447
  81.7 25.7 %collective-permute-start.8 = (bf16[128,1152]{1,0:T(8,128)(2,1)S(1)}, bf16[128,1152]{1,0:T(8,128)(2,1)S(1)}, u32[]{:S(2)}, u32[]{:S(2)}) collective-permute-start(bf16[128,1152]{1,0:T(8,128)(2,1)S(1)} %get-tuple-element.34), channel_id=1, source_target_pairs={{0,24},{8,0},{16,8},{24,16},{1,25},{9,1},{17,9},{25,17},{2,26},{10... | collective-permute-start | bytes 884744 | tf_op jit(solution)/shard_map/ppermute | solution.py:362
  84.2 23.3 %collective-permute-start.9 = (bf16[128,1152]{1,0:T(8,128)(2,1)S(1)}, bf16[128,1152]{1,0:T(8,128)(2,1)S(1)}, u32[]{:S(2)}, u32[]{:S(2)}) collective-permute-start(bf16[128,1152]{1,0:T(8,128)(2,1)S(1)} %get-tuple-element.35), channel_id=1, source_target_pairs={{0,16},{8,24},{16,0},{24,8},{1,17},{9,25},{17,1},{25,9},{2,18},{10... | collective-permute-start | bytes 884744 | tf_op jit(solution)/shard_map/ppermute | solution.py:362
  86.7 20.8 %collective-permute-start.10 = (bf16[128,1152]{1,0:T(8,128)(2,1)S(1)}, bf16[128,1152]{1,0:T(8,128)(2,1)S(1)}, u32[]{:S(2)}, u32[]{:S(2)}) collective-permute-start(bf16[128,1152]{1,0:T(8,128)(2,1)S(1)} %get-tuple-element.36), channel_id=1, source_target_pairs={{0,8},{8,16},{16,24},{24,0},{1,9},{9,17},{17,25},{25,1},{2,10},{10... | collective-permute-start | bytes 884744 | tf_op jit(solution)/shard_map/ppermute | solution.py:362
  98.4 31.2 %all-to-all-start.3 = ((bf16[16,80,128]{2,1,0:T(8,128)(2,1)}), bf16[16,80,128]{2,1,0:T(8,128)(2,1)S(1)}, u32[]{:S(2)}, u32[]{:S(2)}) async-start(bf16[16,80,128]{2,1,0:T(8,128)(2,1)} %image_finish.1), calls=%async_computation.3 | async-start | bytes 655360 | tf_op jit(solution)/shard_map/all_to_all | solution.py:457
  107.5 0.9 copy-start.2
  108.4 0.9 copy-start.4
  109.3 0.9 copy-start.6
  110.2 0.9 copy-start.8
  111.7 21.8 %collective-permute-start.11 = (bf16[288,128]{1,0:T(8,128)(2,1)S(1)}, bf16[288,128]{1,0:T(8,128)(2,1)S(1)}, u32[]{:S(2)}, u32[]{:S(2)}) collective-permute-start(bf16[288,128]{1,0:T(8,128)(2,1)S(1)} %get-tuple-element.38), channel_id=1, source_target_pairs={{0,3},{1,0},{2,1},{3,2},{4,7},{5,4},{6,5},{7,6},{8,11},{9,8},{10,9... | collective-permute-start | bytes 221192 | tf_op jit(solution)/shard_map/ppermute | solution.py:362
  117.4 16.2 %collective-permute-start.12 = (bf16[288,128]{1,0:T(8,128)(2,1)S(1)}, bf16[288,128]{1,0:T(8,128)(2,1)S(1)}, u32[]{:S(2)}, u32[]{:S(2)}) collective-permute-start(bf16[288,128]{1,0:T(8,128)(2,1)S(1)} %get-tuple-element.39), channel_id=1, source_target_pairs={{0,2},{1,3},{2,0},{3,1},{4,6},{5,7},{6,4},{7,5},{8,10},{9,11},{10,... | collective-permute-start | bytes 221192 | tf_op jit(solution)/shard_map/ppermute | solution.py:362
  119.3 14.3 %collective-permute-start.13 = (bf16[288,128]{1,0:T(8,128)(2,1)S(1)}, bf16[288,128]{1,0:T(8,128)(2,1)S(1)}, u32[]{:S(2)}, u32[]{:S(2)}) collective-permute-start(bf16[288,128]{1,0:T(8,128)(2,1)S(1)} %get-tuple-element.40), channel_id=1, source_target_pairs={{0,1},{1,2},{2,3},{3,0},{4,5},{5,6},{6,7},{7,4},{8,9},{9,10},{10,1... | collective-permute-start | bytes 221192 | tf_op jit(solution)/shard_map/ppermute | solution.py:362
  130.3 8.6 %all-to-all-start.4 = ((f32[4,8,128]{2,1,0:T(8,128)}), f32[4,8,128]{2,1,0:T(8,128)S(1)}, u32[]{:S(2)}, u32[]{:S(2)}) async-start(f32[4,8,128]{2,1,0:T(8,128)} %sums.1.refs_1_), calls=%async_computation.4 | async-start | bytes 32768 | tf_op jit(solution)/shard_map/all_to_all | solution.py:465

commit v12 on v11

--- a/solution.py
+++ b/solution.py
@@ -135,6 +135,10 @@
         found += [r[:, :lanes], r[:, lanes : 2 * lanes]]
     found.append(jnp.concatenate([r[:, 2 * lanes :] for r in rows], axis=1))
     return units_of(found)
+
+
+def keep_kernel(strip, out):
+    out[...] = strip[...]
 
 
 def text_unit_kernel(p0, p1, p2, p3, out):
@@ -377,7 +381,8 @@
     f32 = jnp.float32
 
     (packed,) = call(pack_kernel, [shape((z_count, chunk_rows, lanes))], "pack", [image.T])
-    parts = [text.T] + [shift(text.T, "zl", k) for k in range(1, strips)]
+    (kept,) = call(keep_kernel, [shape((strip, rows))], "keep", [text.T])
+    parts = [kept] + [shift(text.T, "zl", k) for k in range(1, strips)]
     arrived = lax.all_to_all(packed, ("zh", "zl"), 0, 0)
     (home_text,) = call(text_unit_kernel, [shape((block, width))], "text_unit", parts, flops=400 * count * block * width)
     texts = [shift(home_text, "y", k) for k in range(1, y_count)]
@@ -387,7 +392,7 @@
         "image_unit",
         [arrived],
         scalars=[place],
-        after=[scales, spot],
+        after=[scales, spot, kept],
     )
     image_rows = lax.all_to_all(units, "x", 0, 0).reshape(count, width)
     other_rows = swap_core(image_rows)

time: 146 us -> 144 us (0.986)
  local copies, waits for them, and re-layouts: 6.89 us -> 2.31 us
  waiting for transfers between devices: 34.4 us -> 36.2 us
    unnamed x18 -> x4, local copies, waits for them, and re-layouts: 6.3 us -> 1.76 us
    all_to_all x1, waiting for transfers between devices: 7.31 us -> 10 us  [shards(): finished = lax.all_to_all(finished, ('zh', 'zl'), 0, 0)]
    pallas_call x13 -> x14, Pallas kernels: 15.4 us -> 16.3 us  [call(): pl.pallas_call(body, out_shape=out_shape, in_specs=[smem] * len(scalars)...]
  transfers between devices with their start and end apart: 19 -> 19, of which waited for: 7 -> 7; matrix products, arithmetic and copies ran while one was open for 0% -> 0% of each run, Pallas kernels for 7% -> 8%
where the time goes in v12:
time: 144 us; the launch traced here: 143 us
  starting transfers between devices  80.5 us (56%)
  waiting for transfers between devices  36.2 us (25%)
  Pallas kernels  16.3 us (11%)
  between operations  7.56 us (5%)
  local copies, waits for them, and re-layouts  2.31 us (2%)
    ppermute x12, starting transfers between devices, shift(): lax.ppermute(value, axis, [(i, (i + k) % count) for i in range(count)])  39.4 us
    pallas_call x14, Pallas kernels, call(): pl.pallas_call(body, out_shape=out_shape, in_specs=[smem] * len(scalars)...  16.3 us
    all_to_all x1, starting transfers between devices, shards(): arrived = lax.all_to_all(packed, ('zh', 'zl'), 0, 0)  15.2 us
    all_to_all x1, waiting for transfers between devices, shards(): finished = lax.all_to_all(finished, ('zh', 'zl'), 0, 0)  10 us
    all_to_all x1, starting transfers between devices, shards(): finished = lax.all_to_all(finished, ('zh', 'zl'), 0, 0)  9.16 us
    all_to_all x1, waiting for transfers between devices, shards(): arrived = lax.all_to_all(packed, ('zh', 'zl'), 0, 0)  8.66 us
    all_to_all x1, waiting for transfers between devices, shards(): combined = lax.all_to_all(combined, 'x', 0, 0)  7.57 us
    all_to_all x1, starting transfers between devices, shards(): image_rows = lax.all_to_all(units, 'x', 0, 0).reshape(count, width)  4.82 us
  transfers between devices with their start and end apart: 19, of which 7 were waited for; matrix products, arithmetic and copies ran while one was open for 0% of the time, Pallas kernels for 8%

profile of v12, /device:TPU:2, one launch (start us, length us, event | category | flops | bytes accessed | tf_op | source)
XLA Modules:
  0.0 143.0 jit_solution(2634371282377301118)
XLA Ops:
  0.6 0.9 copy-done.1
  1.5 0.9 pack.1
  2.4 15.2 %all-to-all-start = ((bf16[16,72,128]{2,1,0:T(8,128)(2,1)}), bf16[16,72,128]{2,1,0:T(8,128)(2,1)S(1)}, u32[]{:S(2)}, u32[]{:S(2)}) async-start(bf16[16,72,128]{2,1,0:T(8,128)(2,1)} %pack.1), calls=%async_computation | async-start | bytes 589824 | tf_op jit(solution)/shard_map/all_to_all | solution.py:386
  17.6 5.6 %collective-permute-start.2 = (bf16[288,128]{1,0:T(8,128)(2,1)}, bf16[288,128]{1,0:T(8,128)(2,1)S(1)}, u32[]{:S(2)}, u32[]{:S(2)}) collective-permute-start(bf16[288,128]{1,0:T(8,128)(2,1)} %bitcast.18), channel_id=1, source_target_pairs={{0,3},{1,0},{2,1},{3,2},{4,7},{5,4},{6,5},{7,6},{8,11},{9,8},{10,9... | collective-permute-start | bytes 221192 | tf_op jit(solution)/shard_map/ppermute | solution.py:366
  23.2 1.9 %collective-permute-start.1 = (bf16[288,128]{1,0:T(8,128)(2,1)}, bf16[288,128]{1,0:T(8,128)(2,1)S(1)}, u32[]{:S(2)}, u32[]{:S(2)}) collective-permute-start(bf16[288,128]{1,0:T(8,128)(2,1)} %bitcast.19), channel_id=1, source_target_pairs={{0,2},{1,3},{2,0},{3,1},{4,6},{5,7},{6,4},{7,5},{8,10},{9,11},{10,... | collective-permute-start | bytes 221192 | tf_op jit(solution)/shard_map/ppermute | solution.py:366
  25.2 3.0 %collective-permute-start = (bf16[288,128]{1,0:T(8,128)(2,1)}, bf16[288,128]{1,0:T(8,128)(2,1)S(1)}, u32[]{:S(2)}, u32[]{:S(2)}) collective-permute-start(bf16[288,128]{1,0:T(8,128)(2,1)} %bitcast.20), channel_id=1, source_target_pairs={{0,1},{1,2},{2,3},{3,0},{4,5},{5,6},{6,7},{7,4},{8,9},{9,10},{10,1... | collective-permute-start | bytes 221192 | tf_op jit(solution)/shard_map/ppermute | solution.py:366
  28.2 0.0 copy-start
  28.2 0.9 copy-done
  30.4 0.1 pad_add_fusion.refs_3_.refs_1_
  30.5 0.1 pad_maximum_fusion.refs_2_.refs_0_
  30.6 8.7 %all-to-all-done.refs_1_ = bf16[16,72,128]{2,1,0:T(8,128)(2,1)S(1)} async-done(((bf16[16,72,128]{2,1,0:T(8,128)(2,1)}), bf16[16,72,128]{2,1,0:T(8,128)(2,1)S(1)}, u32[]{:S(2)}, u32[]{:S(2)}) %all-to-all-start) | async-done | bytes 294944 | tf_op jit(solution)/shard_map/all_to_all | solution.py:386
  39.3 1.4 image_unit.1
  40.6 4.8 %all-to-all-start.1 = ((bf16[4,128,1152]{2,1,0:T(8,128)(2,1)}), bf16[4,128,1152]{2,1,0:T(8,128)(2,1)S(1)}, u32[]{:S(2)}, u32[]{:S(2)}) async-start(bf16[4,128,1152]{2,1,0:T(8,128)(2,1)} %image_unit.1), calls=%async_computation.1 | async-start | bytes 2359296 | tf_op jit(solution)/shard_map/all_to_all | solution.py:397
  45.4 0.4 text_unit.1.refs_3_
  45.8 4.9 %collective-permute-start.5 = (bf16[128,1152]{1,0:T(8,128)(2,1)S(1)}, bf16[128,1152]{1,0:T(8,128)(2,1)S(1)}, u32[]{:S(2)}, u32[]{:S(2)}) collective-permute-start(bf16[128,1152]{1,0:T(8,128)(2,1)S(1)} %text_unit.1.refs_3_), channel_id=1, source_target_pairs={{0,24},{8,0},{16,8},{24,16},{1,25},{9,1},{17,9},{25,17},{2,26},{10... | collective-permute-start | bytes 884744 | tf_op jit(solution)/shard_map/ppermute | solution.py:366
  50.8 2.5 %collective-permute-start.4 = (bf16[128,1152]{1,0:T(8,128)(2,1)S(1)}, bf16[128,1152]{1,0:T(8,128)(2,1)S(1)}, u32[]{:S(2)}, u32[]{:S(2)}) collective-permute-start(bf16[128,1152]{1,0:T(8,128)(2,1)S(1)} %text_unit.1.refs_3_), channel_id=1, source_target_pairs={{0,16},{8,24},{16,0},{24,8},{1,17},{9,25},{17,1},{25,9},{2,18},{10... | collective-permute-start | bytes 884744 | tf_op jit(solution)/shard_map/ppermute | solution.py:366
  53.3 2.9 %collective-permute-start.3 = (bf16[128,1152]{1,0:T(8,128)(2,1)S(1)}, bf16[128,1152]{1,0:T(8,128)(2,1)S(1)}, u32[]{:S(2)}, u32[]{:S(2)}) collective-permute-start(bf16[128,1152]{1,0:T(8,128)(2,1)S(1)} %text_unit.1.refs_3_), channel_id=1, source_target_pairs={{0,8},{8,16},{16,24},{24,0},{1,9},{9,17},{17,25},{25,1},{2,10},{10... | collective-permute-start | bytes 884744 | tf_op jit(solution)/shard_map/ppermute | solution.py:366
  56.2 1.9 %collective-permute-start.6 = (bf16[512,1152]{1,0:T(8,128)(2,1)S(1)}, bf16[512,1152]{1,0:T(8,128)(2,1)S(1)}, u32[]{:S(2)}, u32[]{:S(2)}) collective-permute-start(bf16[512,1152]{1,0:T(8,128)(2,1)S(1)} %bitcast.14), channel_id=1, source_target_pairs={{0,4},{4,0},{1,5},{5,1},{2,6},{6,2},{3,7},{7,3},{8,12},{12,8},{9,1... | collective-permute-start | bytes 3538952 | tf_op jit(solution)/shard_map/ppermute | solution.py:361
  58.1 1.1 home.1
  59.3 0.0 collective-permute-done.5.refs_5_
  59.3 1.7 %collective-permute-done.4.refs_4_ = bf16[128,1152]{1,0:T(8,128)(2,1)S(1)} collective-permute-done((bf16[128,1152]{1,0:T(8,128)(2,1)S(1)}, bf16[128,1152]{1,0:T(8,128)(2,1)S(1)}, u32[]{:S(2)}, u32[]{:S(2)}) %collective-permute-start.4) | collective-permute-done | bytes 294944 | tf_op jit(solution)/shard_map/ppermute | solution.py:366
  61.0 3.1 %collective-permute-done.3.refs_3_ = bf16[128,1152]{1,0:T(8,128)(2,1)S(1)} collective-permute-done((bf16[128,1152]{1,0:T(8,128)(2,1)S(1)}, bf16[128,1152]{1,0:T(8,128)(2,1)S(1)}, u32[]{:S(2)}, u32[]{:S(2)}) %collective-permute-start.3) | collective-permute-done | bytes 294944 | tf_op jit(solution)/shard_map/ppermute | solution.py:366
  64.0 2.2 %own.1 = (bf16[512,1152]{1,0:T(8,128)(2,1)S(1)}, bf16[512,512]{1,0:T(8,128)(2,1)S(1)}, bf16[512,1152]{1,0:T(8,128)(2,1)S(1)}, f32[24,128]{1,0:T(8,128)S(1)}) custom-call(f32[2]{0:T(128)S(1)} %pad_maximum_fusion.refs_2_.refs_0_, bf16[512,1152]{1,0:T(8,128)(2,1)S(1)} %bitcast.16, bf16[128,1152]{1,0:T(8,128)(2,1)S(1)} %get-tuple-element.23.refs_2_, ...), custom_call_target="tpu_custom_call" | custom-call | flops 1207959552 | bytes 5398528 | tf_op jit(solution)/shard_map/own/pallas_call | solution.py:38
  66.3 0.0 collective-permute-done.6.refs_1_.refs_3_
  66.3 2.4 %other.1 = (bf16[528,1152]{1,0:T(8,128)(2,1)S(1)}, bf16[512,512]{1,0:T(8,128)(2,1)S(1)}, f32[16,128]{1,0:T(8,128)S(1)}) custom-call(f32[2]{0:T(128)S(1)} %pad_maximum_fusion.refs_2_.refs_0_, bf16[512,1152]{1,0:T(8,128)(2,1)S(1)} %collective-permute-done.6.refs_1_.refs_3_, bf16[512,1152]{1,0:T(8,128)(2,1)S(1)} %get-tuple-element.27.refs_2_, ...), custom_call_target="tpu_custom_call" | custom-call | flops 1207959552 | bytes 4120576 | tf_op jit(solution)/shard_map/other/pallas_call | solution.py:38
  68.7 1.9 %collective-permute-start.7 = (bf16[528,1152]{1,0:T(8,128)(2,1)S(1)}, bf16[528,1152]{1,0:T(8,128)(2,1)S(1)}, u32[]{:S(2)}, u32[]{:S(2)}) collective-permute-start(bf16[528,1152]{1,0:T(8,128)(2,1)S(1)} %get-tuple-element.29), channel_id=1, source_target_pairs={{0,4},{4,0},{1,5},{5,1},{2,6},{6,2},{3,7},{7,3},{8,12},{12,8},{9,1... | collective-permute-start | bytes 3649544 | tf_op jit(solution)/shard_map/ppermute | solution.py:361
  70.6 1.6 %text_back.1 = (bf16[128,1152]{1,0:T(8,128)(2,1)S(1)}, bf16[128,1152]{1,0:T(8,128)(2,1)S(1)}, bf16[128,1152]{1,0:T(8,128)(2,1)S(1)}, bf16[128,1152]{1,0:T(8,128)(2,1)S(1)}) custom-call(bf16[512,512]{1,0:T(8,128)(2,1)S(1)} %get-tuple-element.31.refs_0_, bf16[512,512]{1,0:T(8,128)(2,1)S(1)} %get-tuple-element.32.refs_1_, bf16[512,1152]{1,0:T(8,128)(2,1)S(1)} %bitcast.17, ...), custom_call_target="tpu_custom_call" | custom-call | flops 1207959552 | bytes 4587520 | tf_op jit(solution)/shard_map/text_back/pallas_call | solution.py:38
  72.2 1.3 collective-permute-done.7.refs_1_
  73.5 1.4 combine.1
  74.9 4.8 %all-to-all-start.2 = ((bf16[4,1168,128]{2,1,0:T(8,128)(2,1)}), bf16[4,1168,128]{2,1,0:T(8,128)(2,1)S(1)}, u32[]{:S(2)}, u32[]{:S(2)}) async-start(bf16[4,1168,128]{2,1,0:T(8,128)(2,1)} %combine.1), calls=%async_computation.2 | async-start | bytes 2392064 | tf_op jit(solution)/shard_map/all_to_all | solution.py:452
  79.7 2.5 %collective-permute-start.8 = (bf16[128,1152]{1,0:T(8,128)(2,1)S(1)}, bf16[128,1152]{1,0:T(8,128)(2,1)S(1)}, u32[]{:S(2)}, u32[]{:S(2)}) collective-permute-start(bf16[128,1152]{1,0:T(8,128)(2,1)S(1)} %get-tuple-element.34), channel_id=1, source_target_pairs={{0,24},{8,0},{16,8},{24,16},{1,25},{9,1},{17,9},{25,17},{2,26},{10... | collective-permute-start | bytes 884744 | tf_op jit(solution)/shard_map/ppermute | solution.py:366
  82.2 2.5 %collective-permute-start.9 = (bf16[128,1152]{1,0:T(8,128)(2,1)S(1)}, bf16[128,1152]{1,0:T(8,128)(2,1)S(1)}, u32[]{:S(2)}, u32[]{:S(2)}) collective-permute-start(bf16[128,1152]{1,0:T(8,128)(2,1)S(1)} %get-tuple-element.35), channel_id=1, source_target_pairs={{0,16},{8,24},{16,0},{24,8},{1,17},{9,25},{17,1},{25,9},{2,18},{10... | collective-permute-start | bytes 884744 | tf_op jit(solution)/shard_map/ppermute | solution.py:366
  84.7 2.9 %collective-permute-start.10 = (bf16[128,1152]{1,0:T(8,128)(2,1)S(1)}, bf16[128,1152]{1,0:T(8,128)(2,1)}, u32[]{:S(2)}, u32[]{:S(2)}) collective-permute-start(bf16[128,1152]{1,0:T(8,128)(2,1)S(1)} %get-tuple-element.36), channel_id=1, source_target_pairs={{0,8},{8,16},{16,24},{24,0},{1,9},{9,17},{17,25},{25,1},{2,10},{10... | collective-permute-start | bytes 884744 | tf_op jit(solution)/shard_map/ppermute | solution.py:366
  87.6 7.6 %all-to-all-done.2.refs_2_ = bf16[4,1168,128]{2,1,0:T(8,128)(2,1)S(1)} async-done(((bf16[4,1168,128]{2,1,0:T(8,128)(2,1)}), bf16[4,1168,128]{2,1,0:T(8,128)(2,1)S(1)}, u32[]{:S(2)}, u32[]{:S(2)}) %all-to-all-start.2) | async-done | bytes 1196064 | tf_op jit(solution)/shard_map/all_to_all | solution.py:452
  95.2 1.2 image_finish.1
  96.4 9.2 %all-to-all-start.3 = ((bf16[16,80,128]{2,1,0:T(8,128)(2,1)}), bf16[16,80,128]{2,1,0:T(8,128)(2,1)S(1)}, u32[]{:S(2)}, u32[]{:S(2)}) async-start(bf16[16,80,128]{2,1,0:T(8,128)(2,1)} %image_finish.1), calls=%async_computation.3 | async-start | bytes 655360 | tf_op jit(solution)/shard_map/all_to_all | solution.py:462
  105.6 0.0 collective-permute-done.8.refs_5_
  105.6 1.6 %text_finish.1 = (bf16[288,128]{1,0:T(8,128)(2,1)S(1)}, bf16[288,128]{1,0:T(8,128)(2,1)S(1)}, bf16[288,128]{1,0:T(8,128)(2,1)S(1)}, bf16[288,128]{1,0:T(8,128)(2,1)S(1)}) custom-call(bf16[288,128]{1,0:T(8,128)(2,1)S(1)} %keep.1.refs_4_.refs_0_, bf16[288,128]{1,0:T(8,128)(2,1)S(1)} %collective-permute-done.refs_1_, ...), custom_call_target="tpu_custom_call" | custom-call | flops 15099494400 | bytes 1769472 | tf_op jit(solution)/shard_map/text_finish/pallas_call | solution.py:38
  107.2 5.6 %collective-permute-start.11 = (bf16[288,128]{1,0:T(8,128)(2,1)S(1)}, bf16[288,128]{1,0:T(8,128)(2,1)S(1)}, u32[]{:S(2)}, u32[]{:S(2)}) collective-permute-start(bf16[288,128]{1,0:T(8,128)(2,1)S(1)} %get-tuple-element.38), channel_id=1, source_target_pairs={{0,3},{1,0},{2,1},{3,2},{4,7},{5,4},{6,5},{7,6},{8,11},{9,8},{10,9... | collective-permute-start | bytes 221192 | tf_op jit(solution)/shard_map/ppermute | solution.py:366
  112.9 1.9 %collective-permute-start.12 = (bf16[288,128]{1,0:T(8,128)(2,1)S(1)}, bf16[288,128]{1,0:T(8,128)(2,1)S(1)}, u32[]{:S(2)}, u32[]{:S(2)}) collective-permute-start(bf16[288,128]{1,0:T(8,128)(2,1)S(1)} %get-tuple-element.39), channel_id=1, source_target_pairs={{0,2},{1,3},{2,0},{3,1},{4,6},{5,7},{6,4},{7,5},{8,10},{9,11},{10,... | collective-permute-start | bytes 221192 | tf_op jit(solution)/shard_map/ppermute | solution.py:366
  114.8 3.0 %collective-permute-start.13 = (bf16[288,128]{1,0:T(8,128)(2,1)S(1)}, bf16[288,128]{1,0:T(8,128)(2,1)S(1)}, u32[]{:S(2)}, u32[]{:S(2)}) collective-permute-start(bf16[288,128]{1,0:T(8,128)(2,1)S(1)} %get-tuple-element.40), channel_id=1, source_target_pairs={{0,1},{1,2},{2,3},{3,0},{4,5},{5,6},{6,7},{7,4},{8,9},{9,10},{10,1... | collective-permute-start | bytes 221192 | tf_op jit(solution)/shard_map/ppermute | solution.py:366
  117.8 10.0 %all-to-all-done.3.refs_0_ = bf16[16,80,128]{2,1,0:T(8,128)(2,1)S(1)} async-done(((bf16[16,80,128]{2,1,0:T(8,128)(2,1)}), bf16[16,80,128]{2,1,0:T(8,128)(2,1)S(1)}, u32[]{:S(2)}, u32[]{:S(2)}) %all-to-all-start.3) | async-done | bytes 327712 | tf_op jit(solution)/shard_map/all_to_all | solution.py:462
  127.9 0.7 sums.1.refs_1_
  128.6 3.2 %all-to-all-start.4 = ((f32[4,8,128]{2,1,0:T(8,128)}), f32[4,8,128]{2,1,0:T(8,128)S(1)}, u32[]{:S(2)}, u32[]{:S(2)}) async-start(f32[4,8,128]{2,1,0:T(8,128)} %sums.1.refs_1_), calls=%async_computation.4 | async-start | bytes 32768 | tf_op jit(solution)/shard_map/all_to_all | solution.py:470
  131.8 0.7 text_last.1
  132.5 0.8 image_last.1
  133.3 3.8 %all-to-all-done.4 = f32[4,8,128]{2,1,0:T(8,128)S(1)} async-done(((f32[4,8,128]{2,1,0:T(8,128)}), f32[4,8,128]{2,1,0:T(8,128)S(1)}, u32[]{:S(2)}, u32[]{:S(2)}) %all-to-all-start.4) | async-done | bytes 16416 | tf_op jit(solution)/shard_map/all_to_all | solution.py:470
  137.2 0.5 fusion
  (12 shorter events, 0.0 us)
Async XLA Ops:
  0.6 0.9 copy-start.1
  2.4 36.8 %all-to-all-start = ((bf16[16,72,128]{2,1,0:T(8,128)(2,1)}), bf16[16,72,128]{2,1,0:T(8,128)(2,1)S(1)}, u32[]{:S(2)}, u32[]{:S(2)}) async-start(bf16[16,72,128]{2,1,0:T(8,128)(2,1)} %pack.1), calls=%async_computation | async-start | bytes 589824 | tf_op jit(solution)/shard_map/all_to_all | solution.py:386
  17.6 27.8 %collective-permute-start.2 = (bf16[288,128]{1,0:T(8,128)(2,1)}, bf16[288,128]{1,0:T(8,128)(2,1)S(1)}, u32[]{:S(2)}, u32[]{:S(2)}) collective-permute-start(bf16[288,128]{1,0:T(8,128)(2,1)} %bitcast.18), channel_id=1, source_target_pairs={{0,3},{1,0},{2,1},{3,2},{4,7},{5,4},{6,5},{7,6},{8,11},{9,8},{10,9... | collective-permute-start | bytes 221192 | tf_op jit(solution)/shard_map/ppermute | solution.py:366
  23.2 22.2 %collective-permute-start.1 = (bf16[288,128]{1,0:T(8,128)(2,1)}, bf16[288,128]{1,0:T(8,128)(2,1)S(1)}, u32[]{:S(2)}, u32[]{:S(2)}) collective-permute-start(bf16[288,128]{1,0:T(8,128)(2,1)} %bitcast.19), channel_id=1, source_target_pairs={{0,2},{1,3},{2,0},{3,1},{4,6},{5,7},{6,4},{7,5},{8,10},{9,11},{10,... | collective-permute-start | bytes 221192 | tf_op jit(solution)/shard_map/ppermute | solution.py:366
  25.2 20.3 %collective-permute-start = (bf16[288,128]{1,0:T(8,128)(2,1)}, bf16[288,128]{1,0:T(8,128)(2,1)S(1)}, u32[]{:S(2)}, u32[]{:S(2)}) collective-permute-start(bf16[288,128]{1,0:T(8,128)(2,1)} %bitcast.20), channel_id=1, source_target_pairs={{0,1},{1,2},{2,3},{3,0},{4,5},{5,6},{6,7},{7,4},{8,9},{9,10},{10,1... | collective-permute-start | bytes 221192 | tf_op jit(solution)/shard_map/ppermute | solution.py:366
  28.2 0.9 copy-start
  40.6 15.6 %all-to-all-start.1 = ((bf16[4,128,1152]{2,1,0:T(8,128)(2,1)}), bf16[4,128,1152]{2,1,0:T(8,128)(2,1)S(1)}, u32[]{:S(2)}, u32[]{:S(2)}) async-start(bf16[4,128,1152]{2,1,0:T(8,128)(2,1)} %image_unit.1), calls=%async_computation.1 | async-start | bytes 2359296 | tf_op jit(solution)/shard_map/all_to_all | solution.py:397
  45.8 13.5 %collective-permute-start.5 = (bf16[128,1152]{1,0:T(8,128)(2,1)S(1)}, bf16[128,1152]{1,0:T(8,128)(2,1)S(1)}, u32[]{:S(2)}, u32[]{:S(2)}) collective-permute-start(bf16[128,1152]{1,0:T(8,128)(2,1)S(1)} %text_unit.1.refs_3_), channel_id=1, source_target_pairs={{0,24},{8,0},{16,8},{24,16},{1,25},{9,1},{17,9},{25,17},{2,26},{10... | collective-permute-start | bytes 884744 | tf_op jit(solution)/shard_map/ppermute | solution.py:366
  50.8 10.2 %collective-permute-start.4 = (bf16[128,1152]{1,0:T(8,128)(2,1)S(1)}, bf16[128,1152]{1,0:T(8,128)(2,1)S(1)}, u32[]{:S(2)}, u32[]{:S(2)}) collective-permute-start(bf16[128,1152]{1,0:T(8,128)(2,1)S(1)} %text_unit.1.refs_3_), channel_id=1, source_target_pairs={{0,16},{8,24},{16,0},{24,8},{1,17},{9,25},{17,1},{25,9},{2,18},{10... | collective-permute-start | bytes 884744 | tf_op jit(solution)/shard_map/ppermute | solution.py:366
  53.3 10.7 %collective-permute-start.3 = (bf16[128,1152]{1,0:T(8,128)(2,1)S(1)}, bf16[128,1152]{1,0:T(8,128)(2,1)S(1)}, u32[]{:S(2)}, u32[]{:S(2)}) collective-permute-start(bf16[128,1152]{1,0:T(8,128)(2,1)S(1)} %text_unit.1.refs_3_), channel_id=1, source_target_pairs={{0,8},{8,16},{16,24},{24,0},{1,9},{9,17},{17,25},{25,1},{2,10},{10... | collective-permute-start | bytes 884744 | tf_op jit(solution)/shard_map/ppermute | solution.py:366
  56.2 10.1 %collective-permute-start.6 = (bf16[512,1152]{1,0:T(8,128)(2,1)S(1)}, bf16[512,1152]{1,0:T(8,128)(2,1)S(1)}, u32[]{:S(2)}, u32[]{:S(2)}) collective-permute-start(bf16[512,1152]{1,0:T(8,128)(2,1)S(1)} %bitcast.14), channel_id=1, source_target_pairs={{0,4},{4,0},{1,5},{5,1},{2,6},{6,2},{3,7},{7,3},{8,12},{12,8},{9,1... | collective-permute-start | bytes 3538952 | tf_op jit(solution)/shard_map/ppermute | solution.py:361
  68.7 4.8 %collective-permute-start.7 = (bf16[528,1152]{1,0:T(8,128)(2,1)S(1)}, bf16[528,1152]{1,0:T(8,128)(2,1)S(1)}, u32[]{:S(2)}, u32[]{:S(2)}) collective-permute-start(bf16[528,1152]{1,0:T(8,128)(2,1)S(1)} %get-tuple-element.29), channel_id=1, source_target_pairs={{0,4},{4,0},{1,5},{5,1},{2,6},{6,2},{3,7},{7,3},{8,12},{12,8},{9,1... | collective-permute-start | bytes 3649544 | tf_op jit(solution)/shard_map/ppermute | solution.py:361
  74.9 20.3 %all-to-all-start.2 = ((bf16[4,1168,128]{2,1,0:T(8,128)(2,1)}), bf16[4,1168,128]{2,1,0:T(8,128)(2,1)S(1)}, u32[]{:S(2)}, u32[]{:S(2)}) async-start(bf16[4,1168,128]{2,1,0:T(8,128)(2,1)} %combine.1), calls=%async_computation.2 | async-start | bytes 2392064 | tf_op jit(solution)/shard_map/all_to_all | solution.py:452
  79.7 25.9 %collective-permute-start.8 = (bf16[128,1152]{1,0:T(8,128)(2,1)S(1)}, bf16[128,1152]{1,0:T(8,128)(2,1)S(1)}, u32[]{:S(2)}, u32[]{:S(2)}) collective-permute-start(bf16[128,1152]{1,0:T(8,128)(2,1)S(1)} %get-tuple-element.34), channel_id=1, source_target_pairs={{0,24},{8,0},{16,8},{24,16},{1,25},{9,1},{17,9},{25,17},{2,26},{10... | collective-permute-start | bytes 884744 | tf_op jit(solution)/shard_map/ppermute | solution.py:366
  82.2 23.4 %collective-permute-start.9 = (bf16[128,1152]{1,0:T(8,128)(2,1)S(1)}, bf16[128,1152]{1,0:T(8,128)(2,1)S(1)}, u32[]{:S(2)}, u32[]{:S(2)}) collective-permute-start(bf16[128,1152]{1,0:T(8,128)(2,1)S(1)} %get-tuple-element.35), channel_id=1, source_target_pairs={{0,16},{8,24},{16,0},{24,8},{1,17},{9,25},{17,1},{25,9},{2,18},{10... | collective-permute-start | bytes 884744 | tf_op jit(solution)/shard_map/ppermute | solution.py:366
  84.7 20.9 %collective-permute-start.10 = (bf16[128,1152]{1,0:T(8,128)(2,1)S(1)}, bf16[128,1152]{1,0:T(8,128)(2,1)}, u32[]{:S(2)}, u32[]{:S(2)}) collective-permute-start(bf16[128,1152]{1,0:T(8,128)(2,1)S(1)} %get-tuple-element.36), channel_id=1, source_target_pairs={{0,8},{8,16},{16,24},{24,0},{1,9},{9,17},{17,25},{25,1},{2,10},{10... | collective-permute-start | bytes 884744 | tf_op jit(solution)/shard_map/ppermute | solution.py:366
  96.4 31.5 %all-to-all-start.3 = ((bf16[16,80,128]{2,1,0:T(8,128)(2,1)}), bf16[16,80,128]{2,1,0:T(8,128)(2,1)S(1)}, u32[]{:S(2)}, u32[]{:S(2)}) async-start(bf16[16,80,128]{2,1,0:T(8,128)(2,1)} %image_finish.1), calls=%async_computation.3 | async-start | bytes 655360 | tf_op jit(solution)/shard_map/all_to_all | solution.py:462
  107.2 24.6 %collective-permute-start.11 = (bf16[288,128]{1,0:T(8,128)(2,1)S(1)}, bf16[288,128]{1,0:T(8,128)(2,1)S(1)}, u32[]{:S(2)}, u32[]{:S(2)}) collective-permute-start(bf16[288,128]{1,0:T(8,128)(2,1)S(1)} %get-tuple-element.38), channel_id=1, source_target_pairs={{0,3},{1,0},{2,1},{3,2},{4,7},{5,4},{6,5},{7,6},{8,11},{9,8},{10,9... | collective-permute-start | bytes 221192 | tf_op jit(solution)/shard_map/ppermute | solution.py:366
  112.9 19.0 %collective-permute-start.12 = (bf16[288,128]{1,0:T(8,128)(2,1)S(1)}, bf16[288,128]{1,0:T(8,128)(2,1)S(1)}, u32[]{:S(2)}, u32[]{:S(2)}) collective-permute-start(bf16[288,128]{1,0:T(8,128)(2,1)S(1)} %get-tuple-element.39), channel_id=1, source_target_pairs={{0,2},{1,3},{2,0},{3,1},{4,6},{5,7},{6,4},{7,5},{8,10},{9,11},{10,... | collective-permute-start | bytes 221192 | tf_op jit(solution)/shard_map/ppermute | solution.py:366
  114.8 17.0 %collective-permute-start.13 = (bf16[288,128]{1,0:T(8,128)(2,1)S(1)}, bf16[288,128]{1,0:T(8,128)(2,1)S(1)}, u32[]{:S(2)}, u32[]{:S(2)}) collective-permute-start(bf16[288,128]{1,0:T(8,128)(2,1)S(1)} %get-tuple-element.40), channel_id=1, source_target_pairs={{0,1},{1,2},{2,3},{3,0},{4,5},{5,6},{6,7},{7,4},{8,9},{9,10},{10,1... | collective-permute-start | bytes 221192 | tf_op jit(solution)/shard_map/ppermute | solution.py:366
  128.6 8.6 %all-to-all-start.4 = ((f32[4,8,128]{2,1,0:T(8,128)}), f32[4,8,128]{2,1,0:T(8,128)S(1)}, u32[]{:S(2)}, u32[]{:S(2)}) async-start(f32[4,8,128]{2,1,0:T(8,128)} %sums.1.refs_1_), calls=%async_computation.4 | async-start | bytes 32768 | tf_op jit(solution)/shard_map/all_to_all | solution.py:470

commit v13 on v12

--- a/solution.py
+++ b/solution.py
@@ -26,7 +26,7 @@
     return jax.ShapeDtypeStruct(tuple(dims), dtype)
 
 
-def call(kernel, out_shape, name, operands, scalars=(), after=(), flops=0, special=0, scratch=()):
+def call(kernel, out_shape, name, operands, scalars=(), after=(), flops=0, special=0, scratch=(), out_specs=None):
     out_shape = tuple(out_shape)
     scalars, operands, after = tuple(scalars), tuple(operands), tuple(after)
     inputs = len(scalars) + len(operands)
@@ -39,7 +39,7 @@
         body,
         out_shape=out_shape,
         in_specs=[smem] * len(scalars) + [vmem] * len(operands) + [anywhere] * len(after),
-        out_specs=(vmem,) * len(out_shape),
+        out_specs=out_specs or (vmem,) * len(out_shape),
         scratch_shapes=list(scratch),
         compiler_params=limits,
         cost_estimate=pl.CostEstimate(flops=flops, bytes_accessed=moved, transcendentals=special),
@@ -118,14 +118,21 @@
     return units_of(unpack_rows(chunks, group))
 
 
-def image_unit_kernel(place, arrived, out):
+def image_unit_kernel(place, arrived, out, buffer, semaphores):
     group = lane_group()
+    copies = []
     for h in range(arrived.shape[0] // strips):
         units, _ = image_units(place, arrived, h, group)
+        rows = pl.ds(h * piece, piece)
         for t in range(tiles):
-            value = units[t].astype(jnp.bfloat16)
-            for k in range(out.shape[0]):
-                out[k, h * piece : (h + 1) * piece, t * lanes : (t + 1) * lanes] = value
+            buffer[rows, t * lanes : (t + 1) * lanes] = units[t].astype(jnp.bfloat16)
+        for k in range(out.shape[0]):
+            copies.append(
+                pltpu.make_async_copy(buffer.at[rows], out.at[k, rows], semaphores.at[h, k])
+            )
+            copies[-1].start()
+    for copy in copies:
+        copy.wait()
 
 
 def text_units(parts):
@@ -271,7 +278,8 @@
     return jnp.concatenate([carry, jnp.zeros((8, lanes), jnp.float32)], axis=0)
 
 
-def combine_kernel(own, given, sums, out):
+def combine_kernel(own, given, sums, out, buffer, semaphores):
+    copies = []
     count, all_rows, _ = out.shape
     block = own.shape[0] // count
     carry = sums[...] + wide(given, pl.ds(own.shape[0], carry_rows), pl.ds(0, lanes))
@@ -281,8 +289,12 @@
         for t in range(tiles):
             columns = pl.ds(t * lanes, lanes)
             value = wide(own, rows, columns) + wide(given, rows, columns)
-            out[k, t * block : (t + 1) * block, :] = value.astype(jnp.bfloat16)
-        out[k, tiles * block : all_rows, :] = carry
+            buffer[k, t * block : (t + 1) * block, :] = value.astype(jnp.bfloat16)
+        buffer[k, tiles * block : all_rows, :] = carry
+        copies.append(pltpu.make_async_copy(buffer.at[k], out.at[k], semaphores.at[k]))
+        copies[-1].start()
+    for copy in copies:
+        copy.wait()
 
 
 def grads_of(units, inverse, grads):
@@ -393,6 +405,11 @@
         [arrived],
         scalars=[place],
         after=[scales, spot, kept],
+        scratch=[
+            pltpu.VMEM((block, width), jnp.bfloat16),
+            pltpu.SemaphoreType.DMA((zh_count, x_count)),
+        ],
+        out_specs=(anywhere,),
     )
     image_rows = lax.all_to_all(units, "x", 0, 0).reshape(count, width)
     other_rows = swap_core(image_rows)
@@ -448,6 +465,11 @@
         "combine",
         [own_back, given_back, sums],
         after=text_backs[:1],
+        scratch=[
+            pltpu.VMEM((x_count, tiles * block + carry_rows, lanes), jnp.bfloat16),
+            pltpu.SemaphoreType.DMA((x_count,)),
+        ],
+        out_specs=(anywhere,),
     )
     combined = lax.all_to_all(combined, "x", 0, 0)
     (finished,) = call(

time: 144 us -> 144 us (level)
  no operation moved by 1% of the time
where the time goes in v13:
time: 144 us; the launch traced here: 143 us
  starting transfers between devices  80.4 us (56%)
  waiting for transfers between devices  36.2 us (25%)
  Pallas kernels  16.1 us (11%)
  between operations  7.57 us (5%)
  local copies, waits for them, and re-layouts  2.31 us (2%)
    ppermute x12, starting transfers between devices, shift(): lax.ppermute(value, axis, [(i, (i + k) % count) for i in range(count)])  39.4 us
    pallas_call x14, Pallas kernels, call(): pl.pallas_call(body, out_shape=out_shape, in_specs=[smem] * len(scalars)...  16.1 us
    all_to_all x1, starting transfers between devices, shards(): arrived = lax.all_to_all(packed, ('zh', 'zl'), 0, 0)  15.2 us
    all_to_all x1, waiting for transfers between devices, shards(): finished = lax.all_to_all(finished, ('zh', 'zl'), 0, 0)  10 us
    all_to_all x1, starting transfers between devices, shards(): finished = lax.all_to_all(finished, ('zh', 'zl'), 0, 0)  9.12 us
    all_to_all x1, waiting for transfers between devices, shards(): arrived = lax.all_to_all(packed, ('zh', 'zl'), 0, 0)  8.66 us
    all_to_all x1, waiting for transfers between devices, shards(): combined = lax.all_to_all(combined, 'x', 0, 0)  7.58 us
    all_to_all x1, starting transfers between devices, shards(): image_rows = lax.all_to_all(units, 'x', 0, 0).reshape(count, width)  4.84 us
  transfers between devices with their start and end apart: 19, of which 7 were waited for; matrix products, arithmetic and copies ran while one was open for 0% of the time, Pallas kernels for 8%

profile of v13, /device:TPU:2, one launch (start us, length us, event | category | flops | bytes accessed | tf_op | source)
XLA Modules:
  0.0 142.8 jit_solution(3069105900701691786)
XLA Ops:
  0.6 0.9 copy-done.1
  1.5 0.9 pack.1
  2.4 15.2 %all-to-all-start = ((bf16[16,72,128]{2,1,0:T(8,128)(2,1)}), bf16[16,72,128]{2,1,0:T(8,128)(2,1)S(1)}, u32[]{:S(2)}, u32[]{:S(2)}) async-start(bf16[16,72,128]{2,1,0:T(8,128)(2,1)} %pack.1), calls=%async_computation | async-start | bytes 589824 | tf_op jit(solution)/shard_map/all_to_all | solution.py:398
  17.6 5.6 %collective-permute-start.2 = (bf16[288,128]{1,0:T(8,128)(2,1)}, bf16[288,128]{1,0:T(8,128)(2,1)S(1)}, u32[]{:S(2)}, u32[]{:S(2)}) collective-permute-start(bf16[288,128]{1,0:T(8,128)(2,1)} %bitcast.18), channel_id=1, source_target_pairs={{0,3},{1,0},{2,1},{3,2},{4,7},{5,4},{6,5},{7,6},{8,11},{9,8},{10,9... | collective-permute-start | bytes 221192 | tf_op jit(solution)/shard_map/ppermute | solution.py:378
  23.2 1.9 %collective-permute-start.1 = (bf16[288,128]{1,0:T(8,128)(2,1)}, bf16[288,128]{1,0:T(8,128)(2,1)S(1)}, u32[]{:S(2)}, u32[]{:S(2)}) collective-permute-start(bf16[288,128]{1,0:T(8,128)(2,1)} %bitcast.19), channel_id=1, source_target_pairs={{0,2},{1,3},{2,0},{3,1},{4,6},{5,7},{6,4},{7,5},{8,10},{9,11},{10,... | collective-permute-start | bytes 221192 | tf_op jit(solution)/shard_map/ppermute | solution.py:378
  25.2 3.0 %collective-permute-start = (bf16[288,128]{1,0:T(8,128)(2,1)}, bf16[288,128]{1,0:T(8,128)(2,1)S(1)}, u32[]{:S(2)}, u32[]{:S(2)}) collective-permute-start(bf16[288,128]{1,0:T(8,128)(2,1)} %bitcast.20), channel_id=1, source_target_pairs={{0,1},{1,2},{2,3},{3,0},{4,5},{5,6},{6,7},{7,4},{8,9},{9,10},{10,1... | collective-permute-start | bytes 221192 | tf_op jit(solution)/shard_map/ppermute | solution.py:378
  28.2 0.0 copy-start
  28.2 0.9 copy-done
  30.4 0.1 pad_add_fusion.refs_3_.refs_1_
  30.5 0.1 pad_maximum_fusion.refs_2_.refs_0_
  30.6 8.7 %all-to-all-done.refs_1_ = bf16[16,72,128]{2,1,0:T(8,128)(2,1)S(1)} async-done(((bf16[16,72,128]{2,1,0:T(8,128)(2,1)}), bf16[16,72,128]{2,1,0:T(8,128)(2,1)S(1)}, u32[]{:S(2)}, u32[]{:S(2)}) %all-to-all-start) | async-done | bytes 294944 | tf_op jit(solution)/shard_map/all_to_all | solution.py:398
  39.3 1.4 image_unit.1
  40.6 4.8 %all-to-all-start.1 = ((bf16[4,128,1152]{2,1,0:T(8,128)(2,1)}), bf16[4,128,1152]{2,1,0:T(8,128)(2,1)S(1)}, u32[]{:S(2)}, u32[]{:S(2)}) async-start(bf16[4,128,1152]{2,1,0:T(8,128)(2,1)} %image_unit.1), calls=%async_computation.1 | async-start | bytes 2359296 | tf_op jit(solution)/shard_map/all_to_all | solution.py:414
  45.5 0.0 collective-permute-done.1.refs_2_
  45.5 0.0 collective-permute-done.refs_1_
  45.5 0.4 text_unit.1.refs_3_
  45.9 4.9 %collective-permute-start.5 = (bf16[128,1152]{1,0:T(8,128)(2,1)S(1)}, bf16[128,1152]{1,0:T(8,128)(2,1)S(1)}, u32[]{:S(2)}, u32[]{:S(2)}) collective-permute-start(bf16[128,1152]{1,0:T(8,128)(2,1)S(1)} %text_unit.1.refs_3_), channel_id=1, source_target_pairs={{0,24},{8,0},{16,8},{24,16},{1,25},{9,1},{17,9},{25,17},{2,26},{10... | collective-permute-start | bytes 884744 | tf_op jit(solution)/shard_map/ppermute | solution.py:378
  50.8 2.5 %collective-permute-start.4 = (bf16[128,1152]{1,0:T(8,128)(2,1)S(1)}, bf16[128,1152]{1,0:T(8,128)(2,1)S(1)}, u32[]{:S(2)}, u32[]{:S(2)}) collective-permute-start(bf16[128,1152]{1,0:T(8,128)(2,1)S(1)} %text_unit.1.refs_3_), channel_id=1, source_target_pairs={{0,16},{8,24},{16,0},{24,8},{1,17},{9,25},{17,1},{25,9},{2,18},{10... | collective-permute-start | bytes 884744 | tf_op jit(solution)/shard_map/ppermute | solution.py:378
  53.3 2.9 %collective-permute-start.3 = (bf16[128,1152]{1,0:T(8,128)(2,1)S(1)}, bf16[128,1152]{1,0:T(8,128)(2,1)S(1)}, u32[]{:S(2)}, u32[]{:S(2)}) collective-permute-start(bf16[128,1152]{1,0:T(8,128)(2,1)S(1)} %text_unit.1.refs_3_), channel_id=1, source_target_pairs={{0,8},{8,16},{16,24},{24,0},{1,9},{9,17},{17,25},{25,1},{2,10},{10... | collective-permute-start | bytes 884744 | tf_op jit(solution)/shard_map/ppermute | solution.py:378
  56.2 0.0 all-to-all-done.1
  56.2 1.9 %collective-permute-start.6 = (bf16[512,1152]{1,0:T(8,128)(2,1)S(1)}, bf16[512,1152]{1,0:T(8,128)(2,1)S(1)}, u32[]{:S(2)}, u32[]{:S(2)}) collective-permute-start(bf16[512,1152]{1,0:T(8,128)(2,1)S(1)} %bitcast.14), channel_id=1, source_target_pairs={{0,4},{4,0},{1,5},{5,1},{2,6},{6,2},{3,7},{7,3},{8,12},{12,8},{9,1... | collective-permute-start | bytes 3538952 | tf_op jit(solution)/shard_map/ppermute | solution.py:373
  58.2 1.1 home.1
  59.3 1.7 %collective-permute-done.4.refs_4_ = bf16[128,1152]{1,0:T(8,128)(2,1)S(1)} collective-permute-done((bf16[128,1152]{1,0:T(8,128)(2,1)S(1)}, bf16[128,1152]{1,0:T(8,128)(2,1)S(1)}, u32[]{:S(2)}, u32[]{:S(2)}) %collective-permute-start.4) | collective-permute-done | bytes 294944 | tf_op jit(solution)/shard_map/ppermute | solution.py:378
  61.0 3.1 %collective-permute-done.3.refs_3_ = bf16[128,1152]{1,0:T(8,128)(2,1)S(1)} collective-permute-done((bf16[128,1152]{1,0:T(8,128)(2,1)S(1)}, bf16[128,1152]{1,0:T(8,128)(2,1)S(1)}, u32[]{:S(2)}, u32[]{:S(2)}) %collective-permute-start.3) | collective-permute-done | bytes 294944 | tf_op jit(solution)/shard_map/ppermute | solution.py:378
  64.1 2.2 %own.1 = (bf16[512,1152]{1,0:T(8,128)(2,1)S(1)}, bf16[512,512]{1,0:T(8,128)(2,1)S(1)}, bf16[512,1152]{1,0:T(8,128)(2,1)S(1)}, f32[24,128]{1,0:T(8,128)S(1)}) custom-call(f32[2]{0:T(128)S(1)} %pad_maximum_fusion.refs_2_.refs_0_, bf16[512,1152]{1,0:T(8,128)(2,1)S(1)} %bitcast.16, bf16[128,1152]{1,0:T(8,128)(2,1)S(1)} %get-tuple-element.23.refs_2_, ...), custom_call_target="tpu_custom_call" | custom-call | flops 1207959552 | bytes 5398528 | tf_op jit(solution)/shard_map/own/pallas_call | solution.py:38
  66.3 2.4 %other.1 = (bf16[528,1152]{1,0:T(8,128)(2,1)S(1)}, bf16[512,512]{1,0:T(8,128)(2,1)S(1)}, f32[16,128]{1,0:T(8,128)S(1)}) custom-call(f32[2]{0:T(128)S(1)} %pad_maximum_fusion.refs_2_.refs_0_, bf16[512,1152]{1,0:T(8,128)(2,1)S(1)} %collective-permute-done.6.refs_1_.refs_3_, bf16[512,1152]{1,0:T(8,128)(2,1)S(1)} %get-tuple-element.27.refs_2_, ...), custom_call_target="tpu_custom_call" | custom-call | flops 1207959552 | bytes 4120576 | tf_op jit(solution)/shard_map/other/pallas_call | solution.py:38
  68.8 1.9 %collective-permute-start.7 = (bf16[528,1152]{1,0:T(8,128)(2,1)S(1)}, bf16[528,1152]{1,0:T(8,128)(2,1)S(1)}, u32[]{:S(2)}, u32[]{:S(2)}) collective-permute-start(bf16[528,1152]{1,0:T(8,128)(2,1)S(1)} %get-tuple-element.29), channel_id=1, source_target_pairs={{0,4},{4,0},{1,5},{5,1},{2,6},{6,2},{3,7},{7,3},{8,12},{12,8},{9,1... | collective-permute-start | bytes 3649544 | tf_op jit(solution)/shard_map/ppermute | solution.py:373
  70.7 1.6 %text_back.1 = (bf16[128,1152]{1,0:T(8,128)(2,1)S(1)}, bf16[128,1152]{1,0:T(8,128)(2,1)S(1)}, bf16[128,1152]{1,0:T(8,128)(2,1)S(1)}, bf16[128,1152]{1,0:T(8,128)(2,1)S(1)}) custom-call(bf16[512,512]{1,0:T(8,128)(2,1)S(1)} %get-tuple-element.31.refs_0_, bf16[512,512]{1,0:T(8,128)(2,1)S(1)} %get-tuple-element.32.refs_1_, bf16[512,1152]{1,0:T(8,128)(2,1)S(1)} %bitcast.17, ...), custom_call_target="tpu_custom_call" | custom-call | flops 1207959552 | bytes 4587520 | tf_op jit(solution)/shard_map/text_back/pallas_call | solution.py:38
  72.3 1.3 collective-permute-done.7.refs_1_
  73.6 1.2 combine.1
  74.7 4.8 %all-to-all-start.2 = ((bf16[4,1168,128]{2,1,0:T(8,128)(2,1)}), bf16[4,1168,128]{2,1,0:T(8,128)(2,1)S(1)}, u32[]{:S(2)}, u32[]{:S(2)}) async-start(bf16[4,1168,128]{2,1,0:T(8,128)(2,1)} %combine.1), calls=%async_computation.2 | async-start | bytes 2392064 | tf_op jit(solution)/shard_map/all_to_all | solution.py:474
  79.5 2.5 %collective-permute-start.8 = (bf16[128,1152]{1,0:T(8,128)(2,1)S(1)}, bf16[128,1152]{1,0:T(8,128)(2,1)S(1)}, u32[]{:S(2)}, u32[]{:S(2)}) collective-permute-start(bf16[128,1152]{1,0:T(8,128)(2,1)S(1)} %get-tuple-element.34), channel_id=1, source_target_pairs={{0,24},{8,0},{16,8},{24,16},{1,25},{9,1},{17,9},{25,17},{2,26},{10... | collective-permute-start | bytes 884744 | tf_op jit(solution)/shard_map/ppermute | solution.py:378
  82.0 2.5 %collective-permute-start.9 = (bf16[128,1152]{1,0:T(8,128)(2,1)S(1)}, bf16[128,1152]{1,0:T(8,128)(2,1)S(1)}, u32[]{:S(2)}, u32[]{:S(2)}) collective-permute-start(bf16[128,1152]{1,0:T(8,128)(2,1)S(1)} %get-tuple-element.35), channel_id=1, source_target_pairs={{0,16},{8,24},{16,0},{24,8},{1,17},{9,25},{17,1},{25,9},{2,18},{10... | collective-permute-start | bytes 884744 | tf_op jit(solution)/shard_map/ppermute | solution.py:378
  84.6 2.9 %collective-permute-start.10 = (bf16[128,1152]{1,0:T(8,128)(2,1)S(1)}, bf16[128,1152]{1,0:T(8,128)(2,1)}, u32[]{:S(2)}, u32[]{:S(2)}) collective-permute-start(bf16[128,1152]{1,0:T(8,128)(2,1)S(1)} %get-tuple-element.36), channel_id=1, source_target_pairs={{0,8},{8,16},{16,24},{24,0},{1,9},{9,17},{17,25},{25,1},{2,10},{10... | collective-permute-start | bytes 884744 | tf_op jit(solution)/shard_map/ppermute | solution.py:378
  87.5 7.6 %all-to-all-done.2.refs_2_ = bf16[4,1168,128]{2,1,0:T(8,128)(2,1)S(1)} async-done(((bf16[4,1168,128]{2,1,0:T(8,128)(2,1)}), bf16[4,1168,128]{2,1,0:T(8,128)(2,1)S(1)}, u32[]{:S(2)}, u32[]{:S(2)}) %all-to-all-start.2) | async-done | bytes 1196064 | tf_op jit(solution)/shard_map/all_to_all | solution.py:474
  95.1 1.2 image_finish.1
  96.2 9.1 %all-to-all-start.3 = ((bf16[16,80,128]{2,1,0:T(8,128)(2,1)}), bf16[16,80,128]{2,1,0:T(8,128)(2,1)S(1)}, u32[]{:S(2)}, u32[]{:S(2)}) async-start(bf16[16,80,128]{2,1,0:T(8,128)(2,1)} %image_finish.1), calls=%async_computation.3 | async-start | bytes 655360 | tf_op jit(solution)/shard_map/all_to_all | solution.py:484
  105.4 1.6 %text_finish.1 = (bf16[288,128]{1,0:T(8,128)(2,1)S(1)}, bf16[288,128]{1,0:T(8,128)(2,1)S(1)}, bf16[288,128]{1,0:T(8,128)(2,1)S(1)}, bf16[288,128]{1,0:T(8,128)(2,1)S(1)}) custom-call(bf16[288,128]{1,0:T(8,128)(2,1)S(1)} %keep.1.refs_4_.refs_0_, bf16[288,128]{1,0:T(8,128)(2,1)S(1)} %collective-permute-done.refs_1_, ...), custom_call_target="tpu_custom_call" | custom-call | flops 15099494400 | bytes 1769472 | tf_op jit(solution)/shard_map/text_finish/pallas_call | solution.py:38
  107.0 5.6 %collective-permute-start.11 = (bf16[288,128]{1,0:T(8,128)(2,1)S(1)}, bf16[288,128]{1,0:T(8,128)(2,1)S(1)}, u32[]{:S(2)}, u32[]{:S(2)}) collective-permute-start(bf16[288,128]{1,0:T(8,128)(2,1)S(1)} %get-tuple-element.38), channel_id=1, source_target_pairs={{0,3},{1,0},{2,1},{3,2},{4,7},{5,4},{6,5},{7,6},{8,11},{9,8},{10,9... | collective-permute-start | bytes 221192 | tf_op jit(solution)/shard_map/ppermute | solution.py:378
  112.7 1.9 %collective-permute-start.12 = (bf16[288,128]{1,0:T(8,128)(2,1)S(1)}, bf16[288,128]{1,0:T(8,128)(2,1)S(1)}, u32[]{:S(2)}, u32[]{:S(2)}) collective-permute-start(bf16[288,128]{1,0:T(8,128)(2,1)S(1)} %get-tuple-element.39), channel_id=1, source_target_pairs={{0,2},{1,3},{2,0},{3,1},{4,6},{5,7},{6,4},{7,5},{8,10},{9,11},{10,... | collective-permute-start | bytes 221192 | tf_op jit(solution)/shard_map/ppermute | solution.py:378
  114.6 3.0 %collective-permute-start.13 = (bf16[288,128]{1,0:T(8,128)(2,1)S(1)}, bf16[288,128]{1,0:T(8,128)(2,1)S(1)}, u32[]{:S(2)}, u32[]{:S(2)}) collective-permute-start(bf16[288,128]{1,0:T(8,128)(2,1)S(1)} %get-tuple-element.40), channel_id=1, source_target_pairs={{0,1},{1,2},{2,3},{3,0},{4,5},{5,6},{6,7},{7,4},{8,9},{9,10},{10,1... | collective-permute-start | bytes 221192 | tf_op jit(solution)/shard_map/ppermute | solution.py:378
  117.6 10.0 %all-to-all-done.3.refs_0_ = bf16[16,80,128]{2,1,0:T(8,128)(2,1)S(1)} async-done(((bf16[16,80,128]{2,1,0:T(8,128)(2,1)}), bf16[16,80,128]{2,1,0:T(8,128)(2,1)S(1)}, u32[]{:S(2)}, u32[]{:S(2)}) %all-to-all-start.3) | async-done | bytes 327712 | tf_op jit(solution)/shard_map/all_to_all | solution.py:484
  127.7 0.7 sums.1.refs_1_
  128.4 3.2 %all-to-all-start.4 = ((f32[4,8,128]{2,1,0:T(8,128)}), f32[4,8,128]{2,1,0:T(8,128)S(1)}, u32[]{:S(2)}, u32[]{:S(2)}) async-start(f32[4,8,128]{2,1,0:T(8,128)} %sums.1.refs_1_), calls=%async_computation.4 | async-start | bytes 32768 | tf_op jit(solution)/shard_map/all_to_all | solution.py:492
  131.7 0.7 text_last.1
  132.3 0.8 image_last.1
  133.1 3.8 %all-to-all-done.4 = f32[4,8,128]{2,1,0:T(8,128)S(1)} async-done(((f32[4,8,128]{2,1,0:T(8,128)}), f32[4,8,128]{2,1,0:T(8,128)S(1)}, u32[]{:S(2)}, u32[]{:S(2)}) %all-to-all-start.4) | async-done | bytes 16416 | tf_op jit(solution)/shard_map/all_to_all | solution.py:492
  137.0 0.5 fusion
  (12 shorter events, 0.0 us)
Async XLA Ops:
  0.6 0.9 copy-start.1
  2.4 36.8 %all-to-all-start = ((bf16[16,72,128]{2,1,0:T(8,128)(2,1)}), bf16[16,72,128]{2,1,0:T(8,128)(2,1)S(1)}, u32[]{:S(2)}, u32[]{:S(2)}) async-start(bf16[16,72,128]{2,1,0:T(8,128)(2,1)} %pack.1), calls=%async_computation | async-start | bytes 589824 | tf_op jit(solution)/shard_map/all_to_all | solution.py:398
  17.6 27.9 %collective-permute-start.2 = (bf16[288,128]{1,0:T(8,128)(2,1)}, bf16[288,128]{1,0:T(8,128)(2,1)S(1)}, u32[]{:S(2)}, u32[]{:S(2)}) collective-permute-start(bf16[288,128]{1,0:T(8,128)(2,1)} %bitcast.18), channel_id=1, source_target_pairs={{0,3},{1,0},{2,1},{3,2},{4,7},{5,4},{6,5},{7,6},{8,11},{9,8},{10,9... | collective-permute-start | bytes 221192 | tf_op jit(solution)/shard_map/ppermute | solution.py:378
  23.2 22.2 %collective-permute-start.1 = (bf16[288,128]{1,0:T(8,128)(2,1)}, bf16[288,128]{1,0:T(8,128)(2,1)S(1)}, u32[]{:S(2)}, u32[]{:S(2)}) collective-permute-start(bf16[288,128]{1,0:T(8,128)(2,1)} %bitcast.19), channel_id=1, source_target_pairs={{0,2},{1,3},{2,0},{3,1},{4,6},{5,7},{6,4},{7,5},{8,10},{9,11},{10,... | collective-permute-start | bytes 221192 | tf_op jit(solution)/shard_map/ppermute | solution.py:378
  25.2 20.3 %collective-permute-start = (bf16[288,128]{1,0:T(8,128)(2,1)}, bf16[288,128]{1,0:T(8,128)(2,1)S(1)}, u32[]{:S(2)}, u32[]{:S(2)}) collective-permute-start(bf16[288,128]{1,0:T(8,128)(2,1)} %bitcast.20), channel_id=1, source_target_pairs={{0,1},{1,2},{2,3},{3,0},{4,5},{5,6},{6,7},{7,4},{8,9},{9,10},{10,1... | collective-permute-start | bytes 221192 | tf_op jit(solution)/shard_map/ppermute | solution.py:378
  28.2 0.9 copy-start
  40.6 15.6 %all-to-all-start.1 = ((bf16[4,128,1152]{2,1,0:T(8,128)(2,1)}), bf16[4,128,1152]{2,1,0:T(8,128)(2,1)S(1)}, u32[]{:S(2)}, u32[]{:S(2)}) async-start(bf16[4,128,1152]{2,1,0:T(8,128)(2,1)} %image_unit.1), calls=%async_computation.1 | async-start | bytes 2359296 | tf_op jit(solution)/shard_map/all_to_all | solution.py:414
  45.9 13.5 %collective-permute-start.5 = (bf16[128,1152]{1,0:T(8,128)(2,1)S(1)}, bf16[128,1152]{1,0:T(8,128)(2,1)S(1)}, u32[]{:S(2)}, u32[]{:S(2)}) collective-permute-start(bf16[128,1152]{1,0:T(8,128)(2,1)S(1)} %text_unit.1.refs_3_), channel_id=1, source_target_pairs={{0,24},{8,0},{16,8},{24,16},{1,25},{9,1},{17,9},{25,17},{2,26},{10... | collective-permute-start | bytes 884744 | tf_op jit(solution)/shard_map/ppermute | solution.py:378
  50.8 10.2 %collective-permute-start.4 = (bf16[128,1152]{1,0:T(8,128)(2,1)S(1)}, bf16[128,1152]{1,0:T(8,128)(2,1)S(1)}, u32[]{:S(2)}, u32[]{:S(2)}) collective-permute-start(bf16[128,1152]{1,0:T(8,128)(2,1)S(1)} %text_unit.1.refs_3_), channel_id=1, source_target_pairs={{0,16},{8,24},{16,0},{24,8},{1,17},{9,25},{17,1},{25,9},{2,18},{10... | collective-permute-start | bytes 884744 | tf_op jit(solution)/shard_map/ppermute | solution.py:378
  53.3 10.7 %collective-permute-start.3 = (bf16[128,1152]{1,0:T(8,128)(2,1)S(1)}, bf16[128,1152]{1,0:T(8,128)(2,1)S(1)}, u32[]{:S(2)}, u32[]{:S(2)}) collective-permute-start(bf16[128,1152]{1,0:T(8,128)(2,1)S(1)} %text_unit.1.refs_3_), channel_id=1, source_target_pairs={{0,8},{8,16},{16,24},{24,0},{1,9},{9,17},{17,25},{25,1},{2,10},{10... | collective-permute-start | bytes 884744 | tf_op jit(solution)/shard_map/ppermute | solution.py:378
  56.2 10.1 %collective-permute-start.6 = (bf16[512,1152]{1,0:T(8,128)(2,1)S(1)}, bf16[512,1152]{1,0:T(8,128)(2,1)S(1)}, u32[]{:S(2)}, u32[]{:S(2)}) collective-permute-start(bf16[512,1152]{1,0:T(8,128)(2,1)S(1)} %bitcast.14), channel_id=1, source_target_pairs={{0,4},{4,0},{1,5},{5,1},{2,6},{6,2},{3,7},{7,3},{8,12},{12,8},{9,1... | collective-permute-start | bytes 3538952 | tf_op jit(solution)/shard_map/ppermute | solution.py:373
  68.8 4.8 %collective-permute-start.7 = (bf16[528,1152]{1,0:T(8,128)(2,1)S(1)}, bf16[528,1152]{1,0:T(8,128)(2,1)S(1)}, u32[]{:S(2)}, u32[]{:S(2)}) collective-permute-start(bf16[528,1152]{1,0:T(8,128)(2,1)S(1)} %get-tuple-element.29), channel_id=1, source_target_pairs={{0,4},{4,0},{1,5},{5,1},{2,6},{6,2},{3,7},{7,3},{8,12},{12,8},{9,1... | collective-permute-start | bytes 3649544 | tf_op jit(solution)/shard_map/ppermute | solution.py:373
  74.7 20.3 %all-to-all-start.2 = ((bf16[4,1168,128]{2,1,0:T(8,128)(2,1)}), bf16[4,1168,128]{2,1,0:T(8,128)(2,1)S(1)}, u32[]{:S(2)}, u32[]{:S(2)}) async-start(bf16[4,1168,128]{2,1,0:T(8,128)(2,1)} %combine.1), calls=%async_computation.2 | async-start | bytes 2392064 | tf_op jit(solution)/shard_map/all_to_all | solution.py:474
  79.5 25.8 %collective-permute-start.8 = (bf16[128,1152]{1,0:T(8,128)(2,1)S(1)}, bf16[128,1152]{1,0:T(8,128)(2,1)S(1)}, u32[]{:S(2)}, u32[]{:S(2)}) collective-permute-start(bf16[128,1152]{1,0:T(8,128)(2,1)S(1)} %get-tuple-element.34), channel_id=1, source_target_pairs={{0,24},{8,0},{16,8},{24,16},{1,25},{9,1},{17,9},{25,17},{2,26},{10... | collective-permute-start | bytes 884744 | tf_op jit(solution)/shard_map/ppermute | solution.py:378
  82.0 23.4 %collective-permute-start.9 = (bf16[128,1152]{1,0:T(8,128)(2,1)S(1)}, bf16[128,1152]{1,0:T(8,128)(2,1)S(1)}, u32[]{:S(2)}, u32[]{:S(2)}) collective-permute-start(bf16[128,1152]{1,0:T(8,128)(2,1)S(1)} %get-tuple-element.35), channel_id=1, source_target_pairs={{0,16},{8,24},{16,0},{24,8},{1,17},{9,25},{17,1},{25,9},{2,18},{10... | collective-permute-start | bytes 884744 | tf_op jit(solution)/shard_map/ppermute | solution.py:378
  84.6 20.8 %collective-permute-start.10 = (bf16[128,1152]{1,0:T(8,128)(2,1)S(1)}, bf16[128,1152]{1,0:T(8,128)(2,1)}, u32[]{:S(2)}, u32[]{:S(2)}) collective-permute-start(bf16[128,1152]{1,0:T(8,128)(2,1)S(1)} %get-tuple-element.36), channel_id=1, source_target_pairs={{0,8},{8,16},{16,24},{24,0},{1,9},{9,17},{17,25},{25,1},{2,10},{10... | collective-permute-start | bytes 884744 | tf_op jit(solution)/shard_map/ppermute | solution.py:378
  96.2 31.4 %all-to-all-start.3 = ((bf16[16,80,128]{2,1,0:T(8,128)(2,1)}), bf16[16,80,128]{2,1,0:T(8,128)(2,1)S(1)}, u32[]{:S(2)}, u32[]{:S(2)}) async-start(bf16[16,80,128]{2,1,0:T(8,128)(2,1)} %image_finish.1), calls=%async_computation.3 | async-start | bytes 655360 | tf_op jit(solution)/shard_map/all_to_all | solution.py:484
  107.0 24.6 %collective-permute-start.11 = (bf16[288,128]{1,0:T(8,128)(2,1)S(1)}, bf16[288,128]{1,0:T(8,128)(2,1)S(1)}, u32[]{:S(2)}, u32[]{:S(2)}) collective-permute-start(bf16[288,128]{1,0:T(8,128)(2,1)S(1)} %get-tuple-element.38), channel_id=1, source_target_pairs={{0,3},{1,0},{2,1},{3,2},{4,7},{5,4},{6,5},{7,6},{8,11},{9,8},{10,9... | collective-permute-start | bytes 221192 | tf_op jit(solution)/shard_map/ppermute | solution.py:378
  112.7 19.0 %collective-permute-start.12 = (bf16[288,128]{1,0:T(8,128)(2,1)S(1)}, bf16[288,128]{1,0:T(8,128)(2,1)S(1)}, u32[]{:S(2)}, u32[]{:S(2)}) collective-permute-start(bf16[288,128]{1,0:T(8,128)(2,1)S(1)} %get-tuple-element.39), channel_id=1, source_target_pairs={{0,2},{1,3},{2,0},{3,1},{4,6},{5,7},{6,4},{7,5},{8,10},{9,11},{10,... | collective-permute-start | bytes 221192 | tf_op jit(solution)/shard_map/ppermute | solution.py:378
  114.6 17.0 %collective-permute-start.13 = (bf16[288,128]{1,0:T(8,128)(2,1)S(1)}, bf16[288,128]{1,0:T(8,128)(2,1)S(1)}, u32[]{:S(2)}, u32[]{:S(2)}) collective-permute-start(bf16[288,128]{1,0:T(8,128)(2,1)S(1)} %get-tuple-element.40), channel_id=1, source_target_pairs={{0,1},{1,2},{2,3},{3,0},{4,5},{5,6},{6,7},{7,4},{8,9},{9,10},{10,1... | collective-permute-start | bytes 221192 | tf_op jit(solution)/shard_map/ppermute | solution.py:378
  128.4 8.6 %all-to-all-start.4 = ((f32[4,8,128]{2,1,0:T(8,128)}), f32[4,8,128]{2,1,0:T(8,128)S(1)}, u32[]{:S(2)}, u32[]{:S(2)}) async-start(f32[4,8,128]{2,1,0:T(8,128)} %sums.1.refs_1_), calls=%async_computation.4 | async-start | bytes 32768 | tf_op jit(solution)/shard_map/all_to_all | solution.py:492
